TPU v7x, 32 devices: a whole 2x2x4 slice. The times are simulated.
32 devices in a mesh: groups: 1, ep: 32 (over z, y, x, core).
Axes of the slice: x: 2, y: 2, z: 4, core: 2. Of those that a mesh axis runs over, the one named last changes fastest.
Arguments:
- queries: bfloat16 [128, 8, 16, 576], P(('groups', 'ep')), may hold values from -48 to 48
- cache: bfloat16 [128, 384, 576], P(('groups', 'ep')), may hold values from -4 to 4
- drafts: bfloat16 [128, 8, 576], P(('groups', 'ep')), may hold values from -8 to 8
- lengths: int32 [128], P(('groups', 'ep')), may hold values from 96 to 384
- value_up: bfloat16 [16, 512, 128], replicated, may hold values from -0.25 to 0.25
- residual: bfloat16 [1024, 2048], P(('groups', 'ep')), may hold values from -20 to 20
- norm_gain: float32 [2048], replicated, may hold values from 0.5 to 1.5
- w_gate: bfloat16 [32, 2048, 704], P('ep'), may hold values from -0.125 to 0.125
- w_up: bfloat16 [32, 2048, 704], P('ep'), may hold values from -0.125 to 0.125
- w_down: bfloat16 [32, 704, 2048], P('ep'), may hold values from -0.15625 to 0.15625
- routes: int32 [1024, 6], P(('groups', 'ep')), may hold values from 0 to 15, all different within a row; in each aligned block of 32 rows (0 to 31, 32 to 63, ...) at most 14 rows name the same one
- combine_weights: float32 [1024, 6], P(('groups', 'ep')), may hold values from 0.05 to 0.4
Outputs:
- layer_out: bfloat16 [1024, 2048], P(('groups', 'ep'))
Inputs may be any that keep to these rules, and one draw needn't show every extreme that they name: `routes`: among the rows of one device, no expert is named more than 14 times over all slots.
All inputs are finite; a program needn't handle non-finite values.
Results may differ from a plain program's by a relative error of at most 0.0043.
Values may be sent and summed in bfloat16 or wider, within the bound.
No kernel may reach another device: no remote copies, remote signals or barrier semaphores. Data moves between devices by JAX's collectives and lax.ppermute only.
A program may use at most 64 MiB of HBM per device.

v0:
```python
import jax
import jax.numpy as jnp
from jax import lax
from jax.sharding import PartitionSpec as P


def swapped(value, axis, apart):
    mask = 2**apart
    pairs = [(source, source ^ mask) for source in range(lax.axis_size(axis))]
    return lax.ppermute(value, axis, pairs)


def attend(queries, cache, drafts, lengths, value_up):
    reqs, draft, heads, width = queries.shape
    latent = value_up.shape[1]
    scale = (value_up.shape[2] + width - latent) ** (-0.5)
    cached = (
        jnp.einsum("rjhk,rck->rjhc", queries, cache, preferred_element_type=jnp.float32) * scale
    )
    own = jnp.einsum("rjhk,rik->rjhi", queries, drafts, preferred_element_type=jnp.float32) * scale
    visible = (jnp.arange(cache.shape[1], dtype=jnp.int32)[None, :] < lengths[:, None])[
        :, None, None, :
    ]
    causal = (
        jnp.arange(draft, dtype=jnp.int32)[None, :] <= jnp.arange(draft, dtype=jnp.int32)[:, None]
    )[None, :, None, :]
    cached = jnp.where(visible, cached, -1e30)
    own = jnp.where(causal, own, -1e30)
    highest = jnp.maximum(
        jnp.max(cached, axis=-1, keepdims=True), jnp.max(own, axis=-1, keepdims=True)
    )
    e_cached = jnp.where(visible, jnp.exp(cached - highest), 0.0)
    e_own = jnp.where(causal, jnp.exp(own - highest), 0.0)
    total = jnp.sum(e_cached, axis=-1, keepdims=True) + jnp.sum(e_own, axis=-1, keepdims=True)
    p_cached = (e_cached / total).astype(jnp.bfloat16)
    p_own = (e_own / total).astype(jnp.bfloat16)
    mixed = jnp.einsum(
        "rjhc,rcl->rjhl", p_cached, cache[..., :latent], preferred_element_type=jnp.float32
    )
    mixed = mixed + jnp.einsum(
        "rjhi,ril->rjhl", p_own, drafts[..., :latent], preferred_element_type=jnp.float32
    )
    mixed = mixed.astype(jnp.bfloat16)
    heads_out = jnp.einsum("rjhl,hlv->rjhv", mixed, value_up, preferred_element_type=jnp.float32)
    return heads_out.reshape(reqs * draft, heads * value_up.shape[2])


def local(
    queries,
    cache,
    drafts,
    lengths,
    value_up,
    residual,
    norm_gain,
    w_gate,
    w_up,
    w_down,
    routes,
    combine_weights,
):
    attended = attend(queries, cache, drafts, lengths, value_up)
    stream = residual.astype(jnp.float32) + attended
    normed = (
        stream * lax.rsqrt(jnp.mean(stream * stream, axis=-1, keepdims=True) + 1e-06) * norm_gain
    ).astype(jnp.bfloat16)
    tokens, width = normed.shape
    top = routes.shape[1]
    devices = lax.axis_size("ep")
    experts = devices // 2
    capacity = min(tokens, 2 * (((tokens * top + experts - 1) // experts + 3) // 2))
    flat = routes.reshape(-1)
    onehot = (flat[:, None] == jnp.arange(experts, dtype=jnp.int32)[None, :]).astype(jnp.int32)
    rank = jnp.cumsum(onehot, axis=0) - onehot
    slot = jnp.sum(rank * onehot, axis=-1)
    position = (flat * capacity + slot).reshape(tokens, top)
    select = jnp.any(
        position[None, :, :] == jnp.arange(experts * capacity, dtype=jnp.int32)[:, None, None],
        axis=-1,
    ).astype(jnp.bfloat16)
    outgoing = (
        jnp.dot(select, normed, preferred_element_type=jnp.float32)
        .astype(jnp.bfloat16)
        .reshape(experts, capacity, width)
    )
    core = lax.axis_index("ep") % 2
    doubled = jnp.broadcast_to(outgoing[:, None], (experts, 2, capacity, width)).reshape(
        devices, capacity, width
    )
    received = lax.all_to_all(doubled, "ep", split_axis=0, concat_axis=0, tiled=True)
    rows = received.reshape(devices * capacity, width)
    gate = jnp.dot(rows, w_gate[0], preferred_element_type=jnp.float32)
    upper = jnp.dot(rows, w_up[0], preferred_element_type=jnp.float32)
    active = (jax.nn.silu(gate) * upper).astype(jnp.bfloat16)
    partial_value = jnp.dot(active, w_down[0], preferred_element_type=jnp.float32).reshape(
        devices, capacity, width
    )
    columns = width // 2
    halves = partial_value.reshape(devices, capacity, 2, columns)
    keep_part = jnp.where(core == 0, halves[:, :, 0], halves[:, :, 1])
    give_part = jnp.where(core == 0, halves[:, :, 1], halves[:, :, 0])
    partner = swapped(give_part, "ep", 0)
    summed = (keep_part + partner).astype(jnp.bfloat16)
    back = lax.all_to_all(summed, "ep", split_axis=0, concat_axis=0, tiled=True).reshape(
        experts, 2, capacity, columns
    )
    expert_out = jnp.transpose(back, (0, 2, 1, 3)).reshape(experts, capacity, width)
    picked = jnp.take(
        expert_out.reshape(experts * capacity, width), position.reshape(-1), axis=0
    ).reshape(tokens, top, width)
    mixed = jnp.sum(combine_weights[:, :, None] * picked.astype(jnp.float32), axis=1)
    return (stream + mixed).astype(jnp.bfloat16)


def solution(mesh):
    placed = (
        P(("groups", "ep"), None, None, None),
        P(("groups", "ep"), None, None),
        P(("groups", "ep"), None, None),
        P(("groups", "ep")),
        P(),
        P(("groups", "ep"), None),
        P(),
        P("ep", None, None),
        P("ep", None, None),
        P("ep", None, None),
        P(("groups", "ep"), None),
        P(("groups", "ep"), None),
    )
    return jax.shard_map(
        local, mesh=mesh, in_specs=placed, out_specs=P(("groups", "ep"), None), check_vma=False
    )
```

profile of v0, /device:TPU:0, one launch (start us, length us, event | category | flops | bytes accessed | tf_op | source)
XLA Modules:
  0.0 144.6 jit_solution(940063323130212494)
XLA Ops:
  0.0 0.9 iota_compare_fusion.3
  0.9 2.4 %fusion.58 = (f32[4,8,16]{2,1,0:T(8,128)S(1)}, f32[4,8,16,384]{3,2,1,0:T(8,128)S(1)}) fusion(bf16[4,8,16,576]{3,2,1,0:T(8,128)(2,1)} %param.12, bf16[4,384,576]{1,2,0:T(8,128)(2,1)} %param.13, pred[4,384]{1,0:T(4,128)(4,1)S(1)} %iota_compare_fusion.3), kind=kOutput, calls=%fused_computation.71 | convolution fusion | flops 227081728 | bytes 3149312 | tf_op jit(solution)/shard_map/rjhk,rck->rjhc/dot_general | solution.py:18
  3.3 1.0 fusion.59
  4.5 0.3 fusion.43
  5.2 0.3 copy.55
  5.4 2.0 %fusion.51 = f32[4,8,16,512]{3,1,0,2:T(8,128)} fusion(bf16[4,8,16,8]{3,1,0,2:T(8,128)(2,1)S(1)} %copy.55, bf16[4,8,576]{2,1,0:T(8,128)(2,1)} %param.14), kind=kOutput, calls=%fused_computation.50 | convolution fusion | flops 4194304 | bytes 1089536 | tf_op jit(solution)/shard_map/rjhi,ril->rjhl/dot_general | solution.py:40
  7.4 4.1 %fusion.36 = f32[4,8,16,128]{3,1,0,2:T(8,128)} fusion(bf16[16,512,128]{2,1,0:T(8,128)(2,1)} %param.16, f32[4,8,16,512]{3,1,0,2:T(8,128)} %fusion.51, bf16[4,384,576]{1,2,0:T(8,128)(2,1)} %param.13, bf16[4,8,16,384]{3,2,1,0:T(8,128)(2,1)S(1)} %divide_convert_fusion), kind=kOutput, calls=%fused_computation.28 | convolution fusion | flops 268959744 | bytes 5373952 | tf_op jit(solution)/shard_map/rjhl,hlv->rjhv/dot_general | solution.py:44
  11.6 1.1 copy.104
  12.7 1.1 multiply_reduce_fusion.1
  14.0 0.6 reduce-window.6
  15.3 2.3 %convolution_convert_fusion = bf16[224,2048]{1,0:T(8,128)(2,1)} fusion(pred[224,32]{0,1:T(8,128)(4,1)S(1)} %fusion.46, f32[2048]{0:T(1024)S(1)} %copy-done.5, f32[32]{0:T(128)S(1)} %add_rsqrt_fusion, f32[4,8,16,128]{3,2,1,0:T(8,128)S(1)} %copy.104, bf16[32,2048]{1,0:T(8,128)(2,1)} %param.17), kind=kOutput, calls=%fused_computation.8 | convolution fusion | flops 30146560 | bytes 1326208 | tf_op jit(solution)/shard_map/dot_general | solution.py:82
  17.6 2.3 %broadcast_in_dim.77 = bf16[16,14,2048]{2,1,0:T(8,128)(2,1)} reshape(bf16[224,2048]{1,0:T(8,128)(2,1)} %convolution_convert_fusion) | data formatting | bytes 1835008 | tf_op jit(solution)/shard_map/broadcast_in_dim | solution.py:87
  19.9 2.8 %broadcast_in_dim.78 = bf16[16,2,14,2048]{3,2,1,0:T(8,128)(2,1)} broadcast(bf16[16,14,2048]{2,1,0:T(8,128)(2,1)} %broadcast_in_dim.77), dimensions={0,2,3} | broadcast | bytes 2752512 | tf_op jit(solution)/shard_map/broadcast_in_dim | solution.py:87
  22.7 7.4 %all-to-all-start = ((bf16[32,14,2048]{2,1,0:T(8,128)(2,1)}), bf16[32,14,2048]{2,1,0:T(8,128)(2,1)}, u32[]{:S(2)}, u32[]{:S(2)}) async-start(bf16[32,14,2048]{2,1,0:T(8,128)(2,1)} %bitcast.125), calls=%async_computation | async-start | bytes 4194304 | tf_op jit(solution)/shard_map/all_to_all | solution.py:90
  30.1 48.9 %all-to-all-done = bf16[32,14,2048]{2,1,0:T(8,128)(2,1)} async-done(((bf16[32,14,2048]{2,1,0:T(8,128)(2,1)}), bf16[32,14,2048]{2,1,0:T(8,128)(2,1)}, u32[]{:S(2)}, u32[]{:S(2)}) %all-to-all-start) | async-done | bytes 1835040 | tf_op jit(solution)/shard_map/all_to_all | solution.py:90
  79.0 3.7 %reshape.138 = bf16[448,2048]{1,0:T(8,128)(2,1)} reshape(bf16[32,14,2048]{2,1,0:T(8,128)(2,1)} %all-to-all-done) | data formatting | bytes 3670016 | tf_op jit(solution)/shard_map/reshape | solution.py:91
  82.7 3.3 %fusion.4 = f32[448,704]{1,0:T(8,128)S(1)} fusion(bf16[448,2048]{1,0:T(8,128)(2,1)} %reshape.138, bf16[1,2048,704]{1,2,0:T(8,128)(2,1)S(1)} %copy-done), kind=kOutput, calls=%fused_computation.6 | convolution fusion | flops 1291845632 | bytes 5980160 | tf_op jit(solution)/shard_map/dot_general | solution.py:92
  86.0 2.6 %fusion.22 = bf16[448,704]{1,0:T(8,128)(2,1)} fusion(bf16[448,2048]{1,0:T(8,128)(2,1)S(1)} %copy-done.2, bf16[1,2048,704]{1,2,0:T(8,128)(2,1)S(1)} %copy-done.8, f32[448,704]{1,0:T(8,128)S(1)} %fusion.4), kind=kOutput, calls=%fused_computation.24 | convolution fusion | flops 1293737984 | bytes 6610944 | tf_op jit(solution)/shard_map/dot_general | solution.py:93
  88.6 2.2 %dot_general.41 = bf16[32,14,704]{2,1,0:T(8,128)(2,1)} reshape(bf16[448,704]{1,0:T(8,128)(2,1)} %fusion.22) | data formatting | bytes 1261568 | tf_op jit(solution)/shard_map/dot_general | solution.py:95
  90.8 3.7 %fusion = f32[32,14,2,1024]{3,0,2,1:T(8,128)S(1)} fusion(bf16[88,2,8,1024]{3,2,1,0:T(8,128)(2,1)} %bitcast.130, bf16[32,14,704,1]{2,1,0,3:T(8,128)(2,1)} %bitcast.127), kind=kOutput, calls=%fused_computation.2 | convolution fusion | flops 1291845632 | bytes 7184384 | tf_op jit(solution)/shard_map/dot_general | solution.py:95
  94.4 0.3 select_bitcast_fusion
  94.8 3.8 %collective-permute-done = f32[32,14,1024]{2,0,1:T(8,128)S(1)} collective-permute-done((f32[32,14,1024]{2,0,1:T(8,128)S(1)}, f32[32,14,1024]{2,0,1:T(8,128)S(1)}, u32[]{:S(2)}, u32[]{:S(2)}) %collective-permute-start) | collective-permute-done | bytes 1835040 | tf_op jit(solution)/shard_map/ppermute | solution.py:10
  98.6 0.7 fusion.10
  99.3 1.5 %copy.69 = bf16[32,14,1024]{2,1,0:T(8,128)(2,1)} copy(bf16[32,14,1024]{2,0,1:T(8,128)(2,1)S(1)} %fusion.10) | data formatting | bytes 1835008 | tf_op jit(solution)/shard_map/convert_element_type | solution.py:103
  100.8 4.3 %all-to-all-start.1 = ((bf16[32,14,1024]{2,1,0:T(8,128)(2,1)}), bf16[32,14,1024]{2,1,0:T(8,128)(2,1)}, u32[]{:S(2)}, u32[]{:S(2)}) async-start(bf16[32,14,1024]{2,1,0:T(8,128)(2,1)} %copy.69), calls=%async_computation.1 | async-start | bytes 2097152 | tf_op jit(solution)/shard_map/all_to_all | solution.py:104
  105.4 25.8 %all-to-all-done.1 = bf16[32,14,1024]{2,1,0:T(8,128)(2,1)} async-done(((bf16[32,14,1024]{2,1,0:T(8,128)(2,1)}), bf16[32,14,1024]{2,1,0:T(8,128)(2,1)}, u32[]{:S(2)}, u32[]{:S(2)}) %all-to-all-start.1) | async-done | bytes 917536 | tf_op jit(solution)/shard_map/all_to_all | solution.py:104
  131.2 2.2 %copy.70 = bf16[16,2,14,1024]{3,1,2,0:T(2,128)(2,1)S(1)} copy(bf16[16,2,14,1024]{3,2,1,0:T(8,128)(2,1)} %bitcast.22) | data formatting | bytes 1835008 | tf_op jit(solution)/shard_map/reshape | solution.py:104
  133.4 1.2 copy.83
  134.5 4.1 %gather_fusion = bf16[192,2048]{1,0:T(8,128)(2,1)} fusion(bf16[224,2048]{1,0:T(8,128)(2,1)} %bitcast.124, s32[1024]{0:T(1024)S(1)} %pad_clamp_fusion), kind=kCustom, calls=%fused_computation | custom fusion | bytes 1573632 | tf_op jit(solution)/shard_map/jit(_take)/gather | solution.py:108
  138.7 2.2 %gather.7 = bf16[32,6,2048]{2,1,0:T(8,128)(2,1)} reshape(bf16[192,2048]{1,0:T(8,128)(2,1)} %gather_fusion) | data formatting | bytes 1572864 | tf_op jit(solution)/shard_map/jit(_take)/gather | solution.py:108
  140.9 2.9 %multiply_reduce_fusion = f32[32,2048]{1,0:T(8,128)S(1)} fusion(bf16[32,6,2048]{2,1,0:T(8,128)(2,1)} %gather.7, f32[32,6]{1,0:T(8,128)S(1)} %copy.57, pred[32,6]{1,0:T(8,128)(4,1)S(1)} %get-tuple-element.5), kind=kLoop, calls=%fused_computation.11 | loop fusion | flops 1507328 | bytes 1049536 | tf_op jit(solution)/shard_map/reduce_sum | solution.py:111
  143.8 0.8 add_convert_fusion
  (44 shorter events, 1.6 us)
Async XLA Ops:
  0.0 82.7 %copy-start = (bf16[1,2048,704]{1,2,0:T(8,128)(2,1)S(1)}, bf16[1,2048,704]{1,2,0:T(8,128)(2,1)}, u32[]{:S(2)}) copy-start(bf16[1,2048,704]{1,2,0:T(8,128)(2,1)} %param.19) | copy-start | bytes 8650756
  0.0 3.3 %copy-start.1 = (bf16[4,8,16,576]{3,2,1,0:T(8,128)(2,1)S(1)}, bf16[4,8,16,576]{3,2,1,0:T(8,128)(2,1)}, u32[]{:S(2)}) copy-start(bf16[4,8,16,576]{3,2,1,0:T(8,128)(2,1)} %param.12) | copy-start | bytes 1769476
  0.0 3.3 %copy-start.4 = (bf16[4,8,576]{2,1,0:T(8,128)(2,1)S(1)}, bf16[4,8,576]{2,1,0:T(8,128)(2,1)}, u32[]{:S(2)}) copy-start(bf16[4,8,576]{2,1,0:T(8,128)(2,1)} %param.14) | copy-start | bytes 110596
  7.4 6.3 %copy-start.6 = (s32[32,6]{0,1:T(8,128)S(1)}, s32[32,6]{0,1:T(8,128)}, u32[]{:S(2)}) copy-start(s32[32,6]{0,1:T(8,128)} %param.22) | copy-start | bytes 2308
  7.4 7.8 %copy-start.5 = (f32[2048]{0:T(1024)S(1)}, f32[2048]{0:T(1024)}, u32[]{:S(2)}) copy-start(f32[2048]{0:T(1024)} %param.18) | copy-start | bytes 24580
  22.7 56.3 %all-to-all-start = ((bf16[32,14,2048]{2,1,0:T(8,128)(2,1)}), bf16[32,14,2048]{2,1,0:T(8,128)(2,1)}, u32[]{:S(2)}, u32[]{:S(2)}) async-start(bf16[32,14,2048]{2,1,0:T(8,128)(2,1)} %bitcast.125), calls=%async_computation | async-start | bytes 4194304 | tf_op jit(solution)/shard_map/all_to_all | solution.py:90
  82.7 3.3 %copy-start.2 = (bf16[448,2048]{1,0:T(8,128)(2,1)S(1)}, bf16[448,2048]{1,0:T(8,128)(2,1)}, u32[]{:S(2)}) copy-start(bf16[448,2048]{1,0:T(8,128)(2,1)} %reshape.138) | copy-start | bytes 5505028
  82.7 3.3 %copy-start.8 = (bf16[1,2048,704]{1,2,0:T(8,128)(2,1)S(1)}, bf16[1,2048,704]{1,2,0:T(8,128)(2,1)}, u32[]{:S(2)}) copy-start(bf16[1,2048,704]{1,2,0:T(8,128)(2,1)} %param.20) | copy-start | bytes 8650756
  94.8 3.9 %collective-permute-start = (f32[32,14,1024]{2,0,1:T(8,128)S(1)}, f32[32,14,1024]{2,0,1:T(8,128)S(1)}, u32[]{:S(2)}, u32[]{:S(2)}) collective-permute-start(f32[32,14,1024]{2,0,1:T(8,128)S(1)} %select_bitcast_fusion), channel_id=1, source_target_pairs={{0,1},{1,0},{2,3},{3,2},{4,5},{5,4},{6,7},{7,6},{8,9},{9,8},{10,11... | collective-permute-start | bytes 5505032 | tf_op jit(solution)/shard_map/ppermute | solution.py:10
  99.3 6.0 %copy-start.7 = (f32[32,6]{0,1:T(8,128)S(1)}, f32[32,6]{0,1:T(8,128)}, u32[]{:S(2)}) copy-start(f32[32,6]{0,1:T(8,128)} %param.23) | copy-start | bytes 2308
  100.8 30.3 %all-to-all-start.1 = ((bf16[32,14,1024]{2,1,0:T(8,128)(2,1)}), bf16[32,14,1024]{2,1,0:T(8,128)(2,1)}, u32[]{:S(2)}, u32[]{:S(2)}) async-start(bf16[32,14,1024]{2,1,0:T(8,128)(2,1)} %copy.69), calls=%async_computation.1 | async-start | bytes 2097152 | tf_op jit(solution)/shard_map/all_to_all | solution.py:104
  138.7 5.2 %copy-start.3 = (bf16[32,2048]{1,0:T(8,128)(2,1)S(1)}, bf16[32,2048]{1,0:T(8,128)(2,1)}, u32[]{:S(2)}) copy-start(bf16[32,2048]{1,0:T(8,128)(2,1)} %param.17) | copy-start | bytes 393220
where the time goes:
time: 145 us
  waiting for transfers between devices  78.4 us (54%)
  local copies, waits for them, and re-layouts  24.3 us (17%)
  matrix products  21.4 us (15%)
  starting transfers between devices  11.8 us (8%)
  other arithmetic  8.31 us (6%)
    all_to_all x1, waiting for transfers between devices, local(): lax.all_to_all(doubled, 'ep', split_axis=0, concat_axis=0, tiled=True)  48.9 us
    all_to_all x1, waiting for transfers between devices, local(): lax.all_to_all(summed, 'ep', split_axis=0, concat_axis=0, tiled=True)  25.8 us
    all_to_all x1, starting transfers between devices, local(): lax.all_to_all(doubled, 'ep', split_axis=0, concat_axis=0, tiled=True)  7.44 us
    gather x2, local copies, waits for them, and re-layouts, local(): jnp.take(expert_out.reshape(experts * capacity, width), position.reshape(...  6.35 us
    broadcast_in_dim x2, local copies, waits for them, and re-layouts, local(): jnp.broadcast_to(outgoing[:, None], (experts, 2, capacity, width))  5.08 us
    all_to_all x1, starting transfers between devices, local(): lax.all_to_all(summed, 'ep', split_axis=0, concat_axis=0, tiled=True)  4.3 us
    dot_general x1, matrix products, attend(): jnp.einsum('rjhl,hlv->rjhv', mixed, value_up, preferred_element_type=jnp....  4.12 us
    ppermute x1, waiting for transfers between devices, swapped(): return lax.ppermute(value, axis, pairs)  3.77 us
  transfers between devices with their start and end apart: 3, of which 3 were waited for; matrix products, arithmetic and copies ran while one was open for 0% of the time, Pallas kernels for 0%

commit v1 on v0

v1 whole, which is shorter than its diff:
```python
import functools

import jax
import jax.numpy as jnp
from jax import lax
from jax.experimental import pallas as pl
from jax.experimental.pallas import tpu as pltpu
from jax.sharding import PartitionSpec as P

F32 = jnp.float32
BF16 = jnp.bfloat16
NT = (((1,), (1,)), ((), ()))
MIB = 1 << 20


def swapped(value, mask):
    pairs = [(source, source ^ mask) for source in range(lax.axis_size("ep"))]
    return lax.ppermute(value, "ep", pairs)


def whole():
    return pl.BlockSpec(memory_space=pltpu.VMEM)


def attend_kernel(
    heads, lengths, queries, cache, drafts, up_hbm, residual, gain, stream, normed, mixed, up, sem
):
    step = pl.program_id(0)
    rows, width = queries.shape[1:]
    slots = cache.shape[2]
    draft = drafts.shape[1]
    latent = up.shape[1]
    vdim = up.shape[2]
    copy = pltpu.make_async_copy(up_hbm, up, sem)

    @pl.when(step == 0)
    def _():
        copy.start()

    scale = (vdim + width - latent) ** (-0.5)
    q = queries[0]
    c = cache[0]
    d = drafts[0]
    cached = jnp.dot(q, c, preferred_element_type=F32) * scale
    own = lax.dot_general(q, d, NT, preferred_element_type=F32) * scale
    visible = lax.broadcasted_iota(jnp.int32, (rows, slots), 1) < lengths[step]
    token = lax.broadcasted_iota(jnp.int32, (rows, draft), 0) // heads
    causal = lax.broadcasted_iota(jnp.int32, (rows, draft), 1) <= token
    cached = jnp.where(visible, cached, -1e30)
    own = jnp.where(causal, own, -1e30)
    highest = jnp.maximum(
        jnp.max(cached, axis=-1, keepdims=True), jnp.max(own, axis=-1, keepdims=True)
    )
    e_cached = jnp.where(visible, jnp.exp(cached - highest), 0.0)
    e_own = jnp.where(causal, jnp.exp(own - highest), 0.0)
    total = jnp.sum(e_cached, axis=-1, keepdims=True) + jnp.sum(e_own, axis=-1, keepdims=True)
    inverse = 1.0 / total
    p_cached = (e_cached * inverse).astype(BF16)
    p_own = (e_own * inverse).astype(BF16)
    out = lax.dot_general(p_cached, c[:latent, :], NT, preferred_element_type=F32)
    out = out + jnp.dot(p_own, d[:, :latent], preferred_element_type=F32)
    lanes = mixed.shape[2]
    for g in range(latent // lanes):
        mixed[g, pl.ds(pl.multiple_of(step * rows, rows), rows), :] = out[
            :, g * lanes : (g + 1) * lanes
        ]

    @pl.when(step == pl.num_programs(0) - 1)
    def _():
        copy.wait()
        tokens = stream.shape[0]
        square = jnp.zeros((tokens, 1), F32)
        for head in range(heads):
            part = jnp.concatenate(
                [mixed[g, pl.ds(head, tokens, stride=heads), :] for g in range(latent // lanes)],
                axis=1,
            ).astype(BF16)
            columns = slice(head * vdim, (head + 1) * vdim)
            value = residual[:, columns].astype(F32) + jnp.dot(
                part, up[head], preferred_element_type=F32
            )
            stream[:, columns] = value
            square = square + jnp.sum(value * value, axis=-1, keepdims=True)
        factor = lax.rsqrt(square / stream.shape[1] + 1e-06)
        normed[...] = (stream[...] * factor * gain[...]).astype(BF16)


def attend(queries, cache, drafts, lengths, value_up, residual, norm_gain):
    reqs, draft, heads, width = queries.shape
    slots = cache.shape[1]
    latent, vdim = value_up.shape[1:]
    tokens, features = residual.shape
    rows = draft * heads
    flops = 2 * reqs * rows * slots * (width + latent) + 2 * tokens * heads * latent * vdim
    return pl.pallas_call(
        functools.partial(attend_kernel, heads),
        grid=(reqs,),
        in_specs=[
            pl.BlockSpec(memory_space=pltpu.SMEM),
            pl.BlockSpec((1, rows, width), lambda r: (r, 0, 0)),
            pl.BlockSpec((1, width, slots), lambda r: (r, 0, 0)),
            pl.BlockSpec((1, draft, width), lambda r: (r, 0, 0)),
            pl.BlockSpec(memory_space=pl.ANY),
            pl.BlockSpec((tokens, features), lambda r: (0, 0)),
            pl.BlockSpec((1, features), lambda r: (0, 0)),
        ],
        out_specs=[
            pl.BlockSpec((tokens, features), lambda r: (0, 0)),
            pl.BlockSpec((tokens, features), lambda r: (0, 0)),
        ],
        out_shape=[
            jax.ShapeDtypeStruct((tokens, features), F32),
            jax.ShapeDtypeStruct((tokens, features), BF16),
        ],
        scratch_shapes=[
            pltpu.VMEM((latent // 128, reqs * rows, 128), F32),
            pltpu.VMEM(value_up.shape, BF16),
            pltpu.SemaphoreType.DMA,
        ],
        cost_estimate=pl.CostEstimate(
            flops=flops, bytes_accessed=6 * MIB, transcendentals=reqs * rows * slots
        ),
        compiler_params=pltpu.CompilerParams(vmem_limit_bytes=24 * MIB),
    )(
        lengths,
        queries.reshape(reqs, rows, width),
        jnp.swapaxes(cache, 1, 2),
        drafts,
        value_up,
        residual,
        norm_gain.reshape(1, features),
    )


def table_kernel(top, tokens, stride, mine, routed, pick, high, low, table):
    experts = mine[...]
    both = routed.shape[1]
    count = experts.shape[0]
    named = jnp.zeros((count, both), F32)
    weight = jnp.zeros((count, both), F32)
    for k in range(top):
        hit = jnp.where(routed[k : k + 1, :] == experts, 1.0, 0.0)
        named = named + hit
        weight = weight + hit * routed[top + k : top + k + 1, :]
    earlier = lax.broadcasted_iota(jnp.int32, (both, both), 0)
    later = lax.broadcasted_iota(jnp.int32, (both, both), 1)
    before = (earlier < later) & ((earlier < tokens) == (later < tokens))
    rank = jnp.dot(
        named.astype(BF16),
        jnp.where(before, 1.0, 0.0).astype(BF16),
        preferred_element_type=F32,
    )
    behind = lax.broadcasted_iota(jnp.int32, (count, both), 1) >= tokens
    place = rank.astype(jnp.int32) + jnp.where(behind, stride, 0)
    place = jnp.where(named > 0.0, place, -1)
    slots = lax.broadcasted_iota(jnp.int32, (2 * stride, both), 0)
    for m in range(count):
        hit = jnp.where(slots == place[m : m + 1, :], 1.0, 0.0)
        rows = slice(2 * stride * m, 2 * stride * (m + 1))
        pick[rows, :] = hit.astype(BF16)
        table[rows, :] = hit * weight[m : m + 1, :]
    turned = table[...].T
    top_bits = turned.astype(BF16)
    high[...] = top_bits
    low[...] = (turned - top_bits.astype(F32)).astype(BF16)


def tables(mine, routed, top, tokens, stride):
    rows = mine.shape[0] * 2 * stride
    both = 2 * tokens
    return pl.pallas_call(
        functools.partial(table_kernel, top, tokens, stride),
        in_specs=[whole()] * 2,
        out_specs=[whole()] * 3,
        out_shape=[
            jax.ShapeDtypeStruct((rows, both), BF16),
            jax.ShapeDtypeStruct((both, rows), BF16),
            jax.ShapeDtypeStruct((both, rows), BF16),
        ],
        scratch_shapes=[pltpu.VMEM((rows, both), F32)],
        cost_estimate=pl.CostEstimate(flops=MIB, bytes_accessed=MIB // 4, transcendentals=0),
        compiler_params=pltpu.CompilerParams(vmem_limit_bytes=16 * MIB),
    )(mine, routed)


def dispatch_kernel(pick, here, there, *blocks):
    both = jnp.concatenate([here[...], there[...]], axis=0)
    rows = blocks[0].shape[0]
    for m, block in enumerate(blocks):
        block[...] = jnp.dot(
            pick[m * rows : (m + 1) * rows, :], both, preferred_element_type=F32
        ).astype(BF16)


def dispatch(pick, here, there, count):
    rows, width = pick.shape[0] // count, here.shape[1]
    return pl.pallas_call(
        dispatch_kernel,
        in_specs=[whole()] * 3,
        out_specs=[whole()] * count,
        out_shape=[jax.ShapeDtypeStruct((rows, width), BF16)] * count,
        cost_estimate=pl.CostEstimate(
            flops=2 * pick.size * width, bytes_accessed=3 * MIB // 2, transcendentals=0
        ),
        compiler_params=pltpu.CompilerParams(vmem_limit_bytes=16 * MIB),
    )(pick, here, there)


def expert_kernel(count, *refs):
    blocks = refs[:count]
    weights = refs[count : count + 6]
    outs = refs[count + 6 : 2 * count + 6]
    held = refs[2 * count + 6 : 2 * count + 12]
    rows_ref, total, sems = refs[2 * count + 12 :]
    copies = [pltpu.make_async_copy(weights[i], held[i], sems.at[i]) for i in range(6)]
    for copy in copies:
        copy.start()
    size = blocks[0].shape[0]
    for m, block in enumerate(blocks):
        rows_ref[m * size : (m + 1) * size, :] = block[...]
    for half in range(2):
        copies[3 * half].wait()
        gate = lax.dot_general(
            rows_ref[...], held[3 * half][...], NT, preferred_element_type=F32
        )
        copies[3 * half + 1].wait()
        upper = lax.dot_general(
            rows_ref[...], held[3 * half + 1][...], NT, preferred_element_type=F32
        )
        active = (gate * (1.0 / (1.0 + jnp.exp(-gate))) * upper).astype(BF16)
        copies[3 * half + 2].wait()
        product = jnp.dot(active, held[3 * half + 2][...], preferred_element_type=F32)
        if half == 0:
            total[...] = product
        else:
            result = (total[...] + product).astype(BF16)
            for m, out in enumerate(outs):
                out[...] = result[m * size : (m + 1) * size, :]


def run_expert(blocks, weights):
    count = len(blocks)
    size, width = blocks[0].shape
    units = weights[0].shape[0]
    return pl.pallas_call(
        functools.partial(expert_kernel, count),
        in_specs=[whole()] * count + [pl.BlockSpec(memory_space=pl.ANY)] * 6,
        out_specs=[whole()] * count,
        out_shape=[jax.ShapeDtypeStruct((size, width), BF16)] * count,
        scratch_shapes=[pltpu.VMEM((units, width), BF16)] * 6
        + [
            pltpu.VMEM((count * size, width), BF16),
            pltpu.VMEM((count * size, width), F32),
            pltpu.SemaphoreType.DMA((6,)),
        ],
        cost_estimate=pl.CostEstimate(
            flops=12 * count * size * width * units,
            bytes_accessed=12 * units * width,
            transcendentals=2 * count * size * units,
        ),
        compiler_params=pltpu.CompilerParams(vmem_limit_bytes=48 * MIB),
    )(*blocks, *weights)


def combine_kernel(high, low, *refs):
    blocks, (here, there) = refs[:-2], refs[-2:]
    rows = jnp.concatenate([block[...] for block in blocks], axis=0)
    total = jnp.dot(high[...], rows, preferred_element_type=F32)
    total = total + jnp.dot(low[...], rows, preferred_element_type=F32)
    tokens = here.shape[0]
    here[...] = total[:tokens]
    there[...] = total[tokens:].astype(BF16)


def combine(high, low, blocks):
    both, rows = high.shape
    width = blocks[0].shape[1]
    return pl.pallas_call(
        combine_kernel,
        in_specs=[whole()] * (2 + len(blocks)),
        out_specs=[whole()] * 2,
        out_shape=[
            jax.ShapeDtypeStruct((both // 2, width), F32),
            jax.ShapeDtypeStruct((both // 2, width), BF16),
        ],
        cost_estimate=pl.CostEstimate(
            flops=4 * both * rows * width, bytes_accessed=3 * MIB // 2, transcendentals=0
        ),
        compiler_params=pltpu.CompilerParams(vmem_limit_bytes=16 * MIB),
    )(high, low, *blocks)


def local(
    queries,
    cache,
    drafts,
    lengths,
    value_up,
    residual,
    norm_gain,
    w_gate,
    w_up,
    w_down,
    routes,
    combine_weights,
):
    tokens, top = routes.shape
    devices = lax.axis_size("ep")
    experts = devices // 2
    near = experts // 2
    capacity = min(tokens, 2 * (((tokens * top + experts - 1) // experts + 3) // 2))
    stride = -(-capacity // 8) * 8

    routed = jnp.concatenate([routes.T.astype(F32), combine_weights.T], axis=0)
    routed = jnp.concatenate([routed, swapped(routed, devices // 2)], axis=1)
    own = [jnp.swapaxes(w_gate, 1, 2)[0], jnp.swapaxes(w_up, 1, 2)[0], w_down[0]]
    weights = own + [swapped(w, 1) for w in own]
    chip = lax.axis_index("ep") // 2
    mine = (chip ^ jnp.arange(near, dtype=jnp.int32)).astype(F32)[:, None]

    stream, normed = attend(queries, cache, drafts, lengths, value_up, residual, norm_gain)
    pick, high, low = tables(mine, routed, top, tokens, stride)
    blocks = dispatch(pick, normed, swapped(normed, devices // 2), near)
    blocks = [swapped(b, 2 * m) if m else b for m, b in enumerate(blocks)]
    blocks = run_expert(blocks, weights)
    blocks = [swapped(b, 2 * m) if m else b for m, b in enumerate(blocks)]
    here, there = combine(high, low, blocks)
    return (stream + (here + swapped(there, devices // 2).astype(F32))).astype(BF16)


def solution(mesh):
    placed = (
        P(("groups", "ep"), None, None, None),
        P(("groups", "ep"), None, None),
        P(("groups", "ep"), None, None),
        P(("groups", "ep")),
        P(),
        P(("groups", "ep"), None),
        P(),
        P("ep", None, None),
        P("ep", None, None),
        P("ep", None, None),
        P(("groups", "ep"), None),
        P(("groups", "ep"), None),
    )
    return jax.shard_map(
        local, mesh=mesh, in_specs=placed, out_specs=P(("groups", "ep"), None), check_vma=False
    )
```

time: 145 us -> 85 us (0.59)
  waiting for transfers between devices: 78.4 us -> 40.8 us
  matrix products: 21.4 us -> 0 us
  local copies, waits for them, and re-layouts: 24.3 us -> 7.19 us
  Pallas kernels: 0 us -> 13.7 us
  starting transfers between devices: 11.8 us -> 20.7 us
  other arithmetic: 8.31 us -> 2.17 us
    all_to_all x2 -> x0, waiting for transfers between devices: 74.7 us -> none  [the longest x1 48.9 us: local(): lax.all_to_all(doubled, 'ep', split_axis=0, concat_axis=0, tiled=True)]
    ppermute x1 -> x20, waiting for transfers between devices: 3.77 us -> 40.8 us  [swapped(): return lax.ppermute(value, 'ep', pairs)]
    dot_general x8 -> x0, matrix products: 21.4 us -> none  [the longest x1 4.12 us: attend(): jnp.einsum('rjhl,hlv->rjhv', mixed, value_up, preferred_element_type=jnp....]
    ppermute x1 -> x20, starting transfers between devices: 0.07 us -> 20.7 us  [swapped(): return lax.ppermute(value, 'ep', pairs)]
    pallas_call x0 -> x5, Pallas kernels: none -> 13.7 us  [the longest x1 7.88 us: run_expert(): pl.pallas_call(functools.partial(expert_kernel, count), in_specs=[whole()...]
    all_to_all x2 -> x0, starting transfers between devices: 11.7 us -> none  [the longest x1 7.44 us: local(): lax.all_to_all(doubled, 'ep', split_axis=0, concat_axis=0, tiled=True)]
    gather x2 -> x0, local copies, waits for them, and re-layouts: 6.35 us -> none  [local(): jnp.take(expert_out.reshape(experts * capacity, width), position.reshape(...]
    reshape x3 -> x0, local copies, waits for them, and re-layouts: 5.96 us -> none  [the longest x1 3.69 us: local(): rows = received.reshape(devices * capacity, width)]
  transfers between devices with their start and end apart: 3 -> 20, of which waited for: 3 -> 13; matrix products, arithmetic and copies ran while one was open for 0% -> 2% of each run, Pallas kernels for 0% -> 6%
where the time goes in v1:
time: 85 us; the launch traced here: 84.6 us
  waiting for transfers between devices  40.8 us (48%)
  starting transfers between devices  20.7 us (24%)
  Pallas kernels  13.7 us (16%)
  local copies, waits for them, and re-layouts  7.19 us (8%)
  other arithmetic  2.17 us (3%)
    ppermute x20, waiting for transfers between devices, swapped(): return lax.ppermute(value, 'ep', pairs)  40.8 us
    ppermute x20, starting transfers between devices, swapped(): return lax.ppermute(value, 'ep', pairs)  20.7 us
    pallas_call x1, Pallas kernels, run_expert(): pl.pallas_call(functools.partial(expert_kernel, count), in_specs=[whole()...  7.88 us
    unnamed x18, local copies, waits for them, and re-layouts  7.19 us
    pallas_call x1, Pallas kernels, attend(): pl.pallas_call(functools.partial(attend_kernel, heads), grid=(reqs,), in_...  4.57 us
  transfers between devices with their start and end apart: 20, of which 13 were waited for; matrix products, arithmetic and copies ran while one was open for 2% of the time, Pallas kernels for 6%

profile of v1, /device:TPU:0, one launch (start us, length us, event | category | flops | bytes accessed | tf_op | source)
XLA Modules:
  0.0 84.6 jit_solution(13319240334994069186)
XLA Ops:
  1.0 0.7 convert_bitcast_fusion
  1.7 0.7 pad_maximum_fusion
  2.4 3.9 %collective-permute-start = (f32[12,32]{1,0:T(8,128)S(1)}, f32[12,32]{1,0:T(8,128)S(1)}, u32[]{:S(2)}, u32[]{:S(2)}) collective-permute-start(f32[12,32]{1,0:T(8,128)S(1)} %pad_maximum_fusion), channel_id=1, source_target_pairs={{0,16},{1,17},{2,18},{3,19},{4,20},{5,21},{6,22},{7,23},{8,24},{9,... | collective-permute-start | bytes 4616 | tf_op jit(solution)/shard_map/ppermute | solution.py:18
  6.3 1.6 %copy-done.1 = bf16[16,512,128]{2,1,0:T(8,128)(2,1)S(1)} copy-done((bf16[16,512,128]{2,1,0:T(8,128)(2,1)S(1)}, bf16[16,512,128]{2,1,0:T(8,128)(2,1)}, u32[]{:S(2)}) %copy-start.1) | copy-done | bytes 2097176
  7.9 1.5 %copy-done.2 = bf16[4,384,576]{1,2,0:T(8,128)(2,1)S(1)} copy-done((bf16[4,384,576]{1,2,0:T(8,128)(2,1)S(1)}, bf16[4,384,576]{1,2,0:T(8,128)(2,1)}, u32[]{:S(2)}) %copy-start.2) | copy-done | bytes 1769496
  9.4 1.1 %copy-done.3 = bf16[4,8,16,576]{3,2,1,0:T(8,128)(2,1)S(1)} copy-done((bf16[4,8,16,576]{3,2,1,0:T(8,128)(2,1)S(1)}, bf16[4,8,16,576]{3,2,1,0:T(8,128)(2,1)}, u32[]{:S(2)}) %copy-start.3) | copy-done | bytes 589848
  10.4 0.9 %copy-done.4 = bf16[32,2048]{1,0:T(8,128)(2,1)S(1)} copy-done((bf16[32,2048]{1,0:T(8,128)(2,1)S(1)}, bf16[32,2048]{1,0:T(8,128)(2,1)}, u32[]{:S(2)}) %copy-start.4) | copy-done | bytes 131096
  11.3 0.8 copy-done.5
  12.1 0.7 copy-done.6
  13.5 4.6 %shard_map.118 = (f32[32,2048]{1,0:T(8,128)S(1)}, bf16[32,2048]{1,0:T(8,128)(2,1)S(1)}) custom-call(s32[4]{0:T(128)S(1)} %copy-done.7, bf16[4,128,576]{2,1,0:T(8,128)(2,1)S(1)} %bitcast.16, bf16[4,576,384]{2,1,0:T(8,128)(2,1)S(1)} %bitcast.15, bf16[4,8,576]{2,1,0:T(8,128)(2,1)S(1)} %copy-done.5, bf16[16,512,128]{2,1,0:T(8,128)(2,1)S(1)} %copy-done.1, ...), custom_call_target="tpu_custom_call" | custom-call | flops 494927872 | bytes 6291456 | tf_op jit(solution)/shard_map/pallas_call | solution.py:95
  18.6 8.6 %collective-permute-done.1.there = bf16[32,2048]{1,0:T(8,128)(2,1)S(1)} collective-permute-done((bf16[32,2048]{1,0:T(8,128)(2,1)S(1)}, bf16[32,2048]{1,0:T(8,128)(2,1)S(1)}, u32[]{:S(2)}, u32[]{:S(2)}) %collective-permute-start.1) | collective-permute-done | bytes 131104 | tf_op jit(solution)/shard_map/ppermute | solution.py:18
  27.5 1.6 %collective-permute-start.2 = (bf16[32,2048]{1,0:T(8,128)(2,1)S(1)}, bf16[32,2048]{1,0:T(8,128)(2,1)S(1)}, u32[]{:S(2)}, u32[]{:S(2)}) collective-permute-start(bf16[32,2048]{1,0:T(8,128)(2,1)S(1)} %get-tuple-element.34), channel_id=1, source_target_pairs={{0,2},{1,3},{2,0},{3,1},{4,6},{5,7},{6,4},{7,5},{8,10},{9,11},{10,... | collective-permute-start | bytes 393224 | tf_op jit(solution)/shard_map/ppermute | solution.py:18
  29.1 1.5 %collective-permute-start.3 = (bf16[32,2048]{1,0:T(8,128)(2,1)S(1)}, bf16[32,2048]{1,0:T(8,128)(2,1)S(1)}, u32[]{:S(2)}, u32[]{:S(2)}) collective-permute-start(bf16[32,2048]{1,0:T(8,128)(2,1)S(1)} %get-tuple-element.35), channel_id=1, source_target_pairs={{0,4},{1,5},{2,6},{3,7},{4,0},{5,1},{6,2},{7,3},{8,12},{9,13},{10,... | collective-permute-start | bytes 393224 | tf_op jit(solution)/shard_map/ppermute | solution.py:18
  30.6 2.0 %collective-permute-done.2.refs_1_ = bf16[32,2048]{1,0:T(8,128)(2,1)S(1)} collective-permute-done((bf16[32,2048]{1,0:T(8,128)(2,1)S(1)}, bf16[32,2048]{1,0:T(8,128)(2,1)S(1)}, u32[]{:S(2)}, u32[]{:S(2)}) %collective-permute-start.2) | collective-permute-done | bytes 131104 | tf_op jit(solution)/shard_map/ppermute | solution.py:18
  32.6 2.4 %collective-permute-start.4 = (bf16[32,2048]{1,0:T(8,128)(2,1)S(1)}, bf16[32,2048]{1,0:T(8,128)(2,1)S(1)}, u32[]{:S(2)}, u32[]{:S(2)}) collective-permute-start(bf16[32,2048]{1,0:T(8,128)(2,1)S(1)} %get-tuple-element.36), channel_id=1, source_target_pairs={{0,6},{1,7},{2,4},{3,5},{4,2},{5,3},{6,0},{7,1},{8,14},{9,15},{10,... | collective-permute-start | bytes 393224 | tf_op jit(solution)/shard_map/ppermute | solution.py:18
  35.5 3.0 %collective-permute-done.4.refs_3_ = bf16[32,2048]{1,0:T(8,128)(2,1)S(1)} collective-permute-done((bf16[32,2048]{1,0:T(8,128)(2,1)S(1)}, bf16[32,2048]{1,0:T(8,128)(2,1)S(1)}, u32[]{:S(2)}, u32[]{:S(2)}) %collective-permute-start.4) | collective-permute-done | bytes 131104 | tf_op jit(solution)/shard_map/ppermute | solution.py:18
  38.5 3.3 %collective-permute-done.5.refs_4_ = bf16[32,2048]{1,0:T(8,128)(2,1)S(1)} collective-permute-done((bf16[32,2048]{1,0:T(8,128)(2,1)S(1)}, bf16[32,2048]{1,0:T(8,128)(2,1)S(1)}, u32[]{:S(2)}, u32[]{:S(2)}) %collective-permute-start.5) | collective-permute-done | bytes 131104 | tf_op jit(solution)/shard_map/ppermute | solution.py:18
  41.8 0.7 collective-permute-start.7
  42.5 1.9 %collective-permute-done.6.refs_5_ = bf16[32,2048]{1,0:T(8,128)(2,1)S(1)} collective-permute-done((bf16[32,2048]{1,0:T(8,128)(2,1)S(1)}, bf16[32,2048]{1,0:T(8,128)(2,1)S(1)}, u32[]{:S(2)}, u32[]{:S(2)}) %collective-permute-start.6) | collective-permute-done | bytes 131104 | tf_op jit(solution)/shard_map/ppermute | solution.py:18
  44.3 1.4 %collective-permute-start.8 = (bf16[32,2048]{1,0:T(8,128)(2,1)S(1)}, bf16[32,2048]{1,0:T(8,128)(2,1)S(1)}, u32[]{:S(2)}, u32[]{:S(2)}) collective-permute-start(bf16[32,2048]{1,0:T(8,128)(2,1)S(1)} %get-tuple-element.40), channel_id=1, source_target_pairs={{0,14},{1,15},{2,12},{3,13},{4,10},{5,11},{6,8},{7,9},{8,6},{9,7},... | collective-permute-start | bytes 393224 | tf_op jit(solution)/shard_map/ppermute | solution.py:18
  45.8 2.9 %collective-permute-done.7.refs_6_ = bf16[32,2048]{1,0:T(8,128)(2,1)S(1)} collective-permute-done((bf16[32,2048]{1,0:T(8,128)(2,1)S(1)}, bf16[32,2048]{1,0:T(8,128)(2,1)S(1)}, u32[]{:S(2)}, u32[]{:S(2)}) %collective-permute-start.7) | collective-permute-done | bytes 131104 | tf_op jit(solution)/shard_map/ppermute | solution.py:18
  48.6 2.4 %collective-permute-done.8.refs_7_ = bf16[32,2048]{1,0:T(8,128)(2,1)S(1)} collective-permute-done((bf16[32,2048]{1,0:T(8,128)(2,1)S(1)}, bf16[32,2048]{1,0:T(8,128)(2,1)S(1)}, u32[]{:S(2)}, u32[]{:S(2)}) %collective-permute-start.8) | collective-permute-done | bytes 131104 | tf_op jit(solution)/shard_map/ppermute | solution.py:18
  51.1 7.9 %shard_map.121 = (bf16[32,2048]{1,0:T(8,128)(2,1)S(1)}, bf16[32,2048]{1,0:T(8,128)(2,1)S(1)}, bf16[32,2048]{1,0:T(8,128)(2,1)S(1)}, bf16[32,2048]{1,0:T(8,128)(2...) custom-call(bf16[32,2048]{1,0:T(8,128)(2,1)S(1)} %get-tuple-element., ...), custom_call_target="tpu_custom_call" | custom-call | flops 4429185024 | bytes 17301504 | tf_op jit(solution)/shard_map/pallas_call | solution.py:245
  59.0 1.6 %collective-permute-start.12 = (bf16[32,2048]{1,0:T(8,128)(2,1)S(1)}, bf16[32,2048]{1,0:T(8,128)(2,1)S(1)}, u32[]{:S(2)}, u32[]{:S(2)}) collective-permute-start(bf16[32,2048]{1,0:T(8,128)(2,1)S(1)} %get-tuple-element.42), channel_id=1, source_target_pairs={{0,2},{1,3},{2,0},{3,1},{4,6},{5,7},{6,4},{7,5},{8,10},{9,11},{10,... | collective-permute-start | bytes 393224 | tf_op jit(solution)/shard_map/ppermute | solution.py:18
  60.5 1.5 %collective-permute-start.13 = (bf16[32,2048]{1,0:T(8,128)(2,1)S(1)}, bf16[32,2048]{1,0:T(8,128)(2,1)S(1)}, u32[]{:S(2)}, u32[]{:S(2)}) collective-permute-start(bf16[32,2048]{1,0:T(8,128)(2,1)S(1)} %get-tuple-element.43), channel_id=1, source_target_pairs={{0,4},{1,5},{2,6},{3,7},{4,0},{5,1},{6,2},{7,3},{8,12},{9,13},{10,... | collective-permute-start | bytes 393224 | tf_op jit(solution)/shard_map/ppermute | solution.py:18
  63.0 2.5 %collective-permute-start.16 = (bf16[32,2048]{1,0:T(8,128)(2,1)S(1)}, bf16[32,2048]{1,0:T(8,128)(2,1)S(1)}, u32[]{:S(2)}, u32[]{:S(2)}) collective-permute-start(bf16[32,2048]{1,0:T(8,128)(2,1)S(1)} %get-tuple-element.46), channel_id=1, source_target_pairs={{0,10},{1,11},{2,8},{3,9},{4,14},{5,15},{6,12},{7,13},{8,2},{9,3},... | collective-permute-start | bytes 393224 | tf_op jit(solution)/shard_map/ppermute | solution.py:18
  65.5 1.0 %collective-permute-start.17 = (bf16[32,2048]{1,0:T(8,128)(2,1)S(1)}, bf16[32,2048]{1,0:T(8,128)(2,1)S(1)}, u32[]{:S(2)}, u32[]{:S(2)}) collective-permute-start(bf16[32,2048]{1,0:T(8,128)(2,1)S(1)} %get-tuple-element.47), channel_id=1, source_target_pairs={{0,12},{1,13},{2,14},{3,15},{4,8},{5,9},{6,10},{7,11},{8,4},{9,5},... | collective-permute-start | bytes 393224 | tf_op jit(solution)/shard_map/ppermute | solution.py:18
  66.5 3.3 %collective-permute-done.13.refs_2_ = bf16[32,2048]{1,0:T(8,128)(2,1)S(1)} collective-permute-done((bf16[32,2048]{1,0:T(8,128)(2,1)S(1)}, bf16[32,2048]{1,0:T(8,128)(2,1)S(1)}, u32[]{:S(2)}, u32[]{:S(2)}) %collective-permute-start.13) | collective-permute-done | bytes 131104 | tf_op jit(solution)/shard_map/ppermute | solution.py:18
  70.4 1.6 %collective-permute-done.17.refs_6_ = bf16[32,2048]{1,0:T(8,128)(2,1)S(1)} collective-permute-done((bf16[32,2048]{1,0:T(8,128)(2,1)S(1)}, bf16[32,2048]{1,0:T(8,128)(2,1)S(1)}, u32[]{:S(2)}, u32[]{:S(2)}) %collective-permute-start.17) | collective-permute-done | bytes 131104 | tf_op jit(solution)/shard_map/ppermute | solution.py:18
  72.0 5.5 %collective-permute-done.18.refs_7_ = bf16[32,2048]{1,0:T(8,128)(2,1)S(1)} collective-permute-done((bf16[32,2048]{1,0:T(8,128)(2,1)S(1)}, bf16[32,2048]{1,0:T(8,128)(2,1)S(1)}, u32[]{:S(2)}, u32[]{:S(2)}) %collective-permute-start.18) | collective-permute-done | bytes 131104 | tf_op jit(solution)/shard_map/ppermute | solution.py:18
  78.6 5.3 %collective-permute-done.19 = bf16[32,2048]{1,0:T(8,128)(2,1)S(1)} collective-permute-done((bf16[32,2048]{1,0:T(8,128)(2,1)S(1)}, bf16[32,2048]{1,0:T(8,128)(2,1)S(1)}, u32[]{:S(2)}, u32[]{:S(2)}) %collective-permute-start.19) | collective-permute-done | bytes 131104 | tf_op jit(solution)/shard_map/ppermute | solution.py:18
  83.9 0.7 add_convert_fusion
  (36 shorter events, 5.6 us)
Async XLA Ops:
  0.0 51.1 %copy-start = (bf16[1,2048,704]{1,2,0:T(8,128)(2,1)S(1)}, bf16[1,2048,704]{1,2,0:T(8,128)(2,1)}, u32[]{:S(2)}) copy-start(bf16[1,2048,704]{1,2,0:T(8,128)(2,1)} %param.19) | copy-start | bytes 8650756
  0.0 51.1 %collective-permute-start.9 = (bf16[704,2048]{1,0:T(8,128)(2,1)}, bf16[704,2048]{1,0:T(8,128)(2,1)}, u32[]{:S(2)}, u32[]{:S(2)}) collective-permute-start(bf16[704,2048]{1,0:T(8,128)(2,1)} %bitcast.13), channel_id=1, source_target_pairs={{0,1},{1,0},{2,3},{3,2},{4,5},{5,4},{6,7},{7,6},{8,9},{9,8},{10,11... | collective-permute-start | bytes 8650760 | tf_op jit(solution)/shard_map/ppermute | solution.py:18
  0.5 50.6 %collective-permute-start.10 = (bf16[704,2048]{1,0:T(8,128)(2,1)}, bf16[704,2048]{1,0:T(8,128)(2,1)}, u32[]{:S(2)}, u32[]{:S(2)}) collective-permute-start(bf16[704,2048]{1,0:T(8,128)(2,1)} %bitcast.18), channel_id=1, source_target_pairs={{0,1},{1,0},{2,3},{3,2},{4,5},{5,4},{6,7},{7,6},{8,9},{9,8},{10,11... | collective-permute-start | bytes 8650760 | tf_op jit(solution)/shard_map/ppermute | solution.py:18
  0.5 50.6 %collective-permute-start.11 = (bf16[704,2048]{1,0:T(8,128)(2,1)}, bf16[704,2048]{1,0:T(8,128)(2,1)}, u32[]{:S(2)}, u32[]{:S(2)}) collective-permute-start(bf16[704,2048]{1,0:T(8,128)(2,1)} %bitcast.20), channel_id=1, source_target_pairs={{0,1},{1,0},{2,3},{3,2},{4,5},{5,4},{6,7},{7,6},{8,9},{9,8},{10,11... | collective-permute-start | bytes 8650760 | tf_op jit(solution)/shard_map/ppermute | solution.py:18
  2.4 15.8 %collective-permute-start = (f32[12,32]{1,0:T(8,128)S(1)}, f32[12,32]{1,0:T(8,128)S(1)}, u32[]{:S(2)}, u32[]{:S(2)}) collective-permute-start(f32[12,32]{1,0:T(8,128)S(1)} %pad_maximum_fusion), channel_id=1, source_target_pairs={{0,16},{1,17},{2,18},{3,19},{4,20},{5,21},{6,22},{7,23},{8,24},{9,... | collective-permute-start | bytes 4616 | tf_op jit(solution)/shard_map/ppermute | solution.py:18
  6.3 1.6 %copy-start.1 = (bf16[16,512,128]{2,1,0:T(8,128)(2,1)S(1)}, bf16[16,512,128]{2,1,0:T(8,128)(2,1)}, u32[]{:S(2)}) copy-start(bf16[16,512,128]{2,1,0:T(8,128)(2,1)} %up_hbm.1) | copy-start | bytes 6291460
  7.9 1.5 %copy-start.2 = (bf16[4,384,576]{1,2,0:T(8,128)(2,1)S(1)}, bf16[4,384,576]{1,2,0:T(8,128)(2,1)}, u32[]{:S(2)}) copy-start(bf16[4,384,576]{1,2,0:T(8,128)(2,1)} %param.13) | copy-start | bytes 5308420
  9.4 1.1 %copy-start.3 = (bf16[4,8,16,576]{3,2,1,0:T(8,128)(2,1)S(1)}, bf16[4,8,16,576]{3,2,1,0:T(8,128)(2,1)}, u32[]{:S(2)}) copy-start(bf16[4,8,16,576]{3,2,1,0:T(8,128)(2,1)} %param.12) | copy-start | bytes 1769476
  10.4 0.9 %copy-start.4 = (bf16[32,2048]{1,0:T(8,128)(2,1)S(1)}, bf16[32,2048]{1,0:T(8,128)(2,1)}, u32[]{:S(2)}) copy-start(bf16[32,2048]{1,0:T(8,128)(2,1)} %residual.1) | copy-start | bytes 393220
  11.3 0.8 copy-start.5
  12.1 0.7 copy-start.6
  12.8 0.7 copy-start.7
  13.5 4.7 %copy-start.8 = (f32[32,6]{0,1:T(8,128)S(1)}, f32[32,6]{0,1:T(8,128)}, u32[]{:S(2)}) copy-start(f32[32,6]{0,1:T(8,128)} %param.23) | copy-start | bytes 2308
  18.1 9.1 %collective-permute-start.1 = (bf16[32,2048]{1,0:T(8,128)(2,1)S(1)}, bf16[32,2048]{1,0:T(8,128)(2,1)S(1)}, u32[]{:S(2)}, u32[]{:S(2)}) collective-permute-start(bf16[32,2048]{1,0:T(8,128)(2,1)S(1)} %get-tuple-element.32.here), channel_id=1, source_target_pairs={{0,16},{1,17},{2,18},{3,19},{4,20},{5,21},{6,22},{7,23},{8,24},{9,... | collective-permute-start | bytes 393224 | tf_op jit(solution)/shard_map/ppermute | solution.py:18
  27.5 5.0 %collective-permute-start.2 = (bf16[32,2048]{1,0:T(8,128)(2,1)S(1)}, bf16[32,2048]{1,0:T(8,128)(2,1)S(1)}, u32[]{:S(2)}, u32[]{:S(2)}) collective-permute-start(bf16[32,2048]{1,0:T(8,128)(2,1)S(1)} %get-tuple-element.34), channel_id=1, source_target_pairs={{0,2},{1,3},{2,0},{3,1},{4,6},{5,7},{6,4},{7,5},{8,10},{9,11},{10,... | collective-permute-start | bytes 393224 | tf_op jit(solution)/shard_map/ppermute | solution.py:18
  29.1 6.4 %collective-permute-start.3 = (bf16[32,2048]{1,0:T(8,128)(2,1)S(1)}, bf16[32,2048]{1,0:T(8,128)(2,1)S(1)}, u32[]{:S(2)}, u32[]{:S(2)}) collective-permute-start(bf16[32,2048]{1,0:T(8,128)(2,1)S(1)} %get-tuple-element.35), channel_id=1, source_target_pairs={{0,4},{1,5},{2,6},{3,7},{4,0},{5,1},{6,2},{7,3},{8,12},{9,13},{10,... | collective-permute-start | bytes 393224 | tf_op jit(solution)/shard_map/ppermute | solution.py:18
  32.6 5.9 %collective-permute-start.4 = (bf16[32,2048]{1,0:T(8,128)(2,1)S(1)}, bf16[32,2048]{1,0:T(8,128)(2,1)S(1)}, u32[]{:S(2)}, u32[]{:S(2)}) collective-permute-start(bf16[32,2048]{1,0:T(8,128)(2,1)S(1)} %get-tuple-element.36), channel_id=1, source_target_pairs={{0,6},{1,7},{2,4},{3,5},{4,2},{5,3},{6,0},{7,1},{8,14},{9,15},{10,... | collective-permute-start | bytes 393224 | tf_op jit(solution)/shard_map/ppermute | solution.py:18
  35.5 6.3 %collective-permute-start.5 = (bf16[32,2048]{1,0:T(8,128)(2,1)S(1)}, bf16[32,2048]{1,0:T(8,128)(2,1)S(1)}, u32[]{:S(2)}, u32[]{:S(2)}) collective-permute-start(bf16[32,2048]{1,0:T(8,128)(2,1)S(1)} %get-tuple-element.37), channel_id=1, source_target_pairs={{0,8},{1,9},{2,10},{3,11},{4,12},{5,13},{6,14},{7,15},{8,0},{9,1},... | collective-permute-start | bytes 393224 | tf_op jit(solution)/shard_map/ppermute | solution.py:18
  38.4 5.9 %collective-permute-start.6 = (bf16[32,2048]{1,0:T(8,128)(2,1)S(1)}, bf16[32,2048]{1,0:T(8,128)(2,1)S(1)}, u32[]{:S(2)}, u32[]{:S(2)}) collective-permute-start(bf16[32,2048]{1,0:T(8,128)(2,1)S(1)} %get-tuple-element.38), channel_id=1, source_target_pairs={{0,10},{1,11},{2,8},{3,9},{4,14},{5,15},{6,12},{7,13},{8,2},{9,3},... | collective-permute-start | bytes 393224 | tf_op jit(solution)/shard_map/ppermute | solution.py:18
  41.8 6.9 %collective-permute-start.7 = (bf16[32,2048]{1,0:T(8,128)(2,1)S(1)}, bf16[32,2048]{1,0:T(8,128)(2,1)S(1)}, u32[]{:S(2)}, u32[]{:S(2)}) collective-permute-start(bf16[32,2048]{1,0:T(8,128)(2,1)S(1)} %get-tuple-element.39), channel_id=1, source_target_pairs={{0,12},{1,13},{2,14},{3,15},{4,8},{5,9},{6,10},{7,11},{8,4},{9,5},... | collective-permute-start | bytes 393224 | tf_op jit(solution)/shard_map/ppermute | solution.py:18
  44.3 6.8 %collective-permute-start.8 = (bf16[32,2048]{1,0:T(8,128)(2,1)S(1)}, bf16[32,2048]{1,0:T(8,128)(2,1)S(1)}, u32[]{:S(2)}, u32[]{:S(2)}) collective-permute-start(bf16[32,2048]{1,0:T(8,128)(2,1)S(1)} %get-tuple-element.40), channel_id=1, source_target_pairs={{0,14},{1,15},{2,12},{3,13},{4,10},{5,11},{6,8},{7,9},{8,6},{9,7},... | collective-permute-start | bytes 393224 | tf_op jit(solution)/shard_map/ppermute | solution.py:18
  59.0 6.5 %collective-permute-start.12 = (bf16[32,2048]{1,0:T(8,128)(2,1)S(1)}, bf16[32,2048]{1,0:T(8,128)(2,1)S(1)}, u32[]{:S(2)}, u32[]{:S(2)}) collective-permute-start(bf16[32,2048]{1,0:T(8,128)(2,1)S(1)} %get-tuple-element.42), channel_id=1, source_target_pairs={{0,2},{1,3},{2,0},{3,1},{4,6},{5,7},{6,4},{7,5},{8,10},{9,11},{10,... | collective-permute-start | bytes 393224 | tf_op jit(solution)/shard_map/ppermute | solution.py:18
  60.5 9.2 %collective-permute-start.13 = (bf16[32,2048]{1,0:T(8,128)(2,1)S(1)}, bf16[32,2048]{1,0:T(8,128)(2,1)S(1)}, u32[]{:S(2)}, u32[]{:S(2)}) collective-permute-start(bf16[32,2048]{1,0:T(8,128)(2,1)S(1)} %get-tuple-element.43), channel_id=1, source_target_pairs={{0,4},{1,5},{2,6},{3,7},{4,0},{5,1},{6,2},{7,3},{8,12},{9,13},{10,... | collective-permute-start | bytes 393224 | tf_op jit(solution)/shard_map/ppermute | solution.py:18
  62.1 7.7 %collective-permute-start.14 = (bf16[32,2048]{1,0:T(8,128)(2,1)S(1)}, bf16[32,2048]{1,0:T(8,128)(2,1)S(1)}, u32[]{:S(2)}, u32[]{:S(2)}) collective-permute-start(bf16[32,2048]{1,0:T(8,128)(2,1)S(1)} %get-tuple-element.44), channel_id=1, source_target_pairs={{0,6},{1,7},{2,4},{3,5},{4,2},{5,3},{6,0},{7,1},{8,14},{9,15},{10,... | collective-permute-start | bytes 393224 | tf_op jit(solution)/shard_map/ppermute | solution.py:18
  62.5 7.2 %collective-permute-start.15 = (bf16[32,2048]{1,0:T(8,128)(2,1)S(1)}, bf16[32,2048]{1,0:T(8,128)(2,1)S(1)}, u32[]{:S(2)}, u32[]{:S(2)}) collective-permute-start(bf16[32,2048]{1,0:T(8,128)(2,1)S(1)} %get-tuple-element.45), channel_id=1, source_target_pairs={{0,8},{1,9},{2,10},{3,11},{4,12},{5,13},{6,14},{7,15},{8,0},{9,1},... | collective-permute-start | bytes 393224 | tf_op jit(solution)/shard_map/ppermute | solution.py:18
  63.0 7.4 %collective-permute-start.16 = (bf16[32,2048]{1,0:T(8,128)(2,1)S(1)}, bf16[32,2048]{1,0:T(8,128)(2,1)S(1)}, u32[]{:S(2)}, u32[]{:S(2)}) collective-permute-start(bf16[32,2048]{1,0:T(8,128)(2,1)S(1)} %get-tuple-element.46), channel_id=1, source_target_pairs={{0,10},{1,11},{2,8},{3,9},{4,14},{5,15},{6,12},{7,13},{8,2},{9,3},... | collective-permute-start | bytes 393224 | tf_op jit(solution)/shard_map/ppermute | solution.py:18
  65.5 6.5 %collective-permute-start.17 = (bf16[32,2048]{1,0:T(8,128)(2,1)S(1)}, bf16[32,2048]{1,0:T(8,128)(2,1)S(1)}, u32[]{:S(2)}, u32[]{:S(2)}) collective-permute-start(bf16[32,2048]{1,0:T(8,128)(2,1)S(1)} %get-tuple-element.47), channel_id=1, source_target_pairs={{0,12},{1,13},{2,14},{3,15},{4,8},{5,9},{6,10},{7,11},{8,4},{9,5},... | collective-permute-start | bytes 393224 | tf_op jit(solution)/shard_map/ppermute | solution.py:18
  69.7 7.8 %collective-permute-start.18 = (bf16[32,2048]{1,0:T(8,128)(2,1)S(1)}, bf16[32,2048]{1,0:T(8,128)(2,1)S(1)}, u32[]{:S(2)}, u32[]{:S(2)}) collective-permute-start(bf16[32,2048]{1,0:T(8,128)(2,1)S(1)} %get-tuple-element.48), channel_id=1, source_target_pairs={{0,14},{1,15},{2,12},{3,13},{4,10},{5,11},{6,8},{7,9},{8,6},{9,7},... | collective-permute-start | bytes 393224 | tf_op jit(solution)/shard_map/ppermute | solution.py:18
  78.0 5.9 %collective-permute-start.19 = (bf16[32,2048]{1,0:T(8,128)(2,1)S(1)}, bf16[32,2048]{1,0:T(8,128)(2,1)S(1)}, u32[]{:S(2)}, u32[]{:S(2)}) collective-permute-start(bf16[32,2048]{1,0:T(8,128)(2,1)S(1)} %get-tuple-element.50), channel_id=1, source_target_pairs={{0,16},{1,17},{2,18},{3,19},{4,20},{5,21},{6,22},{7,23},{8,24},{9,... | collective-permute-start | bytes 393224 | tf_op jit(solution)/shard_map/ppermute | solution.py:18

commit v2 on v1

v2 whole, which is shorter than its diff:
```python
import functools

import jax
import jax.numpy as jnp
from jax import lax
from jax.experimental import pallas as pl
from jax.experimental.pallas import tpu as pltpu
from jax.sharding import PartitionSpec as P

F32 = jnp.float32
BF16 = jnp.bfloat16
NT = (((1,), (1,)), ((), ()))
MIB = 1 << 20


def swapped(value, mask):
    pairs = [(source, source ^ mask) for source in range(lax.axis_size("ep"))]
    return lax.ppermute(value, "ep", pairs)


def whole():
    return pl.BlockSpec(memory_space=pltpu.VMEM)


def attend_kernel(heads, *refs):
    given, (stream, normed), held = refs[:7], refs[7:9], refs[9:16]
    mixed, sems = refs[16:]
    lengths, queries, cache, drafts, up, residual, gain = held
    reqs, rows, width = queries.shape
    parts = [(0, None), (3, None)]
    parts += [(i, r) for r in range(reqs) for i in (1, 2)]
    parts += [(4, None), (5, None), (6, None)]
    copies = {}
    for n, (i, r) in enumerate(parts):
        source, target = (given[i], held[i]) if r is None else (given[i].at[r], held[i].at[r])
        copies[i, r] = pltpu.make_async_copy(source, target, sems.at[n])
        copies[i, r].start()
    slots = cache.shape[2]
    draft = drafts.shape[1]
    latent, vdim = up.shape[1:]
    lanes = mixed.shape[2]
    scale = (vdim + width - latent) ** (-0.5)
    position = lax.broadcasted_iota(jnp.int32, (rows, slots), 1)
    token = lax.broadcasted_iota(jnp.int32, (rows, draft), 0) // heads
    causal = lax.broadcasted_iota(jnp.int32, (rows, draft), 1) <= token
    copies[0, None].wait()
    copies[3, None].wait()
    for r in range(reqs):
        copies[1, r].wait()
        copies[2, r].wait()
        q, c, d = queries[r], cache[r], drafts[r]
        cached = jnp.dot(q, c, preferred_element_type=F32) * scale
        own = lax.dot_general(q, d, NT, preferred_element_type=F32) * scale
        visible = position < lengths[r]
        cached = jnp.where(visible, cached, -1e30)
        own = jnp.where(causal, own, -1e30)
        highest = jnp.maximum(
            jnp.max(cached, axis=-1, keepdims=True), jnp.max(own, axis=-1, keepdims=True)
        )
        e_cached = jnp.where(visible, jnp.exp(cached - highest), 0.0)
        e_own = jnp.where(causal, jnp.exp(own - highest), 0.0)
        total = jnp.sum(e_cached, axis=-1, keepdims=True) + jnp.sum(e_own, axis=-1, keepdims=True)
        inverse = 1.0 / total
        p_cached = (e_cached * inverse).astype(BF16)
        p_own = (e_own * inverse).astype(BF16)
        out = lax.dot_general(p_cached, c[:latent, :], NT, preferred_element_type=F32)
        out = out + jnp.dot(p_own, d[:, :latent], preferred_element_type=F32)
        for g in range(latent // lanes):
            mixed[g, r * rows : (r + 1) * rows, :] = out[:, g * lanes : (g + 1) * lanes]
    for i in (4, 5, 6):
        copies[i, None].wait()
    tokens = stream.shape[0]
    square = jnp.zeros((tokens, 1), F32)
    for head in range(heads):
        part = jnp.concatenate(
            [mixed[g, pl.ds(head, tokens, stride=heads), :] for g in range(latent // lanes)],
            axis=1,
        ).astype(BF16)
        columns = slice(head * vdim, (head + 1) * vdim)
        value = residual[:, columns].astype(F32) + jnp.dot(
            part, up[head], preferred_element_type=F32
        )
        stream[:, columns] = value
        square = square + jnp.sum(value * value, axis=-1, keepdims=True)
    factor = lax.rsqrt(square / stream.shape[1] + 1e-06)
    normed[...] = (stream[...] * factor * gain[...]).astype(BF16)


def attend(queries, cache, drafts, lengths, value_up, residual, norm_gain):
    reqs, draft, heads, width = queries.shape
    slots = cache.shape[1]
    latent, vdim = value_up.shape[1:]
    tokens, features = residual.shape
    rows = draft * heads
    flops = 2 * reqs * rows * slots * (width + latent) + 2 * tokens * heads * latent * vdim
    operands = (
        lengths,
        queries.reshape(reqs, rows, width),
        jnp.swapaxes(cache, 1, 2),
        drafts,
        value_up,
        residual,
        norm_gain.reshape(1, features),
    )
    return pl.pallas_call(
        functools.partial(attend_kernel, heads),
        in_specs=[pl.BlockSpec(memory_space=pltpu.HBM)] * 7,
        out_specs=[whole()] * 2,
        out_shape=[
            jax.ShapeDtypeStruct((tokens, features), F32),
            jax.ShapeDtypeStruct((tokens, features), BF16),
        ],
        scratch_shapes=[pltpu.SMEM(lengths.shape, jnp.int32)]
        + [pltpu.VMEM(o.shape, o.dtype) for o in operands[1:]]
        + [
            pltpu.VMEM((latent // 128, reqs * rows, 128), F32),
            pltpu.SemaphoreType.DMA((2 * reqs + 5,)),
        ],
        cost_estimate=pl.CostEstimate(
            flops=flops, bytes_accessed=6 * MIB, transcendentals=reqs * rows * slots
        ),
        compiler_params=pltpu.CompilerParams(vmem_limit_bytes=60 * MIB),
    )(*operands)


def table_kernel(top, tokens, stride, mine, routed, pick, high, low, table):
    experts = mine[...]
    both = routed.shape[1]
    count = experts.shape[0]
    named = jnp.zeros((count, both), F32)
    weight = jnp.zeros((count, both), F32)
    for k in range(top):
        hit = jnp.where(routed[k : k + 1, :] == experts, 1.0, 0.0)
        named = named + hit
        weight = weight + hit * routed[top + k : top + k + 1, :]
    earlier = lax.broadcasted_iota(jnp.int32, (both, both), 0)
    later = lax.broadcasted_iota(jnp.int32, (both, both), 1)
    before = (earlier < later) & ((earlier < tokens) == (later < tokens))
    rank = jnp.dot(
        named.astype(BF16),
        jnp.where(before, 1.0, 0.0).astype(BF16),
        preferred_element_type=F32,
    )
    behind = lax.broadcasted_iota(jnp.int32, (count, both), 1) >= tokens
    place = rank.astype(jnp.int32) + jnp.where(behind, stride, 0)
    place = jnp.where(named > 0.0, place, -1)
    slots = lax.broadcasted_iota(jnp.int32, (2 * stride, both), 0)
    for m in range(count):
        hit = jnp.where(slots == place[m : m + 1, :], 1.0, 0.0)
        rows = slice(2 * stride * m, 2 * stride * (m + 1))
        pick[rows, :] = hit.astype(BF16)
        table[rows, :] = hit * weight[m : m + 1, :]
    turned = table[...].T
    top_bits = turned.astype(BF16)
    high[...] = top_bits
    low[...] = (turned - top_bits.astype(F32)).astype(BF16)


def tables(mine, routed, top, tokens, stride):
    rows = mine.shape[0] * 2 * stride
    both = 2 * tokens
    return pl.pallas_call(
        functools.partial(table_kernel, top, tokens, stride),
        in_specs=[whole()] * 2,
        out_specs=[whole()] * 3,
        out_shape=[
            jax.ShapeDtypeStruct((rows, both), BF16),
            jax.ShapeDtypeStruct((both, rows), BF16),
            jax.ShapeDtypeStruct((both, rows), BF16),
        ],
        scratch_shapes=[pltpu.VMEM((rows, both), F32)],
        cost_estimate=pl.CostEstimate(flops=MIB, bytes_accessed=MIB // 4, transcendentals=0),
        compiler_params=pltpu.CompilerParams(vmem_limit_bytes=16 * MIB),
    )(mine, routed)


def dispatch_kernel(pick, here, there, *blocks):
    both = jnp.concatenate([here[...], there[...]], axis=0)
    rows = blocks[0].shape[0]
    for m, block in enumerate(blocks):
        block[...] = jnp.dot(
            pick[m * rows : (m + 1) * rows, :], both, preferred_element_type=F32
        ).astype(BF16)


def dispatch(pick, here, there, count):
    rows, width = pick.shape[0] // count, here.shape[1]
    return pl.pallas_call(
        dispatch_kernel,
        in_specs=[whole()] * 3,
        out_specs=[whole()] * count,
        out_shape=[jax.ShapeDtypeStruct((rows, width), BF16)] * count,
        cost_estimate=pl.CostEstimate(
            flops=2 * pick.size * width, bytes_accessed=3 * MIB // 2, transcendentals=0
        ),
        compiler_params=pltpu.CompilerParams(vmem_limit_bytes=16 * MIB),
    )(pick, here, there)


def load_kernel(*refs):
    count = len(refs) // 2
    sems = refs[-1]
    copies = [
        pltpu.make_async_copy(refs[i], refs[count + i], sems.at[i]) for i in range(count)
    ]
    for copy in copies:
        copy.start()
    for copy in copies:
        copy.wait()


def load(weights, room):
    return pl.pallas_call(
        load_kernel,
        in_specs=[pl.BlockSpec(memory_space=pl.ANY)] * len(weights),
        out_specs=[whole()] * len(weights),
        out_shape=[jax.ShapeDtypeStruct(w.shape, w.dtype) for w in weights],
        scratch_shapes=[pltpu.SemaphoreType.DMA((len(weights),))],
        cost_estimate=pl.CostEstimate(
            flops=0, bytes_accessed=2 * sum(2 * w.size for w in weights), transcendentals=0
        ),
        compiler_params=pltpu.CompilerParams(vmem_limit_bytes=room * MIB),
    )(*weights)


def expert_kernel(count, *refs):
    blocks = refs[:count]
    near, far = refs[count : count + 3], refs[count + 3 : count + 6]
    outs = refs[count + 6 : 2 * count + 6]
    held = refs[2 * count + 6 : 2 * count + 9]
    rows_ref, total, sems = refs[2 * count + 9 :]
    copies = [pltpu.make_async_copy(far[i], held[i], sems.at[i]) for i in range(3)]
    for copy in copies:
        copy.start()
    size = blocks[0].shape[0]
    for m, block in enumerate(blocks):
        rows_ref[m * size : (m + 1) * size, :] = block[...]

    def half(weights, ready):
        w_gate, w_up, w_down = weights
        ready(0)
        gate = lax.dot_general(rows_ref[...], w_gate[...], NT, preferred_element_type=F32)
        ready(1)
        upper = lax.dot_general(rows_ref[...], w_up[...], NT, preferred_element_type=F32)
        active = (gate * (1.0 / (1.0 + jnp.exp(-gate))) * upper).astype(BF16)
        ready(2)
        return jnp.dot(active, w_down[...], preferred_element_type=F32)

    total[...] = half(near, lambda i: None)
    result = (total[...] + half(held, lambda i: copies[i].wait())).astype(BF16)
    for m, out in enumerate(outs):
        out[...] = result[m * size : (m + 1) * size, :]


def run_expert(blocks, near, far):
    count = len(blocks)
    size, width = blocks[0].shape
    units = near[0].shape[0]
    return pl.pallas_call(
        functools.partial(expert_kernel, count),
        in_specs=[whole()] * (count + 3) + [pl.BlockSpec(memory_space=pl.ANY)] * 3,
        out_specs=[whole()] * count,
        out_shape=[jax.ShapeDtypeStruct((size, width), BF16)] * count,
        scratch_shapes=[pltpu.VMEM((units, width), BF16)] * 3
        + [
            pltpu.VMEM((count * size, width), BF16),
            pltpu.VMEM((count * size, width), F32),
            pltpu.SemaphoreType.DMA((3,)),
        ],
        cost_estimate=pl.CostEstimate(
            flops=12 * count * size * width * units,
            bytes_accessed=12 * units * width,
            transcendentals=2 * count * size * units,
        ),
        compiler_params=pltpu.CompilerParams(vmem_limit_bytes=36 * MIB),
    )(*blocks, *near, *far)


def combine_kernel(high, low, *refs):
    blocks, (here, there) = refs[:-2], refs[-2:]
    rows = jnp.concatenate([block[...] for block in blocks], axis=0)
    total = jnp.dot(high[...], rows, preferred_element_type=F32)
    total = total + jnp.dot(low[...], rows, preferred_element_type=F32)
    tokens = here.shape[0]
    here[...] = total[:tokens]
    there[...] = total[tokens:].astype(BF16)


def combine(high, low, blocks):
    both, rows = high.shape
    width = blocks[0].shape[1]
    return pl.pallas_call(
        combine_kernel,
        in_specs=[whole()] * (2 + len(blocks)),
        out_specs=[whole()] * 2,
        out_shape=[
            jax.ShapeDtypeStruct((both // 2, width), F32),
            jax.ShapeDtypeStruct((both // 2, width), BF16),
        ],
        cost_estimate=pl.CostEstimate(
            flops=4 * both * rows * width, bytes_accessed=3 * MIB // 2, transcendentals=0
        ),
        compiler_params=pltpu.CompilerParams(vmem_limit_bytes=16 * MIB),
    )(high, low, *blocks)


def local(
    queries,
    cache,
    drafts,
    lengths,
    value_up,
    residual,
    norm_gain,
    w_gate,
    w_up,
    w_down,
    routes,
    combine_weights,
):
    tokens, top = routes.shape
    devices = lax.axis_size("ep")
    experts = devices // 2
    near = experts // 2
    capacity = min(tokens, 2 * (((tokens * top + experts - 1) // experts + 3) // 2))
    stride = -(-capacity // 8) * 8

    routed = jnp.concatenate([routes.T.astype(F32), combine_weights.T], axis=0)
    own = [jnp.swapaxes(w_gate, 1, 2)[0], jnp.swapaxes(w_up, 1, 2)[0], w_down[0]]
    other = [swapped(w, 1) for w in own]
    chip = lax.axis_index("ep") // 2
    mine = (chip ^ jnp.arange(near, dtype=jnp.int32)).astype(F32)[:, None]

    stream, normed = attend(queries, cache, drafts, lengths, value_up, residual, norm_gain)
    routed, normed, own = lax.optimization_barrier((routed, normed, own))
    across = swapped(normed, devices // 2)
    routed = jnp.concatenate([routed, swapped(routed, devices // 2)], axis=1)
    pick, high, low = tables(mine, routed, top, tokens, stride)
    own = load(own, 44)
    across, own, other = lax.optimization_barrier((across, own, other))
    blocks = dispatch(pick, normed, across, near)
    blocks = [swapped(b, 2 * m) if m else b for m, b in enumerate(blocks)]
    blocks = run_expert(blocks, own, other)
    blocks = [swapped(b, 2 * m) if m else b for m, b in enumerate(blocks)]
    here, there = combine(high, low, blocks)
    return (stream + (here + swapped(there, devices // 2).astype(F32))).astype(BF16)


def solution(mesh):
    placed = (
        P(("groups", "ep"), None, None, None),
        P(("groups", "ep"), None, None),
        P(("groups", "ep"), None, None),
        P(("groups", "ep")),
        P(),
        P(("groups", "ep"), None),
        P(),
        P("ep", None, None),
        P("ep", None, None),
        P("ep", None, None),
        P(("groups", "ep"), None),
        P(("groups", "ep"), None),
    )
    return jax.shard_map(
        local, mesh=mesh, in_specs=placed, out_specs=P(("groups", "ep"), None), check_vma=False
    )
```

time: 85 us -> 68.7 us (0.81)
  waiting for transfers between devices: 40.8 us -> 24.3 us
  local copies, waits for them, and re-layouts: 7.19 us -> 0.01 us
  starting transfers between devices: 20.7 us -> 25.8 us
  Pallas kernels: 13.7 us -> 17.5 us
  other arithmetic: 2.17 us -> 0.8 us
    ppermute x20, waiting for transfers between devices: 40.8 us -> 24.3 us  [swapped(): return lax.ppermute(value, 'ep', pairs)]
    unnamed x18 -> x8, local copies, waits for them, and re-layouts: 7.19 us -> 0.01 us
    ppermute x20, starting transfers between devices: 20.7 us -> 25.8 us  [swapped(): return lax.ppermute(value, 'ep', pairs)]
    pallas_call x1 -> x2, Pallas kernels: 4.57 us -> 9.63 us  [the longest x1 6.04 us: attend(): pl.pallas_call(functools.partial(attend_kernel, heads), in_specs=[pl.Bloc...]
    pallas_call x1, Pallas kernels: 7.88 us -> 6.71 us  [run_expert(): pl.pallas_call(functools.partial(expert_kernel, count), in_specs=[whole()...]
  transfers between devices with their start and end apart: 20 -> 20, of which waited for: 13 -> 10; matrix products, arithmetic and copies ran while one was open for 2% -> 0% of each run, Pallas kernels for 6% -> 14%
where the time goes in v2:
time: 68.7 us; the launch traced here: 68.6 us
  starting transfers between devices  25.8 us (38%)
  waiting for transfers between devices  24.3 us (35%)
  Pallas kernels  17.5 us (25%)
  other arithmetic  0.8 us (1%)
    ppermute x20, starting transfers between devices, swapped(): return lax.ppermute(value, 'ep', pairs)  25.8 us
    ppermute x20, waiting for transfers between devices, swapped(): return lax.ppermute(value, 'ep', pairs)  24.3 us
    pallas_call x1, Pallas kernels, run_expert(): pl.pallas_call(functools.partial(expert_kernel, count), in_specs=[whole()...  6.71 us
    pallas_call x1, Pallas kernels, attend(): pl.pallas_call(functools.partial(attend_kernel, heads), in_specs=[pl.Bloc...  6.04 us
    pallas_call x1, Pallas kernels, load(): pl.pallas_call(load_kernel, in_specs=[pl.BlockSpec(memory_space=pl.ANY)]...  3.59 us
  transfers between devices with their start and end apart: 20, of which 10 were waited for; matrix products, arithmetic and copies ran while one was open for 0% of the time, Pallas kernels for 14%

profile of v2, /device:TPU:0, one launch (start us, length us, event | category | flops | bytes accessed | tf_op | source)
XLA Modules:
  0.0 68.6 jit_solution(13393358511085136000)
XLA Ops:
  0.0 0.5 collective-permute-start.2
  0.5 0.4 collective-permute-start.4
  1.0 6.0 %shard_map.118 = (f32[32,2048]{1,0:T(8,128)}, bf16[32,2048]{1,0:T(8,128)(2,1)}) custom-call(s32[4]{0:T(128)} %refs_0_.1, bf16[4,128,576]{2,1,0:T(8,128)(2,1)} %bitcast.20, bf16[4,576,384]{2,1,0:T(8,128)(2,1)} %bitcast.19, bf16[4,8,576]{2,1,0:T(8,128)(2,1)} %refs_3_.1, bf16[16,512,128]{2,1,0:T(8,128)(2,1)} %refs_4_.1, bf16[32,2048]{1,0:T(8,128)(2,1)} %refs_5_.1, ...), custom_call_target="tpu_custom_call" | custom-call | flops 494927872 | bytes 6291456 | tf_op jit(solution)/shard_map/pallas_call | solution.py:105
  7.1 3.7 %collective-permute-start = (f32[12,32]{1,0:T(8,128)S(1)}, f32[12,32]{1,0:T(8,128)S(1)}, u32[]{:S(2)}, u32[]{:S(2)}) collective-permute-start(f32[12,32]{1,0:T(8,128)S(1)} %pad_maximum_fusion), channel_id=1, source_target_pairs={{0,16},{1,17},{2,18},{3,19},{4,20},{5,21},{6,22},{7,23},{8,24},{9,... | collective-permute-start | bytes 4616 | tf_op jit(solution)/shard_map/ppermute | solution.py:18
  10.9 3.6 %shard_map.120 = (bf16[704,2048]{1,0:T(8,128)(2,1)S(1)}, bf16[704,2048]{1,0:T(8,128)(2,1)S(1)}, bf16[704,2048]{1,0:T(8,128)(2,1)S(1)}) custom-call(bf16[704,2048]{1,0:T(8,128)(2,1)} %bitcast.14, bf16[704,2048]{1,0:T(8,128)(2,1)} %bitcast.16, bf16[704,2048]{1,0:T(8,128)(2,1)} %bitcast.18), custom_call_target="tpu_custom_call" | custom-call | bytes 17301504 | tf_op jit(solution)/shard_map/pallas_call | solution.py:213
  14.9 5.4 %collective-permute-done.1.there = bf16[32,2048]{1,0:T(8,128)(2,1)S(1)} collective-permute-done((bf16[32,2048]{1,0:T(8,128)(2,1)}, bf16[32,2048]{1,0:T(8,128)(2,1)S(1)}, u32[]{:S(2)}, u32[]{:S(2)}) %collective-permute-start.1) | collective-permute-done | bytes 131104 | tf_op jit(solution)/shard_map/ppermute | solution.py:18
  20.3 0.4 shard_map.121
  20.7 1.6 %collective-permute-start.5 = (bf16[32,2048]{1,0:T(8,128)(2,1)S(1)}, bf16[32,2048]{1,0:T(8,128)(2,1)S(1)}, u32[]{:S(2)}, u32[]{:S(2)}) collective-permute-start(bf16[32,2048]{1,0:T(8,128)(2,1)S(1)} %get-tuple-element.58), channel_id=1, source_target_pairs={{0,2},{1,3},{2,0},{3,1},{4,6},{5,7},{6,4},{7,5},{8,10},{9,11},{10,... | collective-permute-start | bytes 393224 | tf_op jit(solution)/shard_map/ppermute | solution.py:18
  22.3 1.5 %collective-permute-start.6 = (bf16[32,2048]{1,0:T(8,128)(2,1)S(1)}, bf16[32,2048]{1,0:T(8,128)(2,1)S(1)}, u32[]{:S(2)}, u32[]{:S(2)}) collective-permute-start(bf16[32,2048]{1,0:T(8,128)(2,1)S(1)} %get-tuple-element.59), channel_id=1, source_target_pairs={{0,4},{1,5},{2,6},{3,7},{4,0},{5,1},{6,2},{7,3},{8,12},{9,13},{10,... | collective-permute-start | bytes 393224 | tf_op jit(solution)/shard_map/ppermute | solution.py:18
  23.8 0.5 collective-permute-start.7
  24.3 3.0 %collective-permute-start.9 = (bf16[32,2048]{1,0:T(8,128)(2,1)S(1)}, bf16[32,2048]{1,0:T(8,128)(2,1)S(1)}, u32[]{:S(2)}, u32[]{:S(2)}) collective-permute-start(bf16[32,2048]{1,0:T(8,128)(2,1)S(1)} %get-tuple-element.62), channel_id=1, source_target_pairs={{0,10},{1,11},{2,8},{3,9},{4,14},{5,15},{6,12},{7,13},{8,2},{9,3},... | collective-permute-start | bytes 393224 | tf_op jit(solution)/shard_map/ppermute | solution.py:18
  27.2 1.0 %collective-permute-start.10 = (bf16[32,2048]{1,0:T(8,128)(2,1)S(1)}, bf16[32,2048]{1,0:T(8,128)(2,1)S(1)}, u32[]{:S(2)}, u32[]{:S(2)}) collective-permute-start(bf16[32,2048]{1,0:T(8,128)(2,1)S(1)} %get-tuple-element.63), channel_id=1, source_target_pairs={{0,12},{1,13},{2,14},{3,15},{4,8},{5,9},{6,10},{7,11},{8,4},{9,5},... | collective-permute-start | bytes 393224 | tf_op jit(solution)/shard_map/ppermute | solution.py:18
  28.2 1.0 %collective-permute-done.6.refs_2_ = bf16[32,2048]{1,0:T(8,128)(2,1)S(1)} collective-permute-done((bf16[32,2048]{1,0:T(8,128)(2,1)S(1)}, bf16[32,2048]{1,0:T(8,128)(2,1)S(1)}, u32[]{:S(2)}, u32[]{:S(2)}) %collective-permute-start.6) | collective-permute-done | bytes 131104 | tf_op jit(solution)/shard_map/ppermute | solution.py:18
  29.2 2.9 %collective-permute-start.11 = (bf16[32,2048]{1,0:T(8,128)(2,1)S(1)}, bf16[32,2048]{1,0:T(8,128)(2,1)S(1)}, u32[]{:S(2)}, u32[]{:S(2)}) collective-permute-start(bf16[32,2048]{1,0:T(8,128)(2,1)S(1)} %get-tuple-element.64), channel_id=1, source_target_pairs={{0,14},{1,15},{2,12},{3,13},{4,10},{5,11},{6,8},{7,9},{8,6},{9,7},... | collective-permute-start | bytes 393224 | tf_op jit(solution)/shard_map/ppermute | solution.py:18
  32.1 2.4 %collective-permute-done.9.refs_5_ = bf16[32,2048]{1,0:T(8,128)(2,1)S(1)} collective-permute-done((bf16[32,2048]{1,0:T(8,128)(2,1)S(1)}, bf16[32,2048]{1,0:T(8,128)(2,1)S(1)}, u32[]{:S(2)}, u32[]{:S(2)}) %collective-permute-start.9) | collective-permute-done | bytes 131104 | tf_op jit(solution)/shard_map/ppermute | solution.py:18
  34.5 2.2 %collective-permute-done.10.refs_6_ = bf16[32,2048]{1,0:T(8,128)(2,1)S(1)} collective-permute-done((bf16[32,2048]{1,0:T(8,128)(2,1)S(1)}, bf16[32,2048]{1,0:T(8,128)(2,1)S(1)}, u32[]{:S(2)}, u32[]{:S(2)}) %collective-permute-start.10) | collective-permute-done | bytes 131104 | tf_op jit(solution)/shard_map/ppermute | solution.py:18
  36.7 1.9 %collective-permute-done.11.refs_7_ = bf16[32,2048]{1,0:T(8,128)(2,1)S(1)} collective-permute-done((bf16[32,2048]{1,0:T(8,128)(2,1)S(1)}, bf16[32,2048]{1,0:T(8,128)(2,1)S(1)}, u32[]{:S(2)}, u32[]{:S(2)}) %collective-permute-start.11) | collective-permute-done | bytes 131104 | tf_op jit(solution)/shard_map/ppermute | solution.py:18
  38.5 6.7 %shard_map.122 = (bf16[32,2048]{1,0:T(8,128)(2,1)S(1)}, bf16[32,2048]{1,0:T(8,128)(2,1)S(1)}, bf16[32,2048]{1,0:T(8,128)(2,1)S(1)}, bf16[32,2048]{1,0:T(8,128)(2...) custom-call(bf16[32,2048]{1,0:T(8,128)(2,1)S(1)} %get-tuple-element., ...), custom_call_target="tpu_custom_call" | custom-call | flops 4429185024 | bytes 17301504 | tf_op jit(solution)/shard_map/pallas_call | solution.py:259
  45.3 0.6 collective-permute-start.12
  45.9 0.6 collective-permute-start.13
  46.5 2.4 %collective-permute-start.14 = (bf16[32,2048]{1,0:T(8,128)(2,1)S(1)}, bf16[32,2048]{1,0:T(8,128)(2,1)S(1)}, u32[]{:S(2)}, u32[]{:S(2)}) collective-permute-start(bf16[32,2048]{1,0:T(8,128)(2,1)S(1)} %get-tuple-element.74), channel_id=1, source_target_pairs={{0,6},{1,7},{2,4},{3,5},{4,2},{5,3},{6,0},{7,1},{8,14},{9,15},{10,... | collective-permute-start | bytes 393224 | tf_op jit(solution)/shard_map/ppermute | solution.py:18
  49.1 1.8 %collective-permute-start.16 = (bf16[32,2048]{1,0:T(8,128)(2,1)S(1)}, bf16[32,2048]{1,0:T(8,128)(2,1)S(1)}, u32[]{:S(2)}, u32[]{:S(2)}) collective-permute-start(bf16[32,2048]{1,0:T(8,128)(2,1)S(1)} %get-tuple-element.76), channel_id=1, source_target_pairs={{0,10},{1,11},{2,8},{3,9},{4,14},{5,15},{6,12},{7,13},{8,2},{9,3},... | collective-permute-start | bytes 393224 | tf_op jit(solution)/shard_map/ppermute | solution.py:18
  50.8 0.9 %collective-permute-done.12.refs_1_ = bf16[32,2048]{1,0:T(8,128)(2,1)S(1)} collective-permute-done((bf16[32,2048]{1,0:T(8,128)(2,1)S(1)}, bf16[32,2048]{1,0:T(8,128)(2,1)S(1)}, u32[]{:S(2)}, u32[]{:S(2)}) %collective-permute-start.12) | collective-permute-done | bytes 131104 | tf_op jit(solution)/shard_map/ppermute | solution.py:18
  51.7 1.1 %collective-permute-start.17 = (bf16[32,2048]{1,0:T(8,128)(2,1)S(1)}, bf16[32,2048]{1,0:T(8,128)(2,1)S(1)}, u32[]{:S(2)}, u32[]{:S(2)}) collective-permute-start(bf16[32,2048]{1,0:T(8,128)(2,1)S(1)} %get-tuple-element.77), channel_id=1, source_target_pairs={{0,12},{1,13},{2,14},{3,15},{4,8},{5,9},{6,10},{7,11},{8,4},{9,5},... | collective-permute-start | bytes 393224 | tf_op jit(solution)/shard_map/ppermute | solution.py:18
  52.9 2.4 %collective-permute-start.18 = (bf16[32,2048]{1,0:T(8,128)(2,1)S(1)}, bf16[32,2048]{1,0:T(8,128)(2,1)S(1)}, u32[]{:S(2)}, u32[]{:S(2)}) collective-permute-start(bf16[32,2048]{1,0:T(8,128)(2,1)S(1)} %get-tuple-element.78), channel_id=1, source_target_pairs={{0,14},{1,15},{2,12},{3,13},{4,10},{5,11},{6,8},{7,9},{8,6},{9,7},... | collective-permute-start | bytes 393224 | tf_op jit(solution)/shard_map/ppermute | solution.py:18
  55.3 1.4 %collective-permute-done.16.refs_5_ = bf16[32,2048]{1,0:T(8,128)(2,1)S(1)} collective-permute-done((bf16[32,2048]{1,0:T(8,128)(2,1)S(1)}, bf16[32,2048]{1,0:T(8,128)(2,1)S(1)}, u32[]{:S(2)}, u32[]{:S(2)}) %collective-permute-start.16) | collective-permute-done | bytes 131104 | tf_op jit(solution)/shard_map/ppermute | solution.py:18
  56.7 1.4 %collective-permute-done.17.refs_6_ = bf16[32,2048]{1,0:T(8,128)(2,1)S(1)} collective-permute-done((bf16[32,2048]{1,0:T(8,128)(2,1)S(1)}, bf16[32,2048]{1,0:T(8,128)(2,1)S(1)}, u32[]{:S(2)}, u32[]{:S(2)}) %collective-permute-start.17) | collective-permute-done | bytes 131104 | tf_op jit(solution)/shard_map/ppermute | solution.py:18
  58.1 2.0 %collective-permute-done.18.refs_7_ = bf16[32,2048]{1,0:T(8,128)(2,1)S(1)} collective-permute-done((bf16[32,2048]{1,0:T(8,128)(2,1)S(1)}, bf16[32,2048]{1,0:T(8,128)(2,1)S(1)}, u32[]{:S(2)}, u32[]{:S(2)}) %collective-permute-start.18) | collective-permute-done | bytes 131104 | tf_op jit(solution)/shard_map/ppermute | solution.py:18
  60.1 0.5 shard_map.123
  60.5 1.5 %collective-permute-start.19 = (bf16[32,2048]{1,0:T(8,128)(2,1)S(1)}, bf16[32,2048]{1,0:T(8,128)(2,1)S(1)}, u32[]{:S(2)}, u32[]{:S(2)}) collective-permute-start(bf16[32,2048]{1,0:T(8,128)(2,1)S(1)} %get-tuple-element.80), channel_id=1, source_target_pairs={{0,16},{1,17},{2,18},{3,19},{4,20},{5,21},{6,22},{7,23},{8,24},{9,... | collective-permute-start | bytes 393224 | tf_op jit(solution)/shard_map/ppermute | solution.py:18
  62.1 5.8 %collective-permute-done.19 = bf16[32,2048]{1,0:T(8,128)(2,1)S(1)} collective-permute-done((bf16[32,2048]{1,0:T(8,128)(2,1)S(1)}, bf16[32,2048]{1,0:T(8,128)(2,1)S(1)}, u32[]{:S(2)}, u32[]{:S(2)}) %collective-permute-start.19) | collective-permute-done | bytes 131104 | tf_op jit(solution)/shard_map/ppermute | solution.py:18
  67.9 0.7 %add_convert_fusion = bf16[32,2048]{1,0:T(8,128)(2,1)} fusion(f32[32,2048]{1,0:T(8,128)S(1)} %copy-done.1, f32[32,2048]{1,0:T(8,128)S(1)} %get-tuple-element.79, bf16[32,2048]{1,0:T(8,128)(2,1)S(1)} %collective-permute-done.19), kind=kLoop, calls=%fused_computation | loop fusion | flops 262144 | bytes 786432 | tf_op jit(solution)/shard_map/convert_element_type | solution.py:346
  (27 shorter events, 0.9 us)
Async XLA Ops:
  0.0 7.0 %copy-start.2 = (s32[32,6]{0,1:T(8,128)S(1)}, s32[32,6]{0,1:T(8,128)}, u32[]{:S(2)}) copy-start(s32[32,6]{0,1:T(8,128)} %param.22) | copy-start | bytes 2308
  0.0 7.0 %copy-start.3 = (f32[32,6]{0,1:T(8,128)S(1)}, f32[32,6]{0,1:T(8,128)}, u32[]{:S(2)}) copy-start(f32[32,6]{0,1:T(8,128)} %param.23) | copy-start | bytes 2308
  0.0 20.3 %collective-permute-start.2 = (bf16[704,2048]{1,0:T(8,128)(2,1)}, bf16[704,2048]{1,0:T(8,128)(2,1)S(1)}, u32[]{:S(2)}, u32[]{:S(2)}) collective-permute-start(bf16[704,2048]{1,0:T(8,128)(2,1)} %bitcast.13), channel_id=1, source_target_pairs={{0,1},{1,0},{2,3},{3,2},{4,5},{5,4},{6,7},{7,6},{8,9},{9,8},{10,11... | collective-permute-start | bytes 8650760 | tf_op jit(solution)/shard_map/ppermute | solution.py:18
  0.5 19.8 %collective-permute-start.3 = (bf16[704,2048]{1,0:T(8,128)(2,1)}, bf16[704,2048]{1,0:T(8,128)(2,1)}, u32[]{:S(2)}, u32[]{:S(2)}) collective-permute-start(bf16[704,2048]{1,0:T(8,128)(2,1)} %bitcast.15), channel_id=1, source_target_pairs={{0,1},{1,0},{2,3},{3,2},{4,5},{5,4},{6,7},{7,6},{8,9},{9,8},{10,11... | collective-permute-start | bytes 8650760 | tf_op jit(solution)/shard_map/ppermute | solution.py:18
  0.5 19.8 %collective-permute-start.4 = (bf16[704,2048]{1,0:T(8,128)(2,1)}, bf16[704,2048]{1,0:T(8,128)(2,1)}, u32[]{:S(2)}, u32[]{:S(2)}) collective-permute-start(bf16[704,2048]{1,0:T(8,128)(2,1)} %bitcast.17), channel_id=1, source_target_pairs={{0,1},{1,0},{2,3},{3,2},{4,5},{5,4},{6,7},{7,6},{8,9},{9,8},{10,11... | collective-permute-start | bytes 8650760 | tf_op jit(solution)/shard_map/ppermute | solution.py:18
  7.1 7.4 %collective-permute-start = (f32[12,32]{1,0:T(8,128)S(1)}, f32[12,32]{1,0:T(8,128)S(1)}, u32[]{:S(2)}, u32[]{:S(2)}) collective-permute-start(f32[12,32]{1,0:T(8,128)S(1)} %pad_maximum_fusion), channel_id=1, source_target_pairs={{0,16},{1,17},{2,18},{3,19},{4,20},{5,21},{6,22},{7,23},{8,24},{9,... | collective-permute-start | bytes 4616 | tf_op jit(solution)/shard_map/ppermute | solution.py:18
  10.8 9.5 %collective-permute-start.1 = (bf16[32,2048]{1,0:T(8,128)(2,1)}, bf16[32,2048]{1,0:T(8,128)(2,1)S(1)}, u32[]{:S(2)}, u32[]{:S(2)}) collective-permute-start(bf16[32,2048]{1,0:T(8,128)(2,1)} %get-tuple-element.49.here), channel_id=1, source_target_pairs={{0,16},{1,17},{2,18},{3,19},{4,20},{5,21},{6,22},{7,23},{8,24},{9,... | collective-permute-start | bytes 393224 | tf_op jit(solution)/shard_map/ppermute | solution.py:18
  10.9 9.4 %copy-start = (bf16[32,2048]{1,0:T(8,128)(2,1)S(1)}, bf16[32,2048]{1,0:T(8,128)(2,1)}, u32[]{:S(2)}) copy-start(bf16[32,2048]{1,0:T(8,128)(2,1)} %get-tuple-element.49.here) | copy-start | bytes 393220
  20.7 6.5 %collective-permute-start.5 = (bf16[32,2048]{1,0:T(8,128)(2,1)S(1)}, bf16[32,2048]{1,0:T(8,128)(2,1)S(1)}, u32[]{:S(2)}, u32[]{:S(2)}) collective-permute-start(bf16[32,2048]{1,0:T(8,128)(2,1)S(1)} %get-tuple-element.58), channel_id=1, source_target_pairs={{0,2},{1,3},{2,0},{3,1},{4,6},{5,7},{6,4},{7,5},{8,10},{9,11},{10,... | collective-permute-start | bytes 393224 | tf_op jit(solution)/shard_map/ppermute | solution.py:18
  22.3 6.9 %collective-permute-start.6 = (bf16[32,2048]{1,0:T(8,128)(2,1)S(1)}, bf16[32,2048]{1,0:T(8,128)(2,1)S(1)}, u32[]{:S(2)}, u32[]{:S(2)}) collective-permute-start(bf16[32,2048]{1,0:T(8,128)(2,1)S(1)} %get-tuple-element.59), channel_id=1, source_target_pairs={{0,4},{1,5},{2,6},{3,7},{4,0},{5,1},{6,2},{7,3},{8,12},{9,13},{10,... | collective-permute-start | bytes 393224 | tf_op jit(solution)/shard_map/ppermute | solution.py:18
  23.8 8.3 %collective-permute-start.7 = (bf16[32,2048]{1,0:T(8,128)(2,1)S(1)}, bf16[32,2048]{1,0:T(8,128)(2,1)S(1)}, u32[]{:S(2)}, u32[]{:S(2)}) collective-permute-start(bf16[32,2048]{1,0:T(8,128)(2,1)S(1)} %get-tuple-element.60), channel_id=1, source_target_pairs={{0,6},{1,7},{2,4},{3,5},{4,2},{5,3},{6,0},{7,1},{8,14},{9,15},{10,... | collective-permute-start | bytes 393224 | tf_op jit(solution)/shard_map/ppermute | solution.py:18
  24.3 7.8 %collective-permute-start.8 = (bf16[32,2048]{1,0:T(8,128)(2,1)S(1)}, bf16[32,2048]{1,0:T(8,128)(2,1)S(1)}, u32[]{:S(2)}, u32[]{:S(2)}) collective-permute-start(bf16[32,2048]{1,0:T(8,128)(2,1)S(1)} %get-tuple-element.61), channel_id=1, source_target_pairs={{0,8},{1,9},{2,10},{3,11},{4,12},{5,13},{6,14},{7,15},{8,0},{9,1},... | collective-permute-start | bytes 393224 | tf_op jit(solution)/shard_map/ppermute | solution.py:18
  24.3 10.2 %collective-permute-start.9 = (bf16[32,2048]{1,0:T(8,128)(2,1)S(1)}, bf16[32,2048]{1,0:T(8,128)(2,1)S(1)}, u32[]{:S(2)}, u32[]{:S(2)}) collective-permute-start(bf16[32,2048]{1,0:T(8,128)(2,1)S(1)} %get-tuple-element.62), channel_id=1, source_target_pairs={{0,10},{1,11},{2,8},{3,9},{4,14},{5,15},{6,12},{7,13},{8,2},{9,3},... | collective-permute-start | bytes 393224 | tf_op jit(solution)/shard_map/ppermute | solution.py:18
  27.2 9.4 %collective-permute-start.10 = (bf16[32,2048]{1,0:T(8,128)(2,1)S(1)}, bf16[32,2048]{1,0:T(8,128)(2,1)S(1)}, u32[]{:S(2)}, u32[]{:S(2)}) collective-permute-start(bf16[32,2048]{1,0:T(8,128)(2,1)S(1)} %get-tuple-element.63), channel_id=1, source_target_pairs={{0,12},{1,13},{2,14},{3,15},{4,8},{5,9},{6,10},{7,11},{8,4},{9,5},... | collective-permute-start | bytes 393224 | tf_op jit(solution)/shard_map/ppermute | solution.py:18
  29.2 9.4 %collective-permute-start.11 = (bf16[32,2048]{1,0:T(8,128)(2,1)S(1)}, bf16[32,2048]{1,0:T(8,128)(2,1)S(1)}, u32[]{:S(2)}, u32[]{:S(2)}) collective-permute-start(bf16[32,2048]{1,0:T(8,128)(2,1)S(1)} %get-tuple-element.64), channel_id=1, source_target_pairs={{0,14},{1,15},{2,12},{3,13},{4,10},{5,11},{6,8},{7,9},{8,6},{9,7},... | collective-permute-start | bytes 393224 | tf_op jit(solution)/shard_map/ppermute | solution.py:18
  38.5 29.3 %copy-start.1 = (f32[32,2048]{1,0:T(8,128)S(1)}, f32[32,2048]{1,0:T(8,128)}, u32[]{:S(2)}) copy-start(f32[32,2048]{1,0:T(8,128)} %get-tuple-element.43) | copy-start | bytes 786436
  45.3 6.4 %collective-permute-start.12 = (bf16[32,2048]{1,0:T(8,128)(2,1)S(1)}, bf16[32,2048]{1,0:T(8,128)(2,1)S(1)}, u32[]{:S(2)}, u32[]{:S(2)}) collective-permute-start(bf16[32,2048]{1,0:T(8,128)(2,1)S(1)} %get-tuple-element.72), channel_id=1, source_target_pairs={{0,2},{1,3},{2,0},{3,1},{4,6},{5,7},{6,4},{7,5},{8,10},{9,11},{10,... | collective-permute-start | bytes 393224 | tf_op jit(solution)/shard_map/ppermute | solution.py:18
  45.9 7.0 %collective-permute-start.13 = (bf16[32,2048]{1,0:T(8,128)(2,1)S(1)}, bf16[32,2048]{1,0:T(8,128)(2,1)S(1)}, u32[]{:S(2)}, u32[]{:S(2)}) collective-permute-start(bf16[32,2048]{1,0:T(8,128)(2,1)S(1)} %get-tuple-element.73), channel_id=1, source_target_pairs={{0,4},{1,5},{2,6},{3,7},{4,0},{5,1},{6,2},{7,3},{8,12},{9,13},{10,... | collective-permute-start | bytes 393224 | tf_op jit(solution)/shard_map/ppermute | solution.py:18
  46.5 8.8 %collective-permute-start.14 = (bf16[32,2048]{1,0:T(8,128)(2,1)S(1)}, bf16[32,2048]{1,0:T(8,128)(2,1)S(1)}, u32[]{:S(2)}, u32[]{:S(2)}) collective-permute-start(bf16[32,2048]{1,0:T(8,128)(2,1)S(1)} %get-tuple-element.74), channel_id=1, source_target_pairs={{0,6},{1,7},{2,4},{3,5},{4,2},{5,3},{6,0},{7,1},{8,14},{9,15},{10,... | collective-permute-start | bytes 393224 | tf_op jit(solution)/shard_map/ppermute | solution.py:18
  48.8 6.4 %collective-permute-start.15 = (bf16[32,2048]{1,0:T(8,128)(2,1)S(1)}, bf16[32,2048]{1,0:T(8,128)(2,1)S(1)}, u32[]{:S(2)}, u32[]{:S(2)}) collective-permute-start(bf16[32,2048]{1,0:T(8,128)(2,1)S(1)} %get-tuple-element.75), channel_id=1, source_target_pairs={{0,8},{1,9},{2,10},{3,11},{4,12},{5,13},{6,14},{7,15},{8,0},{9,1},... | collective-permute-start | bytes 393224 | tf_op jit(solution)/shard_map/ppermute | solution.py:18
  49.1 7.6 %collective-permute-start.16 = (bf16[32,2048]{1,0:T(8,128)(2,1)S(1)}, bf16[32,2048]{1,0:T(8,128)(2,1)S(1)}, u32[]{:S(2)}, u32[]{:S(2)}) collective-permute-start(bf16[32,2048]{1,0:T(8,128)(2,1)S(1)} %get-tuple-element.76), channel_id=1, source_target_pairs={{0,10},{1,11},{2,8},{3,9},{4,14},{5,15},{6,12},{7,13},{8,2},{9,3},... | collective-permute-start | bytes 393224 | tf_op jit(solution)/shard_map/ppermute | solution.py:18
  51.7 6.4 %collective-permute-start.17 = (bf16[32,2048]{1,0:T(8,128)(2,1)S(1)}, bf16[32,2048]{1,0:T(8,128)(2,1)S(1)}, u32[]{:S(2)}, u32[]{:S(2)}) collective-permute-start(bf16[32,2048]{1,0:T(8,128)(2,1)S(1)} %get-tuple-element.77), channel_id=1, source_target_pairs={{0,12},{1,13},{2,14},{3,15},{4,8},{5,9},{6,10},{7,11},{8,4},{9,5},... | collective-permute-start | bytes 393224 | tf_op jit(solution)/shard_map/ppermute | solution.py:18
  52.9 7.2 %collective-permute-start.18 = (bf16[32,2048]{1,0:T(8,128)(2,1)S(1)}, bf16[32,2048]{1,0:T(8,128)(2,1)S(1)}, u32[]{:S(2)}, u32[]{:S(2)}) collective-permute-start(bf16[32,2048]{1,0:T(8,128)(2,1)S(1)} %get-tuple-element.78), channel_id=1, source_target_pairs={{0,14},{1,15},{2,12},{3,13},{4,10},{5,11},{6,8},{7,9},{8,6},{9,7},... | collective-permute-start | bytes 393224 | tf_op jit(solution)/shard_map/ppermute | solution.py:18
  60.5 7.3 %collective-permute-start.19 = (bf16[32,2048]{1,0:T(8,128)(2,1)S(1)}, bf16[32,2048]{1,0:T(8,128)(2,1)S(1)}, u32[]{:S(2)}, u32[]{:S(2)}) collective-permute-start(bf16[32,2048]{1,0:T(8,128)(2,1)S(1)} %get-tuple-element.80), channel_id=1, source_target_pairs={{0,16},{1,17},{2,18},{3,19},{4,20},{5,21},{6,22},{7,23},{8,24},{9,... | collective-permute-start | bytes 393224 | tf_op jit(solution)/shard_map/ppermute | solution.py:18

commit v3 on v2

--- a/solution.py
+++ b/solution.py
@@ -18,13 +18,18 @@
     return lax.ppermute(value, "ep", pairs)
 
 
+def exchanged(blocks):
+    last = len(blocks) - 1
+    return [swapped(b, 2 * (last - i)) if i < last else b for i, b in enumerate(blocks)]
+
+
 def whole():
     return pl.BlockSpec(memory_space=pltpu.VMEM)
 
 
 def attend_kernel(heads, *refs):
-    given, (stream, normed), held = refs[:7], refs[7:9], refs[9:16]
-    mixed, sems = refs[16:]
+    given, (routes, shares), (stream, normed) = refs[:7], refs[7:9], refs[9:11]
+    held, (mixed, sems) = refs[11:18], refs[18:]
     lengths, queries, cache, drafts, up, residual, gain = held
     reqs, rows, width = queries.shape
     parts = [(0, None), (3, None)]
@@ -83,10 +88,28 @@
         stream[:, columns] = value
         square = square + jnp.sum(value * value, axis=-1, keepdims=True)
     factor = lax.rsqrt(square / stream.shape[1] + 1e-06)
-    normed[...] = (stream[...] * factor * gain[...]).astype(BF16)
-
-
-def attend(queries, cache, drafts, lengths, value_up, residual, norm_gain):
+    features = stream.shape[1]
+    normed[:, :features] = (stream[...] * factor * gain[...]).astype(BF16)
+    normed[:, features:] = packed(routes[...], shares[...], tokens)
+
+
+def packed(routes, shares, tokens):
+    top = routes.shape[0]
+    first = shares.astype(BF16).astype(F32)
+    second = (shares - first).astype(BF16).astype(F32)
+    third = shares - first - second
+    rows = jnp.concatenate([routes.astype(F32), first, second, third], axis=1)
+    rest = jnp.zeros((tokens - top, rows.shape[1]), F32)
+    return jnp.concatenate([rows, rest], axis=0).astype(BF16)
+
+
+def unpacked(block, top, tokens):
+    rows = block[...].astype(F32)[:top]
+    parts = [rows[:, i * tokens : (i + 1) * tokens] for i in range(4)]
+    return parts[0], parts[1] + parts[2] + parts[3]
+
+
+def attend(queries, cache, drafts, lengths, value_up, residual, norm_gain, routes, shares):
     reqs, draft, heads, width = queries.shape
     slots = cache.shape[1]
     latent, vdim = value_up.shape[1:]
@@ -104,11 +127,11 @@
     )
     return pl.pallas_call(
         functools.partial(attend_kernel, heads),
-        in_specs=[pl.BlockSpec(memory_space=pltpu.HBM)] * 7,
+        in_specs=[pl.BlockSpec(memory_space=pltpu.HBM)] * 7 + [whole()] * 2,
         out_specs=[whole()] * 2,
         out_shape=[
             jax.ShapeDtypeStruct((tokens, features), F32),
-            jax.ShapeDtypeStruct((tokens, features), BF16),
+            jax.ShapeDtypeStruct((tokens, features + 4 * tokens), BF16),
         ],
         scratch_shapes=[pltpu.SMEM(lengths.shape, jnp.int32)]
         + [pltpu.VMEM(o.shape, o.dtype) for o in operands[1:]]
@@ -120,19 +143,25 @@
             flops=flops, bytes_accessed=6 * MIB, transcendentals=reqs * rows * slots
         ),
         compiler_params=pltpu.CompilerParams(vmem_limit_bytes=60 * MIB),
-    )(*operands)
-
-
-def table_kernel(top, tokens, stride, mine, routed, pick, high, low, table):
+    )(*operands, routes, shares)
+
+
+def dispatch_kernel(top, stride, mine, here, there, high, low, *refs):
+    blocks, table = refs[:-1], refs[-1]
+    tokens, features = here.shape[0], blocks[0].shape[1]
+    here_routes, here_shares = unpacked(here.at[:, features:], top, tokens)
+    there_routes, there_shares = unpacked(there.at[:, features:], top, tokens)
+    routes = jnp.concatenate([here_routes, there_routes], axis=1)
+    shares = jnp.concatenate([here_shares, there_shares], axis=1)
     experts = mine[...]
-    both = routed.shape[1]
+    both = 2 * tokens
     count = experts.shape[0]
     named = jnp.zeros((count, both), F32)
     weight = jnp.zeros((count, both), F32)
     for k in range(top):
-        hit = jnp.where(routed[k : k + 1, :] == experts, 1.0, 0.0)
+        hit = jnp.where(routes[k : k + 1, :] == experts, 1.0, 0.0)
         named = named + hit
-        weight = weight + hit * routed[top + k : top + k + 1, :]
+        weight = weight + hit * shares[k : k + 1, :]
     earlier = lax.broadcasted_iota(jnp.int32, (both, both), 0)
     later = lax.broadcasted_iota(jnp.int32, (both, both), 1)
     before = (earlier < later) & ((earlier < tokens) == (later < tokens))
@@ -145,56 +174,33 @@
     place = rank.astype(jnp.int32) + jnp.where(behind, stride, 0)
     place = jnp.where(named > 0.0, place, -1)
     slots = lax.broadcasted_iota(jnp.int32, (2 * stride, both), 0)
-    for m in range(count):
+    rows = jnp.concatenate([here[:, :features], there[:, :features]], axis=0)
+    for m, block in enumerate(blocks):
         hit = jnp.where(slots == place[m : m + 1, :], 1.0, 0.0)
-        rows = slice(2 * stride * m, 2 * stride * (m + 1))
-        pick[rows, :] = hit.astype(BF16)
-        table[rows, :] = hit * weight[m : m + 1, :]
+        table[2 * stride * m : 2 * stride * (m + 1), :] = hit * weight[m : m + 1, :]
+        block[...] = jnp.dot(hit.astype(BF16), rows, preferred_element_type=F32).astype(BF16)
     turned = table[...].T
     top_bits = turned.astype(BF16)
     high[...] = top_bits
     low[...] = (turned - top_bits.astype(F32)).astype(BF16)
 
 
-def tables(mine, routed, top, tokens, stride):
-    rows = mine.shape[0] * 2 * stride
-    both = 2 * tokens
-    return pl.pallas_call(
-        functools.partial(table_kernel, top, tokens, stride),
-        in_specs=[whole()] * 2,
-        out_specs=[whole()] * 3,
-        out_shape=[
-            jax.ShapeDtypeStruct((rows, both), BF16),
-            jax.ShapeDtypeStruct((both, rows), BF16),
-            jax.ShapeDtypeStruct((both, rows), BF16),
-        ],
+def dispatch(mine, here, there, top, stride):
+    count, both = mine.shape[0], 2 * here.shape[0]
+    width = here.shape[1] - 2 * both
+    rows = count * 2 * stride
+    return pl.pallas_call(
+        functools.partial(dispatch_kernel, top, stride),
+        in_specs=[whole()] * 3,
+        out_specs=[whole()] * (2 + count),
+        out_shape=[jax.ShapeDtypeStruct((both, rows), BF16)] * 2
+        + [jax.ShapeDtypeStruct((2 * stride, width), BF16)] * count,
         scratch_shapes=[pltpu.VMEM((rows, both), F32)],
-        cost_estimate=pl.CostEstimate(flops=MIB, bytes_accessed=MIB // 4, transcendentals=0),
+        cost_estimate=pl.CostEstimate(
+            flops=2 * rows * both * width, bytes_accessed=3 * MIB // 2, transcendentals=0
+        ),
         compiler_params=pltpu.CompilerParams(vmem_limit_bytes=16 * MIB),
-    )(mine, routed)
-
-
-def dispatch_kernel(pick, here, there, *blocks):
-    both = jnp.concatenate([here[...], there[...]], axis=0)
-    rows = blocks[0].shape[0]
-    for m, block in enumerate(blocks):
-        block[...] = jnp.dot(
-            pick[m * rows : (m + 1) * rows, :], both, preferred_element_type=F32
-        ).astype(BF16)
-
-
-def dispatch(pick, here, there, count):
-    rows, width = pick.shape[0] // count, here.shape[1]
-    return pl.pallas_call(
-        dispatch_kernel,
-        in_specs=[whole()] * 3,
-        out_specs=[whole()] * count,
-        out_shape=[jax.ShapeDtypeStruct((rows, width), BF16)] * count,
-        cost_estimate=pl.CostEstimate(
-            flops=2 * pick.size * width, bytes_accessed=3 * MIB // 2, transcendentals=0
-        ),
-        compiler_params=pltpu.CompilerParams(vmem_limit_bytes=16 * MIB),
-    )(pick, here, there)
+    )(mine, here, there)
 
 
 def load_kernel(*refs):
@@ -325,23 +331,21 @@
     capacity = min(tokens, 2 * (((tokens * top + experts - 1) // experts + 3) // 2))
     stride = -(-capacity // 8) * 8
 
-    routed = jnp.concatenate([routes.T.astype(F32), combine_weights.T], axis=0)
     own = [jnp.swapaxes(w_gate, 1, 2)[0], jnp.swapaxes(w_up, 1, 2)[0], w_down[0]]
     other = [swapped(w, 1) for w in own]
     chip = lax.axis_index("ep") // 2
-    mine = (chip ^ jnp.arange(near, dtype=jnp.int32)).astype(F32)[:, None]
-
-    stream, normed = attend(queries, cache, drafts, lengths, value_up, residual, norm_gain)
-    routed, normed, own = lax.optimization_barrier((routed, normed, own))
+    mine = (chip ^ jnp.arange(near - 1, -1, -1, dtype=jnp.int32)).astype(F32)[:, None]
+
+    stream, normed = attend(
+        queries, cache, drafts, lengths, value_up, residual, norm_gain, routes.T, combine_weights.T
+    )
+    normed, own = lax.optimization_barrier((normed, own))
     across = swapped(normed, devices // 2)
-    routed = jnp.concatenate([routed, swapped(routed, devices // 2)], axis=1)
-    pick, high, low = tables(mine, routed, top, tokens, stride)
     own = load(own, 44)
     across, own, other = lax.optimization_barrier((across, own, other))
-    blocks = dispatch(pick, normed, across, near)
-    blocks = [swapped(b, 2 * m) if m else b for m, b in enumerate(blocks)]
-    blocks = run_expert(blocks, own, other)
-    blocks = [swapped(b, 2 * m) if m else b for m, b in enumerate(blocks)]
+    high, low, *blocks = dispatch(mine, normed, across, top, stride)
+    blocks = exchanged(blocks)
+    blocks = exchanged(run_expert(blocks, own, other))
     here, there = combine(high, low, blocks)
     return (stream + (here + swapped(there, devices // 2).astype(F32))).astype(BF16)
 

time: 68.7 us -> 68 us (0.990)
  waiting for transfers between devices: 24.3 us -> 21.4 us
  starting transfers between devices: 25.8 us -> 27.5 us
    ppermute x20 -> x19, waiting for transfers between devices: 24.3 us -> 21.4 us  [swapped(): return lax.ppermute(value, 'ep', pairs)]
    ppermute x20 -> x19, starting transfers between devices: 25.8 us -> 27.5 us  [swapped(): return lax.ppermute(value, 'ep', pairs)]
    pallas_call x1, Pallas kernels: 6.04 us -> 6.75 us  [attend(): pl.pallas_call(functools.partial(attend_kernel, heads), in_specs=[pl.Bloc...]
  transfers between devices with their start and end apart: 20 -> 19, of which waited for: 10 -> 13; matrix products, arithmetic and copies ran while one was open for 0% -> 0% of each run, Pallas kernels for 14% -> 15%
where the time goes in v3:
time: 68 us; the launch traced here: 67.8 us
  starting transfers between devices  27.5 us (40%)
  waiting for transfers between devices  21.4 us (31%)
  Pallas kernels  18.1 us (27%)
  other arithmetic  0.71 us (1%)
    ppermute x19, starting transfers between devices, swapped(): return lax.ppermute(value, 'ep', pairs)  27.5 us
    ppermute x19, waiting for transfers between devices, swapped(): return lax.ppermute(value, 'ep', pairs)  21.4 us
    pallas_call x1, Pallas kernels, attend(): pl.pallas_call(functools.partial(attend_kernel, heads), in_specs=[pl.Bloc...  6.75 us
    pallas_call x1, Pallas kernels, run_expert(): pl.pallas_call(functools.partial(expert_kernel, count), in_specs=[whole()...  6.71 us
    pallas_call x1, Pallas kernels, load(): pl.pallas_call(load_kernel, in_specs=[pl.BlockSpec(memory_space=pl.ANY)]...  3.59 us
  transfers between devices with their start and end apart: 19, of which 13 were waited for; matrix products, arithmetic and copies ran while one was open for 0% of the time, Pallas kernels for 15%

profile of v3, /device:TPU:0, one launch (start us, length us, event | category | flops | bytes accessed | tf_op | source)
XLA Modules:
  0.0 67.8 jit_solution(3084741586047384776)
XLA Ops:
  1.0 6.7 %shard_map.118 = (f32[32,2048]{1,0:T(8,128)}, bf16[32,2176]{1,0:T(8,128)(2,1)}) custom-call(s32[4]{0:T(128)} %refs_0_.1, bf16[4,128,576]{2,1,0:T(8,128)(2,1)} %bitcast.19, bf16[4,576,384]{2,1,0:T(8,128)(2,1)} %bitcast.18, bf16[4,8,576]{2,1,0:T(8,128)(2,1)} %refs_3_.1, bf16[16,512,128]{2,1,0:T(8,128)(2,1)} %refs_4_.1, bf16[32,2048]{1,0:T(8,128)(2,1)} %refs_5_.1, ...), custom_call_target="tpu_custom_call" | custom-call | flops 494927872 | bytes 6291456 | tf_op jit(solution)/shard_map/pallas_call | solution.py:128
  7.7 3.7 %collective-permute-start = (bf16[32,2176]{1,0:T(8,128)(2,1)}, bf16[32,2176]{1,0:T(8,128)(2,1)S(1)}, u32[]{:S(2)}, u32[]{:S(2)}) collective-permute-start(bf16[32,2176]{1,0:T(8,128)(2,1)} %get-tuple-element.43.here), channel_id=1, source_target_pairs={{0,16},{1,17},{2,18},{3,19},{4,20},{5,21},{6,22},{7,23},{8,24},{9,... | collective-permute-start | bytes 417800 | tf_op jit(solution)/shard_map/ppermute | solution.py:18
  11.4 3.6 %shard_map.119 = (bf16[704,2048]{1,0:T(8,128)(2,1)S(1)}, bf16[704,2048]{1,0:T(8,128)(2,1)S(1)}, bf16[704,2048]{1,0:T(8,128)(2,1)S(1)}) custom-call(bf16[704,2048]{1,0:T(8,128)(2,1)} %bitcast.13, bf16[704,2048]{1,0:T(8,128)(2,1)} %bitcast.15, bf16[704,2048]{1,0:T(8,128)(2,1)} %bitcast.17), custom_call_target="tpu_custom_call" | custom-call | bytes 17301504 | tf_op jit(solution)/shard_map/pallas_call | solution.py:219
  15.0 3.9 %collective-permute-done.there = bf16[32,2176]{1,0:T(8,128)(2,1)S(1)} collective-permute-done((bf16[32,2176]{1,0:T(8,128)(2,1)}, bf16[32,2176]{1,0:T(8,128)(2,1)S(1)}, u32[]{:S(2)}, u32[]{:S(2)}) %collective-permute-start) | collective-permute-done | bytes 139296 | tf_op jit(solution)/shard_map/ppermute | solution.py:18
  18.9 0.6 shard_map.120
  19.6 2.8 %collective-permute-start.4 = (bf16[32,2048]{1,0:T(8,128)(2,1)S(1)}, bf16[32,2048]{1,0:T(8,128)(2,1)S(1)}, u32[]{:S(2)}, u32[]{:S(2)}) collective-permute-start(bf16[32,2048]{1,0:T(8,128)(2,1)S(1)} %get-tuple-element.53), channel_id=1, source_target_pairs={{0,14},{1,15},{2,12},{3,13},{4,10},{5,11},{6,8},{7,9},{8,6},{9,7},... | collective-permute-start | bytes 393224 | tf_op jit(solution)/shard_map/ppermute | solution.py:18
  22.3 1.2 %collective-permute-start.5 = (bf16[32,2048]{1,0:T(8,128)(2,1)S(1)}, bf16[32,2048]{1,0:T(8,128)(2,1)S(1)}, u32[]{:S(2)}, u32[]{:S(2)}) collective-permute-start(bf16[32,2048]{1,0:T(8,128)(2,1)S(1)} %get-tuple-element.54), channel_id=1, source_target_pairs={{0,12},{1,13},{2,14},{3,15},{4,8},{5,9},{6,10},{7,11},{8,4},{9,5},... | collective-permute-start | bytes 393224 | tf_op jit(solution)/shard_map/ppermute | solution.py:18
  23.5 0.8 %collective-permute-start.6 = (bf16[32,2048]{1,0:T(8,128)(2,1)S(1)}, bf16[32,2048]{1,0:T(8,128)(2,1)S(1)}, u32[]{:S(2)}, u32[]{:S(2)}) collective-permute-start(bf16[32,2048]{1,0:T(8,128)(2,1)S(1)} %get-tuple-element.55), channel_id=1, source_target_pairs={{0,10},{1,11},{2,8},{3,9},{4,14},{5,15},{6,12},{7,13},{8,2},{9,3},... | collective-permute-start | bytes 393224 | tf_op jit(solution)/shard_map/ppermute | solution.py:18
  24.3 1.2 %collective-permute-start.7 = (bf16[32,2048]{1,0:T(8,128)(2,1)S(1)}, bf16[32,2048]{1,0:T(8,128)(2,1)S(1)}, u32[]{:S(2)}, u32[]{:S(2)}) collective-permute-start(bf16[32,2048]{1,0:T(8,128)(2,1)S(1)} %get-tuple-element.56), channel_id=1, source_target_pairs={{0,8},{1,9},{2,10},{3,11},{4,12},{5,13},{6,14},{7,15},{8,0},{9,1},... | collective-permute-start | bytes 393224 | tf_op jit(solution)/shard_map/ppermute | solution.py:18
  25.5 2.5 %collective-permute-start.8 = (bf16[32,2048]{1,0:T(8,128)(2,1)S(1)}, bf16[32,2048]{1,0:T(8,128)(2,1)S(1)}, u32[]{:S(2)}, u32[]{:S(2)}) collective-permute-start(bf16[32,2048]{1,0:T(8,128)(2,1)S(1)} %get-tuple-element.57), channel_id=1, source_target_pairs={{0,6},{1,7},{2,4},{3,5},{4,2},{5,3},{6,0},{7,1},{8,14},{9,15},{10,... | collective-permute-start | bytes 393224 | tf_op jit(solution)/shard_map/ppermute | solution.py:18
  28.0 1.5 %collective-permute-start.9 = (bf16[32,2048]{1,0:T(8,128)(2,1)S(1)}, bf16[32,2048]{1,0:T(8,128)(2,1)S(1)}, u32[]{:S(2)}, u32[]{:S(2)}) collective-permute-start(bf16[32,2048]{1,0:T(8,128)(2,1)S(1)} %get-tuple-element.58), channel_id=1, source_target_pairs={{0,4},{1,5},{2,6},{3,7},{4,0},{5,1},{6,2},{7,3},{8,12},{9,13},{10,... | collective-permute-start | bytes 393224 | tf_op jit(solution)/shard_map/ppermute | solution.py:18
  29.5 1.8 %collective-permute-done.5.refs_1_ = bf16[32,2048]{1,0:T(8,128)(2,1)S(1)} collective-permute-done((bf16[32,2048]{1,0:T(8,128)(2,1)S(1)}, bf16[32,2048]{1,0:T(8,128)(2,1)S(1)}, u32[]{:S(2)}, u32[]{:S(2)}) %collective-permute-start.5) | collective-permute-done | bytes 131104 | tf_op jit(solution)/shard_map/ppermute | solution.py:18
  31.4 0.8 %collective-permute-start.10 = (bf16[32,2048]{1,0:T(8,128)(2,1)S(1)}, bf16[32,2048]{1,0:T(8,128)(2,1)S(1)}, u32[]{:S(2)}, u32[]{:S(2)}) collective-permute-start(bf16[32,2048]{1,0:T(8,128)(2,1)S(1)} %get-tuple-element.59), channel_id=1, source_target_pairs={{0,2},{1,3},{2,0},{3,1},{4,6},{5,7},{6,4},{7,5},{8,10},{9,11},{10,... | collective-permute-start | bytes 393224 | tf_op jit(solution)/shard_map/ppermute | solution.py:18
  32.2 1.3 %collective-permute-done.6.refs_2_ = bf16[32,2048]{1,0:T(8,128)(2,1)S(1)} collective-permute-done((bf16[32,2048]{1,0:T(8,128)(2,1)S(1)}, bf16[32,2048]{1,0:T(8,128)(2,1)S(1)}, u32[]{:S(2)}, u32[]{:S(2)}) %collective-permute-start.6) | collective-permute-done | bytes 131104 | tf_op jit(solution)/shard_map/ppermute | solution.py:18
  33.6 1.6 %collective-permute-done.7.refs_3_ = bf16[32,2048]{1,0:T(8,128)(2,1)S(1)} collective-permute-done((bf16[32,2048]{1,0:T(8,128)(2,1)S(1)}, bf16[32,2048]{1,0:T(8,128)(2,1)S(1)}, u32[]{:S(2)}, u32[]{:S(2)}) %collective-permute-start.7) | collective-permute-done | bytes 131104 | tf_op jit(solution)/shard_map/ppermute | solution.py:18
  35.2 1.1 %collective-permute-done.10.refs_6_ = bf16[32,2048]{1,0:T(8,128)(2,1)S(1)} collective-permute-done((bf16[32,2048]{1,0:T(8,128)(2,1)S(1)}, bf16[32,2048]{1,0:T(8,128)(2,1)S(1)}, u32[]{:S(2)}, u32[]{:S(2)}) %collective-permute-start.10) | collective-permute-done | bytes 131104 | tf_op jit(solution)/shard_map/ppermute | solution.py:18
  36.3 6.7 %shard_map.121 = (bf16[32,2048]{1,0:T(8,128)(2,1)S(1)}, bf16[32,2048]{1,0:T(8,128)(2,1)S(1)}, bf16[32,2048]{1,0:T(8,128)(2,1)S(1)}, bf16[32,2048]{1,0:T(8,128)(2...) custom-call(bf16[32,2048]{1,0:T(8,128)(2,1)S(1)} %collective-permute, ...), custom_call_target="tpu_custom_call" | custom-call | flops 4429185024 | bytes 17301504 | tf_op jit(solution)/shard_map/pallas_call | solution.py:265
  43.1 2.5 %collective-permute-start.11 = (bf16[32,2048]{1,0:T(8,128)(2,1)S(1)}, bf16[32,2048]{1,0:T(8,128)(2,1)S(1)}, u32[]{:S(2)}, u32[]{:S(2)}) collective-permute-start(bf16[32,2048]{1,0:T(8,128)(2,1)S(1)} %get-tuple-element.67), channel_id=1, source_target_pairs={{0,14},{1,15},{2,12},{3,13},{4,10},{5,11},{6,8},{7,9},{8,6},{9,7},... | collective-permute-start | bytes 393224 | tf_op jit(solution)/shard_map/ppermute | solution.py:18
  45.5 1.4 %collective-permute-start.12 = (bf16[32,2048]{1,0:T(8,128)(2,1)S(1)}, bf16[32,2048]{1,0:T(8,128)(2,1)S(1)}, u32[]{:S(2)}, u32[]{:S(2)}) collective-permute-start(bf16[32,2048]{1,0:T(8,128)(2,1)S(1)} %get-tuple-element.68), channel_id=1, source_target_pairs={{0,12},{1,13},{2,14},{3,15},{4,8},{5,9},{6,10},{7,11},{8,4},{9,5},... | collective-permute-start | bytes 393224 | tf_op jit(solution)/shard_map/ppermute | solution.py:18
  46.9 1.2 %collective-permute-start.13 = (bf16[32,2048]{1,0:T(8,128)(2,1)S(1)}, bf16[32,2048]{1,0:T(8,128)(2,1)S(1)}, u32[]{:S(2)}, u32[]{:S(2)}) collective-permute-start(bf16[32,2048]{1,0:T(8,128)(2,1)S(1)} %get-tuple-element.69), channel_id=1, source_target_pairs={{0,10},{1,11},{2,8},{3,9},{4,14},{5,15},{6,12},{7,13},{8,2},{9,3},... | collective-permute-start | bytes 393224 | tf_op jit(solution)/shard_map/ppermute | solution.py:18
  48.1 0.8 %collective-permute-start.14 = (bf16[32,2048]{1,0:T(8,128)(2,1)S(1)}, bf16[32,2048]{1,0:T(8,128)(2,1)S(1)}, u32[]{:S(2)}, u32[]{:S(2)}) collective-permute-start(bf16[32,2048]{1,0:T(8,128)(2,1)S(1)} %get-tuple-element.70), channel_id=1, source_target_pairs={{0,8},{1,9},{2,10},{3,11},{4,12},{5,13},{6,14},{7,15},{8,0},{9,1},... | collective-permute-start | bytes 393224 | tf_op jit(solution)/shard_map/ppermute | solution.py:18
  49.0 1.7 %collective-permute-start.15 = (bf16[32,2048]{1,0:T(8,128)(2,1)S(1)}, bf16[32,2048]{1,0:T(8,128)(2,1)S(1)}, u32[]{:S(2)}, u32[]{:S(2)}) collective-permute-start(bf16[32,2048]{1,0:T(8,128)(2,1)S(1)} %get-tuple-element.71), channel_id=1, source_target_pairs={{0,6},{1,7},{2,4},{3,5},{4,2},{5,3},{6,0},{7,1},{8,14},{9,15},{10,... | collective-permute-start | bytes 393224 | tf_op jit(solution)/shard_map/ppermute | solution.py:18
  50.7 0.6 collective-permute-done.11.refs_0_
  51.3 1.5 %collective-permute-start.16 = (bf16[32,2048]{1,0:T(8,128)(2,1)S(1)}, bf16[32,2048]{1,0:T(8,128)(2,1)S(1)}, u32[]{:S(2)}, u32[]{:S(2)}) collective-permute-start(bf16[32,2048]{1,0:T(8,128)(2,1)S(1)} %get-tuple-element.72), channel_id=1, source_target_pairs={{0,4},{1,5},{2,6},{3,7},{4,0},{5,1},{6,2},{7,3},{8,12},{9,13},{10,... | collective-permute-start | bytes 393224 | tf_op jit(solution)/shard_map/ppermute | solution.py:18
  52.9 1.4 %collective-permute-done.12.refs_1_ = bf16[32,2048]{1,0:T(8,128)(2,1)S(1)} collective-permute-done((bf16[32,2048]{1,0:T(8,128)(2,1)S(1)}, bf16[32,2048]{1,0:T(8,128)(2,1)S(1)}, u32[]{:S(2)}, u32[]{:S(2)}) %collective-permute-start.12) | collective-permute-done | bytes 131104 | tf_op jit(solution)/shard_map/ppermute | solution.py:18
  54.2 0.6 collective-permute-start.17
  54.9 1.3 %collective-permute-done.13.refs_2_ = bf16[32,2048]{1,0:T(8,128)(2,1)S(1)} collective-permute-done((bf16[32,2048]{1,0:T(8,128)(2,1)S(1)}, bf16[32,2048]{1,0:T(8,128)(2,1)S(1)}, u32[]{:S(2)}, u32[]{:S(2)}) %collective-permute-start.13) | collective-permute-done | bytes 131104 | tf_op jit(solution)/shard_map/ppermute | solution.py:18
  56.1 1.0 %collective-permute-done.14.refs_3_ = bf16[32,2048]{1,0:T(8,128)(2,1)S(1)} collective-permute-done((bf16[32,2048]{1,0:T(8,128)(2,1)S(1)}, bf16[32,2048]{1,0:T(8,128)(2,1)S(1)}, u32[]{:S(2)}, u32[]{:S(2)}) %collective-permute-start.14) | collective-permute-done | bytes 131104 | tf_op jit(solution)/shard_map/ppermute | solution.py:18
  57.7 1.5 %collective-permute-done.17.refs_6_ = bf16[32,2048]{1,0:T(8,128)(2,1)S(1)} collective-permute-done((bf16[32,2048]{1,0:T(8,128)(2,1)S(1)}, bf16[32,2048]{1,0:T(8,128)(2,1)S(1)}, u32[]{:S(2)}, u32[]{:S(2)}) %collective-permute-start.17) | collective-permute-done | bytes 131104 | tf_op jit(solution)/shard_map/ppermute | solution.py:18
  59.7 2.2 %collective-permute-start.18 = (bf16[32,2048]{1,0:T(8,128)(2,1)S(1)}, bf16[32,2048]{1,0:T(8,128)(2,1)S(1)}, u32[]{:S(2)}, u32[]{:S(2)}) collective-permute-start(bf16[32,2048]{1,0:T(8,128)(2,1)S(1)} %get-tuple-element.76), channel_id=1, source_target_pairs={{0,16},{1,17},{2,18},{3,19},{4,20},{5,21},{6,22},{7,23},{8,24},{9,... | collective-permute-start | bytes 393224 | tf_op jit(solution)/shard_map/ppermute | solution.py:18
  61.9 5.2 %collective-permute-done.18 = bf16[32,2048]{1,0:T(8,128)(2,1)S(1)} collective-permute-done((bf16[32,2048]{1,0:T(8,128)(2,1)S(1)}, bf16[32,2048]{1,0:T(8,128)(2,1)S(1)}, u32[]{:S(2)}, u32[]{:S(2)}) %collective-permute-start.18) | collective-permute-done | bytes 131104 | tf_op jit(solution)/shard_map/ppermute | solution.py:18
  67.1 0.7 %add_convert_fusion = bf16[32,2048]{1,0:T(8,128)(2,1)} fusion(f32[32,2048]{1,0:T(8,128)S(1)} %copy-done.1, f32[32,2048]{1,0:T(8,128)S(1)} %get-tuple-element.75, bf16[32,2048]{1,0:T(8,128)(2,1)S(1)} %collective-permute-done.18), kind=kLoop, calls=%fused_computation | loop fusion | flops 262144 | bytes 786432 | tf_op jit(solution)/shard_map/convert_element_type | solution.py:350
  (17 shorter events, 2.1 us)
Async XLA Ops:
  0.0 18.9 %collective-permute-start.1 = (bf16[704,2048]{1,0:T(8,128)(2,1)}, bf16[704,2048]{1,0:T(8,128)(2,1)S(1)}, u32[]{:S(2)}, u32[]{:S(2)}) collective-permute-start(bf16[704,2048]{1,0:T(8,128)(2,1)} %bitcast.12), channel_id=1, source_target_pairs={{0,1},{1,0},{2,3},{3,2},{4,5},{5,4},{6,7},{7,6},{8,9},{9,8},{10,11... | collective-permute-start | bytes 8650760 | tf_op jit(solution)/shard_map/ppermute | solution.py:18
  0.5 18.5 %collective-permute-start.2 = (bf16[704,2048]{1,0:T(8,128)(2,1)}, bf16[704,2048]{1,0:T(8,128)(2,1)}, u32[]{:S(2)}, u32[]{:S(2)}) collective-permute-start(bf16[704,2048]{1,0:T(8,128)(2,1)} %bitcast.14), channel_id=1, source_target_pairs={{0,1},{1,0},{2,3},{3,2},{4,5},{5,4},{6,7},{7,6},{8,9},{9,8},{10,11... | collective-permute-start | bytes 8650760 | tf_op jit(solution)/shard_map/ppermute | solution.py:18
  0.5 18.4 %collective-permute-start.3 = (bf16[704,2048]{1,0:T(8,128)(2,1)}, bf16[704,2048]{1,0:T(8,128)(2,1)}, u32[]{:S(2)}, u32[]{:S(2)}) collective-permute-start(bf16[704,2048]{1,0:T(8,128)(2,1)} %bitcast.16), channel_id=1, source_target_pairs={{0,1},{1,0},{2,3},{3,2},{4,5},{5,4},{6,7},{7,6},{8,9},{9,8},{10,11... | collective-permute-start | bytes 8650760 | tf_op jit(solution)/shard_map/ppermute | solution.py:18
  7.7 11.2 %collective-permute-start = (bf16[32,2176]{1,0:T(8,128)(2,1)}, bf16[32,2176]{1,0:T(8,128)(2,1)S(1)}, u32[]{:S(2)}, u32[]{:S(2)}) collective-permute-start(bf16[32,2176]{1,0:T(8,128)(2,1)} %get-tuple-element.43.here), channel_id=1, source_target_pairs={{0,16},{1,17},{2,18},{3,19},{4,20},{5,21},{6,22},{7,23},{8,24},{9,... | collective-permute-start | bytes 417800 | tf_op jit(solution)/shard_map/ppermute | solution.py:18
  11.4 7.6 %copy-start = (bf16[32,2176]{1,0:T(8,128)(2,1)S(1)}, bf16[32,2176]{1,0:T(8,128)(2,1)}, u32[]{:S(2)}) copy-start(bf16[32,2176]{1,0:T(8,128)(2,1)} %get-tuple-element.43.here) | copy-start | bytes 417796
  19.6 8.4 %collective-permute-start.4 = (bf16[32,2048]{1,0:T(8,128)(2,1)S(1)}, bf16[32,2048]{1,0:T(8,128)(2,1)S(1)}, u32[]{:S(2)}, u32[]{:S(2)}) collective-permute-start(bf16[32,2048]{1,0:T(8,128)(2,1)S(1)} %get-tuple-element.53), channel_id=1, source_target_pairs={{0,14},{1,15},{2,12},{3,13},{4,10},{5,11},{6,8},{7,9},{8,6},{9,7},... | collective-permute-start | bytes 393224 | tf_op jit(solution)/shard_map/ppermute | solution.py:18
  22.3 9.0 %collective-permute-start.5 = (bf16[32,2048]{1,0:T(8,128)(2,1)S(1)}, bf16[32,2048]{1,0:T(8,128)(2,1)S(1)}, u32[]{:S(2)}, u32[]{:S(2)}) collective-permute-start(bf16[32,2048]{1,0:T(8,128)(2,1)S(1)} %get-tuple-element.54), channel_id=1, source_target_pairs={{0,12},{1,13},{2,14},{3,15},{4,8},{5,9},{6,10},{7,11},{8,4},{9,5},... | collective-permute-start | bytes 393224 | tf_op jit(solution)/shard_map/ppermute | solution.py:18
  23.5 10.0 %collective-permute-start.6 = (bf16[32,2048]{1,0:T(8,128)(2,1)S(1)}, bf16[32,2048]{1,0:T(8,128)(2,1)S(1)}, u32[]{:S(2)}, u32[]{:S(2)}) collective-permute-start(bf16[32,2048]{1,0:T(8,128)(2,1)S(1)} %get-tuple-element.55), channel_id=1, source_target_pairs={{0,10},{1,11},{2,8},{3,9},{4,14},{5,15},{6,12},{7,13},{8,2},{9,3},... | collective-permute-start | bytes 393224 | tf_op jit(solution)/shard_map/ppermute | solution.py:18
  24.3 10.8 %collective-permute-start.7 = (bf16[32,2048]{1,0:T(8,128)(2,1)S(1)}, bf16[32,2048]{1,0:T(8,128)(2,1)S(1)}, u32[]{:S(2)}, u32[]{:S(2)}) collective-permute-start(bf16[32,2048]{1,0:T(8,128)(2,1)S(1)} %get-tuple-element.56), channel_id=1, source_target_pairs={{0,8},{1,9},{2,10},{3,11},{4,12},{5,13},{6,14},{7,15},{8,0},{9,1},... | collective-permute-start | bytes 393224 | tf_op jit(solution)/shard_map/ppermute | solution.py:18
  25.5 9.6 %collective-permute-start.8 = (bf16[32,2048]{1,0:T(8,128)(2,1)S(1)}, bf16[32,2048]{1,0:T(8,128)(2,1)S(1)}, u32[]{:S(2)}, u32[]{:S(2)}) collective-permute-start(bf16[32,2048]{1,0:T(8,128)(2,1)S(1)} %get-tuple-element.57), channel_id=1, source_target_pairs={{0,6},{1,7},{2,4},{3,5},{4,2},{5,3},{6,0},{7,1},{8,14},{9,15},{10,... | collective-permute-start | bytes 393224 | tf_op jit(solution)/shard_map/ppermute | solution.py:18
  28.0 7.2 %collective-permute-start.9 = (bf16[32,2048]{1,0:T(8,128)(2,1)S(1)}, bf16[32,2048]{1,0:T(8,128)(2,1)S(1)}, u32[]{:S(2)}, u32[]{:S(2)}) collective-permute-start(bf16[32,2048]{1,0:T(8,128)(2,1)S(1)} %get-tuple-element.58), channel_id=1, source_target_pairs={{0,4},{1,5},{2,6},{3,7},{4,0},{5,1},{6,2},{7,3},{8,12},{9,13},{10,... | collective-permute-start | bytes 393224 | tf_op jit(solution)/shard_map/ppermute | solution.py:18
  31.4 5.0 %collective-permute-start.10 = (bf16[32,2048]{1,0:T(8,128)(2,1)S(1)}, bf16[32,2048]{1,0:T(8,128)(2,1)S(1)}, u32[]{:S(2)}, u32[]{:S(2)}) collective-permute-start(bf16[32,2048]{1,0:T(8,128)(2,1)S(1)} %get-tuple-element.59), channel_id=1, source_target_pairs={{0,2},{1,3},{2,0},{3,1},{4,6},{5,7},{6,4},{7,5},{8,10},{9,11},{10,... | collective-permute-start | bytes 393224 | tf_op jit(solution)/shard_map/ppermute | solution.py:18
  36.3 30.7 %copy-start.1 = (f32[32,2048]{1,0:T(8,128)S(1)}, f32[32,2048]{1,0:T(8,128)}, u32[]{:S(2)}) copy-start(f32[32,2048]{1,0:T(8,128)} %get-tuple-element.41) | copy-start | bytes 786436
  43.1 8.3 %collective-permute-start.11 = (bf16[32,2048]{1,0:T(8,128)(2,1)S(1)}, bf16[32,2048]{1,0:T(8,128)(2,1)S(1)}, u32[]{:S(2)}, u32[]{:S(2)}) collective-permute-start(bf16[32,2048]{1,0:T(8,128)(2,1)S(1)} %get-tuple-element.67), channel_id=1, source_target_pairs={{0,14},{1,15},{2,12},{3,13},{4,10},{5,11},{6,8},{7,9},{8,6},{9,7},... | collective-permute-start | bytes 393224 | tf_op jit(solution)/shard_map/ppermute | solution.py:18
  45.5 8.7 %collective-permute-start.12 = (bf16[32,2048]{1,0:T(8,128)(2,1)S(1)}, bf16[32,2048]{1,0:T(8,128)(2,1)S(1)}, u32[]{:S(2)}, u32[]{:S(2)}) collective-permute-start(bf16[32,2048]{1,0:T(8,128)(2,1)S(1)} %get-tuple-element.68), channel_id=1, source_target_pairs={{0,12},{1,13},{2,14},{3,15},{4,8},{5,9},{6,10},{7,11},{8,4},{9,5},... | collective-permute-start | bytes 393224 | tf_op jit(solution)/shard_map/ppermute | solution.py:18
  46.9 9.2 %collective-permute-start.13 = (bf16[32,2048]{1,0:T(8,128)(2,1)S(1)}, bf16[32,2048]{1,0:T(8,128)(2,1)S(1)}, u32[]{:S(2)}, u32[]{:S(2)}) collective-permute-start(bf16[32,2048]{1,0:T(8,128)(2,1)S(1)} %get-tuple-element.69), channel_id=1, source_target_pairs={{0,10},{1,11},{2,8},{3,9},{4,14},{5,15},{6,12},{7,13},{8,2},{9,3},... | collective-permute-start | bytes 393224 | tf_op jit(solution)/shard_map/ppermute | solution.py:18
  48.1 9.1 %collective-permute-start.14 = (bf16[32,2048]{1,0:T(8,128)(2,1)S(1)}, bf16[32,2048]{1,0:T(8,128)(2,1)S(1)}, u32[]{:S(2)}, u32[]{:S(2)}) collective-permute-start(bf16[32,2048]{1,0:T(8,128)(2,1)S(1)} %get-tuple-element.70), channel_id=1, source_target_pairs={{0,8},{1,9},{2,10},{3,11},{4,12},{5,13},{6,14},{7,15},{8,0},{9,1},... | collective-permute-start | bytes 393224 | tf_op jit(solution)/shard_map/ppermute | solution.py:18
  49.0 8.7 %collective-permute-start.15 = (bf16[32,2048]{1,0:T(8,128)(2,1)S(1)}, bf16[32,2048]{1,0:T(8,128)(2,1)S(1)}, u32[]{:S(2)}, u32[]{:S(2)}) collective-permute-start(bf16[32,2048]{1,0:T(8,128)(2,1)S(1)} %get-tuple-element.71), channel_id=1, source_target_pairs={{0,6},{1,7},{2,4},{3,5},{4,2},{5,3},{6,0},{7,1},{8,14},{9,15},{10,... | collective-permute-start | bytes 393224 | tf_op jit(solution)/shard_map/ppermute | solution.py:18
  51.3 6.4 %collective-permute-start.16 = (bf16[32,2048]{1,0:T(8,128)(2,1)S(1)}, bf16[32,2048]{1,0:T(8,128)(2,1)S(1)}, u32[]{:S(2)}, u32[]{:S(2)}) collective-permute-start(bf16[32,2048]{1,0:T(8,128)(2,1)S(1)} %get-tuple-element.72), channel_id=1, source_target_pairs={{0,4},{1,5},{2,6},{3,7},{4,0},{5,1},{6,2},{7,3},{8,12},{9,13},{10,... | collective-permute-start | bytes 393224 | tf_op jit(solution)/shard_map/ppermute | solution.py:18
  54.2 5.0 %collective-permute-start.17 = (bf16[32,2048]{1,0:T(8,128)(2,1)S(1)}, bf16[32,2048]{1,0:T(8,128)(2,1)S(1)}, u32[]{:S(2)}, u32[]{:S(2)}) collective-permute-start(bf16[32,2048]{1,0:T(8,128)(2,1)S(1)} %get-tuple-element.73), channel_id=1, source_target_pairs={{0,2},{1,3},{2,0},{3,1},{4,6},{5,7},{6,4},{7,5},{8,10},{9,11},{10,... | collective-permute-start | bytes 393224 | tf_op jit(solution)/shard_map/ppermute | solution.py:18
  59.7 7.4 %collective-permute-start.18 = (bf16[32,2048]{1,0:T(8,128)(2,1)S(1)}, bf16[32,2048]{1,0:T(8,128)(2,1)S(1)}, u32[]{:S(2)}, u32[]{:S(2)}) collective-permute-start(bf16[32,2048]{1,0:T(8,128)(2,1)S(1)} %get-tuple-element.76), channel_id=1, source_target_pairs={{0,16},{1,17},{2,18},{3,19},{4,20},{5,21},{6,22},{7,23},{8,24},{9,... | collective-permute-start | bytes 393224 | tf_op jit(solution)/shard_map/ppermute | solution.py:18

commit v4 on v3

--- a/solution.py
+++ b/solution.py
@@ -28,67 +28,60 @@
 
 
 def attend_kernel(heads, *refs):
-    given, (routes, shares), (stream, normed) = refs[:7], refs[7:9], refs[9:11]
-    held, (mixed, sems) = refs[11:18], refs[18:]
-    lengths, queries, cache, drafts, up, residual, gain = held
+    given, (stream, normed), held = refs[:9], refs[9:11], refs[11:20]
+    mixed, sems = refs[20:]
+    lengths, drafts, queries, cache, up, residual, gain, routes, shares = held
     reqs, rows, width = queries.shape
-    parts = [(0, None), (3, None)]
-    parts += [(i, r) for r in range(reqs) for i in (1, 2)]
-    parts += [(4, None), (5, None), (6, None)]
-    copies = {}
-    for n, (i, r) in enumerate(parts):
-        source, target = (given[i], held[i]) if r is None else (given[i].at[r], held[i].at[r])
-        copies[i, r] = pltpu.make_async_copy(source, target, sems.at[n])
-        copies[i, r].start()
-    slots = cache.shape[2]
+    slots = given[3].shape[2]
     draft = drafts.shape[1]
     latent, vdim = up.shape[1:]
     lanes = mixed.shape[2]
+    columns = cache.shape[2]
+    copies = {}
+    order = [(0, None), (1, None)] + [(i, r) for r in range(reqs) for i in (2, 3)]
+    for n, (i, r) in enumerate(order + [(i, None) for i in range(4, 9)]):
+        source, target = (given[i], held[i]) if r is None else (given[i].at[r], held[i].at[r])
+        if i == 3:
+            target = target.at[:, :slots]
+        copies[i, r] = pltpu.make_async_copy(source, target, sems.at[n])
+        copies[i, r].start()
     scale = (vdim + width - latent) ** (-0.5)
-    position = lax.broadcasted_iota(jnp.int32, (rows, slots), 1)
-    token = lax.broadcasted_iota(jnp.int32, (rows, draft), 0) // heads
-    causal = lax.broadcasted_iota(jnp.int32, (rows, draft), 1) <= token
+    place = lax.broadcasted_iota(jnp.int32, (rows, columns), 1)
+    token = lax.broadcasted_iota(jnp.int32, (rows, columns), 0) // heads
+    causal = (place >= slots) & (place - slots <= token)
     copies[0, None].wait()
-    copies[3, None].wait()
+    copies[1, None].wait()
     for r in range(reqs):
-        copies[1, r].wait()
+        d = jnp.concatenate(
+            [drafts[r].astype(F32), jnp.zeros((columns - slots - draft, width), F32)], axis=0
+        )
+        cache[r, :, slots:] = d.T.astype(BF16)
+    for r in range(reqs):
         copies[2, r].wait()
-        q, c, d = queries[r], cache[r], drafts[r]
-        cached = jnp.dot(q, c, preferred_element_type=F32) * scale
-        own = lax.dot_general(q, d, NT, preferred_element_type=F32) * scale
-        visible = position < lengths[r]
-        cached = jnp.where(visible, cached, -1e30)
-        own = jnp.where(causal, own, -1e30)
-        highest = jnp.maximum(
-            jnp.max(cached, axis=-1, keepdims=True), jnp.max(own, axis=-1, keepdims=True)
-        )
-        e_cached = jnp.where(visible, jnp.exp(cached - highest), 0.0)
-        e_own = jnp.where(causal, jnp.exp(own - highest), 0.0)
-        total = jnp.sum(e_cached, axis=-1, keepdims=True) + jnp.sum(e_own, axis=-1, keepdims=True)
-        inverse = 1.0 / total
-        p_cached = (e_cached * inverse).astype(BF16)
-        p_own = (e_own * inverse).astype(BF16)
-        out = lax.dot_general(p_cached, c[:latent, :], NT, preferred_element_type=F32)
-        out = out + jnp.dot(p_own, d[:, :latent], preferred_element_type=F32)
+        copies[3, r].wait()
+        score = jnp.dot(queries[r], cache[r], preferred_element_type=F32) * scale
+        score = jnp.where((place < lengths[r]) | causal, score, -1e30)
+        e = jnp.exp(score - jnp.max(score, axis=-1, keepdims=True))
+        p = (e * (1.0 / jnp.sum(e, axis=-1, keepdims=True))).astype(BF16)
+        out = lax.dot_general(p, cache[r, :latent, :], NT, preferred_element_type=F32)
         for g in range(latent // lanes):
             mixed[g, r * rows : (r + 1) * rows, :] = out[:, g * lanes : (g + 1) * lanes]
-    for i in (4, 5, 6):
+    for i in range(4, 9):
         copies[i, None].wait()
-    tokens = stream.shape[0]
+    tokens, features = stream.shape
     square = jnp.zeros((tokens, 1), F32)
     for head in range(heads):
         part = jnp.concatenate(
             [mixed[g, pl.ds(head, tokens, stride=heads), :] for g in range(latent // lanes)],
             axis=1,
         ).astype(BF16)
-        columns = slice(head * vdim, (head + 1) * vdim)
-        value = residual[:, columns].astype(F32) + jnp.dot(
+        at = slice(head * vdim, (head + 1) * vdim)
+        value = residual[:, at].astype(F32) + jnp.dot(
             part, up[head], preferred_element_type=F32
         )
-        stream[:, columns] = value
+        stream[:, at] = value
         square = square + jnp.sum(value * value, axis=-1, keepdims=True)
-    factor = lax.rsqrt(square / stream.shape[1] + 1e-06)
-    features = stream.shape[1]
+    factor = lax.rsqrt(square / features + 1e-06)
     normed[:, :features] = (stream[...] * factor * gain[...]).astype(BF16)
     normed[:, features:] = packed(routes[...], shares[...], tokens)
 
@@ -118,32 +111,36 @@
     flops = 2 * reqs * rows * slots * (width + latent) + 2 * tokens * heads * latent * vdim
     operands = (
         lengths,
+        drafts,
         queries.reshape(reqs, rows, width),
         jnp.swapaxes(cache, 1, 2),
-        drafts,
         value_up,
         residual,
         norm_gain.reshape(1, features),
-    )
+        routes,
+        shares,
+    )
+    held = [pltpu.VMEM(o.shape, o.dtype) for o in operands]
+    held[0] = pltpu.SMEM(lengths.shape, jnp.int32)
+    held[3] = pltpu.VMEM((reqs, width, (slots + draft + 127) // 128 * 128), BF16)
     return pl.pallas_call(
         functools.partial(attend_kernel, heads),
-        in_specs=[pl.BlockSpec(memory_space=pltpu.HBM)] * 7 + [whole()] * 2,
+        in_specs=[pl.BlockSpec(memory_space=pltpu.HBM)] * 9,
         out_specs=[whole()] * 2,
         out_shape=[
             jax.ShapeDtypeStruct((tokens, features), F32),
             jax.ShapeDtypeStruct((tokens, features + 4 * tokens), BF16),
         ],
-        scratch_shapes=[pltpu.SMEM(lengths.shape, jnp.int32)]
-        + [pltpu.VMEM(o.shape, o.dtype) for o in operands[1:]]
+        scratch_shapes=held
         + [
             pltpu.VMEM((latent // 128, reqs * rows, 128), F32),
-            pltpu.SemaphoreType.DMA((2 * reqs + 5,)),
+            pltpu.SemaphoreType.DMA((2 * reqs + 7,)),
         ],
         cost_estimate=pl.CostEstimate(
             flops=flops, bytes_accessed=6 * MIB, transcendentals=reqs * rows * slots
         ),
         compiler_params=pltpu.CompilerParams(vmem_limit_bytes=60 * MIB),
-    )(*operands, routes, shares)
+    )(*operands)
 
 
 def dispatch_kernel(top, stride, mine, here, there, high, low, *refs):
@@ -233,11 +230,11 @@
     blocks = refs[:count]
     near, far = refs[count : count + 3], refs[count + 3 : count + 6]
     outs = refs[count + 6 : 2 * count + 6]
-    held = refs[2 * count + 6 : 2 * count + 9]
-    rows_ref, total, sems = refs[2 * count + 9 :]
-    copies = [pltpu.make_async_copy(far[i], held[i], sems.at[i]) for i in range(3)]
-    for copy in copies:
-        copy.start()
+    held = refs[2 * count + 6 : 2 * count + 8]
+    rows_ref, total, sems = refs[2 * count + 8 :]
+    copies = {i: pltpu.make_async_copy(far[i], held[i - 1], sems.at[i - 1]) for i in (1, 2)}
+    for i in (1, 2):
+        copies[i].start()
     size = blocks[0].shape[0]
     for m, block in enumerate(blocks):
         rows_ref[m * size : (m + 1) * size, :] = block[...]
@@ -253,7 +250,8 @@
         return jnp.dot(active, w_down[...], preferred_element_type=F32)
 
     total[...] = half(near, lambda i: None)
-    result = (total[...] + half(held, lambda i: copies[i].wait())).astype(BF16)
+    far_half = half((far[0], *held), lambda i: i and copies[i].wait())
+    result = (total[...] + far_half).astype(BF16)
     for m, out in enumerate(outs):
         out[...] = result[m * size : (m + 1) * size, :]
 
@@ -264,14 +262,14 @@
     units = near[0].shape[0]
     return pl.pallas_call(
         functools.partial(expert_kernel, count),
-        in_specs=[whole()] * (count + 3) + [pl.BlockSpec(memory_space=pl.ANY)] * 3,
+        in_specs=[whole()] * (count + 4) + [pl.BlockSpec(memory_space=pl.ANY)] * 2,
         out_specs=[whole()] * count,
         out_shape=[jax.ShapeDtypeStruct((size, width), BF16)] * count,
-        scratch_shapes=[pltpu.VMEM((units, width), BF16)] * 3
+        scratch_shapes=[pltpu.VMEM((units, width), BF16)] * 2
         + [
             pltpu.VMEM((count * size, width), BF16),
             pltpu.VMEM((count * size, width), F32),
-            pltpu.SemaphoreType.DMA((3,)),
+            pltpu.SemaphoreType.DMA((2,)),
         ],
         cost_estimate=pl.CostEstimate(
             flops=12 * count * size * width * units,

time: 68 us -> 67.5 us (level)
    pallas_call x1, Pallas kernels: 6.75 us -> 5.44 us  [attend(): pl.pallas_call(functools.partial(attend_kernel, heads), in_specs=[pl.Bloc...]
    pallas_call x1, Pallas kernels: 6.71 us -> 7.61 us  [run_expert(): pl.pallas_call(functools.partial(expert_kernel, count), in_specs=[whole()...]
  transfers between devices with their start and end apart: 19 -> 19, of which waited for: 13 -> 13; matrix products, arithmetic and copies ran while one was open for 0% -> 0% of each run, Pallas kernels for 15% -> 13%
where the time goes in v4:
time: 67.5 us; the launch traced here: 67.4 us
  starting transfers between devices  27.6 us (41%)
  waiting for transfers between devices  21.3 us (32%)
  Pallas kernels  17.7 us (26%)
  other arithmetic  0.71 us (1%)
    ppermute x19, starting transfers between devices, swapped(): return lax.ppermute(value, 'ep', pairs)  27.6 us
    ppermute x19, waiting for transfers between devices, swapped(): return lax.ppermute(value, 'ep', pairs)  21.3 us
    pallas_call x1, Pallas kernels, run_expert(): pl.pallas_call(functools.partial(expert_kernel, count), in_specs=[whole()...  7.61 us
    pallas_call x1, Pallas kernels, attend(): pl.pallas_call(functools.partial(attend_kernel, heads), in_specs=[pl.Bloc...  5.44 us
    pallas_call x1, Pallas kernels, load(): pl.pallas_call(load_kernel, in_specs=[pl.BlockSpec(memory_space=pl.ANY)]...  3.59 us
  transfers between devices with their start and end apart: 19, of which 13 were waited for; matrix products, arithmetic and copies ran while one was open for 0% of the time, Pallas kernels for 13%

profile of v4, /device:TPU:0, one launch (start us, length us, event | category | flops | bytes accessed | tf_op | source)
XLA Modules:
  0.0 67.4 jit_solution(6884092622639221526)
XLA Ops:
  1.0 5.4 %shard_map.118 = (f32[32,2048]{1,0:T(8,128)}, bf16[32,2176]{1,0:T(8,128)(2,1)}) custom-call(s32[4]{0:T(128)} %refs_0_.1, bf16[4,8,576]{2,1,0:T(8,128)(2,1)} %refs_1_.1, bf16[4,128,576]{2,1,0:T(8,128)(2,1)} %bitcast.19, bf16[4,576,384]{2,1,0:T(8,128)(2,1)} %bitcast.18, bf16[16,512,128]{2,1,0:T(8,128)(2,1)} %refs_4_.1, bf16[32,2048]{1,0:T(8,128)(2,1)} %refs_5_.1, ...), custom_call_target="tpu_custom_call" | custom-call | flops 494927872 | bytes 6291456 | tf_op jit(solution)/shard_map/pallas_call | solution.py:126
  6.4 3.7 %collective-permute-start = (bf16[32,2176]{1,0:T(8,128)(2,1)}, bf16[32,2176]{1,0:T(8,128)(2,1)S(1)}, u32[]{:S(2)}, u32[]{:S(2)}) collective-permute-start(bf16[32,2176]{1,0:T(8,128)(2,1)} %get-tuple-element.43.here), channel_id=1, source_target_pairs={{0,16},{1,17},{2,18},{3,19},{4,20},{5,21},{6,22},{7,23},{8,24},{9,... | collective-permute-start | bytes 417800 | tf_op jit(solution)/shard_map/ppermute | solution.py:18
  10.1 3.6 %shard_map.119 = (bf16[704,2048]{1,0:T(8,128)(2,1)S(1)}, bf16[704,2048]{1,0:T(8,128)(2,1)S(1)}, bf16[704,2048]{1,0:T(8,128)(2,1)S(1)}) custom-call(bf16[704,2048]{1,0:T(8,128)(2,1)} %bitcast.13, bf16[704,2048]{1,0:T(8,128)(2,1)} %bitcast.15, bf16[704,2048]{1,0:T(8,128)(2,1)} %bitcast.17), custom_call_target="tpu_custom_call" | custom-call | bytes 17301504 | tf_op jit(solution)/shard_map/pallas_call | solution.py:216
  13.7 3.9 %collective-permute-done.there = bf16[32,2176]{1,0:T(8,128)(2,1)S(1)} collective-permute-done((bf16[32,2176]{1,0:T(8,128)(2,1)}, bf16[32,2176]{1,0:T(8,128)(2,1)S(1)}, u32[]{:S(2)}, u32[]{:S(2)}) %collective-permute-start) | collective-permute-done | bytes 139296 | tf_op jit(solution)/shard_map/ppermute | solution.py:18
  17.6 0.6 shard_map.120
  18.3 2.8 %collective-permute-start.4 = (bf16[32,2048]{1,0:T(8,128)(2,1)S(1)}, bf16[32,2048]{1,0:T(8,128)(2,1)S(1)}, u32[]{:S(2)}, u32[]{:S(2)}) collective-permute-start(bf16[32,2048]{1,0:T(8,128)(2,1)S(1)} %get-tuple-element.53), channel_id=1, source_target_pairs={{0,14},{1,15},{2,12},{3,13},{4,10},{5,11},{6,8},{7,9},{8,6},{9,7},... | collective-permute-start | bytes 393224 | tf_op jit(solution)/shard_map/ppermute | solution.py:18
  21.0 1.2 %collective-permute-start.5 = (bf16[32,2048]{1,0:T(8,128)(2,1)S(1)}, bf16[32,2048]{1,0:T(8,128)(2,1)S(1)}, u32[]{:S(2)}, u32[]{:S(2)}) collective-permute-start(bf16[32,2048]{1,0:T(8,128)(2,1)S(1)} %get-tuple-element.54), channel_id=1, source_target_pairs={{0,12},{1,13},{2,14},{3,15},{4,8},{5,9},{6,10},{7,11},{8,4},{9,5},... | collective-permute-start | bytes 393224 | tf_op jit(solution)/shard_map/ppermute | solution.py:18
  22.2 0.8 %collective-permute-start.6 = (bf16[32,2048]{1,0:T(8,128)(2,1)S(1)}, bf16[32,2048]{1,0:T(8,128)(2,1)S(1)}, u32[]{:S(2)}, u32[]{:S(2)}) collective-permute-start(bf16[32,2048]{1,0:T(8,128)(2,1)S(1)} %get-tuple-element.55), channel_id=1, source_target_pairs={{0,10},{1,11},{2,8},{3,9},{4,14},{5,15},{6,12},{7,13},{8,2},{9,3},... | collective-permute-start | bytes 393224 | tf_op jit(solution)/shard_map/ppermute | solution.py:18
  23.0 1.2 %collective-permute-start.7 = (bf16[32,2048]{1,0:T(8,128)(2,1)S(1)}, bf16[32,2048]{1,0:T(8,128)(2,1)S(1)}, u32[]{:S(2)}, u32[]{:S(2)}) collective-permute-start(bf16[32,2048]{1,0:T(8,128)(2,1)S(1)} %get-tuple-element.56), channel_id=1, source_target_pairs={{0,8},{1,9},{2,10},{3,11},{4,12},{5,13},{6,14},{7,15},{8,0},{9,1},... | collective-permute-start | bytes 393224 | tf_op jit(solution)/shard_map/ppermute | solution.py:18
  24.2 2.5 %collective-permute-start.8 = (bf16[32,2048]{1,0:T(8,128)(2,1)S(1)}, bf16[32,2048]{1,0:T(8,128)(2,1)S(1)}, u32[]{:S(2)}, u32[]{:S(2)}) collective-permute-start(bf16[32,2048]{1,0:T(8,128)(2,1)S(1)} %get-tuple-element.57), channel_id=1, source_target_pairs={{0,6},{1,7},{2,4},{3,5},{4,2},{5,3},{6,0},{7,1},{8,14},{9,15},{10,... | collective-permute-start | bytes 393224 | tf_op jit(solution)/shard_map/ppermute | solution.py:18
  26.7 1.5 %collective-permute-start.9 = (bf16[32,2048]{1,0:T(8,128)(2,1)S(1)}, bf16[32,2048]{1,0:T(8,128)(2,1)S(1)}, u32[]{:S(2)}, u32[]{:S(2)}) collective-permute-start(bf16[32,2048]{1,0:T(8,128)(2,1)S(1)} %get-tuple-element.58), channel_id=1, source_target_pairs={{0,4},{1,5},{2,6},{3,7},{4,0},{5,1},{6,2},{7,3},{8,12},{9,13},{10,... | collective-permute-start | bytes 393224 | tf_op jit(solution)/shard_map/ppermute | solution.py:18
  28.2 1.8 %collective-permute-done.5.refs_1_ = bf16[32,2048]{1,0:T(8,128)(2,1)S(1)} collective-permute-done((bf16[32,2048]{1,0:T(8,128)(2,1)S(1)}, bf16[32,2048]{1,0:T(8,128)(2,1)S(1)}, u32[]{:S(2)}, u32[]{:S(2)}) %collective-permute-start.5) | collective-permute-done | bytes 131104 | tf_op jit(solution)/shard_map/ppermute | solution.py:18
  30.0 0.8 %collective-permute-start.10 = (bf16[32,2048]{1,0:T(8,128)(2,1)S(1)}, bf16[32,2048]{1,0:T(8,128)(2,1)S(1)}, u32[]{:S(2)}, u32[]{:S(2)}) collective-permute-start(bf16[32,2048]{1,0:T(8,128)(2,1)S(1)} %get-tuple-element.59), channel_id=1, source_target_pairs={{0,2},{1,3},{2,0},{3,1},{4,6},{5,7},{6,4},{7,5},{8,10},{9,11},{10,... | collective-permute-start | bytes 393224 | tf_op jit(solution)/shard_map/ppermute | solution.py:18
  30.9 1.4 %collective-permute-done.6.refs_2_ = bf16[32,2048]{1,0:T(8,128)(2,1)S(1)} collective-permute-done((bf16[32,2048]{1,0:T(8,128)(2,1)S(1)}, bf16[32,2048]{1,0:T(8,128)(2,1)S(1)}, u32[]{:S(2)}, u32[]{:S(2)}) %collective-permute-start.6) | collective-permute-done | bytes 131104 | tf_op jit(solution)/shard_map/ppermute | solution.py:18
  32.2 1.5 %collective-permute-done.7.refs_3_ = bf16[32,2048]{1,0:T(8,128)(2,1)S(1)} collective-permute-done((bf16[32,2048]{1,0:T(8,128)(2,1)S(1)}, bf16[32,2048]{1,0:T(8,128)(2,1)S(1)}, u32[]{:S(2)}, u32[]{:S(2)}) %collective-permute-start.7) | collective-permute-done | bytes 131104 | tf_op jit(solution)/shard_map/ppermute | solution.py:18
  33.9 1.1 %collective-permute-done.10.refs_6_ = bf16[32,2048]{1,0:T(8,128)(2,1)S(1)} collective-permute-done((bf16[32,2048]{1,0:T(8,128)(2,1)S(1)}, bf16[32,2048]{1,0:T(8,128)(2,1)S(1)}, u32[]{:S(2)}, u32[]{:S(2)}) %collective-permute-start.10) | collective-permute-done | bytes 131104 | tf_op jit(solution)/shard_map/ppermute | solution.py:18
  35.0 7.6 %shard_map.121 = (bf16[32,2048]{1,0:T(8,128)(2,1)S(1)}, bf16[32,2048]{1,0:T(8,128)(2,1)S(1)}, bf16[32,2048]{1,0:T(8,128)(2,1)S(1)}, bf16[32,2048]{1,0:T(8,128)(2...) custom-call(bf16[32,2048]{1,0:T(8,128)(2,1)S(1)} %collective-permute, ...), custom_call_target="tpu_custom_call" | custom-call | flops 4429185024 | bytes 17301504 | tf_op jit(solution)/shard_map/pallas_call | solution.py:263
  42.6 2.5 %collective-permute-start.11 = (bf16[32,2048]{1,0:T(8,128)(2,1)S(1)}, bf16[32,2048]{1,0:T(8,128)(2,1)S(1)}, u32[]{:S(2)}, u32[]{:S(2)}) collective-permute-start(bf16[32,2048]{1,0:T(8,128)(2,1)S(1)} %get-tuple-element.67), channel_id=1, source_target_pairs={{0,14},{1,15},{2,12},{3,13},{4,10},{5,11},{6,8},{7,9},{8,6},{9,7},... | collective-permute-start | bytes 393224 | tf_op jit(solution)/shard_map/ppermute | solution.py:18
  45.1 1.4 %collective-permute-start.12 = (bf16[32,2048]{1,0:T(8,128)(2,1)S(1)}, bf16[32,2048]{1,0:T(8,128)(2,1)S(1)}, u32[]{:S(2)}, u32[]{:S(2)}) collective-permute-start(bf16[32,2048]{1,0:T(8,128)(2,1)S(1)} %get-tuple-element.68), channel_id=1, source_target_pairs={{0,12},{1,13},{2,14},{3,15},{4,8},{5,9},{6,10},{7,11},{8,4},{9,5},... | collective-permute-start | bytes 393224 | tf_op jit(solution)/shard_map/ppermute | solution.py:18
  46.5 1.2 %collective-permute-start.13 = (bf16[32,2048]{1,0:T(8,128)(2,1)S(1)}, bf16[32,2048]{1,0:T(8,128)(2,1)S(1)}, u32[]{:S(2)}, u32[]{:S(2)}) collective-permute-start(bf16[32,2048]{1,0:T(8,128)(2,1)S(1)} %get-tuple-element.69), channel_id=1, source_target_pairs={{0,10},{1,11},{2,8},{3,9},{4,14},{5,15},{6,12},{7,13},{8,2},{9,3},... | collective-permute-start | bytes 393224 | tf_op jit(solution)/shard_map/ppermute | solution.py:18
  47.7 0.8 %collective-permute-start.14 = (bf16[32,2048]{1,0:T(8,128)(2,1)S(1)}, bf16[32,2048]{1,0:T(8,128)(2,1)S(1)}, u32[]{:S(2)}, u32[]{:S(2)}) collective-permute-start(bf16[32,2048]{1,0:T(8,128)(2,1)S(1)} %get-tuple-element.70), channel_id=1, source_target_pairs={{0,8},{1,9},{2,10},{3,11},{4,12},{5,13},{6,14},{7,15},{8,0},{9,1},... | collective-permute-start | bytes 393224 | tf_op jit(solution)/shard_map/ppermute | solution.py:18
  48.5 1.8 %collective-permute-start.15 = (bf16[32,2048]{1,0:T(8,128)(2,1)S(1)}, bf16[32,2048]{1,0:T(8,128)(2,1)S(1)}, u32[]{:S(2)}, u32[]{:S(2)}) collective-permute-start(bf16[32,2048]{1,0:T(8,128)(2,1)S(1)} %get-tuple-element.71), channel_id=1, source_target_pairs={{0,6},{1,7},{2,4},{3,5},{4,2},{5,3},{6,0},{7,1},{8,14},{9,15},{10,... | collective-permute-start | bytes 393224 | tf_op jit(solution)/shard_map/ppermute | solution.py:18
  50.3 0.6 collective-permute-done.11.refs_0_
  50.9 1.6 %collective-permute-start.16 = (bf16[32,2048]{1,0:T(8,128)(2,1)S(1)}, bf16[32,2048]{1,0:T(8,128)(2,1)S(1)}, u32[]{:S(2)}, u32[]{:S(2)}) collective-permute-start(bf16[32,2048]{1,0:T(8,128)(2,1)S(1)} %get-tuple-element.72), channel_id=1, source_target_pairs={{0,4},{1,5},{2,6},{3,7},{4,0},{5,1},{6,2},{7,3},{8,12},{9,13},{10,... | collective-permute-start | bytes 393224 | tf_op jit(solution)/shard_map/ppermute | solution.py:18
  52.4 1.4 %collective-permute-done.12.refs_1_ = bf16[32,2048]{1,0:T(8,128)(2,1)S(1)} collective-permute-done((bf16[32,2048]{1,0:T(8,128)(2,1)S(1)}, bf16[32,2048]{1,0:T(8,128)(2,1)S(1)}, u32[]{:S(2)}, u32[]{:S(2)}) %collective-permute-start.12) | collective-permute-done | bytes 131104 | tf_op jit(solution)/shard_map/ppermute | solution.py:18
  53.8 0.6 collective-permute-start.17
  54.4 1.3 %collective-permute-done.13.refs_2_ = bf16[32,2048]{1,0:T(8,128)(2,1)S(1)} collective-permute-done((bf16[32,2048]{1,0:T(8,128)(2,1)S(1)}, bf16[32,2048]{1,0:T(8,128)(2,1)S(1)}, u32[]{:S(2)}, u32[]{:S(2)}) %collective-permute-start.13) | collective-permute-done | bytes 131104 | tf_op jit(solution)/shard_map/ppermute | solution.py:18
  55.7 1.0 %collective-permute-done.14.refs_3_ = bf16[32,2048]{1,0:T(8,128)(2,1)S(1)} collective-permute-done((bf16[32,2048]{1,0:T(8,128)(2,1)S(1)}, bf16[32,2048]{1,0:T(8,128)(2,1)S(1)}, u32[]{:S(2)}, u32[]{:S(2)}) %collective-permute-start.14) | collective-permute-done | bytes 131104 | tf_op jit(solution)/shard_map/ppermute | solution.py:18
  57.3 1.5 %collective-permute-done.17.refs_6_ = bf16[32,2048]{1,0:T(8,128)(2,1)S(1)} collective-permute-done((bf16[32,2048]{1,0:T(8,128)(2,1)S(1)}, bf16[32,2048]{1,0:T(8,128)(2,1)S(1)}, u32[]{:S(2)}, u32[]{:S(2)}) %collective-permute-start.17) | collective-permute-done | bytes 131104 | tf_op jit(solution)/shard_map/ppermute | solution.py:18
  59.3 2.3 %collective-permute-start.18 = (bf16[32,2048]{1,0:T(8,128)(2,1)S(1)}, bf16[32,2048]{1,0:T(8,128)(2,1)S(1)}, u32[]{:S(2)}, u32[]{:S(2)}) collective-permute-start(bf16[32,2048]{1,0:T(8,128)(2,1)S(1)} %get-tuple-element.76), channel_id=1, source_target_pairs={{0,16},{1,17},{2,18},{3,19},{4,20},{5,21},{6,22},{7,23},{8,24},{9,... | collective-permute-start | bytes 393224 | tf_op jit(solution)/shard_map/ppermute | solution.py:18
  61.5 5.1 %collective-permute-done.18 = bf16[32,2048]{1,0:T(8,128)(2,1)S(1)} collective-permute-done((bf16[32,2048]{1,0:T(8,128)(2,1)S(1)}, bf16[32,2048]{1,0:T(8,128)(2,1)S(1)}, u32[]{:S(2)}, u32[]{:S(2)}) %collective-permute-start.18) | collective-permute-done | bytes 131104 | tf_op jit(solution)/shard_map/ppermute | solution.py:18
  66.7 0.7 %add_convert_fusion = bf16[32,2048]{1,0:T(8,128)(2,1)} fusion(f32[32,2048]{1,0:T(8,128)S(1)} %copy-done.1, f32[32,2048]{1,0:T(8,128)S(1)} %get-tuple-element.75, bf16[32,2048]{1,0:T(8,128)(2,1)S(1)} %collective-permute-done.18), kind=kLoop, calls=%fused_computation | loop fusion | flops 262144 | bytes 786432 | tf_op jit(solution)/shard_map/convert_element_type | solution.py:348
  (17 shorter events, 2.1 us)
Async XLA Ops:
  0.0 17.6 %collective-permute-start.1 = (bf16[704,2048]{1,0:T(8,128)(2,1)}, bf16[704,2048]{1,0:T(8,128)(2,1)S(1)}, u32[]{:S(2)}, u32[]{:S(2)}) collective-permute-start(bf16[704,2048]{1,0:T(8,128)(2,1)} %bitcast.12), channel_id=1, source_target_pairs={{0,1},{1,0},{2,3},{3,2},{4,5},{5,4},{6,7},{7,6},{8,9},{9,8},{10,11... | collective-permute-start | bytes 8650760 | tf_op jit(solution)/shard_map/ppermute | solution.py:18
  0.5 17.2 %collective-permute-start.2 = (bf16[704,2048]{1,0:T(8,128)(2,1)}, bf16[704,2048]{1,0:T(8,128)(2,1)}, u32[]{:S(2)}, u32[]{:S(2)}) collective-permute-start(bf16[704,2048]{1,0:T(8,128)(2,1)} %bitcast.14), channel_id=1, source_target_pairs={{0,1},{1,0},{2,3},{3,2},{4,5},{5,4},{6,7},{7,6},{8,9},{9,8},{10,11... | collective-permute-start | bytes 8650760 | tf_op jit(solution)/shard_map/ppermute | solution.py:18
  0.5 17.1 %collective-permute-start.3 = (bf16[704,2048]{1,0:T(8,128)(2,1)}, bf16[704,2048]{1,0:T(8,128)(2,1)}, u32[]{:S(2)}, u32[]{:S(2)}) collective-permute-start(bf16[704,2048]{1,0:T(8,128)(2,1)} %bitcast.16), channel_id=1, source_target_pairs={{0,1},{1,0},{2,3},{3,2},{4,5},{5,4},{6,7},{7,6},{8,9},{9,8},{10,11... | collective-permute-start | bytes 8650760 | tf_op jit(solution)/shard_map/ppermute | solution.py:18
  6.4 11.2 %collective-permute-start = (bf16[32,2176]{1,0:T(8,128)(2,1)}, bf16[32,2176]{1,0:T(8,128)(2,1)S(1)}, u32[]{:S(2)}, u32[]{:S(2)}) collective-permute-start(bf16[32,2176]{1,0:T(8,128)(2,1)} %get-tuple-element.43.here), channel_id=1, source_target_pairs={{0,16},{1,17},{2,18},{3,19},{4,20},{5,21},{6,22},{7,23},{8,24},{9,... | collective-permute-start | bytes 417800 | tf_op jit(solution)/shard_map/ppermute | solution.py:18
  10.1 7.5 %copy-start = (bf16[32,2176]{1,0:T(8,128)(2,1)S(1)}, bf16[32,2176]{1,0:T(8,128)(2,1)}, u32[]{:S(2)}) copy-start(bf16[32,2176]{1,0:T(8,128)(2,1)} %get-tuple-element.43.here) | copy-start | bytes 417796
  18.3 8.4 %collective-permute-start.4 = (bf16[32,2048]{1,0:T(8,128)(2,1)S(1)}, bf16[32,2048]{1,0:T(8,128)(2,1)S(1)}, u32[]{:S(2)}, u32[]{:S(2)}) collective-permute-start(bf16[32,2048]{1,0:T(8,128)(2,1)S(1)} %get-tuple-element.53), channel_id=1, source_target_pairs={{0,14},{1,15},{2,12},{3,13},{4,10},{5,11},{6,8},{7,9},{8,6},{9,7},... | collective-permute-start | bytes 393224 | tf_op jit(solution)/shard_map/ppermute | solution.py:18
  21.0 9.0 %collective-permute-start.5 = (bf16[32,2048]{1,0:T(8,128)(2,1)S(1)}, bf16[32,2048]{1,0:T(8,128)(2,1)S(1)}, u32[]{:S(2)}, u32[]{:S(2)}) collective-permute-start(bf16[32,2048]{1,0:T(8,128)(2,1)S(1)} %get-tuple-element.54), channel_id=1, source_target_pairs={{0,12},{1,13},{2,14},{3,15},{4,8},{5,9},{6,10},{7,11},{8,4},{9,5},... | collective-permute-start | bytes 393224 | tf_op jit(solution)/shard_map/ppermute | solution.py:18
  22.2 10.0 %collective-permute-start.6 = (bf16[32,2048]{1,0:T(8,128)(2,1)S(1)}, bf16[32,2048]{1,0:T(8,128)(2,1)S(1)}, u32[]{:S(2)}, u32[]{:S(2)}) collective-permute-start(bf16[32,2048]{1,0:T(8,128)(2,1)S(1)} %get-tuple-element.55), channel_id=1, source_target_pairs={{0,10},{1,11},{2,8},{3,9},{4,14},{5,15},{6,12},{7,13},{8,2},{9,3},... | collective-permute-start | bytes 393224 | tf_op jit(solution)/shard_map/ppermute | solution.py:18
  23.0 10.8 %collective-permute-start.7 = (bf16[32,2048]{1,0:T(8,128)(2,1)S(1)}, bf16[32,2048]{1,0:T(8,128)(2,1)S(1)}, u32[]{:S(2)}, u32[]{:S(2)}) collective-permute-start(bf16[32,2048]{1,0:T(8,128)(2,1)S(1)} %get-tuple-element.56), channel_id=1, source_target_pairs={{0,8},{1,9},{2,10},{3,11},{4,12},{5,13},{6,14},{7,15},{8,0},{9,1},... | collective-permute-start | bytes 393224 | tf_op jit(solution)/shard_map/ppermute | solution.py:18
  24.2 9.6 %collective-permute-start.8 = (bf16[32,2048]{1,0:T(8,128)(2,1)S(1)}, bf16[32,2048]{1,0:T(8,128)(2,1)S(1)}, u32[]{:S(2)}, u32[]{:S(2)}) collective-permute-start(bf16[32,2048]{1,0:T(8,128)(2,1)S(1)} %get-tuple-element.57), channel_id=1, source_target_pairs={{0,6},{1,7},{2,4},{3,5},{4,2},{5,3},{6,0},{7,1},{8,14},{9,15},{10,... | collective-permute-start | bytes 393224 | tf_op jit(solution)/shard_map/ppermute | solution.py:18
  26.7 7.2 %collective-permute-start.9 = (bf16[32,2048]{1,0:T(8,128)(2,1)S(1)}, bf16[32,2048]{1,0:T(8,128)(2,1)S(1)}, u32[]{:S(2)}, u32[]{:S(2)}) collective-permute-start(bf16[32,2048]{1,0:T(8,128)(2,1)S(1)} %get-tuple-element.58), channel_id=1, source_target_pairs={{0,4},{1,5},{2,6},{3,7},{4,0},{5,1},{6,2},{7,3},{8,12},{9,13},{10,... | collective-permute-start | bytes 393224 | tf_op jit(solution)/shard_map/ppermute | solution.py:18
  30.0 5.0 %collective-permute-start.10 = (bf16[32,2048]{1,0:T(8,128)(2,1)S(1)}, bf16[32,2048]{1,0:T(8,128)(2,1)S(1)}, u32[]{:S(2)}, u32[]{:S(2)}) collective-permute-start(bf16[32,2048]{1,0:T(8,128)(2,1)S(1)} %get-tuple-element.59), channel_id=1, source_target_pairs={{0,2},{1,3},{2,0},{3,1},{4,6},{5,7},{6,4},{7,5},{8,10},{9,11},{10,... | collective-permute-start | bytes 393224 | tf_op jit(solution)/shard_map/ppermute | solution.py:18
  35.0 31.7 %copy-start.1 = (f32[32,2048]{1,0:T(8,128)S(1)}, f32[32,2048]{1,0:T(8,128)}, u32[]{:S(2)}) copy-start(f32[32,2048]{1,0:T(8,128)} %get-tuple-element.41) | copy-start | bytes 786436
  42.6 8.2 %collective-permute-start.11 = (bf16[32,2048]{1,0:T(8,128)(2,1)S(1)}, bf16[32,2048]{1,0:T(8,128)(2,1)S(1)}, u32[]{:S(2)}, u32[]{:S(2)}) collective-permute-start(bf16[32,2048]{1,0:T(8,128)(2,1)S(1)} %get-tuple-element.67), channel_id=1, source_target_pairs={{0,14},{1,15},{2,12},{3,13},{4,10},{5,11},{6,8},{7,9},{8,6},{9,7},... | collective-permute-start | bytes 393224 | tf_op jit(solution)/shard_map/ppermute | solution.py:18
  45.1 8.7 %collective-permute-start.12 = (bf16[32,2048]{1,0:T(8,128)(2,1)S(1)}, bf16[32,2048]{1,0:T(8,128)(2,1)S(1)}, u32[]{:S(2)}, u32[]{:S(2)}) collective-permute-start(bf16[32,2048]{1,0:T(8,128)(2,1)S(1)} %get-tuple-element.68), channel_id=1, source_target_pairs={{0,12},{1,13},{2,14},{3,15},{4,8},{5,9},{6,10},{7,11},{8,4},{9,5},... | collective-permute-start | bytes 393224 | tf_op jit(solution)/shard_map/ppermute | solution.py:18
  46.5 9.2 %collective-permute-start.13 = (bf16[32,2048]{1,0:T(8,128)(2,1)S(1)}, bf16[32,2048]{1,0:T(8,128)(2,1)S(1)}, u32[]{:S(2)}, u32[]{:S(2)}) collective-permute-start(bf16[32,2048]{1,0:T(8,128)(2,1)S(1)} %get-tuple-element.69), channel_id=1, source_target_pairs={{0,10},{1,11},{2,8},{3,9},{4,14},{5,15},{6,12},{7,13},{8,2},{9,3},... | collective-permute-start | bytes 393224 | tf_op jit(solution)/shard_map/ppermute | solution.py:18
  47.7 9.1 %collective-permute-start.14 = (bf16[32,2048]{1,0:T(8,128)(2,1)S(1)}, bf16[32,2048]{1,0:T(8,128)(2,1)S(1)}, u32[]{:S(2)}, u32[]{:S(2)}) collective-permute-start(bf16[32,2048]{1,0:T(8,128)(2,1)S(1)} %get-tuple-element.70), channel_id=1, source_target_pairs={{0,8},{1,9},{2,10},{3,11},{4,12},{5,13},{6,14},{7,15},{8,0},{9,1},... | collective-permute-start | bytes 393224 | tf_op jit(solution)/shard_map/ppermute | solution.py:18
  48.5 8.7 %collective-permute-start.15 = (bf16[32,2048]{1,0:T(8,128)(2,1)S(1)}, bf16[32,2048]{1,0:T(8,128)(2,1)S(1)}, u32[]{:S(2)}, u32[]{:S(2)}) collective-permute-start(bf16[32,2048]{1,0:T(8,128)(2,1)S(1)} %get-tuple-element.71), channel_id=1, source_target_pairs={{0,6},{1,7},{2,4},{3,5},{4,2},{5,3},{6,0},{7,1},{8,14},{9,15},{10,... | collective-permute-start | bytes 393224 | tf_op jit(solution)/shard_map/ppermute | solution.py:18
  50.9 6.4 %collective-permute-start.16 = (bf16[32,2048]{1,0:T(8,128)(2,1)S(1)}, bf16[32,2048]{1,0:T(8,128)(2,1)S(1)}, u32[]{:S(2)}, u32[]{:S(2)}) collective-permute-start(bf16[32,2048]{1,0:T(8,128)(2,1)S(1)} %get-tuple-element.72), channel_id=1, source_target_pairs={{0,4},{1,5},{2,6},{3,7},{4,0},{5,1},{6,2},{7,3},{8,12},{9,13},{10,... | collective-permute-start | bytes 393224 | tf_op jit(solution)/shard_map/ppermute | solution.py:18
  53.8 5.0 %collective-permute-start.17 = (bf16[32,2048]{1,0:T(8,128)(2,1)S(1)}, bf16[32,2048]{1,0:T(8,128)(2,1)S(1)}, u32[]{:S(2)}, u32[]{:S(2)}) collective-permute-start(bf16[32,2048]{1,0:T(8,128)(2,1)S(1)} %get-tuple-element.73), channel_id=1, source_target_pairs={{0,2},{1,3},{2,0},{3,1},{4,6},{5,7},{6,4},{7,5},{8,10},{9,11},{10,... | collective-permute-start | bytes 393224 | tf_op jit(solution)/shard_map/ppermute | solution.py:18
  59.3 7.4 %collective-permute-start.18 = (bf16[32,2048]{1,0:T(8,128)(2,1)S(1)}, bf16[32,2048]{1,0:T(8,128)(2,1)S(1)}, u32[]{:S(2)}, u32[]{:S(2)}) collective-permute-start(bf16[32,2048]{1,0:T(8,128)(2,1)S(1)} %get-tuple-element.76), channel_id=1, source_target_pairs={{0,16},{1,17},{2,18},{3,19},{4,20},{5,21},{6,22},{7,23},{8,24},{9,... | collective-permute-start | bytes 393224 | tf_op jit(solution)/shard_map/ppermute | solution.py:18

commit v5 on v4

--- a/solution.py
+++ b/solution.py
@@ -139,7 +139,7 @@
         cost_estimate=pl.CostEstimate(
             flops=flops, bytes_accessed=6 * MIB, transcendentals=reqs * rows * slots
         ),
-        compiler_params=pltpu.CompilerParams(vmem_limit_bytes=60 * MIB),
+        compiler_params=pltpu.CompilerParams(vmem_limit_bytes=56 * MIB),
     )(*operands)
 
 
@@ -227,57 +227,45 @@
 
 
 def expert_kernel(count, *refs):
-    blocks = refs[:count]
-    near, far = refs[count : count + 3], refs[count + 3 : count + 6]
+    blocks, weights = refs[:count], refs[count : count + 6]
     outs = refs[count + 6 : 2 * count + 6]
-    held = refs[2 * count + 6 : 2 * count + 8]
-    rows_ref, total, sems = refs[2 * count + 8 :]
-    copies = {i: pltpu.make_async_copy(far[i], held[i - 1], sems.at[i - 1]) for i in (1, 2)}
-    for i in (1, 2):
-        copies[i].start()
-    size = blocks[0].shape[0]
+    rows, active = refs[2 * count + 6 :]
+    size, width = blocks[0].shape
     for m, block in enumerate(blocks):
-        rows_ref[m * size : (m + 1) * size, :] = block[...]
-
-    def half(weights, ready):
-        w_gate, w_up, w_down = weights
-        ready(0)
-        gate = lax.dot_general(rows_ref[...], w_gate[...], NT, preferred_element_type=F32)
-        ready(1)
-        upper = lax.dot_general(rows_ref[...], w_up[...], NT, preferred_element_type=F32)
-        active = (gate * (1.0 / (1.0 + jnp.exp(-gate))) * upper).astype(BF16)
-        ready(2)
-        return jnp.dot(active, w_down[...], preferred_element_type=F32)
-
-    total[...] = half(near, lambda i: None)
-    far_half = half((far[0], *held), lambda i: i and copies[i].wait())
-    result = (total[...] + far_half).astype(BF16)
-    for m, out in enumerate(outs):
-        out[...] = result[m * size : (m + 1) * size, :]
-
-
-def run_expert(blocks, near, far):
+        rows[m * size : (m + 1) * size, :] = block[...]
+    for half in range(2):
+        w_gate, w_up = weights[3 * half : 3 * half + 2]
+        gate = lax.dot_general(rows[...], w_gate[...], NT, preferred_element_type=F32)
+        upper = lax.dot_general(rows[...], w_up[...], NT, preferred_element_type=F32)
+        active[half] = (gate * (1.0 / (1.0 + jnp.exp(-gate))) * upper).astype(BF16)
+    for at in range(0, width, 512):
+        columns = slice(at, at + 512)
+        result = jnp.dot(active[0], weights[2][:, columns], preferred_element_type=F32)
+        result = result + jnp.dot(active[1], weights[5][:, columns], preferred_element_type=F32)
+        for m, out in enumerate(outs):
+            out[:, columns] = result[m * size : (m + 1) * size, :].astype(BF16)
+
+
+def run_expert(blocks, weights):
     count = len(blocks)
     size, width = blocks[0].shape
-    units = near[0].shape[0]
+    units = weights[0].shape[0]
     return pl.pallas_call(
         functools.partial(expert_kernel, count),
-        in_specs=[whole()] * (count + 4) + [pl.BlockSpec(memory_space=pl.ANY)] * 2,
+        in_specs=[whole()] * (count + 6),
         out_specs=[whole()] * count,
         out_shape=[jax.ShapeDtypeStruct((size, width), BF16)] * count,
-        scratch_shapes=[pltpu.VMEM((units, width), BF16)] * 2
-        + [
+        scratch_shapes=[
             pltpu.VMEM((count * size, width), BF16),
-            pltpu.VMEM((count * size, width), F32),
-            pltpu.SemaphoreType.DMA((2,)),
+            pltpu.VMEM((2, count * size, units), BF16),
         ],
         cost_estimate=pl.CostEstimate(
             flops=12 * count * size * width * units,
             bytes_accessed=12 * units * width,
             transcendentals=2 * count * size * units,
         ),
-        compiler_params=pltpu.CompilerParams(vmem_limit_bytes=36 * MIB),
-    )(*blocks, *near, *far)
+        compiler_params=pltpu.CompilerParams(vmem_limit_bytes=20 * MIB),
+    )(*blocks, *weights)
 
 
 def combine_kernel(high, low, *refs):
@@ -343,7 +331,8 @@
     across, own, other = lax.optimization_barrier((across, own, other))
     high, low, *blocks = dispatch(mine, normed, across, top, stride)
     blocks = exchanged(blocks)
-    blocks = exchanged(run_expert(blocks, own, other))
+    blocks[2], *late = lax.optimization_barrier((blocks[2], *other[1:]))
+    blocks = exchanged(run_expert(blocks, [*own, other[0], *load(late, 38)]))
     here, there = combine(high, low, blocks)
     return (stream + (here + swapped(there, devices // 2).astype(F32))).astype(BF16)
 

time: 67.5 us -> 66.7 us (0.988)
  waiting for transfers between devices: 21.3 us -> 19.4 us
  starting transfers between devices: 27.6 us -> 28.5 us
    pallas_call x1 -> x2, Pallas kernels: 3.59 us -> 6.29 us  [load(): pl.pallas_call(load_kernel, in_specs=[pl.BlockSpec(memory_space=pl.ANY)]...]
    pallas_call x1, Pallas kernels: 7.61 us -> 5.08 us  [run_expert(): pl.pallas_call(functools.partial(expert_kernel, count), in_specs=[whole()...]
    ppermute x19, waiting for transfers between devices: 21.3 us -> 19.4 us  [swapped(): return lax.ppermute(value, 'ep', pairs)]
    ppermute x19, starting transfers between devices: 27.6 us -> 28.5 us  [swapped(): return lax.ppermute(value, 'ep', pairs)]
  transfers between devices with their start and end apart: 19 -> 19, of which waited for: 13 -> 11; matrix products, arithmetic and copies ran while one was open for 0% -> 0% of each run, Pallas kernels for 13% -> 18%
where the time goes in v5:
time: 66.7 us; the launch traced here: 66.5 us
  starting transfers between devices  28.5 us (43%)
  waiting for transfers between devices  19.4 us (29%)
  Pallas kernels  17.9 us (27%)
  other arithmetic  0.71 us (1%)
    ppermute x19, starting transfers between devices, swapped(): return lax.ppermute(value, 'ep', pairs)  28.5 us
    ppermute x19, waiting for transfers between devices, swapped(): return lax.ppermute(value, 'ep', pairs)  19.4 us
    pallas_call x2, Pallas kernels, load(): pl.pallas_call(load_kernel, in_specs=[pl.BlockSpec(memory_space=pl.ANY)]...  6.29 us
    pallas_call x1, Pallas kernels, attend(): pl.pallas_call(functools.partial(attend_kernel, heads), in_specs=[pl.Bloc...  5.44 us
    pallas_call x1, Pallas kernels, run_expert(): pl.pallas_call(functools.partial(expert_kernel, count), in_specs=[whole()...  5.08 us
  transfers between devices with their start and end apart: 19, of which 11 were waited for; matrix products, arithmetic and copies ran while one was open for 0% of the time, Pallas kernels for 18%

profile of v5, /device:TPU:0, one launch (start us, length us, event | category | flops | bytes accessed | tf_op | source)
XLA Modules:
  0.0 66.5 jit_solution(17838768555208874747)
XLA Ops:
  1.0 5.4 %shard_map.118 = (f32[32,2048]{1,0:T(8,128)}, bf16[32,2176]{1,0:T(8,128)(2,1)}) custom-call(s32[4]{0:T(128)} %refs_0_.1, bf16[4,8,576]{2,1,0:T(8,128)(2,1)} %refs_1_.1, bf16[4,128,576]{2,1,0:T(8,128)(2,1)} %bitcast.19, bf16[4,576,384]{2,1,0:T(8,128)(2,1)} %bitcast.18, bf16[16,512,128]{2,1,0:T(8,128)(2,1)} %refs_4_.1, bf16[32,2048]{1,0:T(8,128)(2,1)} %refs_5_.1, ...), custom_call_target="tpu_custom_call" | custom-call | flops 494927872 | bytes 6291456 | tf_op jit(solution)/shard_map/pallas_call | solution.py:126
  6.4 3.7 %collective-permute-start = (bf16[32,2176]{1,0:T(8,128)(2,1)}, bf16[32,2176]{1,0:T(8,128)(2,1)S(1)}, u32[]{:S(2)}, u32[]{:S(2)}) collective-permute-start(bf16[32,2176]{1,0:T(8,128)(2,1)} %get-tuple-element.48.here), channel_id=1, source_target_pairs={{0,16},{1,17},{2,18},{3,19},{4,20},{5,21},{6,22},{7,23},{8,24},{9,... | collective-permute-start | bytes 417800 | tf_op jit(solution)/shard_map/ppermute | solution.py:18
  10.1 3.6 %shard_map.119 = (bf16[704,2048]{1,0:T(8,128)(2,1)S(1)}, bf16[704,2048]{1,0:T(8,128)(2,1)S(1)}, bf16[704,2048]{1,0:T(8,128)(2,1)S(1)}) custom-call(bf16[704,2048]{1,0:T(8,128)(2,1)} %bitcast.13, bf16[704,2048]{1,0:T(8,128)(2,1)} %bitcast.15, bf16[704,2048]{1,0:T(8,128)(2,1)} %bitcast.17), custom_call_target="tpu_custom_call" | custom-call | bytes 17301504 | tf_op jit(solution)/shard_map/pallas_call | solution.py:216
  13.7 3.9 %collective-permute-done.there = bf16[32,2176]{1,0:T(8,128)(2,1)S(1)} collective-permute-done((bf16[32,2176]{1,0:T(8,128)(2,1)}, bf16[32,2176]{1,0:T(8,128)(2,1)S(1)}, u32[]{:S(2)}, u32[]{:S(2)}) %collective-permute-start) | collective-permute-done | bytes 139296 | tf_op jit(solution)/shard_map/ppermute | solution.py:18
  17.6 0.6 shard_map.120
  18.3 2.8 %collective-permute-start.4 = (bf16[32,2048]{1,0:T(8,128)(2,1)S(1)}, bf16[32,2048]{1,0:T(8,128)(2,1)S(1)}, u32[]{:S(2)}, u32[]{:S(2)}) collective-permute-start(bf16[32,2048]{1,0:T(8,128)(2,1)S(1)} %get-tuple-element.58), channel_id=1, source_target_pairs={{0,14},{1,15},{2,12},{3,13},{4,10},{5,11},{6,8},{7,9},{8,6},{9,7},... | collective-permute-start | bytes 393224 | tf_op jit(solution)/shard_map/ppermute | solution.py:18
  21.0 1.2 %collective-permute-start.6 = (bf16[32,2048]{1,0:T(8,128)(2,1)S(1)}, bf16[32,2048]{1,0:T(8,128)(2,1)S(1)}, u32[]{:S(2)}, u32[]{:S(2)}) collective-permute-start(bf16[32,2048]{1,0:T(8,128)(2,1)S(1)} %get-tuple-element.60), channel_id=1, source_target_pairs={{0,10},{1,11},{2,8},{3,9},{4,14},{5,15},{6,12},{7,13},{8,2},{9,3},... | collective-permute-start | bytes 393224 | tf_op jit(solution)/shard_map/ppermute | solution.py:18
  22.3 0.7 %collective-permute-start.5 = (bf16[32,2048]{1,0:T(8,128)(2,1)S(1)}, bf16[32,2048]{1,0:T(8,128)(2,1)S(1)}, u32[]{:S(2)}, u32[]{:S(2)}) collective-permute-start(bf16[32,2048]{1,0:T(8,128)(2,1)S(1)} %get-tuple-element.59), channel_id=1, source_target_pairs={{0,12},{1,13},{2,14},{3,15},{4,8},{5,9},{6,10},{7,11},{8,4},{9,5},... | collective-permute-start | bytes 393224 | tf_op jit(solution)/shard_map/ppermute | solution.py:18
  23.0 1.2 %collective-permute-start.7 = (bf16[32,2048]{1,0:T(8,128)(2,1)S(1)}, bf16[32,2048]{1,0:T(8,128)(2,1)S(1)}, u32[]{:S(2)}, u32[]{:S(2)}) collective-permute-start(bf16[32,2048]{1,0:T(8,128)(2,1)S(1)} %get-tuple-element.64), channel_id=1, source_target_pairs={{0,8},{1,9},{2,10},{3,11},{4,12},{5,13},{6,14},{7,15},{8,0},{9,1},... | collective-permute-start | bytes 393224 | tf_op jit(solution)/shard_map/ppermute | solution.py:18
  24.2 2.5 %collective-permute-start.8 = (bf16[32,2048]{1,0:T(8,128)(2,1)S(1)}, bf16[32,2048]{1,0:T(8,128)(2,1)S(1)}, u32[]{:S(2)}, u32[]{:S(2)}) collective-permute-start(bf16[32,2048]{1,0:T(8,128)(2,1)S(1)} %get-tuple-element.65), channel_id=1, source_target_pairs={{0,6},{1,7},{2,4},{3,5},{4,2},{5,3},{6,0},{7,1},{8,14},{9,15},{10,... | collective-permute-start | bytes 393224 | tf_op jit(solution)/shard_map/ppermute | solution.py:18
  26.7 1.3 %collective-permute-start.9 = (bf16[32,2048]{1,0:T(8,128)(2,1)S(1)}, bf16[32,2048]{1,0:T(8,128)(2,1)S(1)}, u32[]{:S(2)}, u32[]{:S(2)}) collective-permute-start(bf16[32,2048]{1,0:T(8,128)(2,1)S(1)} %get-tuple-element.66), channel_id=1, source_target_pairs={{0,4},{1,5},{2,6},{3,7},{4,0},{5,1},{6,2},{7,3},{8,12},{9,13},{10,... | collective-permute-start | bytes 393224 | tf_op jit(solution)/shard_map/ppermute | solution.py:18
  27.9 1.3 %collective-permute-done.6.refs_2_ = bf16[32,2048]{1,0:T(8,128)(2,1)S(1)} collective-permute-done((bf16[32,2048]{1,0:T(8,128)(2,1)S(1)}, bf16[32,2048]{1,0:T(8,128)(2,1)S(1)}, u32[]{:S(2)}, u32[]{:S(2)}) %collective-permute-start.6) | collective-permute-done | bytes 131104 | tf_op jit(solution)/shard_map/ppermute | solution.py:18
  29.3 1.6 %collective-permute-start.10 = (bf16[32,2048]{1,0:T(8,128)(2,1)S(1)}, bf16[32,2048]{1,0:T(8,128)(2,1)S(1)}, u32[]{:S(2)}, u32[]{:S(2)}) collective-permute-start(bf16[32,2048]{1,0:T(8,128)(2,1)S(1)} %get-tuple-element.67), channel_id=1, source_target_pairs={{0,2},{1,3},{2,0},{3,1},{4,6},{5,7},{6,4},{7,5},{8,10},{9,11},{10,... | collective-permute-start | bytes 393224 | tf_op jit(solution)/shard_map/ppermute | solution.py:18
  30.9 2.7 %shard_map.121 = (bf16[704,2048]{1,0:T(8,128)(2,1)S(1)}, bf16[704,2048]{1,0:T(8,128)(2,1)S(1)}) custom-call(bf16[704,2048]{1,0:T(8,128)(2,1)} %collective-permute-done.2.refs_0_, bf16[704,2048]{1,0:T(8,128)(2,1)} %collective-permute-done.3.refs_1_), custom_call_target="tpu_custom_call" | custom-call | bytes 11534336 | tf_op jit(solution)/shard_map/pallas_call | solution.py:216
  33.8 1.6 %collective-permute-done.9.refs_5_ = bf16[32,2048]{1,0:T(8,128)(2,1)S(1)} collective-permute-done((bf16[32,2048]{1,0:T(8,128)(2,1)S(1)}, bf16[32,2048]{1,0:T(8,128)(2,1)S(1)}, u32[]{:S(2)}, u32[]{:S(2)}) %collective-permute-start.9) | collective-permute-done | bytes 131104 | tf_op jit(solution)/shard_map/ppermute | solution.py:18
  35.5 5.1 %shard_map.122 = (bf16[32,2048]{1,0:T(8,128)(2,1)S(1)}, bf16[32,2048]{1,0:T(8,128)(2,1)S(1)}, bf16[32,2048]{1,0:T(8,128)(2,1)S(1)}, bf16[32,2048]{1,0:T(8,128)(2...) custom-call(bf16[32,2048]{1,0:T(8,128)(2,1)S(1)} %collective-permute, ...), custom_call_target="tpu_custom_call" | custom-call | flops 4429185024 | bytes 17301504 | tf_op jit(solution)/shard_map/pallas_call | solution.py:253
  40.5 2.7 %collective-permute-start.11 = (bf16[32,2048]{1,0:T(8,128)(2,1)S(1)}, bf16[32,2048]{1,0:T(8,128)(2,1)S(1)}, u32[]{:S(2)}, u32[]{:S(2)}) collective-permute-start(bf16[32,2048]{1,0:T(8,128)(2,1)S(1)} %get-tuple-element.77), channel_id=1, source_target_pairs={{0,14},{1,15},{2,12},{3,13},{4,10},{5,11},{6,8},{7,9},{8,6},{9,7},... | collective-permute-start | bytes 393224 | tf_op jit(solution)/shard_map/ppermute | solution.py:18
  43.2 0.7 %collective-permute-start.12 = (bf16[32,2048]{1,0:T(8,128)(2,1)S(1)}, bf16[32,2048]{1,0:T(8,128)(2,1)S(1)}, u32[]{:S(2)}, u32[]{:S(2)}) collective-permute-start(bf16[32,2048]{1,0:T(8,128)(2,1)S(1)} %get-tuple-element.78), channel_id=1, source_target_pairs={{0,12},{1,13},{2,14},{3,15},{4,8},{5,9},{6,10},{7,11},{8,4},{9,5},... | collective-permute-start | bytes 393224 | tf_op jit(solution)/shard_map/ppermute | solution.py:18
  43.9 1.9 %collective-permute-start.13 = (bf16[32,2048]{1,0:T(8,128)(2,1)S(1)}, bf16[32,2048]{1,0:T(8,128)(2,1)S(1)}, u32[]{:S(2)}, u32[]{:S(2)}) collective-permute-start(bf16[32,2048]{1,0:T(8,128)(2,1)S(1)} %get-tuple-element.79), channel_id=1, source_target_pairs={{0,10},{1,11},{2,8},{3,9},{4,14},{5,15},{6,12},{7,13},{8,2},{9,3},... | collective-permute-start | bytes 393224 | tf_op jit(solution)/shard_map/ppermute | solution.py:18
  45.8 0.7 %collective-permute-start.14 = (bf16[32,2048]{1,0:T(8,128)(2,1)S(1)}, bf16[32,2048]{1,0:T(8,128)(2,1)S(1)}, u32[]{:S(2)}, u32[]{:S(2)}) collective-permute-start(bf16[32,2048]{1,0:T(8,128)(2,1)S(1)} %get-tuple-element.80), channel_id=1, source_target_pairs={{0,8},{1,9},{2,10},{3,11},{4,12},{5,13},{6,14},{7,15},{8,0},{9,1},... | collective-permute-start | bytes 393224 | tf_op jit(solution)/shard_map/ppermute | solution.py:18
  46.5 1.8 %collective-permute-start.15 = (bf16[32,2048]{1,0:T(8,128)(2,1)S(1)}, bf16[32,2048]{1,0:T(8,128)(2,1)S(1)}, u32[]{:S(2)}, u32[]{:S(2)}) collective-permute-start(bf16[32,2048]{1,0:T(8,128)(2,1)S(1)} %get-tuple-element.81), channel_id=1, source_target_pairs={{0,6},{1,7},{2,4},{3,5},{4,2},{5,3},{6,0},{7,1},{8,14},{9,15},{10,... | collective-permute-start | bytes 393224 | tf_op jit(solution)/shard_map/ppermute | solution.py:18
  48.2 1.1 %collective-permute-done.11.refs_0_ = bf16[32,2048]{1,0:T(8,128)(2,1)S(1)} collective-permute-done((bf16[32,2048]{1,0:T(8,128)(2,1)S(1)}, bf16[32,2048]{1,0:T(8,128)(2,1)S(1)}, u32[]{:S(2)}, u32[]{:S(2)}) %collective-permute-start.11) | collective-permute-done | bytes 131104 | tf_op jit(solution)/shard_map/ppermute | solution.py:18
  49.3 0.9 %collective-permute-start.16 = (bf16[32,2048]{1,0:T(8,128)(2,1)S(1)}, bf16[32,2048]{1,0:T(8,128)(2,1)S(1)}, u32[]{:S(2)}, u32[]{:S(2)}) collective-permute-start(bf16[32,2048]{1,0:T(8,128)(2,1)S(1)} %get-tuple-element.82), channel_id=1, source_target_pairs={{0,4},{1,5},{2,6},{3,7},{4,0},{5,1},{6,2},{7,3},{8,12},{9,13},{10,... | collective-permute-start | bytes 393224 | tf_op jit(solution)/shard_map/ppermute | solution.py:18
  50.3 1.9 %collective-permute-done.12.refs_1_ = bf16[32,2048]{1,0:T(8,128)(2,1)S(1)} collective-permute-done((bf16[32,2048]{1,0:T(8,128)(2,1)S(1)}, bf16[32,2048]{1,0:T(8,128)(2,1)S(1)}, u32[]{:S(2)}, u32[]{:S(2)}) %collective-permute-start.12) | collective-permute-done | bytes 131104 | tf_op jit(solution)/shard_map/ppermute | solution.py:18
  52.1 1.1 %collective-permute-start.17 = (bf16[32,2048]{1,0:T(8,128)(2,1)S(1)}, bf16[32,2048]{1,0:T(8,128)(2,1)S(1)}, u32[]{:S(2)}, u32[]{:S(2)}) collective-permute-start(bf16[32,2048]{1,0:T(8,128)(2,1)S(1)} %get-tuple-element.83), channel_id=1, source_target_pairs={{0,2},{1,3},{2,0},{3,1},{4,6},{5,7},{6,4},{7,5},{8,10},{9,11},{10,... | collective-permute-start | bytes 393224 | tf_op jit(solution)/shard_map/ppermute | solution.py:18
  53.2 1.0 %collective-permute-done.13.refs_2_ = bf16[32,2048]{1,0:T(8,128)(2,1)S(1)} collective-permute-done((bf16[32,2048]{1,0:T(8,128)(2,1)S(1)}, bf16[32,2048]{1,0:T(8,128)(2,1)S(1)}, u32[]{:S(2)}, u32[]{:S(2)}) %collective-permute-start.13) | collective-permute-done | bytes 131104 | tf_op jit(solution)/shard_map/ppermute | solution.py:18
  54.2 1.5 %collective-permute-done.14.refs_3_ = bf16[32,2048]{1,0:T(8,128)(2,1)S(1)} collective-permute-done((bf16[32,2048]{1,0:T(8,128)(2,1)S(1)}, bf16[32,2048]{1,0:T(8,128)(2,1)S(1)}, u32[]{:S(2)}, u32[]{:S(2)}) %collective-permute-start.14) | collective-permute-done | bytes 131104 | tf_op jit(solution)/shard_map/ppermute | solution.py:18
  55.6 0.6 collective-permute-done.16.refs_5_
  56.3 0.8 %collective-permute-done.17.refs_6_ = bf16[32,2048]{1,0:T(8,128)(2,1)S(1)} collective-permute-done((bf16[32,2048]{1,0:T(8,128)(2,1)S(1)}, bf16[32,2048]{1,0:T(8,128)(2,1)S(1)}, u32[]{:S(2)}, u32[]{:S(2)}) %collective-permute-start.17) | collective-permute-done | bytes 131104 | tf_op jit(solution)/shard_map/ppermute | solution.py:18
  57.6 2.8 %collective-permute-start.18 = (bf16[32,2048]{1,0:T(8,128)(2,1)S(1)}, bf16[32,2048]{1,0:T(8,128)(2,1)S(1)}, u32[]{:S(2)}, u32[]{:S(2)}) collective-permute-start(bf16[32,2048]{1,0:T(8,128)(2,1)S(1)} %get-tuple-element.86), channel_id=1, source_target_pairs={{0,16},{1,17},{2,18},{3,19},{4,20},{5,21},{6,22},{7,23},{8,24},{9,... | collective-permute-start | bytes 393224 | tf_op jit(solution)/shard_map/ppermute | solution.py:18
  60.4 5.4 %collective-permute-done.18 = bf16[32,2048]{1,0:T(8,128)(2,1)S(1)} collective-permute-done((bf16[32,2048]{1,0:T(8,128)(2,1)S(1)}, bf16[32,2048]{1,0:T(8,128)(2,1)S(1)}, u32[]{:S(2)}, u32[]{:S(2)}) %collective-permute-start.18) | collective-permute-done | bytes 131104 | tf_op jit(solution)/shard_map/ppermute | solution.py:18
  65.8 0.7 %add_convert_fusion = bf16[32,2048]{1,0:T(8,128)(2,1)} fusion(f32[32,2048]{1,0:T(8,128)S(1)} %copy-done.1, f32[32,2048]{1,0:T(8,128)S(1)} %get-tuple-element.85, bf16[32,2048]{1,0:T(8,128)(2,1)S(1)} %collective-permute-done.18), kind=kLoop, calls=%fused_computation | loop fusion | flops 262144 | bytes 786432 | tf_op jit(solution)/shard_map/convert_element_type | solution.py:337
  (18 shorter events, 1.6 us)
Async XLA Ops:
  0.0 17.6 %collective-permute-start.1 = (bf16[704,2048]{1,0:T(8,128)(2,1)}, bf16[704,2048]{1,0:T(8,128)(2,1)S(1)}, u32[]{:S(2)}, u32[]{:S(2)}) collective-permute-start(bf16[704,2048]{1,0:T(8,128)(2,1)} %bitcast.12), channel_id=1, source_target_pairs={{0,1},{1,0},{2,3},{3,2},{4,5},{5,4},{6,7},{7,6},{8,9},{9,8},{10,11... | collective-permute-start | bytes 8650760 | tf_op jit(solution)/shard_map/ppermute | solution.py:18
  0.5 17.2 %collective-permute-start.2 = (bf16[704,2048]{1,0:T(8,128)(2,1)}, bf16[704,2048]{1,0:T(8,128)(2,1)}, u32[]{:S(2)}, u32[]{:S(2)}) collective-permute-start(bf16[704,2048]{1,0:T(8,128)(2,1)} %bitcast.14), channel_id=1, source_target_pairs={{0,1},{1,0},{2,3},{3,2},{4,5},{5,4},{6,7},{7,6},{8,9},{9,8},{10,11... | collective-permute-start | bytes 8650760 | tf_op jit(solution)/shard_map/ppermute | solution.py:18
  0.5 17.1 %collective-permute-start.3 = (bf16[704,2048]{1,0:T(8,128)(2,1)}, bf16[704,2048]{1,0:T(8,128)(2,1)}, u32[]{:S(2)}, u32[]{:S(2)}) collective-permute-start(bf16[704,2048]{1,0:T(8,128)(2,1)} %bitcast.16), channel_id=1, source_target_pairs={{0,1},{1,0},{2,3},{3,2},{4,5},{5,4},{6,7},{7,6},{8,9},{9,8},{10,11... | collective-permute-start | bytes 8650760 | tf_op jit(solution)/shard_map/ppermute | solution.py:18
  6.4 11.2 %collective-permute-start = (bf16[32,2176]{1,0:T(8,128)(2,1)}, bf16[32,2176]{1,0:T(8,128)(2,1)S(1)}, u32[]{:S(2)}, u32[]{:S(2)}) collective-permute-start(bf16[32,2176]{1,0:T(8,128)(2,1)} %get-tuple-element.48.here), channel_id=1, source_target_pairs={{0,16},{1,17},{2,18},{3,19},{4,20},{5,21},{6,22},{7,23},{8,24},{9,... | collective-permute-start | bytes 417800 | tf_op jit(solution)/shard_map/ppermute | solution.py:18
  10.1 7.5 %copy-start = (bf16[32,2176]{1,0:T(8,128)(2,1)S(1)}, bf16[32,2176]{1,0:T(8,128)(2,1)}, u32[]{:S(2)}) copy-start(bf16[32,2176]{1,0:T(8,128)(2,1)} %get-tuple-element.48.here) | copy-start | bytes 417796
  18.3 8.4 %collective-permute-start.4 = (bf16[32,2048]{1,0:T(8,128)(2,1)S(1)}, bf16[32,2048]{1,0:T(8,128)(2,1)S(1)}, u32[]{:S(2)}, u32[]{:S(2)}) collective-permute-start(bf16[32,2048]{1,0:T(8,128)(2,1)S(1)} %get-tuple-element.58), channel_id=1, source_target_pairs={{0,14},{1,15},{2,12},{3,13},{4,10},{5,11},{6,8},{7,9},{8,6},{9,7},... | collective-permute-start | bytes 393224 | tf_op jit(solution)/shard_map/ppermute | solution.py:18
  21.0 8.2 %collective-permute-start.6 = (bf16[32,2048]{1,0:T(8,128)(2,1)S(1)}, bf16[32,2048]{1,0:T(8,128)(2,1)S(1)}, u32[]{:S(2)}, u32[]{:S(2)}) collective-permute-start(bf16[32,2048]{1,0:T(8,128)(2,1)S(1)} %get-tuple-element.60), channel_id=1, source_target_pairs={{0,10},{1,11},{2,8},{3,9},{4,14},{5,15},{6,12},{7,13},{8,2},{9,3},... | collective-permute-start | bytes 393224 | tf_op jit(solution)/shard_map/ppermute | solution.py:18
  22.3 11.4 %collective-permute-start.5 = (bf16[32,2048]{1,0:T(8,128)(2,1)S(1)}, bf16[32,2048]{1,0:T(8,128)(2,1)S(1)}, u32[]{:S(2)}, u32[]{:S(2)}) collective-permute-start(bf16[32,2048]{1,0:T(8,128)(2,1)S(1)} %get-tuple-element.59), channel_id=1, source_target_pairs={{0,12},{1,13},{2,14},{3,15},{4,8},{5,9},{6,10},{7,11},{8,4},{9,5},... | collective-permute-start | bytes 393224 | tf_op jit(solution)/shard_map/ppermute | solution.py:18
  23.0 10.8 %collective-permute-start.7 = (bf16[32,2048]{1,0:T(8,128)(2,1)S(1)}, bf16[32,2048]{1,0:T(8,128)(2,1)S(1)}, u32[]{:S(2)}, u32[]{:S(2)}) collective-permute-start(bf16[32,2048]{1,0:T(8,128)(2,1)S(1)} %get-tuple-element.64), channel_id=1, source_target_pairs={{0,8},{1,9},{2,10},{3,11},{4,12},{5,13},{6,14},{7,15},{8,0},{9,1},... | collective-permute-start | bytes 393224 | tf_op jit(solution)/shard_map/ppermute | solution.py:18
  24.2 9.6 %collective-permute-start.8 = (bf16[32,2048]{1,0:T(8,128)(2,1)S(1)}, bf16[32,2048]{1,0:T(8,128)(2,1)S(1)}, u32[]{:S(2)}, u32[]{:S(2)}) collective-permute-start(bf16[32,2048]{1,0:T(8,128)(2,1)S(1)} %get-tuple-element.65), channel_id=1, source_target_pairs={{0,6},{1,7},{2,4},{3,5},{4,2},{5,3},{6,0},{7,1},{8,14},{9,15},{10,... | collective-permute-start | bytes 393224 | tf_op jit(solution)/shard_map/ppermute | solution.py:18
  26.7 8.8 %collective-permute-start.9 = (bf16[32,2048]{1,0:T(8,128)(2,1)S(1)}, bf16[32,2048]{1,0:T(8,128)(2,1)S(1)}, u32[]{:S(2)}, u32[]{:S(2)}) collective-permute-start(bf16[32,2048]{1,0:T(8,128)(2,1)S(1)} %get-tuple-element.66), channel_id=1, source_target_pairs={{0,4},{1,5},{2,6},{3,7},{4,0},{5,1},{6,2},{7,3},{8,12},{9,13},{10,... | collective-permute-start | bytes 393224 | tf_op jit(solution)/shard_map/ppermute | solution.py:18
  29.3 6.2 %collective-permute-start.10 = (bf16[32,2048]{1,0:T(8,128)(2,1)S(1)}, bf16[32,2048]{1,0:T(8,128)(2,1)S(1)}, u32[]{:S(2)}, u32[]{:S(2)}) collective-permute-start(bf16[32,2048]{1,0:T(8,128)(2,1)S(1)} %get-tuple-element.67), channel_id=1, source_target_pairs={{0,2},{1,3},{2,0},{3,1},{4,6},{5,7},{6,4},{7,5},{8,10},{9,11},{10,... | collective-permute-start | bytes 393224 | tf_op jit(solution)/shard_map/ppermute | solution.py:18
  35.5 30.4 %copy-start.1 = (f32[32,2048]{1,0:T(8,128)S(1)}, f32[32,2048]{1,0:T(8,128)}, u32[]{:S(2)}) copy-start(f32[32,2048]{1,0:T(8,128)} %get-tuple-element.46) | copy-start | bytes 786436
  40.5 8.8 %collective-permute-start.11 = (bf16[32,2048]{1,0:T(8,128)(2,1)S(1)}, bf16[32,2048]{1,0:T(8,128)(2,1)S(1)}, u32[]{:S(2)}, u32[]{:S(2)}) collective-permute-start(bf16[32,2048]{1,0:T(8,128)(2,1)S(1)} %get-tuple-element.77), channel_id=1, source_target_pairs={{0,14},{1,15},{2,12},{3,13},{4,10},{5,11},{6,8},{7,9},{8,6},{9,7},... | collective-permute-start | bytes 393224 | tf_op jit(solution)/shard_map/ppermute | solution.py:18
  43.2 8.9 %collective-permute-start.12 = (bf16[32,2048]{1,0:T(8,128)(2,1)S(1)}, bf16[32,2048]{1,0:T(8,128)(2,1)S(1)}, u32[]{:S(2)}, u32[]{:S(2)}) collective-permute-start(bf16[32,2048]{1,0:T(8,128)(2,1)S(1)} %get-tuple-element.78), channel_id=1, source_target_pairs={{0,12},{1,13},{2,14},{3,15},{4,8},{5,9},{6,10},{7,11},{8,4},{9,5},... | collective-permute-start | bytes 393224 | tf_op jit(solution)/shard_map/ppermute | solution.py:18
  43.9 10.3 %collective-permute-start.13 = (bf16[32,2048]{1,0:T(8,128)(2,1)S(1)}, bf16[32,2048]{1,0:T(8,128)(2,1)S(1)}, u32[]{:S(2)}, u32[]{:S(2)}) collective-permute-start(bf16[32,2048]{1,0:T(8,128)(2,1)S(1)} %get-tuple-element.79), channel_id=1, source_target_pairs={{0,10},{1,11},{2,8},{3,9},{4,14},{5,15},{6,12},{7,13},{8,2},{9,3},... | collective-permute-start | bytes 393224 | tf_op jit(solution)/shard_map/ppermute | solution.py:18
  45.8 9.9 %collective-permute-start.14 = (bf16[32,2048]{1,0:T(8,128)(2,1)S(1)}, bf16[32,2048]{1,0:T(8,128)(2,1)S(1)}, u32[]{:S(2)}, u32[]{:S(2)}) collective-permute-start(bf16[32,2048]{1,0:T(8,128)(2,1)S(1)} %get-tuple-element.80), channel_id=1, source_target_pairs={{0,8},{1,9},{2,10},{3,11},{4,12},{5,13},{6,14},{7,15},{8,0},{9,1},... | collective-permute-start | bytes 393224 | tf_op jit(solution)/shard_map/ppermute | solution.py:18
  46.5 9.2 %collective-permute-start.15 = (bf16[32,2048]{1,0:T(8,128)(2,1)S(1)}, bf16[32,2048]{1,0:T(8,128)(2,1)S(1)}, u32[]{:S(2)}, u32[]{:S(2)}) collective-permute-start(bf16[32,2048]{1,0:T(8,128)(2,1)S(1)} %get-tuple-element.81), channel_id=1, source_target_pairs={{0,6},{1,7},{2,4},{3,5},{4,2},{5,3},{6,0},{7,1},{8,14},{9,15},{10,... | collective-permute-start | bytes 393224 | tf_op jit(solution)/shard_map/ppermute | solution.py:18
  49.3 6.9 %collective-permute-start.16 = (bf16[32,2048]{1,0:T(8,128)(2,1)S(1)}, bf16[32,2048]{1,0:T(8,128)(2,1)S(1)}, u32[]{:S(2)}, u32[]{:S(2)}) collective-permute-start(bf16[32,2048]{1,0:T(8,128)(2,1)S(1)} %get-tuple-element.82), channel_id=1, source_target_pairs={{0,4},{1,5},{2,6},{3,7},{4,0},{5,1},{6,2},{7,3},{8,12},{9,13},{10,... | collective-permute-start | bytes 393224 | tf_op jit(solution)/shard_map/ppermute | solution.py:18
  52.1 5.0 %collective-permute-start.17 = (bf16[32,2048]{1,0:T(8,128)(2,1)S(1)}, bf16[32,2048]{1,0:T(8,128)(2,1)S(1)}, u32[]{:S(2)}, u32[]{:S(2)}) collective-permute-start(bf16[32,2048]{1,0:T(8,128)(2,1)S(1)} %get-tuple-element.83), channel_id=1, source_target_pairs={{0,2},{1,3},{2,0},{3,1},{4,6},{5,7},{6,4},{7,5},{8,10},{9,11},{10,... | collective-permute-start | bytes 393224 | tf_op jit(solution)/shard_map/ppermute | solution.py:18
  57.6 8.3 %collective-permute-start.18 = (bf16[32,2048]{1,0:T(8,128)(2,1)S(1)}, bf16[32,2048]{1,0:T(8,128)(2,1)S(1)}, u32[]{:S(2)}, u32[]{:S(2)}) collective-permute-start(bf16[32,2048]{1,0:T(8,128)(2,1)S(1)} %get-tuple-element.86), channel_id=1, source_target_pairs={{0,16},{1,17},{2,18},{3,19},{4,20},{5,21},{6,22},{7,23},{8,24},{9,... | collective-permute-start | bytes 393224 | tf_op jit(solution)/shard_map/ppermute | solution.py:18

commit v6 on v5

--- a/solution.py
+++ b/solution.py
@@ -21,6 +21,24 @@
 def exchanged(blocks):
     last = len(blocks) - 1
     return [swapped(b, 2 * (last - i)) if i < last else b for i, b in enumerate(blocks)]
+
+
+def returned(rows, near):
+    groups = [
+        [first + 2 * i + core for i in range(near)]
+        for first in range(0, lax.axis_size("ep"), 2 * near)
+        for core in range(2)
+    ]
+    blocks = rows.reshape(near, rows.shape[0] // near, rows.shape[1])
+    got = lax.all_to_all(
+        blocks, "ep", split_axis=0, concat_axis=0, tiled=True, axis_index_groups=groups
+    )
+    return got.reshape(rows.shape)
+
+
+def block_of(place, count, size):
+    local = (lax.axis_index("ep") // 2) % count
+    return pl.ds(pl.multiple_of((local ^ (count - 1 - place)) * size, size), size)
 
 
 def whole():
@@ -174,7 +192,7 @@
     rows = jnp.concatenate([here[:, :features], there[:, :features]], axis=0)
     for m, block in enumerate(blocks):
         hit = jnp.where(slots == place[m : m + 1, :], 1.0, 0.0)
-        table[2 * stride * m : 2 * stride * (m + 1), :] = hit * weight[m : m + 1, :]
+        table[block_of(m, count, 2 * stride), :] = hit * weight[m : m + 1, :]
         block[...] = jnp.dot(hit.astype(BF16), rows, preferred_element_type=F32).astype(BF16)
     turned = table[...].T
     top_bits = turned.astype(BF16)
@@ -228,8 +246,7 @@
 
 def expert_kernel(count, *refs):
     blocks, weights = refs[:count], refs[count : count + 6]
-    outs = refs[count + 6 : 2 * count + 6]
-    rows, active = refs[2 * count + 6 :]
+    out, rows, active = refs[count + 6 :]
     size, width = blocks[0].shape
     for m, block in enumerate(blocks):
         rows[m * size : (m + 1) * size, :] = block[...]
@@ -242,8 +259,9 @@
         columns = slice(at, at + 512)
         result = jnp.dot(active[0], weights[2][:, columns], preferred_element_type=F32)
         result = result + jnp.dot(active[1], weights[5][:, columns], preferred_element_type=F32)
-        for m, out in enumerate(outs):
-            out[:, columns] = result[m * size : (m + 1) * size, :].astype(BF16)
+        for m in range(count):
+            part = result[m * size : (m + 1) * size, :]
+            out[block_of(m, count, size), columns] = part.astype(BF16)
 
 
 def run_expert(blocks, weights):
@@ -253,8 +271,8 @@
     return pl.pallas_call(
         functools.partial(expert_kernel, count),
         in_specs=[whole()] * (count + 6),
-        out_specs=[whole()] * count,
-        out_shape=[jax.ShapeDtypeStruct((size, width), BF16)] * count,
+        out_specs=whole(),
+        out_shape=jax.ShapeDtypeStruct((count * size, width), BF16),
         scratch_shapes=[
             pltpu.VMEM((count * size, width), BF16),
             pltpu.VMEM((2, count * size, units), BF16),
@@ -268,32 +286,29 @@
     )(*blocks, *weights)
 
 
-def combine_kernel(high, low, *refs):
-    blocks, (here, there) = refs[:-2], refs[-2:]
-    rows = jnp.concatenate([block[...] for block in blocks], axis=0)
-    total = jnp.dot(high[...], rows, preferred_element_type=F32)
-    total = total + jnp.dot(low[...], rows, preferred_element_type=F32)
+def combine_kernel(high, low, rows, here, there):
+    total = jnp.dot(high[...], rows[...], preferred_element_type=F32)
+    total = total + jnp.dot(low[...], rows[...], preferred_element_type=F32)
     tokens = here.shape[0]
     here[...] = total[:tokens]
     there[...] = total[tokens:].astype(BF16)
 
 
-def combine(high, low, blocks):
-    both, rows = high.shape
-    width = blocks[0].shape[1]
+def combine(high, low, rows):
+    both, width = high.shape[0], rows.shape[1]
     return pl.pallas_call(
         combine_kernel,
-        in_specs=[whole()] * (2 + len(blocks)),
+        in_specs=[whole()] * 3,
         out_specs=[whole()] * 2,
         out_shape=[
             jax.ShapeDtypeStruct((both // 2, width), F32),
             jax.ShapeDtypeStruct((both // 2, width), BF16),
         ],
         cost_estimate=pl.CostEstimate(
-            flops=4 * both * rows * width, bytes_accessed=3 * MIB // 2, transcendentals=0
+            flops=4 * high.size * width, bytes_accessed=3 * MIB // 2, transcendentals=0
         ),
         compiler_params=pltpu.CompilerParams(vmem_limit_bytes=16 * MIB),
-    )(high, low, *blocks)
+    )(high, low, rows)
 
 
 def local(
@@ -332,8 +347,8 @@
     high, low, *blocks = dispatch(mine, normed, across, top, stride)
     blocks = exchanged(blocks)
     blocks[2], *late = lax.optimization_barrier((blocks[2], *other[1:]))
-    blocks = exchanged(run_expert(blocks, [*own, other[0], *load(late, 38)]))
-    here, there = combine(high, low, blocks)
+    rows = returned(run_expert(blocks, [*own, other[0], *load(late, 38)]), near)
+    here, there = combine(high, low, rows)
     return (stream + (here + swapped(there, devices // 2).astype(F32))).astype(BF16)
 
 

time: 66.7 us -> 69 us (1.034)
  blocking collectives: 0 us -> 18.9 us
  starting transfers between devices: 28.5 us -> 19.3 us
  waiting for transfers between devices: 19.4 us -> 11.9 us
    all_to_all x0 -> x1, blocking collectives: none -> 18.9 us  [returned(): lax.all_to_all(blocks, 'ep', split_axis=0, concat_axis=0, tiled=True, axi...]
    ppermute x19 -> x12, starting transfers between devices: 28.5 us -> 19.3 us  [swapped(): return lax.ppermute(value, 'ep', pairs)]
    ppermute x19 -> x12, waiting for transfers between devices: 19.4 us -> 11.9 us  [swapped(): return lax.ppermute(value, 'ep', pairs)]
  transfers between devices with their start and end apart: 19 -> 12, of which waited for: 11 -> 5; matrix products, arithmetic and copies ran while one was open for 0% -> 0% of each run, Pallas kernels for 18% -> 17%
where the time goes in v6:
time: 69 us; the launch traced here: 68.8 us
  starting transfers between devices  19.3 us (28%)
  blocking collectives  18.9 us (27%)
  Pallas kernels  17.9 us (26%)
  waiting for transfers between devices  11.9 us (17%)
  other arithmetic  0.71 us (1%)
    ppermute x12, starting transfers between devices, swapped(): return lax.ppermute(value, 'ep', pairs)  19.3 us
    all_to_all x1, blocking collectives, returned(): lax.all_to_all(blocks, 'ep', split_axis=0, concat_axis=0, tiled=True, axi...  18.9 us
    ppermute x12, waiting for transfers between devices, swapped(): return lax.ppermute(value, 'ep', pairs)  11.9 us
    pallas_call x2, Pallas kernels, load(): pl.pallas_call(load_kernel, in_specs=[pl.BlockSpec(memory_space=pl.ANY)]...  6.29 us
    pallas_call x1, Pallas kernels, attend(): pl.pallas_call(functools.partial(attend_kernel, heads), in_specs=[pl.Bloc...  5.44 us
    pallas_call x1, Pallas kernels, run_expert(): pl.pallas_call(functools.partial(expert_kernel, count), in_specs=[whole()...  5.08 us
  transfers between devices with their start and end apart: 12, of which 5 were waited for; matrix products, arithmetic and copies ran while one was open for 0% of the time, Pallas kernels for 17%

profile of v6, /device:TPU:0, one launch (start us, length us, event | category | flops | bytes accessed | tf_op | source)
XLA Modules:
  0.0 68.8 jit_solution(5513841976766265109)
XLA Ops:
  0.0 0.5 collective-permute-start.1
  0.5 0.1 collective-permute-start.2
  0.5 0.5 collective-permute-start.3
  1.0 5.4 %shard_map.118 = (f32[32,2048]{1,0:T(8,128)}, bf16[32,2176]{1,0:T(8,128)(2,1)}) custom-call(s32[4]{0:T(128)} %refs_0_.1, bf16[4,8,576]{2,1,0:T(8,128)(2,1)} %refs_1_.1, bf16[4,128,576]{2,1,0:T(8,128)(2,1)} %bitcast.23, bf16[4,576,384]{2,1,0:T(8,128)(2,1)} %bitcast.22, bf16[16,512,128]{2,1,0:T(8,128)(2,1)} %refs_4_.1, bf16[32,2048]{1,0:T(8,128)(2,1)} %refs_5_.1, ...), custom_call_target="tpu_custom_call" | custom-call | flops 494927872 | bytes 6291456 | tf_op jit(solution)/shard_map/pallas_call | solution.py:144
  6.4 3.7 %collective-permute-start = (bf16[32,2176]{1,0:T(8,128)(2,1)}, bf16[32,2176]{1,0:T(8,128)(2,1)S(1)}, u32[]{:S(2)}, u32[]{:S(2)}) collective-permute-start(bf16[32,2176]{1,0:T(8,128)(2,1)} %get-tuple-element.40.here), channel_id=1, source_target_pairs={{0,16},{1,17},{2,18},{3,19},{4,20},{5,21},{6,22},{7,23},{8,24},{9,... | collective-permute-start | bytes 417800 | tf_op jit(solution)/shard_map/ppermute | solution.py:18
  10.1 3.6 %shard_map.119 = (bf16[704,2048]{1,0:T(8,128)(2,1)S(1)}, bf16[704,2048]{1,0:T(8,128)(2,1)S(1)}, bf16[704,2048]{1,0:T(8,128)(2,1)S(1)}) custom-call(bf16[704,2048]{1,0:T(8,128)(2,1)} %bitcast.17, bf16[704,2048]{1,0:T(8,128)(2,1)} %bitcast.19, bf16[704,2048]{1,0:T(8,128)(2,1)} %bitcast.21), custom_call_target="tpu_custom_call" | custom-call | bytes 17301504 | tf_op jit(solution)/shard_map/pallas_call | solution.py:234
  13.7 3.9 %collective-permute-done.there = bf16[32,2176]{1,0:T(8,128)(2,1)S(1)} collective-permute-done((bf16[32,2176]{1,0:T(8,128)(2,1)}, bf16[32,2176]{1,0:T(8,128)(2,1)S(1)}, u32[]{:S(2)}, u32[]{:S(2)}) %collective-permute-start) | collective-permute-done | bytes 139296 | tf_op jit(solution)/shard_map/ppermute | solution.py:18
  17.6 0.0 collective-permute-done.1.refs_11_
  17.6 0.0 collective-permute-done.2.refs_0_
  17.6 0.0 collective-permute-done.3.refs_1_
  17.6 0.6 shard_map.120
  18.3 2.8 %collective-permute-start.4 = (bf16[32,2048]{1,0:T(8,128)(2,1)S(1)}, bf16[32,2048]{1,0:T(8,128)(2,1)S(1)}, u32[]{:S(2)}, u32[]{:S(2)}) collective-permute-start(bf16[32,2048]{1,0:T(8,128)(2,1)S(1)} %get-tuple-element.50), channel_id=1, source_target_pairs={{0,14},{1,15},{2,12},{3,13},{4,10},{5,11},{6,8},{7,9},{8,6},{9,7},... | collective-permute-start | bytes 393224 | tf_op jit(solution)/shard_map/ppermute | solution.py:18
  21.0 1.2 %collective-permute-start.6 = (bf16[32,2048]{1,0:T(8,128)(2,1)S(1)}, bf16[32,2048]{1,0:T(8,128)(2,1)S(1)}, u32[]{:S(2)}, u32[]{:S(2)}) collective-permute-start(bf16[32,2048]{1,0:T(8,128)(2,1)S(1)} %get-tuple-element.52), channel_id=1, source_target_pairs={{0,10},{1,11},{2,8},{3,9},{4,14},{5,15},{6,12},{7,13},{8,2},{9,3},... | collective-permute-start | bytes 393224 | tf_op jit(solution)/shard_map/ppermute | solution.py:18
  22.3 0.7 %collective-permute-start.5 = (bf16[32,2048]{1,0:T(8,128)(2,1)S(1)}, bf16[32,2048]{1,0:T(8,128)(2,1)S(1)}, u32[]{:S(2)}, u32[]{:S(2)}) collective-permute-start(bf16[32,2048]{1,0:T(8,128)(2,1)S(1)} %get-tuple-element.51), channel_id=1, source_target_pairs={{0,12},{1,13},{2,14},{3,15},{4,8},{5,9},{6,10},{7,11},{8,4},{9,5},... | collective-permute-start | bytes 393224 | tf_op jit(solution)/shard_map/ppermute | solution.py:18
  23.0 1.2 %collective-permute-start.7 = (bf16[32,2048]{1,0:T(8,128)(2,1)S(1)}, bf16[32,2048]{1,0:T(8,128)(2,1)S(1)}, u32[]{:S(2)}, u32[]{:S(2)}) collective-permute-start(bf16[32,2048]{1,0:T(8,128)(2,1)S(1)} %get-tuple-element.56), channel_id=1, source_target_pairs={{0,8},{1,9},{2,10},{3,11},{4,12},{5,13},{6,14},{7,15},{8,0},{9,1},... | collective-permute-start | bytes 393224 | tf_op jit(solution)/shard_map/ppermute | solution.py:18
  24.2 2.5 %collective-permute-start.8 = (bf16[32,2048]{1,0:T(8,128)(2,1)S(1)}, bf16[32,2048]{1,0:T(8,128)(2,1)S(1)}, u32[]{:S(2)}, u32[]{:S(2)}) collective-permute-start(bf16[32,2048]{1,0:T(8,128)(2,1)S(1)} %get-tuple-element.57), channel_id=1, source_target_pairs={{0,6},{1,7},{2,4},{3,5},{4,2},{5,3},{6,0},{7,1},{8,14},{9,15},{10,... | collective-permute-start | bytes 393224 | tf_op jit(solution)/shard_map/ppermute | solution.py:18
  26.7 0.0 collective-permute-done.4.refs_0_
  26.7 1.3 %collective-permute-start.9 = (bf16[32,2048]{1,0:T(8,128)(2,1)S(1)}, bf16[32,2048]{1,0:T(8,128)(2,1)S(1)}, u32[]{:S(2)}, u32[]{:S(2)}) collective-permute-start(bf16[32,2048]{1,0:T(8,128)(2,1)S(1)} %get-tuple-element.58), channel_id=1, source_target_pairs={{0,4},{1,5},{2,6},{3,7},{4,0},{5,1},{6,2},{7,3},{8,12},{9,13},{10,... | collective-permute-start | bytes 393224 | tf_op jit(solution)/shard_map/ppermute | solution.py:18
  27.9 1.3 %collective-permute-done.6.refs_2_ = bf16[32,2048]{1,0:T(8,128)(2,1)S(1)} collective-permute-done((bf16[32,2048]{1,0:T(8,128)(2,1)S(1)}, bf16[32,2048]{1,0:T(8,128)(2,1)S(1)}, u32[]{:S(2)}, u32[]{:S(2)}) %collective-permute-start.6) | collective-permute-done | bytes 131104 | tf_op jit(solution)/shard_map/ppermute | solution.py:18
  29.3 1.6 %collective-permute-start.10 = (bf16[32,2048]{1,0:T(8,128)(2,1)S(1)}, bf16[32,2048]{1,0:T(8,128)(2,1)S(1)}, u32[]{:S(2)}, u32[]{:S(2)}) collective-permute-start(bf16[32,2048]{1,0:T(8,128)(2,1)S(1)} %get-tuple-element.59), channel_id=1, source_target_pairs={{0,2},{1,3},{2,0},{3,1},{4,6},{5,7},{6,4},{7,5},{8,10},{9,11},{10,... | collective-permute-start | bytes 393224 | tf_op jit(solution)/shard_map/ppermute | solution.py:18
  30.9 2.7 %shard_map.121 = (bf16[704,2048]{1,0:T(8,128)(2,1)S(1)}, bf16[704,2048]{1,0:T(8,128)(2,1)S(1)}) custom-call(bf16[704,2048]{1,0:T(8,128)(2,1)} %collective-permute-done.2.refs_0_, bf16[704,2048]{1,0:T(8,128)(2,1)} %collective-permute-done.3.refs_1_), custom_call_target="tpu_custom_call" | custom-call | bytes 11534336 | tf_op jit(solution)/shard_map/pallas_call | solution.py:234
  33.6 0.0 collective-permute-done.5.refs_1_
  33.6 0.2 collective-permute-done.7.refs_3_
  33.8 0.0 collective-permute-done.8.refs_4_
  33.8 1.7 %collective-permute-done.9.refs_5_ = bf16[32,2048]{1,0:T(8,128)(2,1)S(1)} collective-permute-done((bf16[32,2048]{1,0:T(8,128)(2,1)S(1)}, bf16[32,2048]{1,0:T(8,128)(2,1)S(1)}, u32[]{:S(2)}, u32[]{:S(2)}) %collective-permute-start.9) | collective-permute-done | bytes 131104 | tf_op jit(solution)/shard_map/ppermute | solution.py:18
  35.5 0.0 collective-permute-done.10.refs_6_
  35.5 5.1 %shard_map.122 = bf16[256,2048]{1,0:T(8,128)(2,1)S(1)} custom-call(bf16[32,2048]{1,0:T(8,128)(2,1)S(1)} %collective-permute-done.4.refs_0_, bf16[32,2048]{1,0:T(8,128)(2,1)S(1)} %collective-permute-done.5.refs_1_, bf16[32,2048]{1,0:T(8,128)(2,1)S(1)} %collective-permute-done.6.refs_2_, bf16[32,2048]{1,0:T(8,128)(2,1)S(1)} %collective-permute-done.7.refs_3_, ...), custom_call_target="tpu_custom_call" | custom-call | flops 4429185024 | bytes 17301504 | tf_op jit(solution)/shard_map/pallas_call | solution.py:271
  40.6 18.9 %all_to_all.5 = bf16[8,32,2048]{2,1,0:T(8,128)(2,1)S(1)} all-to-all(bf16[8,32,2048]{2,1,0:T(8,128)(2,1)S(1)} %bitcast.14), channel_id=1, replica_groups={{0,2,4,6,8,10,12,14},{1,3,5,7,9,11,13,15},{16,18,20,22,24,26,28,30},{17..., dimensions={0} | all-to-all | bytes 2097152 | tf_op jit(solution)/shard_map/all_to_all | solution.py:33
  59.5 0.5 shard_map.123
  60.0 3.3 %collective-permute-start.11 = (bf16[32,2048]{1,0:T(8,128)(2,1)S(1)}, bf16[32,2048]{1,0:T(8,128)(2,1)S(1)}, u32[]{:S(2)}, u32[]{:S(2)}) collective-permute-start(bf16[32,2048]{1,0:T(8,128)(2,1)S(1)} %get-tuple-element.70), channel_id=1, source_target_pairs={{0,16},{1,17},{2,18},{3,19},{4,20},{5,21},{6,22},{7,23},{8,24},{9,... | collective-permute-start | bytes 393224 | tf_op jit(solution)/shard_map/ppermute | solution.py:18
  63.3 4.8 %collective-permute-done.11 = bf16[32,2048]{1,0:T(8,128)(2,1)S(1)} collective-permute-done((bf16[32,2048]{1,0:T(8,128)(2,1)S(1)}, bf16[32,2048]{1,0:T(8,128)(2,1)S(1)}, u32[]{:S(2)}, u32[]{:S(2)}) %collective-permute-start.11) | collective-permute-done | bytes 131104 | tf_op jit(solution)/shard_map/ppermute | solution.py:18
  68.1 0.7 %add_convert_fusion = bf16[32,2048]{1,0:T(8,128)(2,1)} fusion(f32[32,2048]{1,0:T(8,128)S(1)} %copy-done.1, f32[32,2048]{1,0:T(8,128)S(1)} %get-tuple-element.69, bf16[32,2048]{1,0:T(8,128)(2,1)S(1)} %collective-permute-done.11), kind=kLoop, calls=%fused_computation | loop fusion | flops 262144 | bytes 786432 | tf_op jit(solution)/shard_map/convert_element_type | solution.py:352
  (5 shorter events, 0.0 us)
Async XLA Ops:
  0.0 17.6 %collective-permute-start.1 = (bf16[704,2048]{1,0:T(8,128)(2,1)}, bf16[704,2048]{1,0:T(8,128)(2,1)S(1)}, u32[]{:S(2)}, u32[]{:S(2)}) collective-permute-start(bf16[704,2048]{1,0:T(8,128)(2,1)} %bitcast.16), channel_id=1, source_target_pairs={{0,1},{1,0},{2,3},{3,2},{4,5},{5,4},{6,7},{7,6},{8,9},{9,8},{10,11... | collective-permute-start | bytes 8650760 | tf_op jit(solution)/shard_map/ppermute | solution.py:18
  0.5 17.2 %collective-permute-start.2 = (bf16[704,2048]{1,0:T(8,128)(2,1)}, bf16[704,2048]{1,0:T(8,128)(2,1)}, u32[]{:S(2)}, u32[]{:S(2)}) collective-permute-start(bf16[704,2048]{1,0:T(8,128)(2,1)} %bitcast.18), channel_id=1, source_target_pairs={{0,1},{1,0},{2,3},{3,2},{4,5},{5,4},{6,7},{7,6},{8,9},{9,8},{10,11... | collective-permute-start | bytes 8650760 | tf_op jit(solution)/shard_map/ppermute | solution.py:18
  0.5 17.1 %collective-permute-start.3 = (bf16[704,2048]{1,0:T(8,128)(2,1)}, bf16[704,2048]{1,0:T(8,128)(2,1)}, u32[]{:S(2)}, u32[]{:S(2)}) collective-permute-start(bf16[704,2048]{1,0:T(8,128)(2,1)} %bitcast.20), channel_id=1, source_target_pairs={{0,1},{1,0},{2,3},{3,2},{4,5},{5,4},{6,7},{7,6},{8,9},{9,8},{10,11... | collective-permute-start | bytes 8650760 | tf_op jit(solution)/shard_map/ppermute | solution.py:18
  6.4 11.2 %collective-permute-start = (bf16[32,2176]{1,0:T(8,128)(2,1)}, bf16[32,2176]{1,0:T(8,128)(2,1)S(1)}, u32[]{:S(2)}, u32[]{:S(2)}) collective-permute-start(bf16[32,2176]{1,0:T(8,128)(2,1)} %get-tuple-element.40.here), channel_id=1, source_target_pairs={{0,16},{1,17},{2,18},{3,19},{4,20},{5,21},{6,22},{7,23},{8,24},{9,... | collective-permute-start | bytes 417800 | tf_op jit(solution)/shard_map/ppermute | solution.py:18
  10.1 7.5 %copy-start = (bf16[32,2176]{1,0:T(8,128)(2,1)S(1)}, bf16[32,2176]{1,0:T(8,128)(2,1)}, u32[]{:S(2)}) copy-start(bf16[32,2176]{1,0:T(8,128)(2,1)} %get-tuple-element.40.here) | copy-start | bytes 417796
  18.3 8.4 %collective-permute-start.4 = (bf16[32,2048]{1,0:T(8,128)(2,1)S(1)}, bf16[32,2048]{1,0:T(8,128)(2,1)S(1)}, u32[]{:S(2)}, u32[]{:S(2)}) collective-permute-start(bf16[32,2048]{1,0:T(8,128)(2,1)S(1)} %get-tuple-element.50), channel_id=1, source_target_pairs={{0,14},{1,15},{2,12},{3,13},{4,10},{5,11},{6,8},{7,9},{8,6},{9,7},... | collective-permute-start | bytes 393224 | tf_op jit(solution)/shard_map/ppermute | solution.py:18
  21.0 8.3 %collective-permute-start.6 = (bf16[32,2048]{1,0:T(8,128)(2,1)S(1)}, bf16[32,2048]{1,0:T(8,128)(2,1)S(1)}, u32[]{:S(2)}, u32[]{:S(2)}) collective-permute-start(bf16[32,2048]{1,0:T(8,128)(2,1)S(1)} %get-tuple-element.52), channel_id=1, source_target_pairs={{0,10},{1,11},{2,8},{3,9},{4,14},{5,15},{6,12},{7,13},{8,2},{9,3},... | collective-permute-start | bytes 393224 | tf_op jit(solution)/shard_map/ppermute | solution.py:18
  22.3 11.4 %collective-permute-start.5 = (bf16[32,2048]{1,0:T(8,128)(2,1)S(1)}, bf16[32,2048]{1,0:T(8,128)(2,1)S(1)}, u32[]{:S(2)}, u32[]{:S(2)}) collective-permute-start(bf16[32,2048]{1,0:T(8,128)(2,1)S(1)} %get-tuple-element.51), channel_id=1, source_target_pairs={{0,12},{1,13},{2,14},{3,15},{4,8},{5,9},{6,10},{7,11},{8,4},{9,5},... | collective-permute-start | bytes 393224 | tf_op jit(solution)/shard_map/ppermute | solution.py:18
  23.0 10.8 %collective-permute-start.7 = (bf16[32,2048]{1,0:T(8,128)(2,1)S(1)}, bf16[32,2048]{1,0:T(8,128)(2,1)S(1)}, u32[]{:S(2)}, u32[]{:S(2)}) collective-permute-start(bf16[32,2048]{1,0:T(8,128)(2,1)S(1)} %get-tuple-element.56), channel_id=1, source_target_pairs={{0,8},{1,9},{2,10},{3,11},{4,12},{5,13},{6,14},{7,15},{8,0},{9,1},... | collective-permute-start | bytes 393224 | tf_op jit(solution)/shard_map/ppermute | solution.py:18
  24.2 9.6 %collective-permute-start.8 = (bf16[32,2048]{1,0:T(8,128)(2,1)S(1)}, bf16[32,2048]{1,0:T(8,128)(2,1)S(1)}, u32[]{:S(2)}, u32[]{:S(2)}) collective-permute-start(bf16[32,2048]{1,0:T(8,128)(2,1)S(1)} %get-tuple-element.57), channel_id=1, source_target_pairs={{0,6},{1,7},{2,4},{3,5},{4,2},{5,3},{6,0},{7,1},{8,14},{9,15},{10,... | collective-permute-start | bytes 393224 | tf_op jit(solution)/shard_map/ppermute | solution.py:18
  26.7 8.8 %collective-permute-start.9 = (bf16[32,2048]{1,0:T(8,128)(2,1)S(1)}, bf16[32,2048]{1,0:T(8,128)(2,1)S(1)}, u32[]{:S(2)}, u32[]{:S(2)}) collective-permute-start(bf16[32,2048]{1,0:T(8,128)(2,1)S(1)} %get-tuple-element.58), channel_id=1, source_target_pairs={{0,4},{1,5},{2,6},{3,7},{4,0},{5,1},{6,2},{7,3},{8,12},{9,13},{10,... | collective-permute-start | bytes 393224 | tf_op jit(solution)/shard_map/ppermute | solution.py:18
  29.3 6.2 %collective-permute-start.10 = (bf16[32,2048]{1,0:T(8,128)(2,1)S(1)}, bf16[32,2048]{1,0:T(8,128)(2,1)S(1)}, u32[]{:S(2)}, u32[]{:S(2)}) collective-permute-start(bf16[32,2048]{1,0:T(8,128)(2,1)S(1)} %get-tuple-element.59), channel_id=1, source_target_pairs={{0,2},{1,3},{2,0},{3,1},{4,6},{5,7},{6,4},{7,5},{8,10},{9,11},{10,... | collective-permute-start | bytes 393224 | tf_op jit(solution)/shard_map/ppermute | solution.py:18
  40.5 27.6 %copy-start.1 = (f32[32,2048]{1,0:T(8,128)S(1)}, f32[32,2048]{1,0:T(8,128)}, u32[]{:S(2)}) copy-start(f32[32,2048]{1,0:T(8,128)} %get-tuple-element.38) | copy-start | bytes 786436
  60.0 8.1 %collective-permute-start.11 = (bf16[32,2048]{1,0:T(8,128)(2,1)S(1)}, bf16[32,2048]{1,0:T(8,128)(2,1)S(1)}, u32[]{:S(2)}, u32[]{:S(2)}) collective-permute-start(bf16[32,2048]{1,0:T(8,128)(2,1)S(1)} %get-tuple-element.70), channel_id=1, source_target_pairs={{0,16},{1,17},{2,18},{3,19},{4,20},{5,21},{6,22},{7,23},{8,24},{9,... | collective-permute-start | bytes 393224 | tf_op jit(solution)/shard_map/ppermute | solution.py:18

commit v7 on v5

--- a/solution.py
+++ b/solution.py
@@ -18,9 +18,18 @@
     return lax.ppermute(value, "ep", pairs)
 
 
+def orders(near):
+    first = list(range(near - 1, -1, -1))
+    return first, first[:1] + [(near - 1) ^ m for m in first[1:-1]] + [0]
+
+
 def exchanged(blocks):
-    last = len(blocks) - 1
-    return [swapped(b, 2 * (last - i)) if i < last else b for i, b in enumerate(blocks)]
+    got = list(blocks)
+    for i, masks in enumerate(zip(*orders(len(blocks)))):
+        pairs = [(d, d ^ 2 * masks[d % 2]) for d in range(lax.axis_size("ep"))]
+        if any(masks):
+            got[i] = lax.ppermute(blocks[i], "ep", pairs)
+    return got
 
 
 def whole():
@@ -143,9 +152,10 @@
     )(*operands)
 
 
-def dispatch_kernel(top, stride, mine, here, there, high, low, *refs):
+def dispatch_kernel(top, mine, here, there, high, low, *refs):
     blocks, table = refs[:-1], refs[-1]
-    tokens, features = here.shape[0], blocks[0].shape[1]
+    tokens, packed_rows = here.shape[0], blocks[0].shape[0]
+    features = 2 * blocks[0].shape[1]
     here_routes, here_shares = unpacked(here.at[:, features:], top, tokens)
     there_routes, there_shares = unpacked(there.at[:, features:], top, tokens)
     routes = jnp.concatenate([here_routes, there_routes], axis=1)
@@ -161,20 +171,26 @@
         weight = weight + hit * shares[k : k + 1, :]
     earlier = lax.broadcasted_iota(jnp.int32, (both, both), 0)
     later = lax.broadcasted_iota(jnp.int32, (both, both), 1)
-    before = (earlier < later) & ((earlier < tokens) == (later < tokens))
     rank = jnp.dot(
         named.astype(BF16),
-        jnp.where(before, 1.0, 0.0).astype(BF16),
+        jnp.where(earlier < later, 1.0, 0.0).astype(BF16),
         preferred_element_type=F32,
-    )
-    behind = lax.broadcasted_iota(jnp.int32, (count, both), 1) >= tokens
-    place = rank.astype(jnp.int32) + jnp.where(behind, stride, 0)
-    place = jnp.where(named > 0.0, place, -1)
-    slots = lax.broadcasted_iota(jnp.int32, (2 * stride, both), 0)
-    rows = jnp.concatenate([here[:, :features], there[:, :features]], axis=0)
+    ).astype(jnp.int32)
+    full, rest = whole_tiles(packed_rows)
+    places = [
+        jnp.where(rank < full, q * full + rank, 2 * full + q * rest + rank - full)
+        for q in range(2)
+    ]
+    place = jnp.concatenate([jnp.where(named > 0.0, p, -1) for p in places], axis=1)
+    weight = jnp.concatenate([weight, weight], axis=1)
+    slots = lax.broadcasted_iota(jnp.int32, (packed_rows, 2 * both), 0)
+    middle = features // 2
+    rows = jnp.concatenate(
+        [r[:, q * middle : (q + 1) * middle] for q in range(2) for r in (here, there)], axis=0
+    )
     for m, block in enumerate(blocks):
         hit = jnp.where(slots == place[m : m + 1, :], 1.0, 0.0)
-        table[2 * stride * m : 2 * stride * (m + 1), :] = hit * weight[m : m + 1, :]
+        table[packed_rows * m : packed_rows * (m + 1), :] = hit * weight[m : m + 1, :]
         block[...] = jnp.dot(hit.astype(BF16), rows, preferred_element_type=F32).astype(BF16)
     turned = table[...].T
     top_bits = turned.astype(BF16)
@@ -182,19 +198,24 @@
     low[...] = (turned - top_bits.astype(F32)).astype(BF16)
 
 
-def dispatch(mine, here, there, top, stride):
+def whole_tiles(packed_rows):
+    full = packed_rows // 2 // 8 * 8
+    return full, packed_rows // 2 - full
+
+
+def dispatch(mine, here, there, top, capacity):
     count, both = mine.shape[0], 2 * here.shape[0]
     width = here.shape[1] - 2 * both
-    rows = count * 2 * stride
+    size = 4 * capacity
     return pl.pallas_call(
-        functools.partial(dispatch_kernel, top, stride),
+        functools.partial(dispatch_kernel, top),
         in_specs=[whole()] * 3,
         out_specs=[whole()] * (2 + count),
-        out_shape=[jax.ShapeDtypeStruct((both, rows), BF16)] * 2
-        + [jax.ShapeDtypeStruct((2 * stride, width), BF16)] * count,
-        scratch_shapes=[pltpu.VMEM((rows, both), F32)],
+        out_shape=[jax.ShapeDtypeStruct((2 * both, count * size), BF16)] * 2
+        + [jax.ShapeDtypeStruct((size, width // 2), BF16)] * count,
+        scratch_shapes=[pltpu.VMEM((count * size, 2 * both), F32)],
         cost_estimate=pl.CostEstimate(
-            flops=2 * rows * both * width, bytes_accessed=3 * MIB // 2, transcendentals=0
+            flops=2 * count * size * both * width, bytes_accessed=3 * MIB // 2, transcendentals=0
         ),
         compiler_params=pltpu.CompilerParams(vmem_limit_bytes=16 * MIB),
     )(mine, here, there)
@@ -230,39 +251,64 @@
     blocks, weights = refs[:count], refs[count : count + 6]
     outs = refs[count + 6 : 2 * count + 6]
     rows, active = refs[2 * count + 6 :]
-    size, width = blocks[0].shape
-    for m, block in enumerate(blocks):
-        rows[m * size : (m + 1) * size, :] = block[...]
+    size, middle = blocks[0].shape
+    full, rest = whole_tiles(size)
+    given = [block[...].astype(F32) for block in blocks]
+    for q in range(2):
+        parts = [g[q * full : (q + 1) * full] for g in given]
+        if rest:
+            parts += [
+                joined(*[g[2 * full :] for g in given[m : m + 2]])[q] for m in range(0, count, 2)
+            ]
+        rows[:, q * middle : (q + 1) * middle] = jnp.concatenate(parts, axis=0).astype(BF16)
     for half in range(2):
         w_gate, w_up = weights[3 * half : 3 * half + 2]
         gate = lax.dot_general(rows[...], w_gate[...], NT, preferred_element_type=F32)
         upper = lax.dot_general(rows[...], w_up[...], NT, preferred_element_type=F32)
         active[half] = (gate * (1.0 / (1.0 + jnp.exp(-gate))) * upper).astype(BF16)
-    for at in range(0, width, 512):
-        columns = slice(at, at + 512)
-        result = jnp.dot(active[0], weights[2][:, columns], preferred_element_type=F32)
-        result = result + jnp.dot(active[1], weights[5][:, columns], preferred_element_type=F32)
+    step = 256
+    for at in range(0, middle, step):
+        made = []
+        for q in range(2):
+            columns = slice(q * middle + at, q * middle + at + step)
+            result = jnp.dot(active[0], weights[2][:, columns], preferred_element_type=F32)
+            made.append(
+                result + jnp.dot(active[1], weights[5][:, columns], preferred_element_type=F32)
+            )
         for m, out in enumerate(outs):
-            out[:, columns] = result[m * size : (m + 1) * size, :].astype(BF16)
+            parts = [r[m * full : (m + 1) * full] for r in made]
+            if rest:
+                first = count * full + m // 2 * 8
+                parts.append(joined(*[r[first : first + 8] for r in made])[m % 2])
+            out[:, at : at + step] = jnp.concatenate(parts, axis=0).astype(BF16)
+
+
+def joined(one, two):
+    upper = lax.broadcasted_iota(jnp.int32, one.shape, 0) < 4
+    return (
+        jnp.where(upper, one, pltpu.roll(two, 4, 0)),
+        jnp.where(upper, pltpu.roll(one, 4, 0), two),
+    )
 
 
 def run_expert(blocks, weights):
     count = len(blocks)
-    size, width = blocks[0].shape
-    units = weights[0].shape[0]
+    size, middle = blocks[0].shape
+    units, width = weights[0].shape
+    rows = count * size // 2
     return pl.pallas_call(
         functools.partial(expert_kernel, count),
         in_specs=[whole()] * (count + 6),
         out_specs=[whole()] * count,
-        out_shape=[jax.ShapeDtypeStruct((size, width), BF16)] * count,
+        out_shape=[jax.ShapeDtypeStruct((size, middle), BF16)] * count,
         scratch_shapes=[
-            pltpu.VMEM((count * size, width), BF16),
-            pltpu.VMEM((2, count * size, units), BF16),
+            pltpu.VMEM((rows, width), BF16),
+            pltpu.VMEM((2, rows, units), BF16),
         ],
         cost_estimate=pl.CostEstimate(
-            flops=12 * count * size * width * units,
+            flops=12 * rows * width * units,
             bytes_accessed=12 * units * width,
-            transcendentals=2 * count * size * units,
+            transcendentals=2 * rows * units,
         ),
         compiler_params=pltpu.CompilerParams(vmem_limit_bytes=20 * MIB),
     )(*blocks, *weights)
@@ -273,14 +319,15 @@
     rows = jnp.concatenate([block[...] for block in blocks], axis=0)
     total = jnp.dot(high[...], rows, preferred_element_type=F32)
     total = total + jnp.dot(low[...], rows, preferred_element_type=F32)
-    tokens = here.shape[0]
-    here[...] = total[:tokens]
-    there[...] = total[tokens:].astype(BF16)
+    tokens, middle = here.shape[0], rows.shape[1]
+    for q in range(2):
+        columns = slice(q * middle, (q + 1) * middle)
+        here[:, columns] = total[2 * q * tokens : (2 * q + 1) * tokens]
+        there[:, columns] = total[(2 * q + 1) * tokens : 2 * (q + 1) * tokens].astype(BF16)
 
 
 def combine(high, low, blocks):
-    both, rows = high.shape
-    width = blocks[0].shape[1]
+    both, width = high.shape[0] // 2, 2 * blocks[0].shape[1]
     return pl.pallas_call(
         combine_kernel,
         in_specs=[whole()] * (2 + len(blocks)),
@@ -290,7 +337,7 @@
             jax.ShapeDtypeStruct((both // 2, width), BF16),
         ],
         cost_estimate=pl.CostEstimate(
-            flops=4 * both * rows * width, bytes_accessed=3 * MIB // 2, transcendentals=0
+            flops=2 * high.size * width, bytes_accessed=3 * MIB // 2, transcendentals=0
         ),
         compiler_params=pltpu.CompilerParams(vmem_limit_bytes=16 * MIB),
     )(high, low, *blocks)
@@ -315,12 +362,12 @@
     experts = devices // 2
     near = experts // 2
     capacity = min(tokens, 2 * (((tokens * top + experts - 1) // experts + 3) // 2))
-    stride = -(-capacity // 8) * 8
 
     own = [jnp.swapaxes(w_gate, 1, 2)[0], jnp.swapaxes(w_up, 1, 2)[0], w_down[0]]
     other = [swapped(w, 1) for w in own]
-    chip = lax.axis_index("ep") // 2
-    mine = (chip ^ jnp.arange(near - 1, -1, -1, dtype=jnp.int32)).astype(F32)[:, None]
+    chip, core = lax.axis_index("ep") // 2, lax.axis_index("ep") % 2
+    masks = jnp.where(core == 0, *[jnp.array(order, jnp.int32) for order in orders(near)])
+    mine = (chip ^ masks).astype(F32)[:, None]
 
     stream, normed = attend(
         queries, cache, drafts, lengths, value_up, residual, norm_gain, routes.T, combine_weights.T
@@ -329,7 +376,7 @@
     across = swapped(normed, devices // 2)
     own = load(own, 44)
     across, own, other = lax.optimization_barrier((across, own, other))
-    high, low, *blocks = dispatch(mine, normed, across, top, stride)
+    high, low, *blocks = dispatch(mine, normed, across, top, capacity)
     blocks = exchanged(blocks)
     blocks[2], *late = lax.optimization_barrier((blocks[2], *other[1:]))
     blocks = exchanged(run_expert(blocks, [*own, other[0], *load(late, 38)]))

time: 66.7 us -> 63.3 us (0.949)
  starting transfers between devices: 28.5 us -> 26.3 us
  waiting for transfers between devices: 19.4 us -> 18.2 us
    ppermute x19 -> x5, starting transfers between devices: 28.5 us -> 7.16 us  [swapped(): return lax.ppermute(value, 'ep', pairs)]
    ppermute x0 -> x14, starting transfers between devices: none -> 19.2 us  [exchanged(): got[i] = lax.ppermute(blocks[i], 'ep', pairs)]
    ppermute x19 -> x5, waiting for transfers between devices: 19.4 us -> 10.1 us  [swapped(): return lax.ppermute(value, 'ep', pairs)]
    ppermute x0 -> x14, waiting for transfers between devices: none -> 8.09 us  [exchanged(): got[i] = lax.ppermute(blocks[i], 'ep', pairs)]
  transfers between devices with their start and end apart: 19 -> 19, of which waited for: 11 -> 10; matrix products, arithmetic and copies ran while one was open for 0% -> 0% of each run, Pallas kernels for 18% -> 19%
where the time goes in v7:
time: 63.3 us; the launch traced here: 63.2 us
  starting transfers between devices  26.3 us (42%)
  waiting for transfers between devices  18.2 us (29%)
  Pallas kernels  17.7 us (28%)
  other arithmetic  0.7 us (1%)
    ppermute x14, starting transfers between devices, exchanged(): got[i] = lax.ppermute(blocks[i], 'ep', pairs)  19.2 us
    ppermute x5, waiting for transfers between devices, swapped(): return lax.ppermute(value, 'ep', pairs)  10.1 us
    ppermute x14, waiting for transfers between devices, exchanged(): got[i] = lax.ppermute(blocks[i], 'ep', pairs)  8.09 us
    ppermute x5, starting transfers between devices, swapped(): return lax.ppermute(value, 'ep', pairs)  7.16 us
    pallas_call x2, Pallas kernels, load(): pl.pallas_call(load_kernel, in_specs=[pl.BlockSpec(memory_space=pl.ANY)]...  6.29 us
    pallas_call x1, Pallas kernels, attend(): pl.pallas_call(functools.partial(attend_kernel, heads), in_specs=[pl.Bloc...  5.45 us
    pallas_call x1, Pallas kernels, run_expert(): pl.pallas_call(functools.partial(expert_kernel, count), in_specs=[whole()...  4.89 us
  transfers between devices with their start and end apart: 19, of which 10 were waited for; matrix products, arithmetic and copies ran while one was open for 0% of the time, Pallas kernels for 19%

profile of v7, /device:TPU:0, one launch (start us, length us, event | category | flops | bytes accessed | tf_op | source)
XLA Modules:
  0.0 63.2 jit_solution(10806469151004713600)
XLA Ops:
  0.0 0.5 collective-permute-start.1
  0.5 0.4 collective-permute-start.3
  1.0 5.5 %shard_map.136 = (f32[32,2048]{1,0:T(8,128)}, bf16[32,2176]{1,0:T(8,128)(2,1)}) custom-call(s32[4]{0:T(128)} %refs_0_.1, bf16[4,8,576]{2,1,0:T(8,128)(2,1)} %refs_1_.1, bf16[4,128,576]{2,1,0:T(8,128)(2,1)} %bitcast.21, bf16[4,576,384]{2,1,0:T(8,128)(2,1)} %bitcast.20, bf16[16,512,128]{2,1,0:T(8,128)(2,1)} %refs_4_.1, bf16[32,2048]{1,0:T(8,128)(2,1)} %refs_5_.1, ...), custom_call_target="tpu_custom_call" | custom-call | flops 494927872 | bytes 6291456 | tf_op jit(solution)/shard_map/pallas_call | solution.py:135
  6.4 3.7 %collective-permute-start = (bf16[32,2176]{1,0:T(8,128)(2,1)}, bf16[32,2176]{1,0:T(8,128)(2,1)S(1)}, u32[]{:S(2)}, u32[]{:S(2)}) collective-permute-start(bf16[32,2176]{1,0:T(8,128)(2,1)} %get-tuple-element.48.here), channel_id=1, source_target_pairs={{0,16},{1,17},{2,18},{3,19},{4,20},{5,21},{6,22},{7,23},{8,24},{9,... | collective-permute-start | bytes 417800 | tf_op jit(solution)/shard_map/ppermute | solution.py:18
  10.3 3.6 %shard_map.137 = (bf16[704,2048]{1,0:T(8,128)(2,1)S(1)}, bf16[704,2048]{1,0:T(8,128)(2,1)S(1)}, bf16[704,2048]{1,0:T(8,128)(2,1)S(1)}) custom-call(bf16[704,2048]{1,0:T(8,128)(2,1)} %bitcast.15, bf16[704,2048]{1,0:T(8,128)(2,1)} %bitcast.17, bf16[704,2048]{1,0:T(8,128)(2,1)} %bitcast.19), custom_call_target="tpu_custom_call" | custom-call | bytes 17301504 | tf_op jit(solution)/shard_map/pallas_call | solution.py:237
  13.9 3.8 %collective-permute-done.there = bf16[32,2176]{1,0:T(8,128)(2,1)S(1)} collective-permute-done((bf16[32,2176]{1,0:T(8,128)(2,1)}, bf16[32,2176]{1,0:T(8,128)(2,1)S(1)}, u32[]{:S(2)}, u32[]{:S(2)}) %collective-permute-start) | collective-permute-done | bytes 139296 | tf_op jit(solution)/shard_map/ppermute | solution.py:18
  17.6 0.7 %shard_map.138 = (bf16[128,448]{1,0:T(8,128)(2,1)S(1)}, bf16[128,448]{1,0:T(8,128)(2,1)S(1)}, bf16[56,1024]{1,0:T(8,128)(2,1)S(1)}, bf16[56,1024]{1,0:T(8,128)(2...) custom-call(f32[8,1]{1,0:T(8,128)S(1)} %copy.15.mine, ...), custom_call_target="tpu_custom_call" | custom-call | flops 117440512 | bytes 1572864 | tf_op jit(solution)/shard_map/pallas_call | solution.py:210
  18.3 2.8 %collective-permute-start.4 = (bf16[56,1024]{1,0:T(8,128)(2,1)S(1)}, bf16[56,1024]{1,0:T(8,128)(2,1)S(1)}, u32[]{:S(2)}, u32[]{:S(2)}) collective-permute-start(bf16[56,1024]{1,0:T(8,128)(2,1)S(1)} %get-tuple-element.58), channel_id=1, source_target_pairs={{0,14},{1,15},{2,12},{3,13},{4,10},{5,11},{6,8},{7,9},{8,6},{9,7},... | collective-permute-start | bytes 344072 | tf_op jit(solution)/shard_map/ppermute | solution.py:31
  21.1 1.2 %collective-permute-start.6 = (bf16[56,1024]{1,0:T(8,128)(2,1)S(1)}, bf16[56,1024]{1,0:T(8,128)(2,1)S(1)}, u32[]{:S(2)}, u32[]{:S(2)}) collective-permute-start(bf16[56,1024]{1,0:T(8,128)(2,1)S(1)} %get-tuple-element.60), channel_id=1, source_target_pairs={{0,10},{1,5},{2,8},{3,7},{4,14},{5,1},{6,12},{7,3},{8,2},{9,13},{1... | collective-permute-start | bytes 344072 | tf_op jit(solution)/shard_map/ppermute | solution.py:31
  22.3 0.7 %collective-permute-start.5 = (bf16[56,1024]{1,0:T(8,128)(2,1)S(1)}, bf16[56,1024]{1,0:T(8,128)(2,1)S(1)}, u32[]{:S(2)}, u32[]{:S(2)}) collective-permute-start(bf16[56,1024]{1,0:T(8,128)(2,1)S(1)} %get-tuple-element.59), channel_id=1, source_target_pairs={{0,12},{1,3},{2,14},{3,1},{4,8},{5,7},{6,10},{7,5},{8,4},{9,11},{1... | collective-permute-start | bytes 344072 | tf_op jit(solution)/shard_map/ppermute | solution.py:31
  23.1 1.2 %collective-permute-start.7 = (bf16[56,1024]{1,0:T(8,128)(2,1)S(1)}, bf16[56,1024]{1,0:T(8,128)(2,1)S(1)}, u32[]{:S(2)}, u32[]{:S(2)}) collective-permute-start(bf16[56,1024]{1,0:T(8,128)(2,1)S(1)} %get-tuple-element.64), channel_id=1, source_target_pairs={{0,8},{1,7},{2,10},{3,5},{4,12},{5,3},{6,14},{7,1},{8,0},{9,15},{1... | collective-permute-start | bytes 344072 | tf_op jit(solution)/shard_map/ppermute | solution.py:31
  24.3 2.5 %collective-permute-start.8 = (bf16[56,1024]{1,0:T(8,128)(2,1)S(1)}, bf16[56,1024]{1,0:T(8,128)(2,1)S(1)}, u32[]{:S(2)}, u32[]{:S(2)}) collective-permute-start(bf16[56,1024]{1,0:T(8,128)(2,1)S(1)} %get-tuple-element.65), channel_id=1, source_target_pairs={{0,6},{1,9},{2,4},{3,11},{4,2},{5,13},{6,0},{7,15},{8,14},{9,1},{1... | collective-permute-start | bytes 344072 | tf_op jit(solution)/shard_map/ppermute | solution.py:31
  26.8 0.5 collective-permute-start.9
  27.6 0.6 collective-permute-start.10
  28.2 2.7 %shard_map.139 = (bf16[704,2048]{1,0:T(8,128)(2,1)S(1)}, bf16[704,2048]{1,0:T(8,128)(2,1)S(1)}) custom-call(bf16[704,2048]{1,0:T(8,128)(2,1)} %collective-permute-done.2.refs_0_, bf16[704,2048]{1,0:T(8,128)(2,1)} %collective-permute-done.3.refs_1_), custom_call_target="tpu_custom_call" | custom-call | bytes 11534336 | tf_op jit(solution)/shard_map/pallas_call | solution.py:237
  30.9 0.5 collective-permute-done.7.refs_3_
  31.6 2.0 %collective-permute-done.9.refs_5_ = bf16[56,1024]{1,0:T(8,128)(2,1)S(1)} collective-permute-done((bf16[56,1024]{1,0:T(8,128)(2,1)S(1)}, bf16[56,1024]{1,0:T(8,128)(2,1)S(1)}, u32[]{:S(2)}, u32[]{:S(2)}) %collective-permute-start.9) | collective-permute-done | bytes 114720 | tf_op jit(solution)/shard_map/ppermute | solution.py:31
  33.6 4.9 %shard_map.140 = (bf16[56,1024]{1,0:T(8,128)(2,1)S(1)}, bf16[56,1024]{1,0:T(8,128)(2,1)S(1)}, bf16[56,1024]{1,0:T(8,128)(2,1)S(1)}, bf16[56,1024]{1,0:T(8,128)(2...) custom-call(bf16[56,1024]{1,0:T(8,128)(2,1)S(1)} %collective-permute, ...), custom_call_target="tpu_custom_call" | custom-call | flops 3875536896 | bytes 17301504 | tf_op jit(solution)/shard_map/pallas_call | solution.py:299
  38.5 2.9 %collective-permute-start.11 = (bf16[56,1024]{1,0:T(8,128)(2,1)S(1)}, bf16[56,1024]{1,0:T(8,128)(2,1)S(1)}, u32[]{:S(2)}, u32[]{:S(2)}) collective-permute-start(bf16[56,1024]{1,0:T(8,128)(2,1)S(1)} %get-tuple-element.77), channel_id=1, source_target_pairs={{0,14},{1,15},{2,12},{3,13},{4,10},{5,11},{6,8},{7,9},{8,6},{9,7},... | collective-permute-start | bytes 344072 | tf_op jit(solution)/shard_map/ppermute | solution.py:31
  41.4 0.7 %collective-permute-start.12 = (bf16[56,1024]{1,0:T(8,128)(2,1)S(1)}, bf16[56,1024]{1,0:T(8,128)(2,1)S(1)}, u32[]{:S(2)}, u32[]{:S(2)}) collective-permute-start(bf16[56,1024]{1,0:T(8,128)(2,1)S(1)} %get-tuple-element.78), channel_id=1, source_target_pairs={{0,12},{1,3},{2,14},{3,1},{4,8},{5,7},{6,10},{7,5},{8,4},{9,11},{1... | collective-permute-start | bytes 344072 | tf_op jit(solution)/shard_map/ppermute | solution.py:31
  42.1 0.9 %collective-permute-start.13 = (bf16[56,1024]{1,0:T(8,128)(2,1)S(1)}, bf16[56,1024]{1,0:T(8,128)(2,1)S(1)}, u32[]{:S(2)}, u32[]{:S(2)}) collective-permute-start(bf16[56,1024]{1,0:T(8,128)(2,1)S(1)} %get-tuple-element.79), channel_id=1, source_target_pairs={{0,10},{1,5},{2,8},{3,7},{4,14},{5,1},{6,12},{7,3},{8,2},{9,13},{1... | collective-permute-start | bytes 344072 | tf_op jit(solution)/shard_map/ppermute | solution.py:31
  43.0 1.4 %collective-permute-start.14 = (bf16[56,1024]{1,0:T(8,128)(2,1)S(1)}, bf16[56,1024]{1,0:T(8,128)(2,1)S(1)}, u32[]{:S(2)}, u32[]{:S(2)}) collective-permute-start(bf16[56,1024]{1,0:T(8,128)(2,1)S(1)} %get-tuple-element.80), channel_id=1, source_target_pairs={{0,8},{1,7},{2,10},{3,5},{4,12},{5,3},{6,14},{7,1},{8,0},{9,15},{1... | collective-permute-start | bytes 344072 | tf_op jit(solution)/shard_map/ppermute | solution.py:31
  44.4 2.0 %collective-permute-start.15 = (bf16[56,1024]{1,0:T(8,128)(2,1)S(1)}, bf16[56,1024]{1,0:T(8,128)(2,1)S(1)}, u32[]{:S(2)}, u32[]{:S(2)}) collective-permute-start(bf16[56,1024]{1,0:T(8,128)(2,1)S(1)} %get-tuple-element.81), channel_id=1, source_target_pairs={{0,6},{1,9},{2,4},{3,11},{4,2},{5,13},{6,0},{7,15},{8,14},{9,1},{1... | collective-permute-start | bytes 344072 | tf_op jit(solution)/shard_map/ppermute | solution.py:31
  46.4 0.7 %collective-permute-start.16 = (bf16[56,1024]{1,0:T(8,128)(2,1)S(1)}, bf16[56,1024]{1,0:T(8,128)(2,1)S(1)}, u32[]{:S(2)}, u32[]{:S(2)}) collective-permute-start(bf16[56,1024]{1,0:T(8,128)(2,1)S(1)} %get-tuple-element.82), channel_id=1, source_target_pairs={{0,4},{1,11},{2,6},{3,9},{4,0},{5,15},{6,2},{7,13},{8,12},{9,3},{1... | collective-permute-start | bytes 344072 | tf_op jit(solution)/shard_map/ppermute | solution.py:31
  47.1 0.9 %collective-permute-done.12.refs_1_ = bf16[56,1024]{1,0:T(8,128)(2,1)S(1)} collective-permute-done((bf16[56,1024]{1,0:T(8,128)(2,1)S(1)}, bf16[56,1024]{1,0:T(8,128)(2,1)S(1)}, u32[]{:S(2)}, u32[]{:S(2)}) %collective-permute-start.12) | collective-permute-done | bytes 114720 | tf_op jit(solution)/shard_map/ppermute | solution.py:31
  47.9 1.0 %collective-permute-start.17 = (bf16[56,1024]{1,0:T(8,128)(2,1)S(1)}, bf16[56,1024]{1,0:T(8,128)(2,1)S(1)}, u32[]{:S(2)}, u32[]{:S(2)}) collective-permute-start(bf16[56,1024]{1,0:T(8,128)(2,1)S(1)} %get-tuple-element.83), channel_id=1, source_target_pairs={{0,2},{1,13},{2,0},{3,15},{4,6},{5,9},{6,4},{7,11},{8,10},{9,5},{1... | collective-permute-start | bytes 344072 | tf_op jit(solution)/shard_map/ppermute | solution.py:31
  49.2 2.8 %collective-permute-done.14.refs_3_ = bf16[56,1024]{1,0:T(8,128)(2,1)S(1)} collective-permute-done((bf16[56,1024]{1,0:T(8,128)(2,1)S(1)}, bf16[56,1024]{1,0:T(8,128)(2,1)S(1)}, u32[]{:S(2)}, u32[]{:S(2)}) %collective-permute-start.14) | collective-permute-done | bytes 114720 | tf_op jit(solution)/shard_map/ppermute | solution.py:31
  51.9 1.3 %collective-permute-done.16.refs_5_ = bf16[56,1024]{1,0:T(8,128)(2,1)S(1)} collective-permute-done((bf16[56,1024]{1,0:T(8,128)(2,1)S(1)}, bf16[56,1024]{1,0:T(8,128)(2,1)S(1)}, u32[]{:S(2)}, u32[]{:S(2)}) %collective-permute-start.16) | collective-permute-done | bytes 114720 | tf_op jit(solution)/shard_map/ppermute | solution.py:31
  53.2 0.4 shard_map.141
  53.7 2.5 %collective-permute-start.18 = (bf16[32,2048]{1,0:T(8,128)(2,1)S(1)}, bf16[32,2048]{1,0:T(8,128)(2,1)S(1)}, u32[]{:S(2)}, u32[]{:S(2)}) collective-permute-start(bf16[32,2048]{1,0:T(8,128)(2,1)S(1)} %get-tuple-element.86), channel_id=1, source_target_pairs={{0,16},{1,17},{2,18},{3,19},{4,20},{5,21},{6,22},{7,23},{8,24},{9,... | collective-permute-start | bytes 393224 | tf_op jit(solution)/shard_map/ppermute | solution.py:18
  56.1 6.3 %collective-permute-done.18 = bf16[32,2048]{1,0:T(8,128)(2,1)S(1)} collective-permute-done((bf16[32,2048]{1,0:T(8,128)(2,1)S(1)}, bf16[32,2048]{1,0:T(8,128)(2,1)S(1)}, u32[]{:S(2)}, u32[]{:S(2)}) %collective-permute-start.18) | collective-permute-done | bytes 131104 | tf_op jit(solution)/shard_map/ppermute | solution.py:18
  62.5 0.7 %add_convert_fusion = bf16[32,2048]{1,0:T(8,128)(2,1)} fusion(f32[32,2048]{1,0:T(8,128)S(1)} %copy-done.1, f32[32,2048]{1,0:T(8,128)S(1)} %get-tuple-element.85, bf16[32,2048]{1,0:T(8,128)(2,1)S(1)} %collective-permute-done.18), kind=kLoop, calls=%fused_computation | loop fusion | flops 262144 | bytes 786432 | tf_op jit(solution)/shard_map/convert_element_type | solution.py:384
  (23 shorter events, 0.9 us)
Async XLA Ops:
  0.0 10.2 %copy-start.2 = (s32[8]{0:T(128)S(1)}, s32[8]{0:T(128)}, u32[]{:S(2)}) copy-start(s32[8]{0:T(128)} %constant.34.clone) | copy-start | bytes 100
  0.0 10.2 %copy-start.3 = (s32[8]{0:T(128)S(1)}, s32[8]{0:T(128)}, u32[]{:S(2)}) copy-start(s32[8]{0:T(128)} %constant.33.clone) | copy-start | bytes 100
  0.0 17.6 %collective-permute-start.1 = (bf16[704,2048]{1,0:T(8,128)(2,1)}, bf16[704,2048]{1,0:T(8,128)(2,1)S(1)}, u32[]{:S(2)}, u32[]{:S(2)}) collective-permute-start(bf16[704,2048]{1,0:T(8,128)(2,1)} %bitcast.14), channel_id=1, source_target_pairs={{0,1},{1,0},{2,3},{3,2},{4,5},{5,4},{6,7},{7,6},{8,9},{9,8},{10,11... | collective-permute-start | bytes 8650760 | tf_op jit(solution)/shard_map/ppermute | solution.py:18
  0.5 17.2 %collective-permute-start.2 = (bf16[704,2048]{1,0:T(8,128)(2,1)}, bf16[704,2048]{1,0:T(8,128)(2,1)}, u32[]{:S(2)}, u32[]{:S(2)}) collective-permute-start(bf16[704,2048]{1,0:T(8,128)(2,1)} %bitcast.16), channel_id=1, source_target_pairs={{0,1},{1,0},{2,3},{3,2},{4,5},{5,4},{6,7},{7,6},{8,9},{9,8},{10,11... | collective-permute-start | bytes 8650760 | tf_op jit(solution)/shard_map/ppermute | solution.py:18
  0.5 17.1 %collective-permute-start.3 = (bf16[704,2048]{1,0:T(8,128)(2,1)}, bf16[704,2048]{1,0:T(8,128)(2,1)}, u32[]{:S(2)}, u32[]{:S(2)}) collective-permute-start(bf16[704,2048]{1,0:T(8,128)(2,1)} %bitcast.18), channel_id=1, source_target_pairs={{0,1},{1,0},{2,3},{3,2},{4,5},{5,4},{6,7},{7,6},{8,9},{9,8},{10,11... | collective-permute-start | bytes 8650760 | tf_op jit(solution)/shard_map/ppermute | solution.py:18
  6.4 11.2 %collective-permute-start = (bf16[32,2176]{1,0:T(8,128)(2,1)}, bf16[32,2176]{1,0:T(8,128)(2,1)S(1)}, u32[]{:S(2)}, u32[]{:S(2)}) collective-permute-start(bf16[32,2176]{1,0:T(8,128)(2,1)} %get-tuple-element.48.here), channel_id=1, source_target_pairs={{0,16},{1,17},{2,18},{3,19},{4,20},{5,21},{6,22},{7,23},{8,24},{9,... | collective-permute-start | bytes 417800 | tf_op jit(solution)/shard_map/ppermute | solution.py:18
  10.3 7.4 %copy-start = (bf16[32,2176]{1,0:T(8,128)(2,1)S(1)}, bf16[32,2176]{1,0:T(8,128)(2,1)}, u32[]{:S(2)}) copy-start(bf16[32,2176]{1,0:T(8,128)(2,1)} %get-tuple-element.48.here) | copy-start | bytes 417796
  18.3 8.4 %collective-permute-start.4 = (bf16[56,1024]{1,0:T(8,128)(2,1)S(1)}, bf16[56,1024]{1,0:T(8,128)(2,1)S(1)}, u32[]{:S(2)}, u32[]{:S(2)}) collective-permute-start(bf16[56,1024]{1,0:T(8,128)(2,1)S(1)} %get-tuple-element.58), channel_id=1, source_target_pairs={{0,14},{1,15},{2,12},{3,13},{4,10},{5,11},{6,8},{7,9},{8,6},{9,7},... | collective-permute-start | bytes 344072 | tf_op jit(solution)/shard_map/ppermute | solution.py:31
  21.1 6.4 %collective-permute-start.6 = (bf16[56,1024]{1,0:T(8,128)(2,1)S(1)}, bf16[56,1024]{1,0:T(8,128)(2,1)S(1)}, u32[]{:S(2)}, u32[]{:S(2)}) collective-permute-start(bf16[56,1024]{1,0:T(8,128)(2,1)S(1)} %get-tuple-element.60), channel_id=1, source_target_pairs={{0,10},{1,5},{2,8},{3,7},{4,14},{5,1},{6,12},{7,3},{8,2},{9,13},{1... | collective-permute-start | bytes 344072 | tf_op jit(solution)/shard_map/ppermute | solution.py:31
  22.3 8.5 %collective-permute-start.5 = (bf16[56,1024]{1,0:T(8,128)(2,1)S(1)}, bf16[56,1024]{1,0:T(8,128)(2,1)S(1)}, u32[]{:S(2)}, u32[]{:S(2)}) collective-permute-start(bf16[56,1024]{1,0:T(8,128)(2,1)S(1)} %get-tuple-element.59), channel_id=1, source_target_pairs={{0,12},{1,3},{2,14},{3,1},{4,8},{5,7},{6,10},{7,5},{8,4},{9,11},{1... | collective-permute-start | bytes 344072 | tf_op jit(solution)/shard_map/ppermute | solution.py:31
  23.1 8.4 %collective-permute-start.7 = (bf16[56,1024]{1,0:T(8,128)(2,1)S(1)}, bf16[56,1024]{1,0:T(8,128)(2,1)S(1)}, u32[]{:S(2)}, u32[]{:S(2)}) collective-permute-start(bf16[56,1024]{1,0:T(8,128)(2,1)S(1)} %get-tuple-element.64), channel_id=1, source_target_pairs={{0,8},{1,7},{2,10},{3,5},{4,12},{5,3},{6,14},{7,1},{8,0},{9,15},{1... | collective-permute-start | bytes 344072 | tf_op jit(solution)/shard_map/ppermute | solution.py:31
  24.3 7.3 %collective-permute-start.8 = (bf16[56,1024]{1,0:T(8,128)(2,1)S(1)}, bf16[56,1024]{1,0:T(8,128)(2,1)S(1)}, u32[]{:S(2)}, u32[]{:S(2)}) collective-permute-start(bf16[56,1024]{1,0:T(8,128)(2,1)S(1)} %get-tuple-element.65), channel_id=1, source_target_pairs={{0,6},{1,9},{2,4},{3,11},{4,2},{5,13},{6,0},{7,15},{8,14},{9,1},{1... | collective-permute-start | bytes 344072 | tf_op jit(solution)/shard_map/ppermute | solution.py:31
  26.8 6.8 %collective-permute-start.9 = (bf16[56,1024]{1,0:T(8,128)(2,1)S(1)}, bf16[56,1024]{1,0:T(8,128)(2,1)S(1)}, u32[]{:S(2)}, u32[]{:S(2)}) collective-permute-start(bf16[56,1024]{1,0:T(8,128)(2,1)S(1)} %get-tuple-element.66), channel_id=1, source_target_pairs={{0,4},{1,11},{2,6},{3,9},{4,0},{5,15},{6,2},{7,13},{8,12},{9,3},{1... | collective-permute-start | bytes 344072 | tf_op jit(solution)/shard_map/ppermute | solution.py:31
  27.6 6.0 %collective-permute-start.10 = (bf16[56,1024]{1,0:T(8,128)(2,1)S(1)}, bf16[56,1024]{1,0:T(8,128)(2,1)S(1)}, u32[]{:S(2)}, u32[]{:S(2)}) collective-permute-start(bf16[56,1024]{1,0:T(8,128)(2,1)S(1)} %get-tuple-element.67), channel_id=1, source_target_pairs={{0,2},{1,13},{2,0},{3,15},{4,6},{5,9},{6,4},{7,11},{8,10},{9,5},{1... | collective-permute-start | bytes 344072 | tf_op jit(solution)/shard_map/ppermute | solution.py:31
  33.6 28.9 %copy-start.1 = (f32[32,2048]{1,0:T(8,128)S(1)}, f32[32,2048]{1,0:T(8,128)}, u32[]{:S(2)}) copy-start(f32[32,2048]{1,0:T(8,128)} %get-tuple-element.46) | copy-start | bytes 786436
  38.5 8.0 %collective-permute-start.11 = (bf16[56,1024]{1,0:T(8,128)(2,1)S(1)}, bf16[56,1024]{1,0:T(8,128)(2,1)S(1)}, u32[]{:S(2)}, u32[]{:S(2)}) collective-permute-start(bf16[56,1024]{1,0:T(8,128)(2,1)S(1)} %get-tuple-element.77), channel_id=1, source_target_pairs={{0,14},{1,15},{2,12},{3,13},{4,10},{5,11},{6,8},{7,9},{8,6},{9,7},... | collective-permute-start | bytes 344072 | tf_op jit(solution)/shard_map/ppermute | solution.py:31
  41.4 6.5 %collective-permute-start.12 = (bf16[56,1024]{1,0:T(8,128)(2,1)S(1)}, bf16[56,1024]{1,0:T(8,128)(2,1)S(1)}, u32[]{:S(2)}, u32[]{:S(2)}) collective-permute-start(bf16[56,1024]{1,0:T(8,128)(2,1)S(1)} %get-tuple-element.78), channel_id=1, source_target_pairs={{0,12},{1,3},{2,14},{3,1},{4,8},{5,7},{6,10},{7,5},{8,4},{9,11},{1... | collective-permute-start | bytes 344072 | tf_op jit(solution)/shard_map/ppermute | solution.py:31
  42.1 7.1 %collective-permute-start.13 = (bf16[56,1024]{1,0:T(8,128)(2,1)S(1)}, bf16[56,1024]{1,0:T(8,128)(2,1)S(1)}, u32[]{:S(2)}, u32[]{:S(2)}) collective-permute-start(bf16[56,1024]{1,0:T(8,128)(2,1)S(1)} %get-tuple-element.79), channel_id=1, source_target_pairs={{0,10},{1,5},{2,8},{3,7},{4,14},{5,1},{6,12},{7,3},{8,2},{9,13},{1... | collective-permute-start | bytes 344072 | tf_op jit(solution)/shard_map/ppermute | solution.py:31
  43.0 8.9 %collective-permute-start.14 = (bf16[56,1024]{1,0:T(8,128)(2,1)S(1)}, bf16[56,1024]{1,0:T(8,128)(2,1)S(1)}, u32[]{:S(2)}, u32[]{:S(2)}) collective-permute-start(bf16[56,1024]{1,0:T(8,128)(2,1)S(1)} %get-tuple-element.80), channel_id=1, source_target_pairs={{0,8},{1,7},{2,10},{3,5},{4,12},{5,3},{6,14},{7,1},{8,0},{9,15},{1... | collective-permute-start | bytes 344072 | tf_op jit(solution)/shard_map/ppermute | solution.py:31
  44.4 7.6 %collective-permute-start.15 = (bf16[56,1024]{1,0:T(8,128)(2,1)S(1)}, bf16[56,1024]{1,0:T(8,128)(2,1)S(1)}, u32[]{:S(2)}, u32[]{:S(2)}) collective-permute-start(bf16[56,1024]{1,0:T(8,128)(2,1)S(1)} %get-tuple-element.81), channel_id=1, source_target_pairs={{0,6},{1,9},{2,4},{3,11},{4,2},{5,13},{6,0},{7,15},{8,14},{9,1},{1... | collective-permute-start | bytes 344072 | tf_op jit(solution)/shard_map/ppermute | solution.py:31
  46.4 6.8 %collective-permute-start.16 = (bf16[56,1024]{1,0:T(8,128)(2,1)S(1)}, bf16[56,1024]{1,0:T(8,128)(2,1)S(1)}, u32[]{:S(2)}, u32[]{:S(2)}) collective-permute-start(bf16[56,1024]{1,0:T(8,128)(2,1)S(1)} %get-tuple-element.82), channel_id=1, source_target_pairs={{0,4},{1,11},{2,6},{3,9},{4,0},{5,15},{6,2},{7,13},{8,12},{9,3},{1... | collective-permute-start | bytes 344072 | tf_op jit(solution)/shard_map/ppermute | solution.py:31
  47.9 5.3 %collective-permute-start.17 = (bf16[56,1024]{1,0:T(8,128)(2,1)S(1)}, bf16[56,1024]{1,0:T(8,128)(2,1)S(1)}, u32[]{:S(2)}, u32[]{:S(2)}) collective-permute-start(bf16[56,1024]{1,0:T(8,128)(2,1)S(1)} %get-tuple-element.83), channel_id=1, source_target_pairs={{0,2},{1,13},{2,0},{3,15},{4,6},{5,9},{6,4},{7,11},{8,10},{9,5},{1... | collective-permute-start | bytes 344072 | tf_op jit(solution)/shard_map/ppermute | solution.py:31
  53.7 8.8 %collective-permute-start.18 = (bf16[32,2048]{1,0:T(8,128)(2,1)S(1)}, bf16[32,2048]{1,0:T(8,128)(2,1)S(1)}, u32[]{:S(2)}, u32[]{:S(2)}) collective-permute-start(bf16[32,2048]{1,0:T(8,128)(2,1)S(1)} %get-tuple-element.86), channel_id=1, source_target_pairs={{0,16},{1,17},{2,18},{3,19},{4,20},{5,21},{6,22},{7,23},{8,24},{9,... | collective-permute-start | bytes 393224 | tf_op jit(solution)/shard_map/ppermute | solution.py:18

commit v8 on v7

--- a/solution.py
+++ b/solution.py
@@ -19,8 +19,12 @@
 
 
 def orders(near):
-    first = list(range(near - 1, -1, -1))
-    return first, first[:1] + [(near - 1) ^ m for m in first[1:-1]] + [0]
+    last = near - 1
+    first = list(range(last, 0, -1))
+    for i in (0, near // 2 - 1):
+        first[i], first[i + 1] = first[i + 1], first[i]
+    second = [m if m == last else last ^ m for m in first]
+    return [*first, 0], [*second, 0]
 
 
 def exchanged(blocks):
@@ -65,20 +69,28 @@
             [drafts[r].astype(F32), jnp.zeros((columns - slots - draft, width), F32)], axis=0
         )
         cache[r, :, slots:] = d.T.astype(BF16)
-    for r in range(reqs):
-        copies[2, r].wait()
-        copies[3, r].wait()
-        score = jnp.dot(queries[r], cache[r], preferred_element_type=F32) * scale
-        score = jnp.where((place < lengths[r]) | causal, score, -1e30)
-        e = jnp.exp(score - jnp.max(score, axis=-1, keepdims=True))
-        p = (e * (1.0 / jnp.sum(e, axis=-1, keepdims=True))).astype(BF16)
-        out = lax.dot_general(p, cache[r, :latent, :], NT, preferred_element_type=F32)
-        for g in range(latent // lanes):
-            mixed[g, r * rows : (r + 1) * rows, :] = out[:, g * lanes : (g + 1) * lanes]
+    for start in range(0, reqs, 2):
+        some = range(start, min(reqs, start + 2))
+        scores, probs = {}, {}
+        for r in some:
+            copies[2, r].wait()
+            copies[3, r].wait()
+        for r in some:
+            score = jnp.dot(queries[r], cache[r], preferred_element_type=F32) * scale
+            scores[r] = jnp.where((place < lengths[r]) | causal, score, -1e30)
+        for r in some:
+            e = jnp.exp(scores[r] - jnp.max(scores[r], axis=-1, keepdims=True))
+            probs[r] = (e * (1.0 / jnp.sum(e, axis=-1, keepdims=True))).astype(BF16)
+        for r in some:
+            out = lax.dot_general(
+                probs[r], cache[r, :latent, :], NT, preferred_element_type=F32
+            )
+            for g in range(latent // lanes):
+                mixed[g, r * rows : (r + 1) * rows, :] = out[:, g * lanes : (g + 1) * lanes]
     for i in range(4, 9):
         copies[i, None].wait()
     tokens, features = stream.shape
-    square = jnp.zeros((tokens, 1), F32)
+    square = jnp.zeros((tokens, vdim), F32)
     for head in range(heads):
         part = jnp.concatenate(
             [mixed[g, pl.ds(head, tokens, stride=heads), :] for g in range(latent // lanes)],
@@ -89,8 +101,9 @@
             part, up[head], preferred_element_type=F32
         )
         stream[:, at] = value
-        square = square + jnp.sum(value * value, axis=-1, keepdims=True)
-    factor = lax.rsqrt(square / features + 1e-06)
+        square = square + value * value
+    mean = jnp.sum(square, axis=-1, keepdims=True) / features
+    factor = lax.rsqrt(mean + 1e-06)
     normed[:, :features] = (stream[...] * factor * gain[...]).astype(BF16)
     normed[:, features:] = packed(routes[...], shares[...], tokens)
 
@@ -314,7 +327,7 @@
     )(*blocks, *weights)
 
 
-def combine_kernel(high, low, *refs):
+def combine_kernel(high, low, stream, *refs):
     blocks, (here, there) = refs[:-2], refs[-2:]
     rows = jnp.concatenate([block[...] for block in blocks], axis=0)
     total = jnp.dot(high[...], rows, preferred_element_type=F32)
@@ -322,15 +335,16 @@
     tokens, middle = here.shape[0], rows.shape[1]
     for q in range(2):
         columns = slice(q * middle, (q + 1) * middle)
-        here[:, columns] = total[2 * q * tokens : (2 * q + 1) * tokens]
+        mine = total[2 * q * tokens : (2 * q + 1) * tokens]
+        here[:, columns] = stream[:, columns] + mine
         there[:, columns] = total[(2 * q + 1) * tokens : 2 * (q + 1) * tokens].astype(BF16)
 
 
-def combine(high, low, blocks):
+def combine(high, low, stream, blocks):
     both, width = high.shape[0] // 2, 2 * blocks[0].shape[1]
     return pl.pallas_call(
         combine_kernel,
-        in_specs=[whole()] * (2 + len(blocks)),
+        in_specs=[whole()] * (3 + len(blocks)),
         out_specs=[whole()] * 2,
         out_shape=[
             jax.ShapeDtypeStruct((both // 2, width), F32),
@@ -340,7 +354,7 @@
             flops=2 * high.size * width, bytes_accessed=3 * MIB // 2, transcendentals=0
         ),
         compiler_params=pltpu.CompilerParams(vmem_limit_bytes=16 * MIB),
-    )(high, low, *blocks)
+    )(high, low, stream, *blocks)
 
 
 def local(
@@ -380,8 +394,8 @@
     blocks = exchanged(blocks)
     blocks[2], *late = lax.optimization_barrier((blocks[2], *other[1:]))
     blocks = exchanged(run_expert(blocks, [*own, other[0], *load(late, 38)]))
-    here, there = combine(high, low, blocks)
-    return (stream + (here + swapped(there, devices // 2).astype(F32))).astype(BF16)
+    here, there = combine(high, low, stream, blocks)
+    return (here + swapped(there, devices // 2).astype(F32)).astype(BF16)
 
 
 def solution(mesh):

time: 63.3 us -> 61.9 us (0.978)
  waiting for transfers between devices: 18.2 us -> 17.2 us
  Pallas kernels: 17.7 us -> 17 us
    ppermute x5, waiting for transfers between devices: 10.1 us -> 8.79 us  [swapped(): return lax.ppermute(value, 'ep', pairs)]
    pallas_call x1, Pallas kernels: 5.45 us -> 4.68 us  [attend(): pl.pallas_call(functools.partial(attend_kernel, heads), in_specs=[pl.Bloc...]
  transfers between devices with their start and end apart: 19 -> 19, of which waited for: 10 -> 9; matrix products, arithmetic and copies ran while one was open for 0% -> 0% of each run, Pallas kernels for 19% -> 18%
where the time goes in v8:
time: 61.9 us; the launch traced here: 61.7 us
  starting transfers between devices  26.7 us (43%)
  waiting for transfers between devices  17.2 us (28%)
  Pallas kernels  17 us (27%)
  other arithmetic  0.69 us (1%)
    ppermute x14, starting transfers between devices, exchanged(): got[i] = lax.ppermute(blocks[i], 'ep', pairs)  19 us
    ppermute x5, waiting for transfers between devices, swapped(): return lax.ppermute(value, 'ep', pairs)  8.79 us
    ppermute x14, waiting for transfers between devices, exchanged(): got[i] = lax.ppermute(blocks[i], 'ep', pairs)  8.41 us
    ppermute x5, starting transfers between devices, swapped(): return lax.ppermute(value, 'ep', pairs)  7.67 us
    pallas_call x2, Pallas kernels, load(): pl.pallas_call(load_kernel, in_specs=[pl.BlockSpec(memory_space=pl.ANY)]...  6.29 us
    pallas_call x1, Pallas kernels, run_expert(): pl.pallas_call(functools.partial(expert_kernel, count), in_specs=[whole()...  4.87 us
    pallas_call x1, Pallas kernels, attend(): pl.pallas_call(functools.partial(attend_kernel, heads), in_specs=[pl.Bloc...  4.68 us
  transfers between devices with their start and end apart: 19, of which 9 were waited for; matrix products, arithmetic and copies ran while one was open for 0% of the time, Pallas kernels for 18%

profile of v8, /device:TPU:0, one launch (start us, length us, event | category | flops | bytes accessed | tf_op | source)
XLA Modules:
  0.0 61.7 jit_solution(5821277801680082837)
XLA Ops:
  0.0 0.5 collective-permute-start.1
  1.0 4.7 %shard_map.136 = (f32[32,2048]{1,0:T(8,128)}, bf16[32,2176]{1,0:T(8,128)(2,1)}) custom-call(s32[4]{0:T(128)} %refs_0_.1, bf16[4,8,576]{2,1,0:T(8,128)(2,1)} %refs_1_.1, bf16[4,128,576]{2,1,0:T(8,128)(2,1)} %bitcast.21, bf16[4,576,384]{2,1,0:T(8,128)(2,1)} %bitcast.20, bf16[16,512,128]{2,1,0:T(8,128)(2,1)} %refs_4_.1, bf16[32,2048]{1,0:T(8,128)(2,1)} %refs_5_.1, ...), custom_call_target="tpu_custom_call" | custom-call | flops 494927872 | bytes 6291456 | tf_op jit(solution)/shard_map/pallas_call | solution.py:148
  5.7 3.7 %collective-permute-start = (bf16[32,2176]{1,0:T(8,128)(2,1)}, bf16[32,2176]{1,0:T(8,128)(2,1)S(1)}, u32[]{:S(2)}, u32[]{:S(2)}) collective-permute-start(bf16[32,2176]{1,0:T(8,128)(2,1)} %get-tuple-element.47.here), channel_id=1, source_target_pairs={{0,16},{1,17},{2,18},{3,19},{4,20},{5,21},{6,22},{7,23},{8,24},{9,... | collective-permute-start | bytes 417800 | tf_op jit(solution)/shard_map/ppermute | solution.py:18
  9.5 3.6 %shard_map.137 = (bf16[704,2048]{1,0:T(8,128)(2,1)S(1)}, bf16[704,2048]{1,0:T(8,128)(2,1)S(1)}, bf16[704,2048]{1,0:T(8,128)(2,1)S(1)}) custom-call(bf16[704,2048]{1,0:T(8,128)(2,1)} %bitcast.15, bf16[704,2048]{1,0:T(8,128)(2,1)} %bitcast.17, bf16[704,2048]{1,0:T(8,128)(2,1)} %bitcast.19), custom_call_target="tpu_custom_call" | custom-call | bytes 17301504 | tf_op jit(solution)/shard_map/pallas_call | solution.py:250
  13.1 3.8 %collective-permute-done.there = bf16[32,2176]{1,0:T(8,128)(2,1)S(1)} collective-permute-done((bf16[32,2176]{1,0:T(8,128)(2,1)}, bf16[32,2176]{1,0:T(8,128)(2,1)S(1)}, u32[]{:S(2)}, u32[]{:S(2)}) %collective-permute-start) | collective-permute-done | bytes 139296 | tf_op jit(solution)/shard_map/ppermute | solution.py:18
  16.9 0.7 %shard_map.138 = (bf16[128,448]{1,0:T(8,128)(2,1)S(1)}, bf16[128,448]{1,0:T(8,128)(2,1)S(1)}, bf16[56,1024]{1,0:T(8,128)(2,1)S(1)}, bf16[56,1024]{1,0:T(8,128)(2...) custom-call(f32[8,1]{1,0:T(8,128)S(1)} %copy.15.mine, ...), custom_call_target="tpu_custom_call" | custom-call | flops 117440512 | bytes 1572864 | tf_op jit(solution)/shard_map/pallas_call | solution.py:223
  17.6 1.9 %collective-permute-start.4 = (bf16[56,1024]{1,0:T(8,128)(2,1)S(1)}, bf16[56,1024]{1,0:T(8,128)(2,1)S(1)}, u32[]{:S(2)}, u32[]{:S(2)}) collective-permute-start(bf16[56,1024]{1,0:T(8,128)(2,1)S(1)} %get-tuple-element.58), channel_id=1, source_target_pairs={{0,12},{1,3},{2,14},{3,1},{4,8},{5,7},{6,10},{7,5},{8,4},{9,11},{1... | collective-permute-start | bytes 344072 | tf_op jit(solution)/shard_map/ppermute | solution.py:35
  19.4 2.2 %collective-permute-start.6 = (bf16[56,1024]{1,0:T(8,128)(2,1)S(1)}, bf16[56,1024]{1,0:T(8,128)(2,1)S(1)}, u32[]{:S(2)}, u32[]{:S(2)}) collective-permute-start(bf16[56,1024]{1,0:T(8,128)(2,1)S(1)} %get-tuple-element.60), channel_id=1, source_target_pairs={{0,10},{1,5},{2,8},{3,7},{4,14},{5,1},{6,12},{7,3},{8,2},{9,13},{1... | collective-permute-start | bytes 344072 | tf_op jit(solution)/shard_map/ppermute | solution.py:35
  21.6 0.7 %collective-permute-start.5 = (bf16[56,1024]{1,0:T(8,128)(2,1)S(1)}, bf16[56,1024]{1,0:T(8,128)(2,1)S(1)}, u32[]{:S(2)}, u32[]{:S(2)}) collective-permute-start(bf16[56,1024]{1,0:T(8,128)(2,1)S(1)} %get-tuple-element.59), channel_id=1, source_target_pairs={{0,14},{1,15},{2,12},{3,13},{4,10},{5,11},{6,8},{7,9},{8,6},{9,7},... | collective-permute-start | bytes 344072 | tf_op jit(solution)/shard_map/ppermute | solution.py:35
  22.3 2.4 %collective-permute-start.7 = (bf16[56,1024]{1,0:T(8,128)(2,1)S(1)}, bf16[56,1024]{1,0:T(8,128)(2,1)S(1)}, u32[]{:S(2)}, u32[]{:S(2)}) collective-permute-start(bf16[56,1024]{1,0:T(8,128)(2,1)S(1)} %get-tuple-element.64), channel_id=1, source_target_pairs={{0,6},{1,9},{2,4},{3,11},{4,2},{5,13},{6,0},{7,15},{8,14},{9,1},{1... | collective-permute-start | bytes 344072 | tf_op jit(solution)/shard_map/ppermute | solution.py:35
  24.7 1.3 %collective-permute-start.8 = (bf16[56,1024]{1,0:T(8,128)(2,1)S(1)}, bf16[56,1024]{1,0:T(8,128)(2,1)S(1)}, u32[]{:S(2)}, u32[]{:S(2)}) collective-permute-start(bf16[56,1024]{1,0:T(8,128)(2,1)S(1)} %get-tuple-element.65), channel_id=1, source_target_pairs={{0,8},{1,7},{2,10},{3,5},{4,12},{5,3},{6,14},{7,1},{8,0},{9,15},{1... | collective-permute-start | bytes 344072 | tf_op jit(solution)/shard_map/ppermute | solution.py:35
  26.0 0.5 collective-permute-start.9
  26.5 1.4 %collective-permute-done.6.refs_2_ = bf16[56,1024]{1,0:T(8,128)(2,1)S(1)} collective-permute-done((bf16[56,1024]{1,0:T(8,128)(2,1)S(1)}, bf16[56,1024]{1,0:T(8,128)(2,1)S(1)}, u32[]{:S(2)}, u32[]{:S(2)}) %collective-permute-start.6) | collective-permute-done | bytes 114720 | tf_op jit(solution)/shard_map/ppermute | solution.py:35
  28.3 2.7 %shard_map.139 = (bf16[704,2048]{1,0:T(8,128)(2,1)S(1)}, bf16[704,2048]{1,0:T(8,128)(2,1)S(1)}) custom-call(bf16[704,2048]{1,0:T(8,128)(2,1)} %collective-permute-done.2.refs_0_, bf16[704,2048]{1,0:T(8,128)(2,1)} %collective-permute-done.3.refs_1_), custom_call_target="tpu_custom_call" | custom-call | bytes 11534336 | tf_op jit(solution)/shard_map/pallas_call | solution.py:250
  31.1 1.1 %collective-permute-done.7.refs_3_ = bf16[56,1024]{1,0:T(8,128)(2,1)S(1)} collective-permute-done((bf16[56,1024]{1,0:T(8,128)(2,1)S(1)}, bf16[56,1024]{1,0:T(8,128)(2,1)S(1)}, u32[]{:S(2)}, u32[]{:S(2)}) %collective-permute-start.7) | collective-permute-done | bytes 114720 | tf_op jit(solution)/shard_map/ppermute | solution.py:35
  32.2 1.0 %collective-permute-done.9.refs_5_ = bf16[56,1024]{1,0:T(8,128)(2,1)S(1)} collective-permute-done((bf16[56,1024]{1,0:T(8,128)(2,1)S(1)}, bf16[56,1024]{1,0:T(8,128)(2,1)S(1)}, u32[]{:S(2)}, u32[]{:S(2)}) %collective-permute-start.9) | collective-permute-done | bytes 114720 | tf_op jit(solution)/shard_map/ppermute | solution.py:35
  33.2 4.9 %shard_map.140 = (bf16[56,1024]{1,0:T(8,128)(2,1)S(1)}, bf16[56,1024]{1,0:T(8,128)(2,1)S(1)}, bf16[56,1024]{1,0:T(8,128)(2,1)S(1)}, bf16[56,1024]{1,0:T(8,128)(2...) custom-call(bf16[56,1024]{1,0:T(8,128)(2,1)S(1)} %collective-permute, ...), custom_call_target="tpu_custom_call" | custom-call | flops 3875536896 | bytes 17301504 | tf_op jit(solution)/shard_map/pallas_call | solution.py:312
  38.1 1.6 %collective-permute-start.11 = (bf16[56,1024]{1,0:T(8,128)(2,1)S(1)}, bf16[56,1024]{1,0:T(8,128)(2,1)S(1)}, u32[]{:S(2)}, u32[]{:S(2)}) collective-permute-start(bf16[56,1024]{1,0:T(8,128)(2,1)S(1)} %get-tuple-element.77), channel_id=1, source_target_pairs={{0,12},{1,3},{2,14},{3,1},{4,8},{5,7},{6,10},{7,5},{8,4},{9,11},{1... | collective-permute-start | bytes 344072 | tf_op jit(solution)/shard_map/ppermute | solution.py:35
  39.7 1.5 %collective-permute-start.12 = (bf16[56,1024]{1,0:T(8,128)(2,1)S(1)}, bf16[56,1024]{1,0:T(8,128)(2,1)S(1)}, u32[]{:S(2)}, u32[]{:S(2)}) collective-permute-start(bf16[56,1024]{1,0:T(8,128)(2,1)S(1)} %get-tuple-element.78), channel_id=1, source_target_pairs={{0,14},{1,15},{2,12},{3,13},{4,10},{5,11},{6,8},{7,9},{8,6},{9,7},... | collective-permute-start | bytes 344072 | tf_op jit(solution)/shard_map/ppermute | solution.py:35
  41.1 1.6 %collective-permute-start.13 = (bf16[56,1024]{1,0:T(8,128)(2,1)S(1)}, bf16[56,1024]{1,0:T(8,128)(2,1)S(1)}, u32[]{:S(2)}, u32[]{:S(2)}) collective-permute-start(bf16[56,1024]{1,0:T(8,128)(2,1)S(1)} %get-tuple-element.79), channel_id=1, source_target_pairs={{0,10},{1,5},{2,8},{3,7},{4,14},{5,1},{6,12},{7,3},{8,2},{9,13},{1... | collective-permute-start | bytes 344072 | tf_op jit(solution)/shard_map/ppermute | solution.py:35
  42.8 1.6 %collective-permute-start.14 = (bf16[56,1024]{1,0:T(8,128)(2,1)S(1)}, bf16[56,1024]{1,0:T(8,128)(2,1)S(1)}, u32[]{:S(2)}, u32[]{:S(2)}) collective-permute-start(bf16[56,1024]{1,0:T(8,128)(2,1)S(1)} %get-tuple-element.80), channel_id=1, source_target_pairs={{0,6},{1,9},{2,4},{3,11},{4,2},{5,13},{6,0},{7,15},{8,14},{9,1},{1... | collective-permute-start | bytes 344072 | tf_op jit(solution)/shard_map/ppermute | solution.py:35
  44.3 1.3 %collective-permute-start.15 = (bf16[56,1024]{1,0:T(8,128)(2,1)S(1)}, bf16[56,1024]{1,0:T(8,128)(2,1)S(1)}, u32[]{:S(2)}, u32[]{:S(2)}) collective-permute-start(bf16[56,1024]{1,0:T(8,128)(2,1)S(1)} %get-tuple-element.81), channel_id=1, source_target_pairs={{0,8},{1,7},{2,10},{3,5},{4,12},{5,3},{6,14},{7,1},{8,0},{9,15},{1... | collective-permute-start | bytes 344072 | tf_op jit(solution)/shard_map/ppermute | solution.py:35
  45.6 0.8 %collective-permute-start.16 = (bf16[56,1024]{1,0:T(8,128)(2,1)S(1)}, bf16[56,1024]{1,0:T(8,128)(2,1)S(1)}, u32[]{:S(2)}, u32[]{:S(2)}) collective-permute-start(bf16[56,1024]{1,0:T(8,128)(2,1)S(1)} %get-tuple-element.82), channel_id=1, source_target_pairs={{0,4},{1,11},{2,6},{3,9},{4,0},{5,15},{6,2},{7,13},{8,12},{9,3},{1... | collective-permute-start | bytes 344072 | tf_op jit(solution)/shard_map/ppermute | solution.py:35
  46.4 1.2 %collective-permute-done.12.refs_1_ = bf16[56,1024]{1,0:T(8,128)(2,1)S(1)} collective-permute-done((bf16[56,1024]{1,0:T(8,128)(2,1)S(1)}, bf16[56,1024]{1,0:T(8,128)(2,1)S(1)}, u32[]{:S(2)}, u32[]{:S(2)}) %collective-permute-start.12) | collective-permute-done | bytes 114720 | tf_op jit(solution)/shard_map/ppermute | solution.py:35
  47.6 1.3 %collective-permute-start.17 = (bf16[56,1024]{1,0:T(8,128)(2,1)S(1)}, bf16[56,1024]{1,0:T(8,128)(2,1)S(1)}, u32[]{:S(2)}, u32[]{:S(2)}) collective-permute-start(bf16[56,1024]{1,0:T(8,128)(2,1)S(1)} %get-tuple-element.83), channel_id=1, source_target_pairs={{0,2},{1,13},{2,0},{3,15},{4,6},{5,9},{6,4},{7,11},{8,10},{9,5},{1... | collective-permute-start | bytes 344072 | tf_op jit(solution)/shard_map/ppermute | solution.py:35
  48.9 1.2 %collective-permute-done.13.refs_2_ = bf16[56,1024]{1,0:T(8,128)(2,1)S(1)} collective-permute-done((bf16[56,1024]{1,0:T(8,128)(2,1)S(1)}, bf16[56,1024]{1,0:T(8,128)(2,1)S(1)}, u32[]{:S(2)}, u32[]{:S(2)}) %collective-permute-start.13) | collective-permute-done | bytes 114720 | tf_op jit(solution)/shard_map/ppermute | solution.py:35
  50.1 1.6 %collective-permute-done.14.refs_3_ = bf16[56,1024]{1,0:T(8,128)(2,1)S(1)} collective-permute-done((bf16[56,1024]{1,0:T(8,128)(2,1)S(1)}, bf16[56,1024]{1,0:T(8,128)(2,1)S(1)}, u32[]{:S(2)}, u32[]{:S(2)}) %collective-permute-start.14) | collective-permute-done | bytes 114720 | tf_op jit(solution)/shard_map/ppermute | solution.py:35
  51.7 0.9 %collective-permute-done.16.refs_5_ = bf16[56,1024]{1,0:T(8,128)(2,1)S(1)} collective-permute-done((bf16[56,1024]{1,0:T(8,128)(2,1)S(1)}, bf16[56,1024]{1,0:T(8,128)(2,1)S(1)}, u32[]{:S(2)}, u32[]{:S(2)}) %collective-permute-start.16) | collective-permute-done | bytes 114720 | tf_op jit(solution)/shard_map/ppermute | solution.py:35
  52.6 0.5 shard_map.141
  53.1 3.0 %collective-permute-start.18 = (bf16[32,2048]{1,0:T(8,128)(2,1)S(1)}, bf16[32,2048]{1,0:T(8,128)(2,1)S(1)}, u32[]{:S(2)}, u32[]{:S(2)}) collective-permute-start(bf16[32,2048]{1,0:T(8,128)(2,1)S(1)} %get-tuple-element.86), channel_id=1, source_target_pairs={{0,16},{1,17},{2,18},{3,19},{4,20},{5,21},{6,22},{7,23},{8,24},{9,... | collective-permute-start | bytes 393224 | tf_op jit(solution)/shard_map/ppermute | solution.py:18
  56.0 5.0 %collective-permute-done.18 = bf16[32,2048]{1,0:T(8,128)(2,1)S(1)} collective-permute-done((bf16[32,2048]{1,0:T(8,128)(2,1)S(1)}, bf16[32,2048]{1,0:T(8,128)(2,1)S(1)}, u32[]{:S(2)}, u32[]{:S(2)}) %collective-permute-start.18) | collective-permute-done | bytes 131104 | tf_op jit(solution)/shard_map/ppermute | solution.py:18
  61.0 0.7 %add_convert_fusion = bf16[32,2048]{1,0:T(8,128)(2,1)} fusion(f32[32,2048]{1,0:T(8,128)S(1)} %get-tuple-element.85, bf16[32,2048]{1,0:T(8,128)(2,1)S(1)} %collective-permute-done.18), kind=kLoop, calls=%fused_computation | loop fusion | flops 196608 | bytes 524288 | tf_op jit(solution)/shard_map/convert_element_type | solution.py:398
  (23 shorter events, 1.0 us)
Async XLA Ops:
  0.0 9.4 %copy-start.2 = (s32[8]{0:T(128)S(1)}, s32[8]{0:T(128)}, u32[]{:S(2)}) copy-start(s32[8]{0:T(128)} %constant.34.clone) | copy-start | bytes 100
  0.0 9.4 %copy-start.3 = (s32[8]{0:T(128)S(1)}, s32[8]{0:T(128)}, u32[]{:S(2)}) copy-start(s32[8]{0:T(128)} %constant.33.clone) | copy-start | bytes 100
  0.0 16.9 %collective-permute-start.1 = (bf16[704,2048]{1,0:T(8,128)(2,1)}, bf16[704,2048]{1,0:T(8,128)(2,1)S(1)}, u32[]{:S(2)}, u32[]{:S(2)}) collective-permute-start(bf16[704,2048]{1,0:T(8,128)(2,1)} %bitcast.14), channel_id=1, source_target_pairs={{0,1},{1,0},{2,3},{3,2},{4,5},{5,4},{6,7},{7,6},{8,9},{9,8},{10,11... | collective-permute-start | bytes 8650760 | tf_op jit(solution)/shard_map/ppermute | solution.py:18
  0.5 16.4 %collective-permute-start.2 = (bf16[704,2048]{1,0:T(8,128)(2,1)}, bf16[704,2048]{1,0:T(8,128)(2,1)}, u32[]{:S(2)}, u32[]{:S(2)}) collective-permute-start(bf16[704,2048]{1,0:T(8,128)(2,1)} %bitcast.16), channel_id=1, source_target_pairs={{0,1},{1,0},{2,3},{3,2},{4,5},{5,4},{6,7},{7,6},{8,9},{9,8},{10,11... | collective-permute-start | bytes 8650760 | tf_op jit(solution)/shard_map/ppermute | solution.py:18
  0.5 16.3 %collective-permute-start.3 = (bf16[704,2048]{1,0:T(8,128)(2,1)}, bf16[704,2048]{1,0:T(8,128)(2,1)}, u32[]{:S(2)}, u32[]{:S(2)}) collective-permute-start(bf16[704,2048]{1,0:T(8,128)(2,1)} %bitcast.18), channel_id=1, source_target_pairs={{0,1},{1,0},{2,3},{3,2},{4,5},{5,4},{6,7},{7,6},{8,9},{9,8},{10,11... | collective-permute-start | bytes 8650760 | tf_op jit(solution)/shard_map/ppermute | solution.py:18
  5.7 11.2 %collective-permute-start = (bf16[32,2176]{1,0:T(8,128)(2,1)}, bf16[32,2176]{1,0:T(8,128)(2,1)S(1)}, u32[]{:S(2)}, u32[]{:S(2)}) collective-permute-start(bf16[32,2176]{1,0:T(8,128)(2,1)} %get-tuple-element.47.here), channel_id=1, source_target_pairs={{0,16},{1,17},{2,18},{3,19},{4,20},{5,21},{6,22},{7,23},{8,24},{9,... | collective-permute-start | bytes 417800 | tf_op jit(solution)/shard_map/ppermute | solution.py:18
  9.5 7.4 %copy-start.1 = (bf16[32,2176]{1,0:T(8,128)(2,1)S(1)}, bf16[32,2176]{1,0:T(8,128)(2,1)}, u32[]{:S(2)}) copy-start(bf16[32,2176]{1,0:T(8,128)(2,1)} %get-tuple-element.47.here) | copy-start | bytes 417796
  17.6 8.4 %collective-permute-start.4 = (bf16[56,1024]{1,0:T(8,128)(2,1)S(1)}, bf16[56,1024]{1,0:T(8,128)(2,1)S(1)}, u32[]{:S(2)}, u32[]{:S(2)}) collective-permute-start(bf16[56,1024]{1,0:T(8,128)(2,1)S(1)} %get-tuple-element.58), channel_id=1, source_target_pairs={{0,12},{1,3},{2,14},{3,1},{4,8},{5,7},{6,10},{7,5},{8,4},{9,11},{1... | collective-permute-start | bytes 344072 | tf_op jit(solution)/shard_map/ppermute | solution.py:35
  19.4 8.5 %collective-permute-start.6 = (bf16[56,1024]{1,0:T(8,128)(2,1)S(1)}, bf16[56,1024]{1,0:T(8,128)(2,1)S(1)}, u32[]{:S(2)}, u32[]{:S(2)}) collective-permute-start(bf16[56,1024]{1,0:T(8,128)(2,1)S(1)} %get-tuple-element.60), channel_id=1, source_target_pairs={{0,10},{1,5},{2,8},{3,7},{4,14},{5,1},{6,12},{7,3},{8,2},{9,13},{1... | collective-permute-start | bytes 344072 | tf_op jit(solution)/shard_map/ppermute | solution.py:35
  21.6 9.4 %collective-permute-start.5 = (bf16[56,1024]{1,0:T(8,128)(2,1)S(1)}, bf16[56,1024]{1,0:T(8,128)(2,1)S(1)}, u32[]{:S(2)}, u32[]{:S(2)}) collective-permute-start(bf16[56,1024]{1,0:T(8,128)(2,1)S(1)} %get-tuple-element.59), channel_id=1, source_target_pairs={{0,14},{1,15},{2,12},{3,13},{4,10},{5,11},{6,8},{7,9},{8,6},{9,7},... | collective-permute-start | bytes 344072 | tf_op jit(solution)/shard_map/ppermute | solution.py:35
  22.3 9.8 %collective-permute-start.7 = (bf16[56,1024]{1,0:T(8,128)(2,1)S(1)}, bf16[56,1024]{1,0:T(8,128)(2,1)S(1)}, u32[]{:S(2)}, u32[]{:S(2)}) collective-permute-start(bf16[56,1024]{1,0:T(8,128)(2,1)S(1)} %get-tuple-element.64), channel_id=1, source_target_pairs={{0,6},{1,9},{2,4},{3,11},{4,2},{5,13},{6,0},{7,15},{8,14},{9,1},{1... | collective-permute-start | bytes 344072 | tf_op jit(solution)/shard_map/ppermute | solution.py:35
  24.7 7.4 %collective-permute-start.8 = (bf16[56,1024]{1,0:T(8,128)(2,1)S(1)}, bf16[56,1024]{1,0:T(8,128)(2,1)S(1)}, u32[]{:S(2)}, u32[]{:S(2)}) collective-permute-start(bf16[56,1024]{1,0:T(8,128)(2,1)S(1)} %get-tuple-element.65), channel_id=1, source_target_pairs={{0,8},{1,7},{2,10},{3,5},{4,12},{5,3},{6,14},{7,1},{8,0},{9,15},{1... | collective-permute-start | bytes 344072 | tf_op jit(solution)/shard_map/ppermute | solution.py:35
  26.0 7.2 %collective-permute-start.9 = (bf16[56,1024]{1,0:T(8,128)(2,1)S(1)}, bf16[56,1024]{1,0:T(8,128)(2,1)S(1)}, u32[]{:S(2)}, u32[]{:S(2)}) collective-permute-start(bf16[56,1024]{1,0:T(8,128)(2,1)S(1)} %get-tuple-element.66), channel_id=1, source_target_pairs={{0,4},{1,11},{2,6},{3,9},{4,0},{5,15},{6,2},{7,13},{8,12},{9,3},{1... | collective-permute-start | bytes 344072 | tf_op jit(solution)/shard_map/ppermute | solution.py:35
  28.0 5.2 %collective-permute-start.10 = (bf16[56,1024]{1,0:T(8,128)(2,1)S(1)}, bf16[56,1024]{1,0:T(8,128)(2,1)S(1)}, u32[]{:S(2)}, u32[]{:S(2)}) collective-permute-start(bf16[56,1024]{1,0:T(8,128)(2,1)S(1)} %get-tuple-element.67), channel_id=1, source_target_pairs={{0,2},{1,13},{2,0},{3,15},{4,6},{5,9},{6,4},{7,11},{8,10},{9,5},{1... | collective-permute-start | bytes 344072 | tf_op jit(solution)/shard_map/ppermute | solution.py:35
  33.2 19.4 %copy-start = (f32[32,2048]{1,0:T(8,128)S(1)}, f32[32,2048]{1,0:T(8,128)}, u32[]{:S(2)}) copy-start(f32[32,2048]{1,0:T(8,128)} %get-tuple-element.57.stream) | copy-start | bytes 786436
  38.1 7.5 %collective-permute-start.11 = (bf16[56,1024]{1,0:T(8,128)(2,1)S(1)}, bf16[56,1024]{1,0:T(8,128)(2,1)S(1)}, u32[]{:S(2)}, u32[]{:S(2)}) collective-permute-start(bf16[56,1024]{1,0:T(8,128)(2,1)S(1)} %get-tuple-element.77), channel_id=1, source_target_pairs={{0,12},{1,3},{2,14},{3,1},{4,8},{5,7},{6,10},{7,5},{8,4},{9,11},{1... | collective-permute-start | bytes 344072 | tf_op jit(solution)/shard_map/ppermute | solution.py:35
  39.7 7.9 %collective-permute-start.12 = (bf16[56,1024]{1,0:T(8,128)(2,1)S(1)}, bf16[56,1024]{1,0:T(8,128)(2,1)S(1)}, u32[]{:S(2)}, u32[]{:S(2)}) collective-permute-start(bf16[56,1024]{1,0:T(8,128)(2,1)S(1)} %get-tuple-element.78), channel_id=1, source_target_pairs={{0,14},{1,15},{2,12},{3,13},{4,10},{5,11},{6,8},{7,9},{8,6},{9,7},... | collective-permute-start | bytes 344072 | tf_op jit(solution)/shard_map/ppermute | solution.py:35
  41.1 9.0 %collective-permute-start.13 = (bf16[56,1024]{1,0:T(8,128)(2,1)S(1)}, bf16[56,1024]{1,0:T(8,128)(2,1)S(1)}, u32[]{:S(2)}, u32[]{:S(2)}) collective-permute-start(bf16[56,1024]{1,0:T(8,128)(2,1)S(1)} %get-tuple-element.79), channel_id=1, source_target_pairs={{0,10},{1,5},{2,8},{3,7},{4,14},{5,1},{6,12},{7,3},{8,2},{9,13},{1... | collective-permute-start | bytes 344072 | tf_op jit(solution)/shard_map/ppermute | solution.py:35
  42.8 9.0 %collective-permute-start.14 = (bf16[56,1024]{1,0:T(8,128)(2,1)S(1)}, bf16[56,1024]{1,0:T(8,128)(2,1)S(1)}, u32[]{:S(2)}, u32[]{:S(2)}) collective-permute-start(bf16[56,1024]{1,0:T(8,128)(2,1)S(1)} %get-tuple-element.80), channel_id=1, source_target_pairs={{0,6},{1,9},{2,4},{3,11},{4,2},{5,13},{6,0},{7,15},{8,14},{9,1},{1... | collective-permute-start | bytes 344072 | tf_op jit(solution)/shard_map/ppermute | solution.py:35
  44.3 7.4 %collective-permute-start.15 = (bf16[56,1024]{1,0:T(8,128)(2,1)S(1)}, bf16[56,1024]{1,0:T(8,128)(2,1)S(1)}, u32[]{:S(2)}, u32[]{:S(2)}) collective-permute-start(bf16[56,1024]{1,0:T(8,128)(2,1)S(1)} %get-tuple-element.81), channel_id=1, source_target_pairs={{0,8},{1,7},{2,10},{3,5},{4,12},{5,3},{6,14},{7,1},{8,0},{9,15},{1... | collective-permute-start | bytes 344072 | tf_op jit(solution)/shard_map/ppermute | solution.py:35
  45.6 7.0 %collective-permute-start.16 = (bf16[56,1024]{1,0:T(8,128)(2,1)S(1)}, bf16[56,1024]{1,0:T(8,128)(2,1)S(1)}, u32[]{:S(2)}, u32[]{:S(2)}) collective-permute-start(bf16[56,1024]{1,0:T(8,128)(2,1)S(1)} %get-tuple-element.82), channel_id=1, source_target_pairs={{0,4},{1,11},{2,6},{3,9},{4,0},{5,15},{6,2},{7,13},{8,12},{9,3},{1... | collective-permute-start | bytes 344072 | tf_op jit(solution)/shard_map/ppermute | solution.py:35
  47.6 5.0 %collective-permute-start.17 = (bf16[56,1024]{1,0:T(8,128)(2,1)S(1)}, bf16[56,1024]{1,0:T(8,128)(2,1)S(1)}, u32[]{:S(2)}, u32[]{:S(2)}) collective-permute-start(bf16[56,1024]{1,0:T(8,128)(2,1)S(1)} %get-tuple-element.83), channel_id=1, source_target_pairs={{0,2},{1,13},{2,0},{3,15},{4,6},{5,9},{6,4},{7,11},{8,10},{9,5},{1... | collective-permute-start | bytes 344072 | tf_op jit(solution)/shard_map/ppermute | solution.py:35
  53.1 8.0 %collective-permute-start.18 = (bf16[32,2048]{1,0:T(8,128)(2,1)S(1)}, bf16[32,2048]{1,0:T(8,128)(2,1)S(1)}, u32[]{:S(2)}, u32[]{:S(2)}) collective-permute-start(bf16[32,2048]{1,0:T(8,128)(2,1)S(1)} %get-tuple-element.86), channel_id=1, source_target_pairs={{0,16},{1,17},{2,18},{3,19},{4,20},{5,21},{6,22},{7,23},{8,24},{9,... | collective-permute-start | bytes 393224 | tf_op jit(solution)/shard_map/ppermute | solution.py:18

commit v9 on v8

--- a/solution.py
+++ b/solution.py
@@ -21,7 +21,7 @@
 def orders(near):
     last = near - 1
     first = list(range(last, 0, -1))
-    for i in (0, near // 2 - 1):
+    for i in (0, near // 2 - 1, near - 3):
         first[i], first[i + 1] = first[i + 1], first[i]
     second = [m if m == last else last ^ m for m in first]
     return [*first, 0], [*second, 0]
@@ -389,7 +389,7 @@
     normed, own = lax.optimization_barrier((normed, own))
     across = swapped(normed, devices // 2)
     own = load(own, 44)
-    across, own, other = lax.optimization_barrier((across, own, other))
+    across, own, *other[:2] = lax.optimization_barrier((across, own, *other[:2]))
     high, low, *blocks = dispatch(mine, normed, across, top, capacity)
     blocks = exchanged(blocks)
     blocks[2], *late = lax.optimization_barrier((blocks[2], *other[1:]))

time: 61.9 us -> 61.5 us (level)
    ppermute x14, waiting for transfers between devices: 8.41 us -> 9.07 us  [exchanged(): got[i] = lax.ppermute(blocks[i], 'ep', pairs)]
    ppermute x14, starting transfers between devices: 19 us -> 18.4 us  [exchanged(): got[i] = lax.ppermute(blocks[i], 'ep', pairs)]
    ppermute x5, waiting for transfers between devices: 8.79 us -> 8.16 us  [swapped(): return lax.ppermute(value, 'ep', pairs)]
  transfers between devices with their start and end apart: 19 -> 19, of which waited for: 9 -> 12; matrix products, arithmetic and copies ran while one was open for 0% -> 0% of each run, Pallas kernels for 18% -> 19%
where the time goes in v9:
time: 61.5 us; the launch traced here: 61.4 us
  starting transfers between devices  26.3 us (43%)
  waiting for transfers between devices  17.2 us (28%)
  Pallas kernels  17 us (28%)
  other arithmetic  0.69 us (1%)
    ppermute x14, starting transfers between devices, exchanged(): got[i] = lax.ppermute(blocks[i], 'ep', pairs)  18.4 us
    ppermute x14, waiting for transfers between devices, exchanged(): got[i] = lax.ppermute(blocks[i], 'ep', pairs)  9.07 us
    ppermute x5, waiting for transfers between devices, swapped(): return lax.ppermute(value, 'ep', pairs)  8.16 us
    ppermute x5, starting transfers between devices, swapped(): return lax.ppermute(value, 'ep', pairs)  7.92 us
    pallas_call x2, Pallas kernels, load(): pl.pallas_call(load_kernel, in_specs=[pl.BlockSpec(memory_space=pl.ANY)]...  6.29 us
    pallas_call x1, Pallas kernels, run_expert(): pl.pallas_call(functools.partial(expert_kernel, count), in_specs=[whole()...  4.87 us
    pallas_call x1, Pallas kernels, attend(): pl.pallas_call(functools.partial(attend_kernel, heads), in_specs=[pl.Bloc...  4.68 us
  transfers between devices with their start and end apart: 19, of which 12 were waited for; matrix products, arithmetic and copies ran while one was open for 0% of the time, Pallas kernels for 19%

profile of v9, /device:TPU:0, one launch (start us, length us, event | category | flops | bytes accessed | tf_op | source)
XLA Modules:
  0.0 61.4 jit_solution(4167196599493224969)
XLA Ops:
  0.0 0.5 collective-permute-start.1
  1.0 4.7 %shard_map.136 = (f32[32,2048]{1,0:T(8,128)}, bf16[32,2176]{1,0:T(8,128)(2,1)}) custom-call(s32[4]{0:T(128)} %refs_0_.1, bf16[4,8,576]{2,1,0:T(8,128)(2,1)} %refs_1_.1, bf16[4,128,576]{2,1,0:T(8,128)(2,1)} %bitcast.21, bf16[4,576,384]{2,1,0:T(8,128)(2,1)} %bitcast.20, bf16[16,512,128]{2,1,0:T(8,128)(2,1)} %refs_4_.1, bf16[32,2048]{1,0:T(8,128)(2,1)} %refs_5_.1, ...), custom_call_target="tpu_custom_call" | custom-call | flops 494927872 | bytes 6291456 | tf_op jit(solution)/shard_map/pallas_call | solution.py:148
  5.7 3.7 %collective-permute-start = (bf16[32,2176]{1,0:T(8,128)(2,1)}, bf16[32,2176]{1,0:T(8,128)(2,1)S(1)}, u32[]{:S(2)}, u32[]{:S(2)}) collective-permute-start(bf16[32,2176]{1,0:T(8,128)(2,1)} %get-tuple-element.46.here), channel_id=1, source_target_pairs={{0,16},{1,17},{2,18},{3,19},{4,20},{5,21},{6,22},{7,23},{8,24},{9,... | collective-permute-start | bytes 417800 | tf_op jit(solution)/shard_map/ppermute | solution.py:18
  9.5 3.6 %shard_map.137 = (bf16[704,2048]{1,0:T(8,128)(2,1)S(1)}, bf16[704,2048]{1,0:T(8,128)(2,1)S(1)}, bf16[704,2048]{1,0:T(8,128)(2,1)S(1)}) custom-call(bf16[704,2048]{1,0:T(8,128)(2,1)} %bitcast.15, bf16[704,2048]{1,0:T(8,128)(2,1)} %bitcast.17, bf16[704,2048]{1,0:T(8,128)(2,1)} %bitcast.19), custom_call_target="tpu_custom_call" | custom-call | bytes 17301504 | tf_op jit(solution)/shard_map/pallas_call | solution.py:250
  13.1 3.8 %collective-permute-done.there = bf16[32,2176]{1,0:T(8,128)(2,1)S(1)} collective-permute-done((bf16[32,2176]{1,0:T(8,128)(2,1)}, bf16[32,2176]{1,0:T(8,128)(2,1)S(1)}, u32[]{:S(2)}, u32[]{:S(2)}) %collective-permute-start) | collective-permute-done | bytes 139296 | tf_op jit(solution)/shard_map/ppermute | solution.py:18
  16.9 0.7 %shard_map.138 = (bf16[128,448]{1,0:T(8,128)(2,1)S(1)}, bf16[128,448]{1,0:T(8,128)(2,1)S(1)}, bf16[56,1024]{1,0:T(8,128)(2,1)S(1)}, bf16[56,1024]{1,0:T(8,128)(2...) custom-call(f32[8,1]{1,0:T(8,128)S(1)} %copy.15.mine, ...), custom_call_target="tpu_custom_call" | custom-call | flops 117440512 | bytes 1572864 | tf_op jit(solution)/shard_map/pallas_call | solution.py:223
  17.6 1.9 %collective-permute-start.3 = (bf16[56,1024]{1,0:T(8,128)(2,1)S(1)}, bf16[56,1024]{1,0:T(8,128)(2,1)S(1)}, u32[]{:S(2)}, u32[]{:S(2)}) collective-permute-start(bf16[56,1024]{1,0:T(8,128)(2,1)S(1)} %get-tuple-element.57), channel_id=1, source_target_pairs={{0,12},{1,3},{2,14},{3,1},{4,8},{5,7},{6,10},{7,5},{8,4},{9,11},{1... | collective-permute-start | bytes 344072 | tf_op jit(solution)/shard_map/ppermute | solution.py:35
  19.4 2.2 %collective-permute-start.5 = (bf16[56,1024]{1,0:T(8,128)(2,1)S(1)}, bf16[56,1024]{1,0:T(8,128)(2,1)S(1)}, u32[]{:S(2)}, u32[]{:S(2)}) collective-permute-start(bf16[56,1024]{1,0:T(8,128)(2,1)S(1)} %get-tuple-element.59), channel_id=1, source_target_pairs={{0,10},{1,5},{2,8},{3,7},{4,14},{5,1},{6,12},{7,3},{8,2},{9,13},{1... | collective-permute-start | bytes 344072 | tf_op jit(solution)/shard_map/ppermute | solution.py:35
  21.6 0.7 %collective-permute-start.4 = (bf16[56,1024]{1,0:T(8,128)(2,1)S(1)}, bf16[56,1024]{1,0:T(8,128)(2,1)S(1)}, u32[]{:S(2)}, u32[]{:S(2)}) collective-permute-start(bf16[56,1024]{1,0:T(8,128)(2,1)S(1)} %get-tuple-element.58), channel_id=1, source_target_pairs={{0,14},{1,15},{2,12},{3,13},{4,10},{5,11},{6,8},{7,9},{8,6},{9,7},... | collective-permute-start | bytes 344072 | tf_op jit(solution)/shard_map/ppermute | solution.py:35
  22.3 2.4 %collective-permute-start.7 = (bf16[56,1024]{1,0:T(8,128)(2,1)S(1)}, bf16[56,1024]{1,0:T(8,128)(2,1)S(1)}, u32[]{:S(2)}, u32[]{:S(2)}) collective-permute-start(bf16[56,1024]{1,0:T(8,128)(2,1)S(1)} %get-tuple-element.62), channel_id=1, source_target_pairs={{0,6},{1,9},{2,4},{3,11},{4,2},{5,13},{6,0},{7,15},{8,14},{9,1},{1... | collective-permute-start | bytes 344072 | tf_op jit(solution)/shard_map/ppermute | solution.py:35
  24.7 1.3 %collective-permute-start.8 = (bf16[56,1024]{1,0:T(8,128)(2,1)S(1)}, bf16[56,1024]{1,0:T(8,128)(2,1)S(1)}, u32[]{:S(2)}, u32[]{:S(2)}) collective-permute-start(bf16[56,1024]{1,0:T(8,128)(2,1)S(1)} %get-tuple-element.63), channel_id=1, source_target_pairs={{0,8},{1,7},{2,10},{3,5},{4,12},{5,3},{6,14},{7,1},{8,0},{9,15},{1... | collective-permute-start | bytes 344072 | tf_op jit(solution)/shard_map/ppermute | solution.py:35
  26.0 0.5 collective-permute-start.9
  26.5 1.4 %collective-permute-done.5.refs_2_ = bf16[56,1024]{1,0:T(8,128)(2,1)S(1)} collective-permute-done((bf16[56,1024]{1,0:T(8,128)(2,1)S(1)}, bf16[56,1024]{1,0:T(8,128)(2,1)S(1)}, u32[]{:S(2)}, u32[]{:S(2)}) %collective-permute-start.5) | collective-permute-done | bytes 114720 | tf_op jit(solution)/shard_map/ppermute | solution.py:35
  27.9 2.7 %shard_map.139 = (bf16[704,2048]{1,0:T(8,128)(2,1)S(1)}, bf16[704,2048]{1,0:T(8,128)(2,1)S(1)}) custom-call(bf16[704,2048]{1,0:T(8,128)(2,1)} %collective-permute-done.2.refs_0_, bf16[704,2048]{1,0:T(8,128)(2,1)} %collective-permute-done.6.refs_1_), custom_call_target="tpu_custom_call" | custom-call | bytes 11534336 | tf_op jit(solution)/shard_map/pallas_call | solution.py:250
  30.7 1.0 %collective-permute-done.7.refs_3_ = bf16[56,1024]{1,0:T(8,128)(2,1)S(1)} collective-permute-done((bf16[56,1024]{1,0:T(8,128)(2,1)S(1)}, bf16[56,1024]{1,0:T(8,128)(2,1)S(1)}, u32[]{:S(2)}, u32[]{:S(2)}) %collective-permute-start.7) | collective-permute-done | bytes 114720 | tf_op jit(solution)/shard_map/ppermute | solution.py:35
  31.8 1.4 %collective-permute-done.9.refs_5_ = bf16[56,1024]{1,0:T(8,128)(2,1)S(1)} collective-permute-done((bf16[56,1024]{1,0:T(8,128)(2,1)S(1)}, bf16[56,1024]{1,0:T(8,128)(2,1)S(1)}, u32[]{:S(2)}, u32[]{:S(2)}) %collective-permute-start.9) | collective-permute-done | bytes 114720 | tf_op jit(solution)/shard_map/ppermute | solution.py:35
  33.2 4.9 %shard_map.140 = (bf16[56,1024]{1,0:T(8,128)(2,1)S(1)}, bf16[56,1024]{1,0:T(8,128)(2,1)S(1)}, bf16[56,1024]{1,0:T(8,128)(2,1)S(1)}, bf16[56,1024]{1,0:T(8,128)(2...) custom-call(bf16[56,1024]{1,0:T(8,128)(2,1)S(1)} %collective-permute, ...), custom_call_target="tpu_custom_call" | custom-call | flops 3875536896 | bytes 17301504 | tf_op jit(solution)/shard_map/pallas_call | solution.py:312
  38.0 1.4 %collective-permute-start.11 = (bf16[56,1024]{1,0:T(8,128)(2,1)S(1)}, bf16[56,1024]{1,0:T(8,128)(2,1)S(1)}, u32[]{:S(2)}, u32[]{:S(2)}) collective-permute-start(bf16[56,1024]{1,0:T(8,128)(2,1)S(1)} %get-tuple-element.75), channel_id=1, source_target_pairs={{0,12},{1,3},{2,14},{3,1},{4,8},{5,7},{6,10},{7,5},{8,4},{9,11},{1... | collective-permute-start | bytes 344072 | tf_op jit(solution)/shard_map/ppermute | solution.py:35
  39.5 1.9 %collective-permute-start.12 = (bf16[56,1024]{1,0:T(8,128)(2,1)S(1)}, bf16[56,1024]{1,0:T(8,128)(2,1)S(1)}, u32[]{:S(2)}, u32[]{:S(2)}) collective-permute-start(bf16[56,1024]{1,0:T(8,128)(2,1)S(1)} %get-tuple-element.76), channel_id=1, source_target_pairs={{0,14},{1,15},{2,12},{3,13},{4,10},{5,11},{6,8},{7,9},{8,6},{9,7},... | collective-permute-start | bytes 344072 | tf_op jit(solution)/shard_map/ppermute | solution.py:35
  41.3 2.0 %collective-permute-start.13 = (bf16[56,1024]{1,0:T(8,128)(2,1)S(1)}, bf16[56,1024]{1,0:T(8,128)(2,1)S(1)}, u32[]{:S(2)}, u32[]{:S(2)}) collective-permute-start(bf16[56,1024]{1,0:T(8,128)(2,1)S(1)} %get-tuple-element.77), channel_id=1, source_target_pairs={{0,10},{1,5},{2,8},{3,7},{4,14},{5,1},{6,12},{7,3},{8,2},{9,13},{1... | collective-permute-start | bytes 344072 | tf_op jit(solution)/shard_map/ppermute | solution.py:35
  43.4 0.7 %collective-permute-start.14 = (bf16[56,1024]{1,0:T(8,128)(2,1)S(1)}, bf16[56,1024]{1,0:T(8,128)(2,1)S(1)}, u32[]{:S(2)}, u32[]{:S(2)}) collective-permute-start(bf16[56,1024]{1,0:T(8,128)(2,1)S(1)} %get-tuple-element.78), channel_id=1, source_target_pairs={{0,6},{1,9},{2,4},{3,11},{4,2},{5,13},{6,0},{7,15},{8,14},{9,1},{1... | collective-permute-start | bytes 344072 | tf_op jit(solution)/shard_map/ppermute | solution.py:35
  44.1 1.1 %collective-permute-start.15 = (bf16[56,1024]{1,0:T(8,128)(2,1)S(1)}, bf16[56,1024]{1,0:T(8,128)(2,1)S(1)}, u32[]{:S(2)}, u32[]{:S(2)}) collective-permute-start(bf16[56,1024]{1,0:T(8,128)(2,1)S(1)} %get-tuple-element.79), channel_id=1, source_target_pairs={{0,8},{1,7},{2,10},{3,5},{4,12},{5,3},{6,14},{7,1},{8,0},{9,15},{1... | collective-permute-start | bytes 344072 | tf_op jit(solution)/shard_map/ppermute | solution.py:35
  45.2 1.5 %collective-permute-start.16 = (bf16[56,1024]{1,0:T(8,128)(2,1)S(1)}, bf16[56,1024]{1,0:T(8,128)(2,1)S(1)}, u32[]{:S(2)}, u32[]{:S(2)}) collective-permute-start(bf16[56,1024]{1,0:T(8,128)(2,1)S(1)} %get-tuple-element.80), channel_id=1, source_target_pairs={{0,2},{1,13},{2,0},{3,15},{4,6},{5,9},{6,4},{7,11},{8,10},{9,5},{1... | collective-permute-start | bytes 344072 | tf_op jit(solution)/shard_map/ppermute | solution.py:35
  46.7 1.1 %collective-permute-done.12.refs_1_ = bf16[56,1024]{1,0:T(8,128)(2,1)S(1)} collective-permute-done((bf16[56,1024]{1,0:T(8,128)(2,1)S(1)}, bf16[56,1024]{1,0:T(8,128)(2,1)S(1)}, u32[]{:S(2)}, u32[]{:S(2)}) %collective-permute-start.12) | collective-permute-done | bytes 114720 | tf_op jit(solution)/shard_map/ppermute | solution.py:35
  47.8 0.8 %collective-permute-start.17 = (bf16[56,1024]{1,0:T(8,128)(2,1)S(1)}, bf16[56,1024]{1,0:T(8,128)(2,1)S(1)}, u32[]{:S(2)}, u32[]{:S(2)}) collective-permute-start(bf16[56,1024]{1,0:T(8,128)(2,1)S(1)} %get-tuple-element.81), channel_id=1, source_target_pairs={{0,4},{1,11},{2,6},{3,9},{4,0},{5,15},{6,2},{7,13},{8,12},{9,3},{1... | collective-permute-start | bytes 344072 | tf_op jit(solution)/shard_map/ppermute | solution.py:35
  49.0 1.8 %collective-permute-done.14.refs_3_ = bf16[56,1024]{1,0:T(8,128)(2,1)S(1)} collective-permute-done((bf16[56,1024]{1,0:T(8,128)(2,1)S(1)}, bf16[56,1024]{1,0:T(8,128)(2,1)S(1)}, u32[]{:S(2)}, u32[]{:S(2)}) %collective-permute-start.14) | collective-permute-done | bytes 114720 | tf_op jit(solution)/shard_map/ppermute | solution.py:35
  50.8 0.6 %collective-permute-done.15.refs_4_ = bf16[56,1024]{1,0:T(8,128)(2,1)S(1)} collective-permute-done((bf16[56,1024]{1,0:T(8,128)(2,1)S(1)}, bf16[56,1024]{1,0:T(8,128)(2,1)S(1)}, u32[]{:S(2)}, u32[]{:S(2)}) %collective-permute-start.15) | collective-permute-done | bytes 114720 | tf_op jit(solution)/shard_map/ppermute | solution.py:35
  51.8 0.8 %collective-permute-done.17.refs_6_ = bf16[56,1024]{1,0:T(8,128)(2,1)S(1)} collective-permute-done((bf16[56,1024]{1,0:T(8,128)(2,1)S(1)}, bf16[56,1024]{1,0:T(8,128)(2,1)S(1)}, u32[]{:S(2)}, u32[]{:S(2)}) %collective-permute-start.17) | collective-permute-done | bytes 114720 | tf_op jit(solution)/shard_map/ppermute | solution.py:35
  52.6 0.5 shard_map.141
  53.1 3.2 %collective-permute-start.18 = (bf16[32,2048]{1,0:T(8,128)(2,1)S(1)}, bf16[32,2048]{1,0:T(8,128)(2,1)S(1)}, u32[]{:S(2)}, u32[]{:S(2)}) collective-permute-start(bf16[32,2048]{1,0:T(8,128)(2,1)S(1)} %get-tuple-element.84), channel_id=1, source_target_pairs={{0,16},{1,17},{2,18},{3,19},{4,20},{5,21},{6,22},{7,23},{8,24},{9,... | collective-permute-start | bytes 393224 | tf_op jit(solution)/shard_map/ppermute | solution.py:18
  56.3 4.4 %collective-permute-done.18 = bf16[32,2048]{1,0:T(8,128)(2,1)S(1)} collective-permute-done((bf16[32,2048]{1,0:T(8,128)(2,1)S(1)}, bf16[32,2048]{1,0:T(8,128)(2,1)S(1)}, u32[]{:S(2)}, u32[]{:S(2)}) %collective-permute-start.18) | collective-permute-done | bytes 131104 | tf_op jit(solution)/shard_map/ppermute | solution.py:18
  60.7 0.7 %add_convert_fusion = bf16[32,2048]{1,0:T(8,128)(2,1)} fusion(f32[32,2048]{1,0:T(8,128)S(1)} %get-tuple-element.83, bf16[32,2048]{1,0:T(8,128)(2,1)S(1)} %collective-permute-done.18), kind=kLoop, calls=%fused_computation | loop fusion | flops 196608 | bytes 524288 | tf_op jit(solution)/shard_map/convert_element_type | solution.py:398
  (23 shorter events, 1.5 us)
Async XLA Ops:
  0.0 9.4 %copy-start.2 = (s32[8]{0:T(128)S(1)}, s32[8]{0:T(128)}, u32[]{:S(2)}) copy-start(s32[8]{0:T(128)} %constant.34.clone) | copy-start | bytes 100
  0.0 9.4 %copy-start.3 = (s32[8]{0:T(128)S(1)}, s32[8]{0:T(128)}, u32[]{:S(2)}) copy-start(s32[8]{0:T(128)} %constant.33.clone) | copy-start | bytes 100
  0.0 16.9 %collective-permute-start.1 = (bf16[704,2048]{1,0:T(8,128)(2,1)}, bf16[704,2048]{1,0:T(8,128)(2,1)S(1)}, u32[]{:S(2)}, u32[]{:S(2)}) collective-permute-start(bf16[704,2048]{1,0:T(8,128)(2,1)} %bitcast.14), channel_id=1, source_target_pairs={{0,1},{1,0},{2,3},{3,2},{4,5},{5,4},{6,7},{7,6},{8,9},{9,8},{10,11... | collective-permute-start | bytes 8650760 | tf_op jit(solution)/shard_map/ppermute | solution.py:18
  0.5 16.4 %collective-permute-start.2 = (bf16[704,2048]{1,0:T(8,128)(2,1)}, bf16[704,2048]{1,0:T(8,128)(2,1)}, u32[]{:S(2)}, u32[]{:S(2)}) collective-permute-start(bf16[704,2048]{1,0:T(8,128)(2,1)} %bitcast.16), channel_id=1, source_target_pairs={{0,1},{1,0},{2,3},{3,2},{4,5},{5,4},{6,7},{7,6},{8,9},{9,8},{10,11... | collective-permute-start | bytes 8650760 | tf_op jit(solution)/shard_map/ppermute | solution.py:18
  0.5 24.2 %collective-permute-start.6 = (bf16[704,2048]{1,0:T(8,128)(2,1)}, bf16[704,2048]{1,0:T(8,128)(2,1)}, u32[]{:S(2)}, u32[]{:S(2)}) collective-permute-start(bf16[704,2048]{1,0:T(8,128)(2,1)} %bitcast.18), channel_id=1, source_target_pairs={{0,1},{1,0},{2,3},{3,2},{4,5},{5,4},{6,7},{7,6},{8,9},{9,8},{10,11... | collective-permute-start | bytes 8650760 | tf_op jit(solution)/shard_map/ppermute | solution.py:18
  5.7 11.2 %collective-permute-start = (bf16[32,2176]{1,0:T(8,128)(2,1)}, bf16[32,2176]{1,0:T(8,128)(2,1)S(1)}, u32[]{:S(2)}, u32[]{:S(2)}) collective-permute-start(bf16[32,2176]{1,0:T(8,128)(2,1)} %get-tuple-element.46.here), channel_id=1, source_target_pairs={{0,16},{1,17},{2,18},{3,19},{4,20},{5,21},{6,22},{7,23},{8,24},{9,... | collective-permute-start | bytes 417800 | tf_op jit(solution)/shard_map/ppermute | solution.py:18
  9.5 7.4 %copy-start.1 = (bf16[32,2176]{1,0:T(8,128)(2,1)S(1)}, bf16[32,2176]{1,0:T(8,128)(2,1)}, u32[]{:S(2)}) copy-start(bf16[32,2176]{1,0:T(8,128)(2,1)} %get-tuple-element.46.here) | copy-start | bytes 417796
  17.6 8.4 %collective-permute-start.3 = (bf16[56,1024]{1,0:T(8,128)(2,1)S(1)}, bf16[56,1024]{1,0:T(8,128)(2,1)S(1)}, u32[]{:S(2)}, u32[]{:S(2)}) collective-permute-start(bf16[56,1024]{1,0:T(8,128)(2,1)S(1)} %get-tuple-element.57), channel_id=1, source_target_pairs={{0,12},{1,3},{2,14},{3,1},{4,8},{5,7},{6,10},{7,5},{8,4},{9,11},{1... | collective-permute-start | bytes 344072 | tf_op jit(solution)/shard_map/ppermute | solution.py:35
  19.4 8.5 %collective-permute-start.5 = (bf16[56,1024]{1,0:T(8,128)(2,1)S(1)}, bf16[56,1024]{1,0:T(8,128)(2,1)S(1)}, u32[]{:S(2)}, u32[]{:S(2)}) collective-permute-start(bf16[56,1024]{1,0:T(8,128)(2,1)S(1)} %get-tuple-element.59), channel_id=1, source_target_pairs={{0,10},{1,5},{2,8},{3,7},{4,14},{5,1},{6,12},{7,3},{8,2},{9,13},{1... | collective-permute-start | bytes 344072 | tf_op jit(solution)/shard_map/ppermute | solution.py:35
  21.6 9.1 %collective-permute-start.4 = (bf16[56,1024]{1,0:T(8,128)(2,1)S(1)}, bf16[56,1024]{1,0:T(8,128)(2,1)S(1)}, u32[]{:S(2)}, u32[]{:S(2)}) collective-permute-start(bf16[56,1024]{1,0:T(8,128)(2,1)S(1)} %get-tuple-element.58), channel_id=1, source_target_pairs={{0,14},{1,15},{2,12},{3,13},{4,10},{5,11},{6,8},{7,9},{8,6},{9,7},... | collective-permute-start | bytes 344072 | tf_op jit(solution)/shard_map/ppermute | solution.py:35
  22.3 9.4 %collective-permute-start.7 = (bf16[56,1024]{1,0:T(8,128)(2,1)S(1)}, bf16[56,1024]{1,0:T(8,128)(2,1)S(1)}, u32[]{:S(2)}, u32[]{:S(2)}) collective-permute-start(bf16[56,1024]{1,0:T(8,128)(2,1)S(1)} %get-tuple-element.62), channel_id=1, source_target_pairs={{0,6},{1,9},{2,4},{3,11},{4,2},{5,13},{6,0},{7,15},{8,14},{9,1},{1... | collective-permute-start | bytes 344072 | tf_op jit(solution)/shard_map/ppermute | solution.py:35
  24.7 7.0 %collective-permute-start.8 = (bf16[56,1024]{1,0:T(8,128)(2,1)S(1)}, bf16[56,1024]{1,0:T(8,128)(2,1)S(1)}, u32[]{:S(2)}, u32[]{:S(2)}) collective-permute-start(bf16[56,1024]{1,0:T(8,128)(2,1)S(1)} %get-tuple-element.63), channel_id=1, source_target_pairs={{0,8},{1,7},{2,10},{3,5},{4,12},{5,3},{6,14},{7,1},{8,0},{9,15},{1... | collective-permute-start | bytes 344072 | tf_op jit(solution)/shard_map/ppermute | solution.py:35
  26.0 7.2 %collective-permute-start.9 = (bf16[56,1024]{1,0:T(8,128)(2,1)S(1)}, bf16[56,1024]{1,0:T(8,128)(2,1)S(1)}, u32[]{:S(2)}, u32[]{:S(2)}) collective-permute-start(bf16[56,1024]{1,0:T(8,128)(2,1)S(1)} %get-tuple-element.64), channel_id=1, source_target_pairs={{0,2},{1,13},{2,0},{3,15},{4,6},{5,9},{6,4},{7,11},{8,10},{9,5},{1... | collective-permute-start | bytes 344072 | tf_op jit(solution)/shard_map/ppermute | solution.py:35
  27.9 5.2 %collective-permute-start.10 = (bf16[56,1024]{1,0:T(8,128)(2,1)S(1)}, bf16[56,1024]{1,0:T(8,128)(2,1)S(1)}, u32[]{:S(2)}, u32[]{:S(2)}) collective-permute-start(bf16[56,1024]{1,0:T(8,128)(2,1)S(1)} %get-tuple-element.65), channel_id=1, source_target_pairs={{0,4},{1,11},{2,6},{3,9},{4,0},{5,15},{6,2},{7,13},{8,12},{9,3},{1... | collective-permute-start | bytes 344072 | tf_op jit(solution)/shard_map/ppermute | solution.py:35
  33.1 19.5 %copy-start = (f32[32,2048]{1,0:T(8,128)S(1)}, f32[32,2048]{1,0:T(8,128)}, u32[]{:S(2)}) copy-start(f32[32,2048]{1,0:T(8,128)} %get-tuple-element.56.stream) | copy-start | bytes 786436
  38.0 7.2 %collective-permute-start.11 = (bf16[56,1024]{1,0:T(8,128)(2,1)S(1)}, bf16[56,1024]{1,0:T(8,128)(2,1)S(1)}, u32[]{:S(2)}, u32[]{:S(2)}) collective-permute-start(bf16[56,1024]{1,0:T(8,128)(2,1)S(1)} %get-tuple-element.75), channel_id=1, source_target_pairs={{0,12},{1,3},{2,14},{3,1},{4,8},{5,7},{6,10},{7,5},{8,4},{9,11},{1... | collective-permute-start | bytes 344072 | tf_op jit(solution)/shard_map/ppermute | solution.py:35
  39.5 8.4 %collective-permute-start.12 = (bf16[56,1024]{1,0:T(8,128)(2,1)S(1)}, bf16[56,1024]{1,0:T(8,128)(2,1)S(1)}, u32[]{:S(2)}, u32[]{:S(2)}) collective-permute-start(bf16[56,1024]{1,0:T(8,128)(2,1)S(1)} %get-tuple-element.76), channel_id=1, source_target_pairs={{0,14},{1,15},{2,12},{3,13},{4,10},{5,11},{6,8},{7,9},{8,6},{9,7},... | collective-permute-start | bytes 344072 | tf_op jit(solution)/shard_map/ppermute | solution.py:35
  41.3 7.7 %collective-permute-start.13 = (bf16[56,1024]{1,0:T(8,128)(2,1)S(1)}, bf16[56,1024]{1,0:T(8,128)(2,1)S(1)}, u32[]{:S(2)}, u32[]{:S(2)}) collective-permute-start(bf16[56,1024]{1,0:T(8,128)(2,1)S(1)} %get-tuple-element.77), channel_id=1, source_target_pairs={{0,10},{1,5},{2,8},{3,7},{4,14},{5,1},{6,12},{7,3},{8,2},{9,13},{1... | collective-permute-start | bytes 344072 | tf_op jit(solution)/shard_map/ppermute | solution.py:35
  43.4 7.4 %collective-permute-start.14 = (bf16[56,1024]{1,0:T(8,128)(2,1)S(1)}, bf16[56,1024]{1,0:T(8,128)(2,1)S(1)}, u32[]{:S(2)}, u32[]{:S(2)}) collective-permute-start(bf16[56,1024]{1,0:T(8,128)(2,1)S(1)} %get-tuple-element.78), channel_id=1, source_target_pairs={{0,6},{1,9},{2,4},{3,11},{4,2},{5,13},{6,0},{7,15},{8,14},{9,1},{1... | collective-permute-start | bytes 344072 | tf_op jit(solution)/shard_map/ppermute | solution.py:35
  44.1 7.3 %collective-permute-start.15 = (bf16[56,1024]{1,0:T(8,128)(2,1)S(1)}, bf16[56,1024]{1,0:T(8,128)(2,1)S(1)}, u32[]{:S(2)}, u32[]{:S(2)}) collective-permute-start(bf16[56,1024]{1,0:T(8,128)(2,1)S(1)} %get-tuple-element.79), channel_id=1, source_target_pairs={{0,8},{1,7},{2,10},{3,5},{4,12},{5,3},{6,14},{7,1},{8,0},{9,15},{1... | collective-permute-start | bytes 344072 | tf_op jit(solution)/shard_map/ppermute | solution.py:35
  45.2 6.6 %collective-permute-start.16 = (bf16[56,1024]{1,0:T(8,128)(2,1)S(1)}, bf16[56,1024]{1,0:T(8,128)(2,1)S(1)}, u32[]{:S(2)}, u32[]{:S(2)}) collective-permute-start(bf16[56,1024]{1,0:T(8,128)(2,1)S(1)} %get-tuple-element.80), channel_id=1, source_target_pairs={{0,2},{1,13},{2,0},{3,15},{4,6},{5,9},{6,4},{7,11},{8,10},{9,5},{1... | collective-permute-start | bytes 344072 | tf_op jit(solution)/shard_map/ppermute | solution.py:35
  47.8 4.8 %collective-permute-start.17 = (bf16[56,1024]{1,0:T(8,128)(2,1)S(1)}, bf16[56,1024]{1,0:T(8,128)(2,1)S(1)}, u32[]{:S(2)}, u32[]{:S(2)}) collective-permute-start(bf16[56,1024]{1,0:T(8,128)(2,1)S(1)} %get-tuple-element.81), channel_id=1, source_target_pairs={{0,4},{1,11},{2,6},{3,9},{4,0},{5,15},{6,2},{7,13},{8,12},{9,3},{1... | collective-permute-start | bytes 344072 | tf_op jit(solution)/shard_map/ppermute | solution.py:35
  53.1 7.6 %collective-permute-start.18 = (bf16[32,2048]{1,0:T(8,128)(2,1)S(1)}, bf16[32,2048]{1,0:T(8,128)(2,1)S(1)}, u32[]{:S(2)}, u32[]{:S(2)}) collective-permute-start(bf16[32,2048]{1,0:T(8,128)(2,1)S(1)} %get-tuple-element.84), channel_id=1, source_target_pairs={{0,16},{1,17},{2,18},{3,19},{4,20},{5,21},{6,22},{7,23},{8,24},{9,... | collective-permute-start | bytes 393224 | tf_op jit(solution)/shard_map/ppermute | solution.py:18

commit v10 on v9

--- a/solution.py
+++ b/solution.py
@@ -266,14 +266,14 @@
     rows, active = refs[2 * count + 6 :]
     size, middle = blocks[0].shape
     full, rest = whole_tiles(size)
-    given = [block[...].astype(F32) for block in blocks]
+    given = [block[...] for block in blocks]
+    ends = [g[2 * full :].astype(F32) for g in given]
     for q in range(2):
         parts = [g[q * full : (q + 1) * full] for g in given]
         if rest:
-            parts += [
-                joined(*[g[2 * full :] for g in given[m : m + 2]])[q] for m in range(0, count, 2)
-            ]
-        rows[:, q * middle : (q + 1) * middle] = jnp.concatenate(parts, axis=0).astype(BF16)
+            pairs = [joined(*ends[m : m + 2])[q] for m in range(0, count, 2)]
+            parts.append(jnp.concatenate(pairs, axis=0).astype(BF16))
+        rows[:, q * middle : (q + 1) * middle] = jnp.concatenate(parts, axis=0)
     for half in range(2):
         w_gate, w_up = weights[3 * half : 3 * half + 2]
         gate = lax.dot_general(rows[...], w_gate[...], NT, preferred_element_type=F32)
@@ -330,8 +330,10 @@
 def combine_kernel(high, low, stream, *refs):
     blocks, (here, there) = refs[:-2], refs[-2:]
     rows = jnp.concatenate([block[...] for block in blocks], axis=0)
-    total = jnp.dot(high[...], rows, preferred_element_type=F32)
-    total = total + jnp.dot(low[...], rows, preferred_element_type=F32)
+    both = high.shape[0]
+    weights = jnp.concatenate([high[...], low[...]], axis=0)
+    total = jnp.dot(weights, rows, preferred_element_type=F32)
+    total = total[:both] + total[both:]
     tokens, middle = here.shape[0], rows.shape[1]
     for q in range(2):
         columns = slice(q * middle, (q + 1) * middle)

time: 61.5 us -> 61.5 us (level)
  no operation moved by 1% of the time
where the time goes in v10:
time: 61.5 us; the launch traced here: 61.3 us
  starting transfers between devices  26.3 us (43%)
  waiting for transfers between devices  17.2 us (28%)
  Pallas kernels  17 us (28%)
  other arithmetic  0.69 us (1%)
    ppermute x14, starting transfers between devices, exchanged(): got[i] = lax.ppermute(blocks[i], 'ep', pairs)  18.4 us
    ppermute x14, waiting for transfers between devices, exchanged(): got[i] = lax.ppermute(blocks[i], 'ep', pairs)  9.04 us
    ppermute x5, waiting for transfers between devices, swapped(): return lax.ppermute(value, 'ep', pairs)  8.14 us
    ppermute x5, starting transfers between devices, swapped(): return lax.ppermute(value, 'ep', pairs)  7.94 us
    pallas_call x2, Pallas kernels, load(): pl.pallas_call(load_kernel, in_specs=[pl.BlockSpec(memory_space=pl.ANY)]...  6.29 us
    pallas_call x1, Pallas kernels, run_expert(): pl.pallas_call(functools.partial(expert_kernel, count), in_specs=[whole()...  4.86 us
    pallas_call x1, Pallas kernels, attend(): pl.pallas_call(functools.partial(attend_kernel, heads), in_specs=[pl.Bloc...  4.68 us
  transfers between devices with their start and end apart: 19, of which 12 were waited for; matrix products, arithmetic and copies ran while one was open for 0% of the time, Pallas kernels for 19%

profile of v10, /device:TPU:0, one launch (start us, length us, event | category | flops | bytes accessed | tf_op | source)
XLA Modules:
  0.0 61.3 jit_solution(6336526290399499362)
XLA Ops:
  0.0 0.5 collective-permute-start.1
  1.0 4.7 %shard_map.136 = (f32[32,2048]{1,0:T(8,128)}, bf16[32,2176]{1,0:T(8,128)(2,1)}) custom-call(s32[4]{0:T(128)} %refs_0_.1, bf16[4,8,576]{2,1,0:T(8,128)(2,1)} %refs_1_.1, bf16[4,128,576]{2,1,0:T(8,128)(2,1)} %bitcast.21, bf16[4,576,384]{2,1,0:T(8,128)(2,1)} %bitcast.20, bf16[16,512,128]{2,1,0:T(8,128)(2,1)} %refs_4_.1, bf16[32,2048]{1,0:T(8,128)(2,1)} %refs_5_.1, ...), custom_call_target="tpu_custom_call" | custom-call | flops 494927872 | bytes 6291456 | tf_op jit(solution)/shard_map/pallas_call | solution.py:148
  5.7 3.7 %collective-permute-start = (bf16[32,2176]{1,0:T(8,128)(2,1)}, bf16[32,2176]{1,0:T(8,128)(2,1)S(1)}, u32[]{:S(2)}, u32[]{:S(2)}) collective-permute-start(bf16[32,2176]{1,0:T(8,128)(2,1)} %get-tuple-element.46.here), channel_id=1, source_target_pairs={{0,16},{1,17},{2,18},{3,19},{4,20},{5,21},{6,22},{7,23},{8,24},{9,... | collective-permute-start | bytes 417800 | tf_op jit(solution)/shard_map/ppermute | solution.py:18
  9.5 3.6 %shard_map.137 = (bf16[704,2048]{1,0:T(8,128)(2,1)S(1)}, bf16[704,2048]{1,0:T(8,128)(2,1)S(1)}, bf16[704,2048]{1,0:T(8,128)(2,1)S(1)}) custom-call(bf16[704,2048]{1,0:T(8,128)(2,1)} %bitcast.15, bf16[704,2048]{1,0:T(8,128)(2,1)} %bitcast.17, bf16[704,2048]{1,0:T(8,128)(2,1)} %bitcast.19), custom_call_target="tpu_custom_call" | custom-call | bytes 17301504 | tf_op jit(solution)/shard_map/pallas_call | solution.py:250
  13.1 3.8 %collective-permute-done.there = bf16[32,2176]{1,0:T(8,128)(2,1)S(1)} collective-permute-done((bf16[32,2176]{1,0:T(8,128)(2,1)}, bf16[32,2176]{1,0:T(8,128)(2,1)S(1)}, u32[]{:S(2)}, u32[]{:S(2)}) %collective-permute-start) | collective-permute-done | bytes 139296 | tf_op jit(solution)/shard_map/ppermute | solution.py:18
  16.9 0.7 %shard_map.138 = (bf16[128,448]{1,0:T(8,128)(2,1)S(1)}, bf16[128,448]{1,0:T(8,128)(2,1)S(1)}, bf16[56,1024]{1,0:T(8,128)(2,1)S(1)}, bf16[56,1024]{1,0:T(8,128)(2...) custom-call(f32[8,1]{1,0:T(8,128)S(1)} %copy.15.mine, ...), custom_call_target="tpu_custom_call" | custom-call | flops 117440512 | bytes 1572864 | tf_op jit(solution)/shard_map/pallas_call | solution.py:223
  17.6 1.9 %collective-permute-start.3 = (bf16[56,1024]{1,0:T(8,128)(2,1)S(1)}, bf16[56,1024]{1,0:T(8,128)(2,1)S(1)}, u32[]{:S(2)}, u32[]{:S(2)}) collective-permute-start(bf16[56,1024]{1,0:T(8,128)(2,1)S(1)} %get-tuple-element.57), channel_id=1, source_target_pairs={{0,12},{1,3},{2,14},{3,1},{4,8},{5,7},{6,10},{7,5},{8,4},{9,11},{1... | collective-permute-start | bytes 344072 | tf_op jit(solution)/shard_map/ppermute | solution.py:35
  19.4 2.2 %collective-permute-start.5 = (bf16[56,1024]{1,0:T(8,128)(2,1)S(1)}, bf16[56,1024]{1,0:T(8,128)(2,1)S(1)}, u32[]{:S(2)}, u32[]{:S(2)}) collective-permute-start(bf16[56,1024]{1,0:T(8,128)(2,1)S(1)} %get-tuple-element.59), channel_id=1, source_target_pairs={{0,10},{1,5},{2,8},{3,7},{4,14},{5,1},{6,12},{7,3},{8,2},{9,13},{1... | collective-permute-start | bytes 344072 | tf_op jit(solution)/shard_map/ppermute | solution.py:35
  21.6 0.7 %collective-permute-start.4 = (bf16[56,1024]{1,0:T(8,128)(2,1)S(1)}, bf16[56,1024]{1,0:T(8,128)(2,1)S(1)}, u32[]{:S(2)}, u32[]{:S(2)}) collective-permute-start(bf16[56,1024]{1,0:T(8,128)(2,1)S(1)} %get-tuple-element.58), channel_id=1, source_target_pairs={{0,14},{1,15},{2,12},{3,13},{4,10},{5,11},{6,8},{7,9},{8,6},{9,7},... | collective-permute-start | bytes 344072 | tf_op jit(solution)/shard_map/ppermute | solution.py:35
  22.3 2.4 %collective-permute-start.7 = (bf16[56,1024]{1,0:T(8,128)(2,1)S(1)}, bf16[56,1024]{1,0:T(8,128)(2,1)S(1)}, u32[]{:S(2)}, u32[]{:S(2)}) collective-permute-start(bf16[56,1024]{1,0:T(8,128)(2,1)S(1)} %get-tuple-element.62), channel_id=1, source_target_pairs={{0,6},{1,9},{2,4},{3,11},{4,2},{5,13},{6,0},{7,15},{8,14},{9,1},{1... | collective-permute-start | bytes 344072 | tf_op jit(solution)/shard_map/ppermute | solution.py:35
  24.7 1.3 %collective-permute-start.8 = (bf16[56,1024]{1,0:T(8,128)(2,1)S(1)}, bf16[56,1024]{1,0:T(8,128)(2,1)S(1)}, u32[]{:S(2)}, u32[]{:S(2)}) collective-permute-start(bf16[56,1024]{1,0:T(8,128)(2,1)S(1)} %get-tuple-element.63), channel_id=1, source_target_pairs={{0,8},{1,7},{2,10},{3,5},{4,12},{5,3},{6,14},{7,1},{8,0},{9,15},{1... | collective-permute-start | bytes 344072 | tf_op jit(solution)/shard_map/ppermute | solution.py:35
  26.0 0.5 collective-permute-start.9
  26.5 1.4 %collective-permute-done.5.refs_2_ = bf16[56,1024]{1,0:T(8,128)(2,1)S(1)} collective-permute-done((bf16[56,1024]{1,0:T(8,128)(2,1)S(1)}, bf16[56,1024]{1,0:T(8,128)(2,1)S(1)}, u32[]{:S(2)}, u32[]{:S(2)}) %collective-permute-start.5) | collective-permute-done | bytes 114720 | tf_op jit(solution)/shard_map/ppermute | solution.py:35
  27.9 2.7 %shard_map.139 = (bf16[704,2048]{1,0:T(8,128)(2,1)S(1)}, bf16[704,2048]{1,0:T(8,128)(2,1)S(1)}) custom-call(bf16[704,2048]{1,0:T(8,128)(2,1)} %collective-permute-done.2.refs_0_, bf16[704,2048]{1,0:T(8,128)(2,1)} %collective-permute-done.6.refs_1_), custom_call_target="tpu_custom_call" | custom-call | bytes 11534336 | tf_op jit(solution)/shard_map/pallas_call | solution.py:250
  30.7 1.0 %collective-permute-done.7.refs_3_ = bf16[56,1024]{1,0:T(8,128)(2,1)S(1)} collective-permute-done((bf16[56,1024]{1,0:T(8,128)(2,1)S(1)}, bf16[56,1024]{1,0:T(8,128)(2,1)S(1)}, u32[]{:S(2)}, u32[]{:S(2)}) %collective-permute-start.7) | collective-permute-done | bytes 114720 | tf_op jit(solution)/shard_map/ppermute | solution.py:35
  31.8 1.4 %collective-permute-done.9.refs_5_ = bf16[56,1024]{1,0:T(8,128)(2,1)S(1)} collective-permute-done((bf16[56,1024]{1,0:T(8,128)(2,1)S(1)}, bf16[56,1024]{1,0:T(8,128)(2,1)S(1)}, u32[]{:S(2)}, u32[]{:S(2)}) %collective-permute-start.9) | collective-permute-done | bytes 114720 | tf_op jit(solution)/shard_map/ppermute | solution.py:35
  33.2 4.9 %shard_map.140 = (bf16[56,1024]{1,0:T(8,128)(2,1)S(1)}, bf16[56,1024]{1,0:T(8,128)(2,1)S(1)}, bf16[56,1024]{1,0:T(8,128)(2,1)S(1)}, bf16[56,1024]{1,0:T(8,128)(2...) custom-call(bf16[56,1024]{1,0:T(8,128)(2,1)S(1)} %collective-permute, ...), custom_call_target="tpu_custom_call" | custom-call | flops 3875536896 | bytes 17301504 | tf_op jit(solution)/shard_map/pallas_call | solution.py:312
  38.0 1.4 %collective-permute-start.11 = (bf16[56,1024]{1,0:T(8,128)(2,1)S(1)}, bf16[56,1024]{1,0:T(8,128)(2,1)S(1)}, u32[]{:S(2)}, u32[]{:S(2)}) collective-permute-start(bf16[56,1024]{1,0:T(8,128)(2,1)S(1)} %get-tuple-element.75), channel_id=1, source_target_pairs={{0,12},{1,3},{2,14},{3,1},{4,8},{5,7},{6,10},{7,5},{8,4},{9,11},{1... | collective-permute-start | bytes 344072 | tf_op jit(solution)/shard_map/ppermute | solution.py:35
  39.5 1.8 %collective-permute-start.12 = (bf16[56,1024]{1,0:T(8,128)(2,1)S(1)}, bf16[56,1024]{1,0:T(8,128)(2,1)S(1)}, u32[]{:S(2)}, u32[]{:S(2)}) collective-permute-start(bf16[56,1024]{1,0:T(8,128)(2,1)S(1)} %get-tuple-element.76), channel_id=1, source_target_pairs={{0,14},{1,15},{2,12},{3,13},{4,10},{5,11},{6,8},{7,9},{8,6},{9,7},... | collective-permute-start | bytes 344072 | tf_op jit(solution)/shard_map/ppermute | solution.py:35
  41.3 2.0 %collective-permute-start.13 = (bf16[56,1024]{1,0:T(8,128)(2,1)S(1)}, bf16[56,1024]{1,0:T(8,128)(2,1)S(1)}, u32[]{:S(2)}, u32[]{:S(2)}) collective-permute-start(bf16[56,1024]{1,0:T(8,128)(2,1)S(1)} %get-tuple-element.77), channel_id=1, source_target_pairs={{0,10},{1,5},{2,8},{3,7},{4,14},{5,1},{6,12},{7,3},{8,2},{9,13},{1... | collective-permute-start | bytes 344072 | tf_op jit(solution)/shard_map/ppermute | solution.py:35
  43.3 0.8 %collective-permute-start.14 = (bf16[56,1024]{1,0:T(8,128)(2,1)S(1)}, bf16[56,1024]{1,0:T(8,128)(2,1)S(1)}, u32[]{:S(2)}, u32[]{:S(2)}) collective-permute-start(bf16[56,1024]{1,0:T(8,128)(2,1)S(1)} %get-tuple-element.78), channel_id=1, source_target_pairs={{0,6},{1,9},{2,4},{3,11},{4,2},{5,13},{6,0},{7,15},{8,14},{9,1},{1... | collective-permute-start | bytes 344072 | tf_op jit(solution)/shard_map/ppermute | solution.py:35
  44.1 1.1 %collective-permute-start.15 = (bf16[56,1024]{1,0:T(8,128)(2,1)S(1)}, bf16[56,1024]{1,0:T(8,128)(2,1)S(1)}, u32[]{:S(2)}, u32[]{:S(2)}) collective-permute-start(bf16[56,1024]{1,0:T(8,128)(2,1)S(1)} %get-tuple-element.79), channel_id=1, source_target_pairs={{0,8},{1,7},{2,10},{3,5},{4,12},{5,3},{6,14},{7,1},{8,0},{9,15},{1... | collective-permute-start | bytes 344072 | tf_op jit(solution)/shard_map/ppermute | solution.py:35
  45.2 1.5 %collective-permute-start.16 = (bf16[56,1024]{1,0:T(8,128)(2,1)S(1)}, bf16[56,1024]{1,0:T(8,128)(2,1)S(1)}, u32[]{:S(2)}, u32[]{:S(2)}) collective-permute-start(bf16[56,1024]{1,0:T(8,128)(2,1)S(1)} %get-tuple-element.80), channel_id=1, source_target_pairs={{0,2},{1,13},{2,0},{3,15},{4,6},{5,9},{6,4},{7,11},{8,10},{9,5},{1... | collective-permute-start | bytes 344072 | tf_op jit(solution)/shard_map/ppermute | solution.py:35
  46.7 1.1 %collective-permute-done.12.refs_1_ = bf16[56,1024]{1,0:T(8,128)(2,1)S(1)} collective-permute-done((bf16[56,1024]{1,0:T(8,128)(2,1)S(1)}, bf16[56,1024]{1,0:T(8,128)(2,1)S(1)}, u32[]{:S(2)}, u32[]{:S(2)}) %collective-permute-start.12) | collective-permute-done | bytes 114720 | tf_op jit(solution)/shard_map/ppermute | solution.py:35
  47.8 0.8 %collective-permute-start.17 = (bf16[56,1024]{1,0:T(8,128)(2,1)S(1)}, bf16[56,1024]{1,0:T(8,128)(2,1)S(1)}, u32[]{:S(2)}, u32[]{:S(2)}) collective-permute-start(bf16[56,1024]{1,0:T(8,128)(2,1)S(1)} %get-tuple-element.81), channel_id=1, source_target_pairs={{0,4},{1,11},{2,6},{3,9},{4,0},{5,15},{6,2},{7,13},{8,12},{9,3},{1... | collective-permute-start | bytes 344072 | tf_op jit(solution)/shard_map/ppermute | solution.py:35
  48.6 0.4 collective-permute-done.13.refs_2_
  49.0 1.7 %collective-permute-done.14.refs_3_ = bf16[56,1024]{1,0:T(8,128)(2,1)S(1)} collective-permute-done((bf16[56,1024]{1,0:T(8,128)(2,1)S(1)}, bf16[56,1024]{1,0:T(8,128)(2,1)S(1)}, u32[]{:S(2)}, u32[]{:S(2)}) %collective-permute-start.14) | collective-permute-done | bytes 114720 | tf_op jit(solution)/shard_map/ppermute | solution.py:35
  50.8 0.7 %collective-permute-done.15.refs_4_ = bf16[56,1024]{1,0:T(8,128)(2,1)S(1)} collective-permute-done((bf16[56,1024]{1,0:T(8,128)(2,1)S(1)}, bf16[56,1024]{1,0:T(8,128)(2,1)S(1)}, u32[]{:S(2)}, u32[]{:S(2)}) %collective-permute-start.15) | collective-permute-done | bytes 114720 | tf_op jit(solution)/shard_map/ppermute | solution.py:35
  51.8 0.8 %collective-permute-done.17.refs_6_ = bf16[56,1024]{1,0:T(8,128)(2,1)S(1)} collective-permute-done((bf16[56,1024]{1,0:T(8,128)(2,1)S(1)}, bf16[56,1024]{1,0:T(8,128)(2,1)S(1)}, u32[]{:S(2)}, u32[]{:S(2)}) %collective-permute-start.17) | collective-permute-done | bytes 114720 | tf_op jit(solution)/shard_map/ppermute | solution.py:35
  53.0 3.2 %collective-permute-start.18 = (bf16[32,2048]{1,0:T(8,128)(2,1)S(1)}, bf16[32,2048]{1,0:T(8,128)(2,1)S(1)}, u32[]{:S(2)}, u32[]{:S(2)}) collective-permute-start(bf16[32,2048]{1,0:T(8,128)(2,1)S(1)} %get-tuple-element.84), channel_id=1, source_target_pairs={{0,16},{1,17},{2,18},{3,19},{4,20},{5,21},{6,22},{7,23},{8,24},{9,... | collective-permute-start | bytes 393224 | tf_op jit(solution)/shard_map/ppermute | solution.py:18
  56.3 4.4 %collective-permute-done.18 = bf16[32,2048]{1,0:T(8,128)(2,1)S(1)} collective-permute-done((bf16[32,2048]{1,0:T(8,128)(2,1)S(1)}, bf16[32,2048]{1,0:T(8,128)(2,1)S(1)}, u32[]{:S(2)}, u32[]{:S(2)}) %collective-permute-start.18) | collective-permute-done | bytes 131104 | tf_op jit(solution)/shard_map/ppermute | solution.py:18
  60.6 0.7 %add_convert_fusion = bf16[32,2048]{1,0:T(8,128)(2,1)} fusion(f32[32,2048]{1,0:T(8,128)S(1)} %get-tuple-element.83, bf16[32,2048]{1,0:T(8,128)(2,1)S(1)} %collective-permute-done.18), kind=kLoop, calls=%fused_computation | loop fusion | flops 196608 | bytes 524288 | tf_op jit(solution)/shard_map/convert_element_type | solution.py:400
  (23 shorter events, 1.6 us)
Async XLA Ops:
  0.0 9.4 %copy-start.2 = (s32[8]{0:T(128)S(1)}, s32[8]{0:T(128)}, u32[]{:S(2)}) copy-start(s32[8]{0:T(128)} %constant.34.clone) | copy-start | bytes 100
  0.0 9.4 %copy-start.3 = (s32[8]{0:T(128)S(1)}, s32[8]{0:T(128)}, u32[]{:S(2)}) copy-start(s32[8]{0:T(128)} %constant.33.clone) | copy-start | bytes 100
  0.0 16.9 %collective-permute-start.1 = (bf16[704,2048]{1,0:T(8,128)(2,1)}, bf16[704,2048]{1,0:T(8,128)(2,1)S(1)}, u32[]{:S(2)}, u32[]{:S(2)}) collective-permute-start(bf16[704,2048]{1,0:T(8,128)(2,1)} %bitcast.14), channel_id=1, source_target_pairs={{0,1},{1,0},{2,3},{3,2},{4,5},{5,4},{6,7},{7,6},{8,9},{9,8},{10,11... | collective-permute-start | bytes 8650760 | tf_op jit(solution)/shard_map/ppermute | solution.py:18
  0.5 16.4 %collective-permute-start.2 = (bf16[704,2048]{1,0:T(8,128)(2,1)}, bf16[704,2048]{1,0:T(8,128)(2,1)}, u32[]{:S(2)}, u32[]{:S(2)}) collective-permute-start(bf16[704,2048]{1,0:T(8,128)(2,1)} %bitcast.16), channel_id=1, source_target_pairs={{0,1},{1,0},{2,3},{3,2},{4,5},{5,4},{6,7},{7,6},{8,9},{9,8},{10,11... | collective-permute-start | bytes 8650760 | tf_op jit(solution)/shard_map/ppermute | solution.py:18
  0.5 24.2 %collective-permute-start.6 = (bf16[704,2048]{1,0:T(8,128)(2,1)}, bf16[704,2048]{1,0:T(8,128)(2,1)}, u32[]{:S(2)}, u32[]{:S(2)}) collective-permute-start(bf16[704,2048]{1,0:T(8,128)(2,1)} %bitcast.18), channel_id=1, source_target_pairs={{0,1},{1,0},{2,3},{3,2},{4,5},{5,4},{6,7},{7,6},{8,9},{9,8},{10,11... | collective-permute-start | bytes 8650760 | tf_op jit(solution)/shard_map/ppermute | solution.py:18
  5.7 11.2 %collective-permute-start = (bf16[32,2176]{1,0:T(8,128)(2,1)}, bf16[32,2176]{1,0:T(8,128)(2,1)S(1)}, u32[]{:S(2)}, u32[]{:S(2)}) collective-permute-start(bf16[32,2176]{1,0:T(8,128)(2,1)} %get-tuple-element.46.here), channel_id=1, source_target_pairs={{0,16},{1,17},{2,18},{3,19},{4,20},{5,21},{6,22},{7,23},{8,24},{9,... | collective-permute-start | bytes 417800 | tf_op jit(solution)/shard_map/ppermute | solution.py:18
  9.5 7.4 %copy-start.1 = (bf16[32,2176]{1,0:T(8,128)(2,1)S(1)}, bf16[32,2176]{1,0:T(8,128)(2,1)}, u32[]{:S(2)}) copy-start(bf16[32,2176]{1,0:T(8,128)(2,1)} %get-tuple-element.46.here) | copy-start | bytes 417796
  17.6 8.4 %collective-permute-start.3 = (bf16[56,1024]{1,0:T(8,128)(2,1)S(1)}, bf16[56,1024]{1,0:T(8,128)(2,1)S(1)}, u32[]{:S(2)}, u32[]{:S(2)}) collective-permute-start(bf16[56,1024]{1,0:T(8,128)(2,1)S(1)} %get-tuple-element.57), channel_id=1, source_target_pairs={{0,12},{1,3},{2,14},{3,1},{4,8},{5,7},{6,10},{7,5},{8,4},{9,11},{1... | collective-permute-start | bytes 344072 | tf_op jit(solution)/shard_map/ppermute | solution.py:35
  19.4 8.5 %collective-permute-start.5 = (bf16[56,1024]{1,0:T(8,128)(2,1)S(1)}, bf16[56,1024]{1,0:T(8,128)(2,1)S(1)}, u32[]{:S(2)}, u32[]{:S(2)}) collective-permute-start(bf16[56,1024]{1,0:T(8,128)(2,1)S(1)} %get-tuple-element.59), channel_id=1, source_target_pairs={{0,10},{1,5},{2,8},{3,7},{4,14},{5,1},{6,12},{7,3},{8,2},{9,13},{1... | collective-permute-start | bytes 344072 | tf_op jit(solution)/shard_map/ppermute | solution.py:35
  21.6 9.1 %collective-permute-start.4 = (bf16[56,1024]{1,0:T(8,128)(2,1)S(1)}, bf16[56,1024]{1,0:T(8,128)(2,1)S(1)}, u32[]{:S(2)}, u32[]{:S(2)}) collective-permute-start(bf16[56,1024]{1,0:T(8,128)(2,1)S(1)} %get-tuple-element.58), channel_id=1, source_target_pairs={{0,14},{1,15},{2,12},{3,13},{4,10},{5,11},{6,8},{7,9},{8,6},{9,7},... | collective-permute-start | bytes 344072 | tf_op jit(solution)/shard_map/ppermute | solution.py:35
  22.3 9.4 %collective-permute-start.7 = (bf16[56,1024]{1,0:T(8,128)(2,1)S(1)}, bf16[56,1024]{1,0:T(8,128)(2,1)S(1)}, u32[]{:S(2)}, u32[]{:S(2)}) collective-permute-start(bf16[56,1024]{1,0:T(8,128)(2,1)S(1)} %get-tuple-element.62), channel_id=1, source_target_pairs={{0,6},{1,9},{2,4},{3,11},{4,2},{5,13},{6,0},{7,15},{8,14},{9,1},{1... | collective-permute-start | bytes 344072 | tf_op jit(solution)/shard_map/ppermute | solution.py:35
  24.7 7.0 %collective-permute-start.8 = (bf16[56,1024]{1,0:T(8,128)(2,1)S(1)}, bf16[56,1024]{1,0:T(8,128)(2,1)S(1)}, u32[]{:S(2)}, u32[]{:S(2)}) collective-permute-start(bf16[56,1024]{1,0:T(8,128)(2,1)S(1)} %get-tuple-element.63), channel_id=1, source_target_pairs={{0,8},{1,7},{2,10},{3,5},{4,12},{5,3},{6,14},{7,1},{8,0},{9,15},{1... | collective-permute-start | bytes 344072 | tf_op jit(solution)/shard_map/ppermute | solution.py:35
  26.0 7.2 %collective-permute-start.9 = (bf16[56,1024]{1,0:T(8,128)(2,1)S(1)}, bf16[56,1024]{1,0:T(8,128)(2,1)S(1)}, u32[]{:S(2)}, u32[]{:S(2)}) collective-permute-start(bf16[56,1024]{1,0:T(8,128)(2,1)S(1)} %get-tuple-element.64), channel_id=1, source_target_pairs={{0,2},{1,13},{2,0},{3,15},{4,6},{5,9},{6,4},{7,11},{8,10},{9,5},{1... | collective-permute-start | bytes 344072 | tf_op jit(solution)/shard_map/ppermute | solution.py:35
  27.9 5.2 %collective-permute-start.10 = (bf16[56,1024]{1,0:T(8,128)(2,1)S(1)}, bf16[56,1024]{1,0:T(8,128)(2,1)S(1)}, u32[]{:S(2)}, u32[]{:S(2)}) collective-permute-start(bf16[56,1024]{1,0:T(8,128)(2,1)S(1)} %get-tuple-element.65), channel_id=1, source_target_pairs={{0,4},{1,11},{2,6},{3,9},{4,0},{5,15},{6,2},{7,13},{8,12},{9,3},{1... | collective-permute-start | bytes 344072 | tf_op jit(solution)/shard_map/ppermute | solution.py:35
  33.1 19.4 %copy-start = (f32[32,2048]{1,0:T(8,128)S(1)}, f32[32,2048]{1,0:T(8,128)}, u32[]{:S(2)}) copy-start(f32[32,2048]{1,0:T(8,128)} %get-tuple-element.56.stream) | copy-start | bytes 786436
  38.0 7.2 %collective-permute-start.11 = (bf16[56,1024]{1,0:T(8,128)(2,1)S(1)}, bf16[56,1024]{1,0:T(8,128)(2,1)S(1)}, u32[]{:S(2)}, u32[]{:S(2)}) collective-permute-start(bf16[56,1024]{1,0:T(8,128)(2,1)S(1)} %get-tuple-element.75), channel_id=1, source_target_pairs={{0,12},{1,3},{2,14},{3,1},{4,8},{5,7},{6,10},{7,5},{8,4},{9,11},{1... | collective-permute-start | bytes 344072 | tf_op jit(solution)/shard_map/ppermute | solution.py:35
  39.5 8.3 %collective-permute-start.12 = (bf16[56,1024]{1,0:T(8,128)(2,1)S(1)}, bf16[56,1024]{1,0:T(8,128)(2,1)S(1)}, u32[]{:S(2)}, u32[]{:S(2)}) collective-permute-start(bf16[56,1024]{1,0:T(8,128)(2,1)S(1)} %get-tuple-element.76), channel_id=1, source_target_pairs={{0,14},{1,15},{2,12},{3,13},{4,10},{5,11},{6,8},{7,9},{8,6},{9,7},... | collective-permute-start | bytes 344072 | tf_op jit(solution)/shard_map/ppermute | solution.py:35
  41.3 7.7 %collective-permute-start.13 = (bf16[56,1024]{1,0:T(8,128)(2,1)S(1)}, bf16[56,1024]{1,0:T(8,128)(2,1)S(1)}, u32[]{:S(2)}, u32[]{:S(2)}) collective-permute-start(bf16[56,1024]{1,0:T(8,128)(2,1)S(1)} %get-tuple-element.77), channel_id=1, source_target_pairs={{0,10},{1,5},{2,8},{3,7},{4,14},{5,1},{6,12},{7,3},{8,2},{9,13},{1... | collective-permute-start | bytes 344072 | tf_op jit(solution)/shard_map/ppermute | solution.py:35
  43.3 7.4 %collective-permute-start.14 = (bf16[56,1024]{1,0:T(8,128)(2,1)S(1)}, bf16[56,1024]{1,0:T(8,128)(2,1)S(1)}, u32[]{:S(2)}, u32[]{:S(2)}) collective-permute-start(bf16[56,1024]{1,0:T(8,128)(2,1)S(1)} %get-tuple-element.78), channel_id=1, source_target_pairs={{0,6},{1,9},{2,4},{3,11},{4,2},{5,13},{6,0},{7,15},{8,14},{9,1},{1... | collective-permute-start | bytes 344072 | tf_op jit(solution)/shard_map/ppermute | solution.py:35
  44.1 7.3 %collective-permute-start.15 = (bf16[56,1024]{1,0:T(8,128)(2,1)S(1)}, bf16[56,1024]{1,0:T(8,128)(2,1)S(1)}, u32[]{:S(2)}, u32[]{:S(2)}) collective-permute-start(bf16[56,1024]{1,0:T(8,128)(2,1)S(1)} %get-tuple-element.79), channel_id=1, source_target_pairs={{0,8},{1,7},{2,10},{3,5},{4,12},{5,3},{6,14},{7,1},{8,0},{9,15},{1... | collective-permute-start | bytes 344072 | tf_op jit(solution)/shard_map/ppermute | solution.py:35
  45.2 6.6 %collective-permute-start.16 = (bf16[56,1024]{1,0:T(8,128)(2,1)S(1)}, bf16[56,1024]{1,0:T(8,128)(2,1)S(1)}, u32[]{:S(2)}, u32[]{:S(2)}) collective-permute-start(bf16[56,1024]{1,0:T(8,128)(2,1)S(1)} %get-tuple-element.80), channel_id=1, source_target_pairs={{0,2},{1,13},{2,0},{3,15},{4,6},{5,9},{6,4},{7,11},{8,10},{9,5},{1... | collective-permute-start | bytes 344072 | tf_op jit(solution)/shard_map/ppermute | solution.py:35
  47.8 4.8 %collective-permute-start.17 = (bf16[56,1024]{1,0:T(8,128)(2,1)S(1)}, bf16[56,1024]{1,0:T(8,128)(2,1)S(1)}, u32[]{:S(2)}, u32[]{:S(2)}) collective-permute-start(bf16[56,1024]{1,0:T(8,128)(2,1)S(1)} %get-tuple-element.81), channel_id=1, source_target_pairs={{0,4},{1,11},{2,6},{3,9},{4,0},{5,15},{6,2},{7,13},{8,12},{9,3},{1... | collective-permute-start | bytes 344072 | tf_op jit(solution)/shard_map/ppermute | solution.py:35
  53.0 7.6 %collective-permute-start.18 = (bf16[32,2048]{1,0:T(8,128)(2,1)S(1)}, bf16[32,2048]{1,0:T(8,128)(2,1)S(1)}, u32[]{:S(2)}, u32[]{:S(2)}) collective-permute-start(bf16[32,2048]{1,0:T(8,128)(2,1)S(1)} %get-tuple-element.84), channel_id=1, source_target_pairs={{0,16},{1,17},{2,18},{3,19},{4,20},{5,21},{6,22},{7,23},{8,24},{9,... | collective-permute-start | bytes 393224 | tf_op jit(solution)/shard_map/ppermute | solution.py:18

commit v11 on v10

--- a/solution.py
+++ b/solution.py
@@ -69,13 +69,12 @@
             [drafts[r].astype(F32), jnp.zeros((columns - slots - draft, width), F32)], axis=0
         )
         cache[r, :, slots:] = d.T.astype(BF16)
-    for start in range(0, reqs, 2):
-        some = range(start, min(reqs, start + 2))
+    for start in range(0, reqs, 4):
+        some = range(start, min(reqs, start + 4))
         scores, probs = {}, {}
         for r in some:
             copies[2, r].wait()
             copies[3, r].wait()
-        for r in some:
             score = jnp.dot(queries[r], cache[r], preferred_element_type=F32) * scale
             scores[r] = jnp.where((place < lengths[r]) | causal, score, -1e30)
         for r in some:

time: 61.5 us -> 61.5 us (level)
  no operation moved by 1% of the time
where the time goes in v11:
time: 61.5 us; the launch traced here: 61.3 us
  starting transfers between devices  26.3 us (43%)
  waiting for transfers between devices  17.2 us (28%)
  Pallas kernels  16.9 us (27%)
  other arithmetic  0.69 us (1%)
    ppermute x14, starting transfers between devices, exchanged(): got[i] = lax.ppermute(blocks[i], 'ep', pairs)  18.4 us
    ppermute x14, waiting for transfers between devices, exchanged(): got[i] = lax.ppermute(blocks[i], 'ep', pairs)  9.03 us
    ppermute x5, waiting for transfers between devices, swapped(): return lax.ppermute(value, 'ep', pairs)  8.2 us
    ppermute x5, starting transfers between devices, swapped(): return lax.ppermute(value, 'ep', pairs)  7.91 us
    pallas_call x2, Pallas kernels, load(): pl.pallas_call(load_kernel, in_specs=[pl.BlockSpec(memory_space=pl.ANY)]...  6.29 us
    pallas_call x1, Pallas kernels, run_expert(): pl.pallas_call(functools.partial(expert_kernel, count), in_specs=[whole()...  4.88 us
    pallas_call x1, Pallas kernels, attend(): pl.pallas_call(functools.partial(attend_kernel, heads), in_specs=[pl.Bloc...  4.65 us
  transfers between devices with their start and end apart: 19, of which 12 were waited for; matrix products, arithmetic and copies ran while one was open for 0% of the time, Pallas kernels for 19%

profile of v11, /device:TPU:0, one launch (start us, length us, event | category | flops | bytes accessed | tf_op | source)
XLA Modules:
  0.0 61.3 jit_solution(11014426868306324722)
XLA Ops:
  0.0 0.5 collective-permute-start.1
  0.5 0.4 collective-permute-start.6
  1.0 4.7 %shard_map.136 = (f32[32,2048]{1,0:T(8,128)}, bf16[32,2176]{1,0:T(8,128)(2,1)}) custom-call(s32[4]{0:T(128)} %refs_0_.1, bf16[4,8,576]{2,1,0:T(8,128)(2,1)} %refs_1_.1, bf16[4,128,576]{2,1,0:T(8,128)(2,1)} %bitcast.21, bf16[4,576,384]{2,1,0:T(8,128)(2,1)} %bitcast.20, bf16[16,512,128]{2,1,0:T(8,128)(2,1)} %refs_4_.1, bf16[32,2048]{1,0:T(8,128)(2,1)} %refs_5_.1, ...), custom_call_target="tpu_custom_call" | custom-call | flops 494927872 | bytes 6291456 | tf_op jit(solution)/shard_map/pallas_call | solution.py:147
  5.6 3.7 %collective-permute-start = (bf16[32,2176]{1,0:T(8,128)(2,1)}, bf16[32,2176]{1,0:T(8,128)(2,1)S(1)}, u32[]{:S(2)}, u32[]{:S(2)}) collective-permute-start(bf16[32,2176]{1,0:T(8,128)(2,1)} %get-tuple-element.46.here), channel_id=1, source_target_pairs={{0,16},{1,17},{2,18},{3,19},{4,20},{5,21},{6,22},{7,23},{8,24},{9,... | collective-permute-start | bytes 417800 | tf_op jit(solution)/shard_map/ppermute | solution.py:18
  9.5 3.6 %shard_map.137 = (bf16[704,2048]{1,0:T(8,128)(2,1)S(1)}, bf16[704,2048]{1,0:T(8,128)(2,1)S(1)}, bf16[704,2048]{1,0:T(8,128)(2,1)S(1)}) custom-call(bf16[704,2048]{1,0:T(8,128)(2,1)} %bitcast.15, bf16[704,2048]{1,0:T(8,128)(2,1)} %bitcast.17, bf16[704,2048]{1,0:T(8,128)(2,1)} %bitcast.19), custom_call_target="tpu_custom_call" | custom-call | bytes 17301504 | tf_op jit(solution)/shard_map/pallas_call | solution.py:249
  13.1 3.8 %collective-permute-done.there = bf16[32,2176]{1,0:T(8,128)(2,1)S(1)} collective-permute-done((bf16[32,2176]{1,0:T(8,128)(2,1)}, bf16[32,2176]{1,0:T(8,128)(2,1)S(1)}, u32[]{:S(2)}, u32[]{:S(2)}) %collective-permute-start) | collective-permute-done | bytes 139296 | tf_op jit(solution)/shard_map/ppermute | solution.py:18
  16.8 0.7 %shard_map.138 = (bf16[128,448]{1,0:T(8,128)(2,1)S(1)}, bf16[128,448]{1,0:T(8,128)(2,1)S(1)}, bf16[56,1024]{1,0:T(8,128)(2,1)S(1)}, bf16[56,1024]{1,0:T(8,128)(2...) custom-call(f32[8,1]{1,0:T(8,128)S(1)} %copy.15.mine, ...), custom_call_target="tpu_custom_call" | custom-call | flops 117440512 | bytes 1572864 | tf_op jit(solution)/shard_map/pallas_call | solution.py:222
  17.5 1.9 %collective-permute-start.3 = (bf16[56,1024]{1,0:T(8,128)(2,1)S(1)}, bf16[56,1024]{1,0:T(8,128)(2,1)S(1)}, u32[]{:S(2)}, u32[]{:S(2)}) collective-permute-start(bf16[56,1024]{1,0:T(8,128)(2,1)S(1)} %get-tuple-element.57), channel_id=1, source_target_pairs={{0,12},{1,3},{2,14},{3,1},{4,8},{5,7},{6,10},{7,5},{8,4},{9,11},{1... | collective-permute-start | bytes 344072 | tf_op jit(solution)/shard_map/ppermute | solution.py:35
  19.4 2.2 %collective-permute-start.5 = (bf16[56,1024]{1,0:T(8,128)(2,1)S(1)}, bf16[56,1024]{1,0:T(8,128)(2,1)S(1)}, u32[]{:S(2)}, u32[]{:S(2)}) collective-permute-start(bf16[56,1024]{1,0:T(8,128)(2,1)S(1)} %get-tuple-element.59), channel_id=1, source_target_pairs={{0,10},{1,5},{2,8},{3,7},{4,14},{5,1},{6,12},{7,3},{8,2},{9,13},{1... | collective-permute-start | bytes 344072 | tf_op jit(solution)/shard_map/ppermute | solution.py:35
  21.6 0.7 %collective-permute-start.4 = (bf16[56,1024]{1,0:T(8,128)(2,1)S(1)}, bf16[56,1024]{1,0:T(8,128)(2,1)S(1)}, u32[]{:S(2)}, u32[]{:S(2)}) collective-permute-start(bf16[56,1024]{1,0:T(8,128)(2,1)S(1)} %get-tuple-element.58), channel_id=1, source_target_pairs={{0,14},{1,15},{2,12},{3,13},{4,10},{5,11},{6,8},{7,9},{8,6},{9,7},... | collective-permute-start | bytes 344072 | tf_op jit(solution)/shard_map/ppermute | solution.py:35
  22.3 2.5 %collective-permute-start.7 = (bf16[56,1024]{1,0:T(8,128)(2,1)S(1)}, bf16[56,1024]{1,0:T(8,128)(2,1)S(1)}, u32[]{:S(2)}, u32[]{:S(2)}) collective-permute-start(bf16[56,1024]{1,0:T(8,128)(2,1)S(1)} %get-tuple-element.62), channel_id=1, source_target_pairs={{0,6},{1,9},{2,4},{3,11},{4,2},{5,13},{6,0},{7,15},{8,14},{9,1},{1... | collective-permute-start | bytes 344072 | tf_op jit(solution)/shard_map/ppermute | solution.py:35
  24.7 1.3 %collective-permute-start.8 = (bf16[56,1024]{1,0:T(8,128)(2,1)S(1)}, bf16[56,1024]{1,0:T(8,128)(2,1)S(1)}, u32[]{:S(2)}, u32[]{:S(2)}) collective-permute-start(bf16[56,1024]{1,0:T(8,128)(2,1)S(1)} %get-tuple-element.63), channel_id=1, source_target_pairs={{0,8},{1,7},{2,10},{3,5},{4,12},{5,3},{6,14},{7,1},{8,0},{9,15},{1... | collective-permute-start | bytes 344072 | tf_op jit(solution)/shard_map/ppermute | solution.py:35
  26.0 0.5 collective-permute-start.9
  26.5 1.4 %collective-permute-done.5.refs_2_ = bf16[56,1024]{1,0:T(8,128)(2,1)S(1)} collective-permute-done((bf16[56,1024]{1,0:T(8,128)(2,1)S(1)}, bf16[56,1024]{1,0:T(8,128)(2,1)S(1)}, u32[]{:S(2)}, u32[]{:S(2)}) %collective-permute-start.5) | collective-permute-done | bytes 114720 | tf_op jit(solution)/shard_map/ppermute | solution.py:35
  27.9 2.7 %shard_map.139 = (bf16[704,2048]{1,0:T(8,128)(2,1)S(1)}, bf16[704,2048]{1,0:T(8,128)(2,1)S(1)}) custom-call(bf16[704,2048]{1,0:T(8,128)(2,1)} %collective-permute-done.2.refs_0_, bf16[704,2048]{1,0:T(8,128)(2,1)} %collective-permute-done.6.refs_1_), custom_call_target="tpu_custom_call" | custom-call | bytes 11534336 | tf_op jit(solution)/shard_map/pallas_call | solution.py:249
  30.7 1.0 %collective-permute-done.7.refs_3_ = bf16[56,1024]{1,0:T(8,128)(2,1)S(1)} collective-permute-done((bf16[56,1024]{1,0:T(8,128)(2,1)S(1)}, bf16[56,1024]{1,0:T(8,128)(2,1)S(1)}, u32[]{:S(2)}, u32[]{:S(2)}) %collective-permute-start.7) | collective-permute-done | bytes 114720 | tf_op jit(solution)/shard_map/ppermute | solution.py:35
  31.8 1.3 %collective-permute-done.9.refs_5_ = bf16[56,1024]{1,0:T(8,128)(2,1)S(1)} collective-permute-done((bf16[56,1024]{1,0:T(8,128)(2,1)S(1)}, bf16[56,1024]{1,0:T(8,128)(2,1)S(1)}, u32[]{:S(2)}, u32[]{:S(2)}) %collective-permute-start.9) | collective-permute-done | bytes 114720 | tf_op jit(solution)/shard_map/ppermute | solution.py:35
  33.1 4.9 %shard_map.140 = (bf16[56,1024]{1,0:T(8,128)(2,1)S(1)}, bf16[56,1024]{1,0:T(8,128)(2,1)S(1)}, bf16[56,1024]{1,0:T(8,128)(2,1)S(1)}, bf16[56,1024]{1,0:T(8,128)(2...) custom-call(bf16[56,1024]{1,0:T(8,128)(2,1)S(1)} %collective-permute, ...), custom_call_target="tpu_custom_call" | custom-call | flops 3875536896 | bytes 17301504 | tf_op jit(solution)/shard_map/pallas_call | solution.py:311
  38.0 1.4 %collective-permute-start.11 = (bf16[56,1024]{1,0:T(8,128)(2,1)S(1)}, bf16[56,1024]{1,0:T(8,128)(2,1)S(1)}, u32[]{:S(2)}, u32[]{:S(2)}) collective-permute-start(bf16[56,1024]{1,0:T(8,128)(2,1)S(1)} %get-tuple-element.75), channel_id=1, source_target_pairs={{0,12},{1,3},{2,14},{3,1},{4,8},{5,7},{6,10},{7,5},{8,4},{9,11},{1... | collective-permute-start | bytes 344072 | tf_op jit(solution)/shard_map/ppermute | solution.py:35
  39.4 1.8 %collective-permute-start.12 = (bf16[56,1024]{1,0:T(8,128)(2,1)S(1)}, bf16[56,1024]{1,0:T(8,128)(2,1)S(1)}, u32[]{:S(2)}, u32[]{:S(2)}) collective-permute-start(bf16[56,1024]{1,0:T(8,128)(2,1)S(1)} %get-tuple-element.76), channel_id=1, source_target_pairs={{0,14},{1,15},{2,12},{3,13},{4,10},{5,11},{6,8},{7,9},{8,6},{9,7},... | collective-permute-start | bytes 344072 | tf_op jit(solution)/shard_map/ppermute | solution.py:35
  41.3 2.0 %collective-permute-start.13 = (bf16[56,1024]{1,0:T(8,128)(2,1)S(1)}, bf16[56,1024]{1,0:T(8,128)(2,1)S(1)}, u32[]{:S(2)}, u32[]{:S(2)}) collective-permute-start(bf16[56,1024]{1,0:T(8,128)(2,1)S(1)} %get-tuple-element.77), channel_id=1, source_target_pairs={{0,10},{1,5},{2,8},{3,7},{4,14},{5,1},{6,12},{7,3},{8,2},{9,13},{1... | collective-permute-start | bytes 344072 | tf_op jit(solution)/shard_map/ppermute | solution.py:35
  43.3 0.7 %collective-permute-start.14 = (bf16[56,1024]{1,0:T(8,128)(2,1)S(1)}, bf16[56,1024]{1,0:T(8,128)(2,1)S(1)}, u32[]{:S(2)}, u32[]{:S(2)}) collective-permute-start(bf16[56,1024]{1,0:T(8,128)(2,1)S(1)} %get-tuple-element.78), channel_id=1, source_target_pairs={{0,6},{1,9},{2,4},{3,11},{4,2},{5,13},{6,0},{7,15},{8,14},{9,1},{1... | collective-permute-start | bytes 344072 | tf_op jit(solution)/shard_map/ppermute | solution.py:35
  44.1 1.1 %collective-permute-start.15 = (bf16[56,1024]{1,0:T(8,128)(2,1)S(1)}, bf16[56,1024]{1,0:T(8,128)(2,1)S(1)}, u32[]{:S(2)}, u32[]{:S(2)}) collective-permute-start(bf16[56,1024]{1,0:T(8,128)(2,1)S(1)} %get-tuple-element.79), channel_id=1, source_target_pairs={{0,8},{1,7},{2,10},{3,5},{4,12},{5,3},{6,14},{7,1},{8,0},{9,15},{1... | collective-permute-start | bytes 344072 | tf_op jit(solution)/shard_map/ppermute | solution.py:35
  45.2 1.5 %collective-permute-start.16 = (bf16[56,1024]{1,0:T(8,128)(2,1)S(1)}, bf16[56,1024]{1,0:T(8,128)(2,1)S(1)}, u32[]{:S(2)}, u32[]{:S(2)}) collective-permute-start(bf16[56,1024]{1,0:T(8,128)(2,1)S(1)} %get-tuple-element.80), channel_id=1, source_target_pairs={{0,2},{1,13},{2,0},{3,15},{4,6},{5,9},{6,4},{7,11},{8,10},{9,5},{1... | collective-permute-start | bytes 344072 | tf_op jit(solution)/shard_map/ppermute | solution.py:35
  46.7 1.1 %collective-permute-done.12.refs_1_ = bf16[56,1024]{1,0:T(8,128)(2,1)S(1)} collective-permute-done((bf16[56,1024]{1,0:T(8,128)(2,1)S(1)}, bf16[56,1024]{1,0:T(8,128)(2,1)S(1)}, u32[]{:S(2)}, u32[]{:S(2)}) %collective-permute-start.12) | collective-permute-done | bytes 114720 | tf_op jit(solution)/shard_map/ppermute | solution.py:35
  47.8 0.8 %collective-permute-start.17 = (bf16[56,1024]{1,0:T(8,128)(2,1)S(1)}, bf16[56,1024]{1,0:T(8,128)(2,1)S(1)}, u32[]{:S(2)}, u32[]{:S(2)}) collective-permute-start(bf16[56,1024]{1,0:T(8,128)(2,1)S(1)} %get-tuple-element.81), channel_id=1, source_target_pairs={{0,4},{1,11},{2,6},{3,9},{4,0},{5,15},{6,2},{7,13},{8,12},{9,3},{1... | collective-permute-start | bytes 344072 | tf_op jit(solution)/shard_map/ppermute | solution.py:35
  49.0 1.8 %collective-permute-done.14.refs_3_ = bf16[56,1024]{1,0:T(8,128)(2,1)S(1)} collective-permute-done((bf16[56,1024]{1,0:T(8,128)(2,1)S(1)}, bf16[56,1024]{1,0:T(8,128)(2,1)S(1)}, u32[]{:S(2)}, u32[]{:S(2)}) %collective-permute-start.14) | collective-permute-done | bytes 114720 | tf_op jit(solution)/shard_map/ppermute | solution.py:35
  50.8 0.6 collective-permute-done.15.refs_4_
  51.8 0.8 %collective-permute-done.17.refs_6_ = bf16[56,1024]{1,0:T(8,128)(2,1)S(1)} collective-permute-done((bf16[56,1024]{1,0:T(8,128)(2,1)S(1)}, bf16[56,1024]{1,0:T(8,128)(2,1)S(1)}, u32[]{:S(2)}, u32[]{:S(2)}) %collective-permute-start.17) | collective-permute-done | bytes 114720 | tf_op jit(solution)/shard_map/ppermute | solution.py:35
  53.0 3.2 %collective-permute-start.18 = (bf16[32,2048]{1,0:T(8,128)(2,1)S(1)}, bf16[32,2048]{1,0:T(8,128)(2,1)S(1)}, u32[]{:S(2)}, u32[]{:S(2)}) collective-permute-start(bf16[32,2048]{1,0:T(8,128)(2,1)S(1)} %get-tuple-element.84), channel_id=1, source_target_pairs={{0,16},{1,17},{2,18},{3,19},{4,20},{5,21},{6,22},{7,23},{8,24},{9,... | collective-permute-start | bytes 393224 | tf_op jit(solution)/shard_map/ppermute | solution.py:18
  56.2 4.4 %collective-permute-done.18 = bf16[32,2048]{1,0:T(8,128)(2,1)S(1)} collective-permute-done((bf16[32,2048]{1,0:T(8,128)(2,1)S(1)}, bf16[32,2048]{1,0:T(8,128)(2,1)S(1)}, u32[]{:S(2)}, u32[]{:S(2)}) %collective-permute-start.18) | collective-permute-done | bytes 131104 | tf_op jit(solution)/shard_map/ppermute | solution.py:18
  60.7 0.7 %add_convert_fusion = bf16[32,2048]{1,0:T(8,128)(2,1)} fusion(f32[32,2048]{1,0:T(8,128)S(1)} %get-tuple-element.83, bf16[32,2048]{1,0:T(8,128)(2,1)S(1)} %collective-permute-done.18), kind=kLoop, calls=%fused_computation | loop fusion | flops 196608 | bytes 524288 | tf_op jit(solution)/shard_map/convert_element_type | solution.py:399
  (23 shorter events, 1.6 us)
Async XLA Ops:
  0.0 9.4 %copy-start.2 = (s32[8]{0:T(128)S(1)}, s32[8]{0:T(128)}, u32[]{:S(2)}) copy-start(s32[8]{0:T(128)} %constant.34.clone) | copy-start | bytes 100
  0.0 9.4 %copy-start.3 = (s32[8]{0:T(128)S(1)}, s32[8]{0:T(128)}, u32[]{:S(2)}) copy-start(s32[8]{0:T(128)} %constant.33.clone) | copy-start | bytes 100
  0.0 16.8 %collective-permute-start.1 = (bf16[704,2048]{1,0:T(8,128)(2,1)}, bf16[704,2048]{1,0:T(8,128)(2,1)S(1)}, u32[]{:S(2)}, u32[]{:S(2)}) collective-permute-start(bf16[704,2048]{1,0:T(8,128)(2,1)} %bitcast.14), channel_id=1, source_target_pairs={{0,1},{1,0},{2,3},{3,2},{4,5},{5,4},{6,7},{7,6},{8,9},{9,8},{10,11... | collective-permute-start | bytes 8650760 | tf_op jit(solution)/shard_map/ppermute | solution.py:18
  0.5 16.4 %collective-permute-start.2 = (bf16[704,2048]{1,0:T(8,128)(2,1)}, bf16[704,2048]{1,0:T(8,128)(2,1)}, u32[]{:S(2)}, u32[]{:S(2)}) collective-permute-start(bf16[704,2048]{1,0:T(8,128)(2,1)} %bitcast.16), channel_id=1, source_target_pairs={{0,1},{1,0},{2,3},{3,2},{4,5},{5,4},{6,7},{7,6},{8,9},{9,8},{10,11... | collective-permute-start | bytes 8650760 | tf_op jit(solution)/shard_map/ppermute | solution.py:18
  0.5 24.2 %collective-permute-start.6 = (bf16[704,2048]{1,0:T(8,128)(2,1)}, bf16[704,2048]{1,0:T(8,128)(2,1)}, u32[]{:S(2)}, u32[]{:S(2)}) collective-permute-start(bf16[704,2048]{1,0:T(8,128)(2,1)} %bitcast.18), channel_id=1, source_target_pairs={{0,1},{1,0},{2,3},{3,2},{4,5},{5,4},{6,7},{7,6},{8,9},{9,8},{10,11... | collective-permute-start | bytes 8650760 | tf_op jit(solution)/shard_map/ppermute | solution.py:18
  5.6 11.2 %collective-permute-start = (bf16[32,2176]{1,0:T(8,128)(2,1)}, bf16[32,2176]{1,0:T(8,128)(2,1)S(1)}, u32[]{:S(2)}, u32[]{:S(2)}) collective-permute-start(bf16[32,2176]{1,0:T(8,128)(2,1)} %get-tuple-element.46.here), channel_id=1, source_target_pairs={{0,16},{1,17},{2,18},{3,19},{4,20},{5,21},{6,22},{7,23},{8,24},{9,... | collective-permute-start | bytes 417800 | tf_op jit(solution)/shard_map/ppermute | solution.py:18
  9.5 7.4 %copy-start.1 = (bf16[32,2176]{1,0:T(8,128)(2,1)S(1)}, bf16[32,2176]{1,0:T(8,128)(2,1)}, u32[]{:S(2)}) copy-start(bf16[32,2176]{1,0:T(8,128)(2,1)} %get-tuple-element.46.here) | copy-start | bytes 417796
  17.5 8.4 %collective-permute-start.3 = (bf16[56,1024]{1,0:T(8,128)(2,1)S(1)}, bf16[56,1024]{1,0:T(8,128)(2,1)S(1)}, u32[]{:S(2)}, u32[]{:S(2)}) collective-permute-start(bf16[56,1024]{1,0:T(8,128)(2,1)S(1)} %get-tuple-element.57), channel_id=1, source_target_pairs={{0,12},{1,3},{2,14},{3,1},{4,8},{5,7},{6,10},{7,5},{8,4},{9,11},{1... | collective-permute-start | bytes 344072 | tf_op jit(solution)/shard_map/ppermute | solution.py:35
  19.4 8.5 %collective-permute-start.5 = (bf16[56,1024]{1,0:T(8,128)(2,1)S(1)}, bf16[56,1024]{1,0:T(8,128)(2,1)S(1)}, u32[]{:S(2)}, u32[]{:S(2)}) collective-permute-start(bf16[56,1024]{1,0:T(8,128)(2,1)S(1)} %get-tuple-element.59), channel_id=1, source_target_pairs={{0,10},{1,5},{2,8},{3,7},{4,14},{5,1},{6,12},{7,3},{8,2},{9,13},{1... | collective-permute-start | bytes 344072 | tf_op jit(solution)/shard_map/ppermute | solution.py:35
  21.6 9.1 %collective-permute-start.4 = (bf16[56,1024]{1,0:T(8,128)(2,1)S(1)}, bf16[56,1024]{1,0:T(8,128)(2,1)S(1)}, u32[]{:S(2)}, u32[]{:S(2)}) collective-permute-start(bf16[56,1024]{1,0:T(8,128)(2,1)S(1)} %get-tuple-element.58), channel_id=1, source_target_pairs={{0,14},{1,15},{2,12},{3,13},{4,10},{5,11},{6,8},{7,9},{8,6},{9,7},... | collective-permute-start | bytes 344072 | tf_op jit(solution)/shard_map/ppermute | solution.py:35
  22.3 9.4 %collective-permute-start.7 = (bf16[56,1024]{1,0:T(8,128)(2,1)S(1)}, bf16[56,1024]{1,0:T(8,128)(2,1)S(1)}, u32[]{:S(2)}, u32[]{:S(2)}) collective-permute-start(bf16[56,1024]{1,0:T(8,128)(2,1)S(1)} %get-tuple-element.62), channel_id=1, source_target_pairs={{0,6},{1,9},{2,4},{3,11},{4,2},{5,13},{6,0},{7,15},{8,14},{9,1},{1... | collective-permute-start | bytes 344072 | tf_op jit(solution)/shard_map/ppermute | solution.py:35
  24.7 7.1 %collective-permute-start.8 = (bf16[56,1024]{1,0:T(8,128)(2,1)S(1)}, bf16[56,1024]{1,0:T(8,128)(2,1)S(1)}, u32[]{:S(2)}, u32[]{:S(2)}) collective-permute-start(bf16[56,1024]{1,0:T(8,128)(2,1)S(1)} %get-tuple-element.63), channel_id=1, source_target_pairs={{0,8},{1,7},{2,10},{3,5},{4,12},{5,3},{6,14},{7,1},{8,0},{9,15},{1... | collective-permute-start | bytes 344072 | tf_op jit(solution)/shard_map/ppermute | solution.py:35
  26.0 7.1 %collective-permute-start.9 = (bf16[56,1024]{1,0:T(8,128)(2,1)S(1)}, bf16[56,1024]{1,0:T(8,128)(2,1)S(1)}, u32[]{:S(2)}, u32[]{:S(2)}) collective-permute-start(bf16[56,1024]{1,0:T(8,128)(2,1)S(1)} %get-tuple-element.64), channel_id=1, source_target_pairs={{0,2},{1,13},{2,0},{3,15},{4,6},{5,9},{6,4},{7,11},{8,10},{9,5},{1... | collective-permute-start | bytes 344072 | tf_op jit(solution)/shard_map/ppermute | solution.py:35
  27.9 5.2 %collective-permute-start.10 = (bf16[56,1024]{1,0:T(8,128)(2,1)S(1)}, bf16[56,1024]{1,0:T(8,128)(2,1)S(1)}, u32[]{:S(2)}, u32[]{:S(2)}) collective-permute-start(bf16[56,1024]{1,0:T(8,128)(2,1)S(1)} %get-tuple-element.65), channel_id=1, source_target_pairs={{0,4},{1,11},{2,6},{3,9},{4,0},{5,15},{6,2},{7,13},{8,12},{9,3},{1... | collective-permute-start | bytes 344072 | tf_op jit(solution)/shard_map/ppermute | solution.py:35
  33.1 19.5 %copy-start = (f32[32,2048]{1,0:T(8,128)S(1)}, f32[32,2048]{1,0:T(8,128)}, u32[]{:S(2)}) copy-start(f32[32,2048]{1,0:T(8,128)} %get-tuple-element.56.stream) | copy-start | bytes 786436
  38.0 7.2 %collective-permute-start.11 = (bf16[56,1024]{1,0:T(8,128)(2,1)S(1)}, bf16[56,1024]{1,0:T(8,128)(2,1)S(1)}, u32[]{:S(2)}, u32[]{:S(2)}) collective-permute-start(bf16[56,1024]{1,0:T(8,128)(2,1)S(1)} %get-tuple-element.75), channel_id=1, source_target_pairs={{0,12},{1,3},{2,14},{3,1},{4,8},{5,7},{6,10},{7,5},{8,4},{9,11},{1... | collective-permute-start | bytes 344072 | tf_op jit(solution)/shard_map/ppermute | solution.py:35
  39.4 8.3 %collective-permute-start.12 = (bf16[56,1024]{1,0:T(8,128)(2,1)S(1)}, bf16[56,1024]{1,0:T(8,128)(2,1)S(1)}, u32[]{:S(2)}, u32[]{:S(2)}) collective-permute-start(bf16[56,1024]{1,0:T(8,128)(2,1)S(1)} %get-tuple-element.76), channel_id=1, source_target_pairs={{0,14},{1,15},{2,12},{3,13},{4,10},{5,11},{6,8},{7,9},{8,6},{9,7},... | collective-permute-start | bytes 344072 | tf_op jit(solution)/shard_map/ppermute | solution.py:35
  41.3 7.7 %collective-permute-start.13 = (bf16[56,1024]{1,0:T(8,128)(2,1)S(1)}, bf16[56,1024]{1,0:T(8,128)(2,1)S(1)}, u32[]{:S(2)}, u32[]{:S(2)}) collective-permute-start(bf16[56,1024]{1,0:T(8,128)(2,1)S(1)} %get-tuple-element.77), channel_id=1, source_target_pairs={{0,10},{1,5},{2,8},{3,7},{4,14},{5,1},{6,12},{7,3},{8,2},{9,13},{1... | collective-permute-start | bytes 344072 | tf_op jit(solution)/shard_map/ppermute | solution.py:35
  43.3 7.5 %collective-permute-start.14 = (bf16[56,1024]{1,0:T(8,128)(2,1)S(1)}, bf16[56,1024]{1,0:T(8,128)(2,1)S(1)}, u32[]{:S(2)}, u32[]{:S(2)}) collective-permute-start(bf16[56,1024]{1,0:T(8,128)(2,1)S(1)} %get-tuple-element.78), channel_id=1, source_target_pairs={{0,6},{1,9},{2,4},{3,11},{4,2},{5,13},{6,0},{7,15},{8,14},{9,1},{1... | collective-permute-start | bytes 344072 | tf_op jit(solution)/shard_map/ppermute | solution.py:35
  44.1 7.4 %collective-permute-start.15 = (bf16[56,1024]{1,0:T(8,128)(2,1)S(1)}, bf16[56,1024]{1,0:T(8,128)(2,1)S(1)}, u32[]{:S(2)}, u32[]{:S(2)}) collective-permute-start(bf16[56,1024]{1,0:T(8,128)(2,1)S(1)} %get-tuple-element.79), channel_id=1, source_target_pairs={{0,8},{1,7},{2,10},{3,5},{4,12},{5,3},{6,14},{7,1},{8,0},{9,15},{1... | collective-permute-start | bytes 344072 | tf_op jit(solution)/shard_map/ppermute | solution.py:35
  45.2 6.6 %collective-permute-start.16 = (bf16[56,1024]{1,0:T(8,128)(2,1)S(1)}, bf16[56,1024]{1,0:T(8,128)(2,1)S(1)}, u32[]{:S(2)}, u32[]{:S(2)}) collective-permute-start(bf16[56,1024]{1,0:T(8,128)(2,1)S(1)} %get-tuple-element.80), channel_id=1, source_target_pairs={{0,2},{1,13},{2,0},{3,15},{4,6},{5,9},{6,4},{7,11},{8,10},{9,5},{1... | collective-permute-start | bytes 344072 | tf_op jit(solution)/shard_map/ppermute | solution.py:35
  47.8 4.8 %collective-permute-start.17 = (bf16[56,1024]{1,0:T(8,128)(2,1)S(1)}, bf16[56,1024]{1,0:T(8,128)(2,1)S(1)}, u32[]{:S(2)}, u32[]{:S(2)}) collective-permute-start(bf16[56,1024]{1,0:T(8,128)(2,1)S(1)} %get-tuple-element.81), channel_id=1, source_target_pairs={{0,4},{1,11},{2,6},{3,9},{4,0},{5,15},{6,2},{7,13},{8,12},{9,3},{1... | collective-permute-start | bytes 344072 | tf_op jit(solution)/shard_map/ppermute | solution.py:35
  53.0 7.6 %collective-permute-start.18 = (bf16[32,2048]{1,0:T(8,128)(2,1)S(1)}, bf16[32,2048]{1,0:T(8,128)(2,1)S(1)}, u32[]{:S(2)}, u32[]{:S(2)}) collective-permute-start(bf16[32,2048]{1,0:T(8,128)(2,1)S(1)} %get-tuple-element.84), channel_id=1, source_target_pairs={{0,16},{1,17},{2,18},{3,19},{4,20},{5,21},{6,22},{7,23},{8,24},{9,... | collective-permute-start | bytes 393224 | tf_op jit(solution)/shard_map/ppermute | solution.py:18
